TPU v7x, 32 devices: a whole 2x2x4 slice. The times are simulated.
32 devices in a mesh: body: 4 (over y, core), blk: 8 (over z, x).
Axes of the slice: x: 2, y: 2, z: 4, core: 2. Of those that a mesh axis runs over, the one named last changes fastest.
Arguments:
- psi_init: float32 [16384, 320], P(('body', 'blk')), may hold values from -6 to 6
- source: float32 [16384, 320], P(('body', 'blk'))
- coupling: bfloat16 [16384, 6, 5, 320], P(('body', 'blk')), may hold values from -0.59765625 to 0.59765625
- diag_inv: bfloat16 [16384, 5, 320], P(('body', 'blk')), as said below
- neighbours: int32 [16384, 6], P(('body', 'blk')), may hold values from 0 to 527, as said below
- seam_perm: int32 [4, 8], P('body'), may hold values from 0 to 7, each once within a row
- fringe_src: int32 [32, 256], P(('body', 'blk')), may hold values from 0 to 511
- fringe_dst: int32 [32, 256], P(('body', 'blk')), may hold values from 0 to 511, as said below
- fringe_weight: float32 [32, 256], P(('body', 'blk')), may hold values from 0.2 to 1
Outputs:
- adjoint: float32 [16384, 320], P(('body', 'blk'))
- residual: float32 [16384, 320], P(('body', 'blk'))
Inputs may be any that keep to these rules, and one draw needn't show every extreme that they name: neighbours[i, m] - 8 - (i mod 512) lies in -8 .. 8. `fringe_dst`: every slot names a receiver block. `diag_inv`: each per-cell 5 x 5 matrix has a positive diagonal.
All inputs are finite; a program needn't handle non-finite values.
Results may differ from a plain program's by a relative error of at most 0.0003.
Values sent between devices are 32-bit elements; how exact they have to be, the bound alone decides.
No kernel may reach another device: no remote copies, remote signals or barrier semaphores. Data moves between devices by JAX's collectives and lax.ppermute only.
A program may use at most 128 MiB of HBM per device.

v0:
```python
import math

import jax
import jax.numpy as jnp
from jax import lax
from jax.sharding import PartitionSpec as P

CELLS = 64
VARS = 5
BW = 320
STEPS = 2


step_cfl = 0.5


def extended_2(value, sides, width):
    for axis, dim in sides:
        peers, length = (lax.axis_size(axis), value.shape[dim])
        up = [(i, (i + 1) % peers) for i in range(peers)]
        down = [(j, i) for i, j in up]
        last = lax.slice_in_dim(value, length - width, length, axis=dim)
        first = lax.slice_in_dim(value, 0, width, axis=dim)
        before = lax.ppermute(last, axis, up)
        after = lax.ppermute(first, axis, down)
        value = jnp.concatenate([before, value, after], axis=dim)
    return value


def rotate(block, sign):
    first = block[:, 2 * CELLS : 3 * CELLS]
    second = block[:, 3 * CELLS : 4 * CELLS]
    cosine = math.cos(2.0 * math.pi / 3.0)
    sine = sign * math.sin(2.0 * math.pi / 3.0)
    return jnp.concatenate(
        [
            block[:, : 2 * CELLS],
            cosine * first - sine * second,
            sine * first + cosine * second,
            block[:, 4 * CELLS :],
        ],
        axis=1,
    )


def shards(
    psi_init,
    source,
    coupling,
    diag_inv,
    neighbours,
    seam_perm,
    fringe_src,
    fringe_dst,
    fringe_weight,
):
    blocks = psi_init.shape[0]
    rim = seam_perm.shape[1]
    blk_index = lax.axis_index("blk")
    blk_last = lax.axis_size("blk") - 1
    body_count = lax.axis_size("body")
    blk_count = lax.axis_size("blk")
    total = blocks * body_count * blk_count * BW
    onehot = (seam_perm[0][:, None] == jnp.arange(rim, dtype=jnp.int32)[None, :]).astype(
        jnp.float32
    )
    table = (fringe_dst[0][None, :] == jnp.arange(blocks, dtype=jnp.int32)[:, None]).astype(
        jnp.float32
    ) * fringe_weight[0][None, :]
    donors = fringe_src[0]
    psi = psi_init
    resid = psi
    first_norm = None
    for step in range(STEPS):
        padded = extended_2(psi, (("blk", 0),), rim)
        lower = padded[:rim]
        upper = padded[blocks + rim :]
        seam_lo = rotate(jnp.dot(onehot, lower, precision=lax.Precision.HIGHEST), 1.0)
        seam_hi = rotate(jnp.dot(onehot.T, upper, precision=lax.Precision.HIGHEST), -1.0)
        lower = jnp.where(blk_index == 0, seam_lo, lower)
        upper = jnp.where(blk_index == blk_last, seam_hi, upper)
        extended = jnp.concatenate([lower, psi, upper], axis=0)
        outgoing = psi[donors]
        incoming = lax.all_to_all(
            outgoing, ("body", "blk"), split_axis=0, concat_axis=0, tiled=True
        )
        near = extended[neighbours]
        prod = coupling.astype(jnp.float32) * near[:, :, None, :]
        prod = jnp.sum(prod, axis=1).reshape(blocks, VARS, VARS, CELLS)
        coupled = jnp.sum(prod, axis=2).reshape(blocks, BW)
        fringe = jnp.dot(table, incoming, precision=lax.Precision.HIGHEST)
        resid = source - psi + coupled + fringe
        norm_now = lax.psum(jnp.sum(resid * resid), ("body", "blk")) / total + 1e-06
        if first_norm is None:
            first_norm = norm_now
        cfl = step_cfl * jnp.sqrt(first_norm / norm_now)
        prod = (diag_inv.astype(jnp.float32) * resid[:, None, :]).reshape(blocks, VARS, VARS, CELLS)
        update = jnp.sum(prod, axis=2).reshape(blocks, BW)
        psi = psi + cfl * update
    return (psi, resid)


def solution(mesh):
    return jax.shard_map(
        shards,
        mesh=mesh,
        in_specs=(
            P(("body", "blk"), None),
            P(("body", "blk"), None),
            P(("body", "blk"), None, None, None),
            P(("body", "blk"), None, None),
            P(("body", "blk"), None),
            P("body", None),
            P(("body", "blk"), None),
            P(("body", "blk"), None),
            P(("body", "blk"), None),
        ),
        out_specs=(P(("body", "blk"), None), P(("body", "blk"), None)),
        check_vma=False,
    )
```

profile of v0, /device:TPU:0, one launch (start us, length us, event | category | flops | bytes accessed | tf_op | source)
XLA Modules:
  0.0 205.9 jit_solution(11567935494582216725)
XLA Ops:
  0.6 1.4 copy.29
  2.0 3.0 %collective-permute-start = (f32[8,320]{1,0:T(8,128)S(1)}, f32[8,320]{1,0:T(8,128)S(1)}, u32[]{:S(2)}, u32[]{:S(2)}) collective-permute-start(f32[8,320]{1,0:T(8,128)S(1)} %get-tuple-element.8), channel_id=1, source_target_pairs={{0,1},{1,2},{2,3},{3,4},{4,5},{5,6},{6,7},{7,0},{8,9},{9,10},{10,1... | collective-permute-start | bytes 30728 | tf_op jit(solution)/shard_map/ppermute | solution.py:24
  5.0 3.1 %collective-permute-start.1 = (f32[8,320]{1,0:T(8,128)S(1)}, f32[8,320]{1,0:T(8,128)S(1)}, u32[]{:S(2)}, u32[]{:S(2)}) collective-permute-start(f32[8,320]{1,0:T(8,128)S(1)} %get-tuple-element.9), channel_id=1, source_target_pairs={{1,0},{2,1},{3,2},{4,3},{5,4},{6,5},{7,6},{0,7},{9,8},{10,9},{11,1... | collective-permute-start | bytes 30728 | tf_op jit(solution)/shard_map/ppermute | solution.py:25
  8.1 0.7 compare_select_fusion.1
  8.8 1.7 gather_fusion.1
  10.5 3.3 %all-to-all-start = ((f32[32,8,320]{2,1,0:T(8,128)}), f32[32,8,320]{2,1,0:T(8,128)S(1)}, u32[]{:S(2)}, u32[]{:S(2)}) async-start(f32[32,8,320]{2,1,0:T(8,128)} %bitcast.7), calls=%async_computation | async-start | bytes 786432 | tf_op jit(solution)/shard_map/all_to_all | solution.py:84
  15.0 12.6 %gather_fusion = f32[3072,320]{1,0:T(8,128)} fusion(f32[528,320]{1,0:T(8,128)S(1)} %pad_maximum_fusion, s32[3072]{0:T(1024)S(1)} %broadcast_clamp_fusion), kind=kCustom, calls=%fused_computation | custom fusion | bytes 7876608 | tf_op jit(solution)/shard_map/gather | solution.py:87
  27.7 6.5 %reshape.72 = f32[512,6,320]{2,1,0:T(8,128)} reshape(f32[3072,320]{1,0:T(8,128)} %gather_fusion) | data formatting | bytes 7864320 | tf_op jit(solution)/shard_map/gather | solution.py:87
  34.2 5.8 %copy.27 = f32[512,6,320]{0,2,1:T(8,128)} copy(f32[512,6,320]{2,1,0:T(8,128)} %reshape.72) | data formatting | bytes 7864320 | tf_op jit(solution)/shard_map/gather | solution.py:87
  40.0 9.0 %fusion = f32[512,5,320]{0,2,1:T(8,128)} fusion(bf16[512,6,5,320]{0,3,2,1:T(8,128)(2,1)} %param.11, f32[512,6,320]{0,2,1:T(8,128)} %copy.27), kind=kLoop, calls=%fused_computation.6 | loop fusion | flops 13926400 | bytes 17039360 | tf_op jit(solution)/shard_map/reduce_sum | solution.py:89
  49.0 3.2 %reduce_sum.73 = f32[512,5,64]{0,2,1:T(8,128)} reduce(f32[512,5,5,64]{0,3,2,1:T(8,128)} %bitcast.31, f32[]{:T(128)} %constant.8.clone.1), dimensions={2}, to_apply=%region_1.2 | reduce | flops 655360 | bytes 3932164 | tf_op jit(solution)/shard_map/reduce_sum | solution.py:90
  52.2 1.3 bitcast_add_fusion
  53.6 1.5 multiply_reduce_fusion.1
  55.1 40.7 %psum.14 = f32[]{:T(128)} all-reduce(f32[]{:T(128)} %get-tuple-element.22), channel_id=1, replica_groups=mesh['body'=4,'blk'=8] {'body','blk'}, use_global_device_ids=true, to_apply=%region_3.4 | all-reduce | flops 1 | bytes 8 | tf_op jit(solution)/shard_map/psum | solution.py:93
  96.5 3.6 %convert_multiply_fusion.3 = f32[512,5,320]{0,2,1:T(8,128)} fusion(bf16[512,5,320]{0,2,1:T(8,128)(2,1)} %param.12, f32[512,320]{0,1:T(8,128)S(1)} %get-tuple-element.23), kind=kLoop, calls=%fused_computation.9 | loop fusion | flops 1638400 | bytes 5570560 | tf_op jit(solution)/shard_map/mul | solution.py:97
  100.1 2.4 %reduce_sum.75 = f32[512,5,64]{0,2,1:T(8,128)S(1)} reduce(f32[512,5,5,64]{0,3,2,1:T(8,128)} %bitcast.32, f32[]{:T(128)} %constant.8.clone.1), dimensions={2}, to_apply=%region_4.5 | reduce | flops 655360 | bytes 3932164 | tf_op jit(solution)/shard_map/reduce_sum | solution.py:98
  102.9 2.3 %collective-permute-start.2 = (f32[8,320]{1,0:T(8,128)S(1)}, f32[8,320]{1,0:T(8,128)S(1)}, u32[]{:S(2)}, u32[]{:S(2)}) collective-permute-start(f32[8,320]{1,0:T(8,128)S(1)} %get-tuple-element.6), channel_id=1, source_target_pairs={{0,1},{1,2},{2,3},{3,4},{4,5},{5,6},{6,7},{7,0},{8,9},{9,10},{10,1... | collective-permute-start | bytes 30728 | tf_op jit(solution)/shard_map/ppermute | solution.py:24
  105.5 1.7 gather_fusion.3
  107.3 2.4 %collective-permute-start.3 = (f32[8,320]{1,0:T(8,128)S(1)}, f32[8,320]{1,0:T(8,128)S(1)}, u32[]{:S(2)}, u32[]{:S(2)}) collective-permute-start(f32[8,320]{1,0:T(8,128)S(1)} %get-tuple-element.7), channel_id=1, source_target_pairs={{1,0},{2,1},{3,2},{4,3},{5,4},{6,5},{7,6},{0,7},{9,8},{10,9},{11,1... | collective-permute-start | bytes 30728 | tf_op jit(solution)/shard_map/ppermute | solution.py:25
  109.7 3.5 %all-to-all-start.1 = ((f32[32,8,320]{2,1,0:T(8,128)}), f32[32,8,320]{2,1,0:T(8,128)}, u32[]{:S(2)}, u32[]{:S(2)}) async-start(f32[32,8,320]{2,1,0:T(8,128)} %bitcast.13), calls=%async_computation.1 | async-start | bytes 786432 | tf_op jit(solution)/shard_map/all_to_all | solution.py:84
  114.1 12.6 %gather_fusion.2 = f32[3072,320]{1,0:T(8,128)} fusion(f32[528,320]{1,0:T(8,128)S(1)} %pad_maximum_fusion.1, s32[3072]{0:T(1024)S(1)} %broadcast_clamp_fusion), kind=kCustom, calls=%fused_computation.2 | custom fusion | bytes 7876608 | tf_op jit(solution)/shard_map/gather | solution.py:87
  126.7 6.5 %reshape.88 = f32[512,6,320]{2,1,0:T(8,128)} reshape(f32[3072,320]{1,0:T(8,128)} %gather_fusion.2) | data formatting | bytes 7864320 | tf_op jit(solution)/shard_map/gather | solution.py:87
  133.2 5.8 %copy.32 = f32[512,6,320]{0,2,1:T(8,128)} copy(f32[512,6,320]{2,1,0:T(8,128)} %reshape.88) | data formatting | bytes 7864320 | tf_op jit(solution)/shard_map/gather | solution.py:87
  139.0 8.9 %fusion.1 = f32[512,5,320]{0,2,1:T(8,128)} fusion(bf16[512,6,5,320]{0,3,2,1:T(8,128)(2,1)} %param.11, f32[512,6,320]{0,2,1:T(8,128)} %copy.32), kind=kLoop, calls=%fused_computation.7 | loop fusion | flops 13926400 | bytes 17039360 | tf_op jit(solution)/shard_map/reduce_sum | solution.py:89
  147.9 3.3 %reduce_sum.77 = f32[512,5,64]{0,2,1:T(8,128)} reduce(f32[512,5,5,64]{0,3,2,1:T(8,128)} %bitcast.33, f32[]{:T(128)} %constant.8.clone.1), dimensions={2}, to_apply=%region_6.7 | reduce | flops 655360 | bytes 3932164 | tf_op jit(solution)/shard_map/reduce_sum | solution.py:90
  151.2 2.2 %copy.33 = f32[512,320]{1,0:T(8,128)} copy(f32[512,320]{0,1:T(8,128)} %bitcast.37) | data formatting | bytes 1310720 | tf_op jit(solution)/shard_map/reshape | solution.py:90
  153.5 3.8 %multiply_reduce_fusion = (f32[]{:T(128)}, f32[512,320]{1,0:T(8,128)}) fusion(f32[32,8,320]{2,1,0:T(8,128)} %all-to-all-done.1, f32[256]{0:T(256)S(1)} %bitcast.39, s32[256]{0:T(256)S(1)} %bitcast.41, f32[512,320]{1,0:T(8,128)} %copy.33, f32[512,320]{1,0:T(8,128)S(1)} %copy.31, f32[512,320]{1,0:T(8,128)S(1)} %add.62), kind=kOutput, calls=%fused_computation.14 | convolution fusion | flops 504397824 | bytes 2951172 | tf_op jit(solution)/shard_map/dot_general | solution.py:91
  157.3 40.4 %psum.15 = f32[]{:T(128)} all-reduce(f32[]{:T(128)} %get-tuple-element.24), channel_id=1, replica_groups=mesh['body'=4,'blk'=8] {'body','blk'}, use_global_device_ids=true, to_apply=%region_8.9 | all-reduce | flops 1 | bytes 8 | tf_op jit(solution)/shard_map/psum | solution.py:93
  198.4 1.4 copy.35
  199.9 2.2 %convert_multiply_fusion.2 = f32[512,5,320]{0,2,1:T(8,128)} fusion(bf16[512,5,320]{0,2,1:T(8,128)(2,1)S(1)} %copy-done, f32[512,320]{0,1:T(8,128)S(1)} %copy.35), kind=kLoop, calls=%fused_computation.8 | loop fusion | flops 1638400 | bytes 5570560 | tf_op jit(solution)/shard_map/mul | solution.py:97
  202.0 2.4 %reduce_sum.79 = f32[512,5,64]{0,2,1:T(8,128)S(1)} reduce(f32[512,5,5,64]{0,3,2,1:T(8,128)} %bitcast.34, f32[]{:T(128)} %constant.8.clone.1), dimensions={2}, to_apply=%region_9.10 | reduce | flops 655360 | bytes 3932164 | tf_op jit(solution)/shard_map/reduce_sum | solution.py:98
  204.8 1.1 copy.37
  (54 shorter events, 3.1 us)
Async XLA Ops:
  0.6 13.2 %copy-start.4 = (s32[512,6]{0,1:T(8,128)S(1)}, s32[512,6]{0,1:T(8,128)}, u32[]{:S(2)}) copy-start(s32[512,6]{0,1:T(8,128)} %param.13) | copy-start | bytes 36868
  0.6 13.6 %copy-start.7 = (s32[1,8]{1,0:T(1,128)S(1)}, s32[1,8]{1,0:T(1,128)}, u32[]{:S(2)}) copy-start(s32[1,8]{1,0:T(1,128)} %param.14) | copy-start | bytes 100
  2.0 12.2 %collective-permute-start = (f32[8,320]{1,0:T(8,128)S(1)}, f32[8,320]{1,0:T(8,128)S(1)}, u32[]{:S(2)}, u32[]{:S(2)}) collective-permute-start(f32[8,320]{1,0:T(8,128)S(1)} %get-tuple-element.8), channel_id=1, source_target_pairs={{0,1},{1,2},{2,3},{3,4},{4,5},{5,6},{6,7},{7,0},{8,9},{9,10},{10,1... | collective-permute-start | bytes 30728 | tf_op jit(solution)/shard_map/ppermute | solution.py:24
  5.0 9.5 %collective-permute-start.1 = (f32[8,320]{1,0:T(8,128)S(1)}, f32[8,320]{1,0:T(8,128)S(1)}, u32[]{:S(2)}, u32[]{:S(2)}) collective-permute-start(f32[8,320]{1,0:T(8,128)S(1)} %get-tuple-element.9), channel_id=1, source_target_pairs={{1,0},{2,1},{3,2},{4,3},{5,4},{6,5},{7,6},{0,7},{9,8},{10,9},{11,1... | collective-permute-start | bytes 30728 | tf_op jit(solution)/shard_map/ppermute | solution.py:25
  10.5 43.0 %all-to-all-start = ((f32[32,8,320]{2,1,0:T(8,128)}), f32[32,8,320]{2,1,0:T(8,128)S(1)}, u32[]{:S(2)}, u32[]{:S(2)}) async-start(f32[32,8,320]{2,1,0:T(8,128)} %bitcast.7), calls=%async_computation | async-start | bytes 786432 | tf_op jit(solution)/shard_map/all_to_all | solution.py:84
  40.0 12.2 %copy-start.1 = (f32[512,320]{0,1:T(8,128)S(1)}, f32[512,320]{0,1:T(8,128)}, u32[]{:S(2)}) copy-start(f32[512,320]{0,1:T(8,128)} %param.9) | copy-start | bytes 1966084
  40.0 12.2 %copy-start.2 = (f32[512,320]{0,1:T(8,128)S(1)}, f32[512,320]{0,1:T(8,128)}, u32[]{:S(2)}) copy-start(f32[512,320]{0,1:T(8,128)} %param.10) | copy-start | bytes 1966084
  49.0 4.5 %copy-start.5 = (f32[1,256]{1,0:T(1,128)S(1)}, f32[1,256]{1,0:T(1,128)}, u32[]{:S(2)}) copy-start(f32[1,256]{1,0:T(1,128)} %param.17) | copy-start | bytes 3076
  49.0 4.5 %copy-start.6 = (s32[1,256]{1,0:T(1,128)S(1)}, s32[1,256]{1,0:T(1,128)}, u32[]{:S(2)}) copy-start(s32[1,256]{1,0:T(1,128)} %param.16) | copy-start | bytes 3076
  102.9 10.3 %collective-permute-start.2 = (f32[8,320]{1,0:T(8,128)S(1)}, f32[8,320]{1,0:T(8,128)S(1)}, u32[]{:S(2)}, u32[]{:S(2)}) collective-permute-start(f32[8,320]{1,0:T(8,128)S(1)} %get-tuple-element.6), channel_id=1, source_target_pairs={{0,1},{1,2},{2,3},{3,4},{4,5},{5,6},{6,7},{7,0},{8,9},{9,10},{10,1... | collective-permute-start | bytes 30728 | tf_op jit(solution)/shard_map/ppermute | solution.py:24
  107.3 6.2 %collective-permute-start.3 = (f32[8,320]{1,0:T(8,128)S(1)}, f32[8,320]{1,0:T(8,128)S(1)}, u32[]{:S(2)}, u32[]{:S(2)}) collective-permute-start(f32[8,320]{1,0:T(8,128)S(1)} %get-tuple-element.7), channel_id=1, source_target_pairs={{1,0},{2,1},{3,2},{4,3},{5,4},{6,5},{7,6},{0,7},{9,8},{10,9},{11,1... | collective-permute-start | bytes 30728 | tf_op jit(solution)/shard_map/ppermute | solution.py:25
  109.7 43.8 %all-to-all-start.1 = ((f32[32,8,320]{2,1,0:T(8,128)}), f32[32,8,320]{2,1,0:T(8,128)}, u32[]{:S(2)}, u32[]{:S(2)}) async-start(f32[32,8,320]{2,1,0:T(8,128)} %bitcast.13), calls=%async_computation.1 | async-start | bytes 786432 | tf_op jit(solution)/shard_map/all_to_all | solution.py:84
  147.9 51.9 %copy-start = (bf16[512,5,320]{0,2,1:T(8,128)(2,1)S(1)}, bf16[512,5,320]{0,2,1:T(8,128)(2,1)}, u32[]{:S(2)}) copy-start(bf16[512,5,320]{0,2,1:T(8,128)(2,1)} %param.12) | copy-start | bytes 4915204
  199.8 2.2 %copy-start.3 = (f32[512,320]{0,1:T(8,128)}, f32[512,320]{0,1:T(8,128)S(1)}, u32[]{:S(2)}) copy-start(f32[512,320]{0,1:T(8,128)S(1)} %copy.35) | copy-start | bytes 1966084
where the time goes:
time: 207 us; the launch traced here: 206 us
  blocking collectives  81.1 us (39%)
  local copies, waits for them, and re-layouts  60.6 us (29%)
  other arithmetic  37.9 us (18%)
  starting transfers between devices  17.6 us (9%)
  matrix products  6.2 us (3%)
  between operations  2.38 us (1%)
    psum x2, blocking collectives, shards(): norm_now = lax.psum(jnp.sum(resid * resid), ('body', 'blk')) / total + 1e-06  81.1 us
    gather x6, local copies, waits for them, and re-layouts, shards(): near = extended[neighbours]  49.9 us
    reduce_sum x2, other arithmetic, shards(): prod = jnp.sum(prod, axis=1).reshape(blocks, VARS, VARS, CELLS)  17.9 us
    all_to_all x2, starting transfers between devices, shards(): lax.all_to_all(outgoing, ('body', 'blk'), split_axis=0, concat_axis=0, ti...  6.77 us
    reduce_sum x2, other arithmetic, shards(): coupled = jnp.sum(prod, axis=2).reshape(blocks, BW)  6.5 us
    mul x2, other arithmetic, shards(): diag_inv.astype(jnp.float32) * resid[:, None, :]  5.8 us
    ppermute x2, starting transfers between devices, extended_2(): after = lax.ppermute(first, axis, down)  5.55 us
    ppermute x2, starting transfers between devices, extended_2(): before = lax.ppermute(last, axis, up)  5.32 us
  transfers between devices with their start and end apart: 6, of which 0 were waited for; matrix products, arithmetic and copies ran while one was open for 41% of the time, Pallas kernels for 0%

commit v1 on v0

v1 whole, which is shorter than its diff:
```python
import functools
import math

import jax
import jax.numpy as jnp
from jax import lax
from jax.experimental import pallas as pl
from jax.experimental.pallas import tpu as pltpu
from jax.sharding import PartitionSpec as P

CELLS = 64
VARS = 5
BW = 320
STEP_CFL = 0.5
LANES = 128
PACK = 16
VMEM_LIMIT = 40 * 1024 * 1024


def split(x):
    high = x.astype(jnp.bfloat16)
    return high, (x - high.astype(jnp.float32)).astype(jnp.bfloat16)


def onehot(mask):
    return jnp.where(mask, 1.0, 0.0).astype(jnp.bfloat16)


def pick(x, table):
    high, low = split(x)
    return jnp.dot(high, table, preferred_element_type=jnp.float32) + jnp.dot(
        low, table, preferred_element_type=jnp.float32
    )


def send_blocks(x, src, perm_ref, out_ref, up_ref, down_ref):
    blocks = x.shape[1]
    slots = src.shape[1]
    rim = up_ref.shape[0]
    index = lax.axis_index("blk")
    at_last = index == lax.axis_size("blk") - 1
    at_first = index == 0
    rows = lax.broadcasted_iota(jnp.int32, (blocks, slots), 0)
    out_ref[...] = pick(x, onehot(rows == src)).T
    sub = lax.broadcasted_iota(jnp.int32, (LANES, LANES), 0)
    lane = lax.broadcasted_iota(jnp.int32, (LANES, LANES), 1)
    lane_row = lane[:1]
    sub_col = sub[:, :1]
    wanted = lane_row
    target = sub_col
    for j in range(rim):
        partner = perm_ref[0, j]
        wanted = jnp.where((lane_row == j) & at_last, partner, wanted)
        target = jnp.where((sub_col == j) & at_first, partner, target)
    to_up = (sub == wanted + (LANES - rim)) & (lane < rim)
    to_down = (target + rim == lane) & (sub < rim)
    rims = pick(x[:, blocks - LANES :], onehot(to_up)) + pick(x[:, :LANES], onehot(to_down))
    turn_up = (lane_row < rim) & at_last
    turn_down = (lane_row >= rim) & at_first
    angle = 2.0 * math.pi / 3.0
    cosine = jnp.where(turn_up | turn_down, math.cos(angle), 1.0)
    sine = jnp.where(turn_up, math.sin(angle), jnp.where(turn_down, -math.sin(angle), 0.0))
    first = rims[2 * CELLS : 3 * CELLS]
    second = rims[3 * CELLS : 4 * CELLS]
    rims = jnp.concatenate(
        [
            rims[: 2 * CELLS],
            cosine * first - sine * second,
            sine * first + cosine * second,
            rims[4 * CELLS :],
        ],
        axis=0,
    ).T
    up_ref[...] = rims[:rim]
    down_ref[...] = rims[rim : 2 * rim]


def donors_kernel(x_ref, src_ref, perm_ref, out_ref, up_ref, down_ref):
    send_blocks(x_ref[...], src_ref[...], perm_ref, out_ref, up_ref, down_ref)


def local_kernel(x_ref, lower_ref, upper_ref, nbr_ref, coup_ref, source_ref, out_ref, high, low, near):
    step = pl.program_id(0)
    blocks = x_ref.shape[1]
    rim = lower_ref.shape[0]
    slots = nbr_ref.shape[0]

    @pl.when(step == 0)
    def _():
        rims = jnp.concatenate(
            [lower_ref[...], upper_ref[...], jnp.zeros((LANES - 2 * rim, BW), jnp.float32)], axis=0
        ).T
        lane = lax.broadcasted_iota(jnp.int32, (BW, LANES), 1)
        moved = pltpu.roll(x_ref[...], rim, 1)
        head = jnp.where(lane < rim, rims, moved[:, :LANES])
        tail = jnp.where(lane < rim, moved[:, :LANES], jnp.where(lane < 2 * rim, rims, 0.0))
        ext = jnp.concatenate([head, moved[:, LANES:], tail], axis=1)
        high[...], low[...] = split(ext)

    start = pl.multiple_of(step * LANES, LANES)
    here = pl.ds(start, LANES)
    window = pl.ds(start, 2 * LANES)
    rows = lax.broadcasted_iota(jnp.int32, (2 * LANES, LANES), 0)
    table = jnp.concatenate(
        [onehot(rows == nbr_ref[m : m + 1, :] - start) for m in range(slots)], axis=1
    )
    near[...] = jnp.dot(high[:, window], table, preferred_element_type=jnp.float32) + jnp.dot(
        low[:, window], table, preferred_element_type=jnp.float32
    )

    def cells(part, carry):
        at = pl.multiple_of(part * PACK, PACK)
        total = [None] * VARS
        for m in range(slots):
            for v in range(VARS):
                value = near[pl.ds(v * CELLS + at, PACK), m * LANES : (m + 1) * LANES]
                for u in range(VARS):
                    term = coup_ref[m, u, pl.ds(v * CELLS + at, PACK), :].astype(jnp.float32) * value
                    total[u] = term if total[u] is None else total[u] + term
        for u in range(VARS):
            span = pl.ds(u * CELLS + at, PACK)
            out_ref[span, :] = source_ref[span, :] - x_ref[span, here] + total[u]
        return carry

    lax.fori_loop(0, CELLS // PACK, cells, 0)


def fringe_residual(local_ref, inc_ref, dst_ref, weight_ref):
    blocks = local_ref.shape[1]
    slots = inc_ref.shape[0]
    rows = lax.broadcasted_iota(jnp.int32, (blocks, slots), 0)
    table = onehot(rows == dst_ref[...])
    high, low = split(inc_ref[...].T * weight_ref[...])
    contract = (((1,), (1,)), ((), ()))
    return (
        local_ref[...]
        + lax.dot_general(high, table, contract, preferred_element_type=jnp.float32)
        + lax.dot_general(low, table, contract, preferred_element_type=jnp.float32)
    )


def precondition(diag_ref, resid_ref, u, at):
    total = None
    for v in range(VARS):
        span = pl.ds(v * CELLS + at, PACK)
        term = diag_ref[u, span, :].astype(jnp.float32) * resid_ref[span, :]
        total = term if total is None else total + term
    return total


def lane_sums(resid):
    square = jnp.sum(resid * resid, axis=0, keepdims=True)
    return sum(square[:, i : i + LANES] for i in range(0, square.shape[1], LANES))


def advance_kernel(
    local_ref, inc_ref, dst_ref, weight_ref, diag_ref, x_ref, src_ref, perm_ref,
    next_ref, norm_ref, out_ref, up_ref, down_ref, resid,
):
    resid[...] = fringe_residual(local_ref, inc_ref, dst_ref, weight_ref)
    norm_ref[...] = lane_sums(resid[...])

    def cells(part, carry):
        at = pl.multiple_of(part * PACK, PACK)
        for u in range(VARS):
            span = pl.ds(u * CELLS + at, PACK)
            next_ref[span, :] = x_ref[span, :] + STEP_CFL * precondition(diag_ref, resid, u, at)
        return carry

    lax.fori_loop(0, CELLS // PACK, cells, 0)
    send_blocks(next_ref[...], src_ref[...], perm_ref, out_ref, up_ref, down_ref)


def residual_kernel(local_ref, inc_ref, dst_ref, weight_ref, norm_ref, resid_ref, sums_ref):
    resid = fringe_residual(local_ref, inc_ref, dst_ref, weight_ref)
    resid_ref[...] = resid
    both = jnp.concatenate([norm_ref[...], lane_sums(resid)], axis=0)
    sums_ref[...] = jnp.broadcast_to(both[None], sums_ref.shape)


def direction_kernel(diag_ref, resid_ref, out_ref):
    def cells(part, carry):
        at = pl.multiple_of(part * PACK, PACK)
        for u in range(VARS):
            out_ref[pl.ds(u * CELLS + at, PACK), :] = precondition(diag_ref, resid_ref, u, at)
        return carry

    lax.fori_loop(0, CELLS // PACK, cells, 0)


def finish_kernel(entries, sums_ref, x_ref, update_ref, out_ref):
    sums = jnp.sum(jnp.sum(sums_ref[...], axis=0), axis=1, keepdims=True) / entries + 1e-06
    cfl = STEP_CFL * jnp.sqrt(sums[0:1] / sums[1:2])
    out_ref[...] = x_ref[...] + cfl * update_ref[...]


VMEM = pl.BlockSpec(memory_space=pltpu.VMEM)
SMEM = pl.BlockSpec(memory_space=pltpu.SMEM)


def f32(*shape):
    return jax.ShapeDtypeStruct(shape, jnp.float32)


def call(kernel, in_specs, out_shape, flops, moved, **more):
    many = isinstance(out_shape, (list, tuple))
    return pl.pallas_call(
        kernel,
        in_specs=in_specs,
        out_specs=more.pop("out_specs", [VMEM] * len(out_shape) if many else VMEM),
        out_shape=out_shape,
        compiler_params=pltpu.CompilerParams(vmem_limit_bytes=VMEM_LIMIT),
        cost_estimate=pl.CostEstimate(flops=flops, bytes_accessed=moved, transcendentals=0),
        **more,
    )


def shards(
    psi_init, source, coupling, diag_inv, neighbours, seam_perm, fringe_src, fringe_dst, fringe_weight
):
    blocks = psi_init.shape[0]
    slots = neighbours.shape[1]
    rim = seam_perm.shape[1]
    fringe = fringe_src.shape[1]
    peers = lax.axis_size("blk")
    devices = lax.axis_size("body") * peers
    up = [(i, (i + 1) % peers) for i in range(peers)]
    down = [(j, i) for i, j in up]
    x = psi_init.T
    source_t = source.T
    coup = coupling.transpose(1, 2, 3, 0)
    diag = diag_inv.transpose(1, 2, 0)
    nbr = neighbours.T
    state = f32(BW, blocks)
    sent = [f32(fringe, BW), f32(rim, BW), f32(rim, BW)]
    size = 4 * BW * blocks

    donors = call(donors_kernel, [VMEM, VMEM, SMEM], sent, 4 * BW * blocks * fringe, 2 * size)
    local = call(
        local_kernel,
        [
            pl.BlockSpec((BW, blocks), lambda i: (0, 0)),
            pl.BlockSpec((rim, BW), lambda i: (0, 0)),
            pl.BlockSpec((rim, BW), lambda i: (0, 0)),
            pl.BlockSpec((slots, LANES), lambda i: (0, i)),
            pl.BlockSpec((slots, VARS, BW, LANES), lambda i: (0, 0, 0, i)),
            pl.BlockSpec((BW, LANES), lambda i: (0, i)),
        ],
        state,
        4 * BW * 2 * LANES * slots * blocks,
        coup.size * 2 + 4 * size,
        grid=(blocks // LANES,),
        out_specs=pl.BlockSpec((BW, LANES), lambda i: (0, i)),
        scratch_shapes=[
            pltpu.VMEM((BW, blocks + LANES), jnp.bfloat16),
            pltpu.VMEM((BW, blocks + LANES), jnp.bfloat16),
            pltpu.VMEM((BW, slots * LANES), jnp.float32),
        ],
    )
    advance = call(
        advance_kernel,
        [VMEM] * 7 + [SMEM],
        [state, f32(1, LANES)] + sent,
        8 * BW * blocks * fringe,
        diag.size * 2 + 4 * size,
        scratch_shapes=[pltpu.VMEM((BW, blocks), jnp.float32)],
    )
    residual = call(
        residual_kernel,
        [VMEM] * 5,
        [state, f32(devices, 2, LANES)],
        4 * BW * blocks * fringe,
        3 * size,
    )
    direction = call(direction_kernel, [VMEM] * 2, state, diag.size * 2, diag.size * 2 + 2 * size)
    finish = call(
        functools.partial(finish_kernel, float(blocks * devices * BW)),
        [VMEM] * 3,
        state,
        2 * BW * blocks,
        3 * size,
    )

    def exchange(rows, to_up, to_down):
        rows = lax.all_to_all(rows, ("body", "blk"), split_axis=0, concat_axis=0, tiled=True)
        return rows, lax.ppermute(to_up, "blk", up), lax.ppermute(to_down, "blk", down)

    incoming, lower, upper = exchange(*donors(x, fringe_src, seam_perm))
    part = local(x, lower, upper, nbr, coup, source_t)
    x, norm, *out = advance(part, incoming, fringe_dst, fringe_weight, diag, x, fringe_src, seam_perm)
    incoming, lower, upper = exchange(*out)
    part = local(x, lower, upper, nbr, coup, source_t)
    resid, sums = residual(part, incoming, fringe_dst, fringe_weight, norm)
    sums = lax.all_to_all(sums, ("body", "blk"), split_axis=0, concat_axis=0, tiled=True)
    x = finish(sums, x, direction(diag, resid))
    return (x.T, resid.T)


def solution(mesh):
    return jax.shard_map(
        shards,
        mesh=mesh,
        in_specs=(
            P(("body", "blk"), None),
            P(("body", "blk"), None),
            P(("body", "blk"), None, None, None),
            P(("body", "blk"), None, None),
            P(("body", "blk"), None),
            P("body", None),
            P(("body", "blk"), None),
            P(("body", "blk"), None),
            P(("body", "blk"), None),
        ),
        out_specs=(P(("body", "blk"), None), P(("body", "blk"), None)),
        check_vma=False,
    )
```

time: 207 us -> 85.6 us (0.41)
  blocking collectives: 81.1 us -> 0 us
  local copies, waits for them, and re-layouts: 60.6 us -> 20.5 us
  other arithmetic: 37.9 us -> 0 us
  waiting for transfers between devices: 0.02 us -> 20.6 us
  Pallas kernels: 0 us -> 20.1 us
  matrix products: 6.2 us -> 0 us
  starting transfers between devices: 17.6 us -> 22.8 us
    psum x2 -> x0, blocking collectives: 81.1 us -> none  [shards(): norm_now = lax.psum(jnp.sum(resid * resid), ('body', 'blk')) / total + 1e-06]
    gather x8 -> x0, local copies, waits for them, and re-layouts: 53.4 us -> none  [the longest x6 49.9 us: shards(): near = extended[neighbours]]
    reduce_sum x6 -> x0, other arithmetic: 29.1 us -> none  [the longest x2 17.9 us: shards(): prod = jnp.sum(prod, axis=1).reshape(blocks, VARS, VARS, CELLS)]
    pallas_call x0 -> x7, Pallas kernels: none -> 20.1 us  [the longest x2 13.5 us: shards(): part = local(x, lower, upper, nbr, coup, source_t)]
    unnamed x19 -> x48, local copies, waits for them, and re-layouts: 2.75 us -> 20.5 us
    ppermute x4, waiting for transfers between devices: 0.01 us -> 14.9 us  [the longest x2 14.9 us: exchange(): lax.ppermute(to_up, 'blk', up)]
    all_to_all x2 -> x3, starting transfers between devices: 6.77 us -> 13.3 us  [the longest x2 10.3 us: exchange(): lax.all_to_all(rows, ('body', 'blk'), split_axis=0, concat_axis=0, tiled=...]
    dot_general x6 -> x0, matrix products: 6.2 us -> none  [the longest x2 5.31 us: shards(): fringe = jnp.dot(table, incoming, precision=lax.Precision.HIGHEST)]
  transfers between devices with their start and end apart: 6 -> 7, of which waited for: 0 -> 3; matrix products, arithmetic and copies ran while one was open for 41% -> 0% of each run, Pallas kernels for 0% -> 16%
where the time goes in v1:
time: 85.6 us; the launch traced here: 84.9 us
  starting transfers between devices  22.8 us (27%)
  waiting for transfers between devices  20.6 us (24%)
  local copies, waits for them, and re-layouts  20.5 us (24%)
  Pallas kernels  20.1 us (23%)
    unnamed x48, local copies, waits for them, and re-layouts  20.5 us
    ppermute x2, waiting for transfers between devices, exchange(): lax.ppermute(to_up, 'blk', up)  14.9 us
    pallas_call x2, Pallas kernels, shards(): part = local(x, lower, upper, nbr, coup, source_t)  13.5 us
    all_to_all x2, starting transfers between devices, exchange(): lax.all_to_all(rows, ('body', 'blk'), split_axis=0, concat_axis=0, tiled=...  10.3 us
    ppermute x2, starting transfers between devices, exchange(): lax.ppermute(to_down, 'blk', down)  5.91 us
    all_to_all x1, waiting for transfers between devices, shards(): lax.all_to_all(sums, ('body', 'blk'), split_axis=0, concat_axis=0, tiled=...  5.75 us
    ppermute x2, starting transfers between devices, exchange(): lax.ppermute(to_up, 'blk', up)  3.64 us
    all_to_all x1, starting transfers between devices, shards(): lax.all_to_all(sums, ('body', 'blk'), split_axis=0, concat_axis=0, tiled=...  2.97 us
  transfers between devices with their start and end apart: 7, of which 3 were waited for; matrix products, arithmetic and copies ran while one was open for 0% of the time, Pallas kernels for 16%

profile of v1, /device:TPU:0, one launch (start us, length us, event | category | flops | bytes accessed | tf_op | source)
XLA Modules:
  0.0 84.9 jit_solution(13604376639281652480)
XLA Ops:
  0.7 1.1 %copy-done.3 = f32[512,320]{0,1:T(8,128)S(1)} copy-done((f32[512,320]{0,1:T(8,128)S(1)}, f32[512,320]{0,1:T(8,128)}, u32[]{:S(2)}) %copy-start.3) | copy-done | bytes 655384
  1.8 0.7 copy-done.18
  2.4 0.7 copy-done.22
  3.1 1.9 %shard_map.104 = (f32[256,320]{1,0:T(8,128)}, f32[8,320]{1,0:T(8,128)S(1)}, f32[8,320]{1,0:T(8,128)S(1)}) custom-call(f32[320,512]{1,0:T(8,128)S(1)} %bitcast.15, s32[1,256]{1,0:T(1,128)S(1)} %copy-done.18, s32[1,8]{1,0:T(1,128)S(1)} %copy-done.22), custom_call_target="tpu_custom_call" | custom-call | flops 167772160 | bytes 1310720 | tf_op jit(solution)/shard_map/pallas_call | solution.py:288
  5.0 7.3 %all-to-all-start = ((f32[32,8,320]{2,1,0:T(8,128)}), f32[32,8,320]{2,1,0:T(8,128)S(1)}, u32[]{:S(2)}, u32[]{:S(2)}) async-start(f32[32,8,320]{2,1,0:T(8,128)} %bitcast.4), calls=%async_computation | async-start | bytes 786432 | tf_op jit(solution)/shard_map/all_to_all | solution.py:285
  12.3 1.8 %collective-permute-start = (f32[8,320]{1,0:T(8,128)S(1)}, f32[8,320]{1,0:T(8,128)S(1)}, u32[]{:S(2)}, u32[]{:S(2)}) collective-permute-start(f32[8,320]{1,0:T(8,128)S(1)} %get-tuple-element.12), channel_id=1, source_target_pairs={{0,1},{1,2},{2,3},{3,4},{4,5},{5,6},{6,7},{7,0},{8,9},{9,10},{10,1... | collective-permute-start | bytes 30728 | tf_op jit(solution)/shard_map/ppermute | solution.py:286
  14.1 3.0 %collective-permute-start.1 = (f32[8,320]{1,0:T(8,128)S(1)}, f32[8,320]{1,0:T(8,128)S(1)}, u32[]{:S(2)}, u32[]{:S(2)}) collective-permute-start(f32[8,320]{1,0:T(8,128)S(1)} %get-tuple-element.13), channel_id=1, source_target_pairs={{1,0},{2,1},{3,2},{4,3},{5,4},{6,5},{7,6},{0,7},{9,8},{10,9},{11,1... | collective-permute-start | bytes 30728 | tf_op jit(solution)/shard_map/ppermute | solution.py:286
  17.1 7.4 %collective-permute-done.lower_ref = f32[8,320]{1,0:T(8,128)S(1)} collective-permute-done((f32[8,320]{1,0:T(8,128)S(1)}, f32[8,320]{1,0:T(8,128)S(1)}, u32[]{:S(2)}, u32[]{:S(2)}) %collective-permute-start) | collective-permute-done | bytes 10272 | tf_op jit(solution)/shard_map/ppermute | solution.py:286
  24.5 3.8 %copy-done = bf16[512,6,5,320]{0,3,2,1:T(8,128)(2,1)S(1)} copy-done((bf16[512,6,5,320]{0,3,2,1:T(8,128)(2,1)S(1)}, bf16[512,6,5,320]{0,3,2,1:T(8,128)(2,1)}, u32[]{:S(2)}) %copy-start) | copy-done | bytes 9830424
  28.3 1.1 %copy-done.4 = f32[512,320]{0,1:T(8,128)S(1)} copy-done((f32[512,320]{0,1:T(8,128)S(1)}, f32[512,320]{0,1:T(8,128)}, u32[]{:S(2)}) %copy-start.4) | copy-done | bytes 655384
  29.4 1.1 %copy-done.6 = f32[512,320]{0,1:T(8,128)S(1)} copy-done((f32[512,320]{0,1:T(8,128)S(1)}, f32[512,320]{0,1:T(8,128)}, u32[]{:S(2)}) %copy-start.6) | copy-done | bytes 655384
  30.5 0.7 copy-done.16
  31.2 6.8 %shard_map.105.local_ref = f32[320,512]{1,0:T(8,128)S(1)} custom-call(f32[320,512]{1,0:T(8,128)S(1)} %bitcast.16, f32[8,320]{1,0:T(8,128)S(1)} %collective-permute-done.lower_ref, f32[8,320]{1,0:T(8,128)S(1)} %collective-permute-done.1.upper_ref, s32[6,512]{1,0:T(8,128)S(1)} %bitcast.24, bf16[6,5,320,512]{3,2,1,0:T(8,128)(2,1)S(1)} %bitcast.11, ...), custom_call_target="tpu_custom_call" | custom-call | flops 1006632960 | bytes 12451840 | tf_op jit(solution)/shard_map/pallas_call | solution.py:289
  38.0 0.8 copy-done.10
  38.9 1.1 %copy-done.11 = f32[320,512]{1,0:T(8,128)S(1)} copy-done((f32[320,512]{1,0:T(8,128)S(1)}, f32[320,512]{1,0:T(8,128)}, u32[]{:S(2)}) %copy-start.11) | copy-done | bytes 655384
  39.9 2.0 %shard_map.106 = (f32[320,512]{1,0:T(8,128)S(1)}, f32[1,128]{1,0:T(1,128)S(1)}, f32[256,320]{1,0:T(8,128)S(1)}, f32[8,320]{1,0:T(8,128)S(1)}, f32[8,320]{1,0:T(8,128)S(1)}) custom-call(f32[320,512]{1,0:T(8,128)S(1)} %copy-done.11, f32[256,320]{1,0:T(8,128)S(1)} %bitcast.20, s32[1,256]{1,0:T(1,128)S(1)} %copy-done.20, f32[1,256]{1,0:T(1,128)S(1)} %copy-done.21, ...), custom_call_target="tpu_custom_call" | custom-call | flops 335544320 | bytes 4259840 | tf_op jit(solution)/shard_map/pallas_call | solution.py:290
  42.0 0.8 copy-done.8
  42.8 0.7 copy-done.15
  43.5 3.0 %all-to-all-start.1 = ((f32[32,8,320]{2,1,0:T(8,128)}), f32[32,8,320]{2,1,0:T(8,128)S(1)}, u32[]{:S(2)}, u32[]{:S(2)}) async-start(f32[32,8,320]{2,1,0:T(8,128)} %bitcast.23), calls=%async_computation.1 | async-start | bytes 786432 | tf_op jit(solution)/shard_map/all_to_all | solution.py:285
  46.5 1.8 %collective-permute-start.2 = (f32[8,320]{1,0:T(8,128)S(1)}, f32[8,320]{1,0:T(8,128)S(1)}, u32[]{:S(2)}, u32[]{:S(2)}) collective-permute-start(f32[8,320]{1,0:T(8,128)S(1)} %get-tuple-element.16), channel_id=1, source_target_pairs={{0,1},{1,2},{2,3},{3,4},{4,5},{5,6},{6,7},{7,0},{8,9},{9,10},{10,1... | collective-permute-start | bytes 30728 | tf_op jit(solution)/shard_map/ppermute | solution.py:286
  48.4 3.0 %collective-permute-start.3 = (f32[8,320]{1,0:T(8,128)S(1)}, f32[8,320]{1,0:T(8,128)S(1)}, u32[]{:S(2)}, u32[]{:S(2)}) collective-permute-start(f32[8,320]{1,0:T(8,128)S(1)} %get-tuple-element.17), channel_id=1, source_target_pairs={{1,0},{2,1},{3,2},{4,3},{5,4},{6,5},{7,6},{0,7},{9,8},{10,9},{11,1... | collective-permute-start | bytes 30728 | tf_op jit(solution)/shard_map/ppermute | solution.py:286
  51.3 7.4 %collective-permute-done.2.lower_ref = f32[8,320]{1,0:T(8,128)S(1)} collective-permute-done((f32[8,320]{1,0:T(8,128)S(1)}, f32[8,320]{1,0:T(8,128)S(1)}, u32[]{:S(2)}, u32[]{:S(2)}) %collective-permute-start.2) | collective-permute-done | bytes 10272 | tf_op jit(solution)/shard_map/ppermute | solution.py:286
  58.8 3.8 %copy-done.1 = bf16[512,6,5,320]{0,3,2,1:T(8,128)(2,1)S(1)} copy-done((bf16[512,6,5,320]{0,3,2,1:T(8,128)(2,1)S(1)}, bf16[512,6,5,320]{0,3,2,1:T(8,128)(2,1)}, u32[]{:S(2)}) %copy-start.1) | copy-done | bytes 9830424
  62.6 1.1 %copy-done.9 = f32[320,512]{1,0:T(8,128)S(1)} copy-done((f32[320,512]{1,0:T(8,128)S(1)}, f32[320,512]{1,0:T(8,128)}, u32[]{:S(2)}) %copy-start.9) | copy-done | bytes 655384
  63.6 6.8 %shard_map.107.local_ref = f32[320,512]{1,0:T(8,128)S(1)} custom-call(f32[320,512]{1,0:T(8,128)S(1)} %copy-done.9, f32[8,320]{1,0:T(8,128)S(1)} %collective-permute-done.2.lower_ref, f32[8,320]{1,0:T(8,128)S(1)} %collective-permute-done.3.upper_ref, s32[6,512]{1,0:T(8,128)S(1)} %bitcast.25, bf16[6,5,320,512]{3,2,1,0:T(8,128)(2,1)S(1)} %bitcast.12, ...), custom_call_target="tpu_custom_call" | custom-call | flops 1006632960 | bytes 12451840 | tf_op jit(solution)/shard_map/pallas_call | solution.py:292
  70.4 0.8 copy-done.12
  71.3 1.1 %copy-done.13 = f32[320,512]{1,0:T(8,128)S(1)} copy-done((f32[320,512]{1,0:T(8,128)S(1)}, f32[320,512]{1,0:T(8,128)}, u32[]{:S(2)}) %copy-start.13) | copy-done | bytes 655384
  72.3 1.2 %shard_map.108 = (f32[320,512]{1,0:T(8,128)}, f32[32,2,128]{2,1,0:T(2,128)}) custom-call(f32[320,512]{1,0:T(8,128)S(1)} %copy-done.13, f32[256,320]{1,0:T(8,128)S(1)} %bitcast.21, s32[1,256]{1,0:T(1,128)S(1)} %copy-done.20, f32[1,256]{1,0:T(1,128)S(1)} %copy-done.21, f32[1,128]{1,0:T(1,128)S(1)} %get-tuple-element.19.norm_ref), custom_call_target="tpu_custom_call" | custom-call | flops 167772160 | bytes 1966080 | tf_op jit(solution)/shard_map/pallas_call | solution.py:293
  73.6 3.0 %all-to-all-start.2 = ((f32[32,2,128]{2,1,0:T(2,128)}), f32[32,2,128]{2,1,0:T(2,128)S(1)}, u32[]{:S(2)}, u32[]{:S(2)}) async-start(f32[32,2,128]{2,1,0:T(2,128)} %get-tuple-element.20), calls=%async_computation.2 | async-start | bytes 65536 | tf_op jit(solution)/shard_map/all_to_all | solution.py:294
  76.6 1.1 %copy-done.14 = f32[320,512]{1,0:T(8,128)S(1)} copy-done((f32[320,512]{1,0:T(8,128)S(1)}, f32[320,512]{1,0:T(8,128)}, u32[]{:S(2)}) %copy-start.14) | copy-done | bytes 655384
  78.0 5.7 %all-to-all-done.2.sums_ref = f32[32,2,128]{2,1,0:T(2,128)S(1)} async-done(((f32[32,2,128]{2,1,0:T(2,128)}), f32[32,2,128]{2,1,0:T(2,128)S(1)}, u32[]{:S(2)}, u32[]{:S(2)}) %all-to-all-start.2) | async-done | bytes 32800 | tf_op jit(solution)/shard_map/all_to_all | solution.py:294
  83.8 1.1 %shard_map.110 = f32[320,512]{1,0:T(8,128)} custom-call(f32[32,2,128]{2,1,0:T(2,128)S(1)} %all-to-all-done.2.sums_ref, f32[320,512]{1,0:T(8,128)S(1)} %copy-done.9, f32[320,512]{1,0:T(8,128)S(1)} %shard_map.109.update_ref), custom_call_target="tpu_custom_call" | custom-call | flops 327680 | bytes 1966080 | tf_op jit(solution)/shard_map/pallas_call | solution.py:295
  (37 shorter events, 0.4 us)
Async XLA Ops:
  0.6 38.2 %copy-start.19 = (s32[1,256]{1,0:T(1,128)S(1)}, s32[1,256]{1,0:T(1,128)}, u32[]{:S(2)}) copy-start(s32[1,256]{1,0:T(1,128)} %src_ref.3) | copy-start | bytes 3076
  0.6 38.2 %copy-start.23 = (s32[1,8]{1,0:T(1,128)S(1)}, s32[1,8]{1,0:T(1,128)}, u32[]{:S(2)}) copy-start(s32[1,8]{1,0:T(1,128)} %perm_ref.3) | copy-start | bytes 100
  0.7 1.1 %copy-start.3 = (f32[512,320]{0,1:T(8,128)S(1)}, f32[512,320]{0,1:T(8,128)}, u32[]{:S(2)}) copy-start(f32[512,320]{0,1:T(8,128)} %param.9) | copy-start | bytes 1966084
  1.8 0.7 copy-start.18
  2.4 0.7 copy-start.22
  3.1 35.7 %copy-start.5 = (f32[512,320]{0,1:T(8,128)S(1)}, f32[512,320]{0,1:T(8,128)}, u32[]{:S(2)}) copy-start(f32[512,320]{0,1:T(8,128)} %param.9) | copy-start | bytes 1966084
  3.1 35.7 %copy-start.20 = (s32[1,256]{1,0:T(1,128)S(1)}, s32[1,256]{1,0:T(1,128)}, u32[]{:S(2)}) copy-start(s32[1,256]{1,0:T(1,128)} %dst_ref.3) | copy-start | bytes 3076
  3.1 35.7 %copy-start.21 = (f32[1,256]{1,0:T(1,128)S(1)}, f32[1,256]{1,0:T(1,128)}, u32[]{:S(2)}) copy-start(f32[1,256]{1,0:T(1,128)} %weight_ref.3) | copy-start | bytes 3076
  3.1 55.7 %copy-start.7 = (f32[512,320]{0,1:T(8,128)S(1)}, f32[512,320]{0,1:T(8,128)}, u32[]{:S(2)}) copy-start(f32[512,320]{0,1:T(8,128)} %param.10) | copy-start | bytes 1966084
  3.1 55.7 %copy-start.17 = (s32[512,6]{0,1:T(8,128)S(1)}, s32[512,6]{0,1:T(8,128)}, u32[]{:S(2)}) copy-start(s32[512,6]{0,1:T(8,128)} %param.13) | copy-start | bytes 36868
  5.0 33.8 %all-to-all-start = ((f32[32,8,320]{2,1,0:T(8,128)}), f32[32,8,320]{2,1,0:T(8,128)S(1)}, u32[]{:S(2)}, u32[]{:S(2)}) async-start(f32[32,8,320]{2,1,0:T(8,128)} %bitcast.4), calls=%async_computation | async-start | bytes 786432 | tf_op jit(solution)/shard_map/all_to_all | solution.py:285
  12.3 12.2 %collective-permute-start = (f32[8,320]{1,0:T(8,128)S(1)}, f32[8,320]{1,0:T(8,128)S(1)}, u32[]{:S(2)}, u32[]{:S(2)}) collective-permute-start(f32[8,320]{1,0:T(8,128)S(1)} %get-tuple-element.12), channel_id=1, source_target_pairs={{0,1},{1,2},{2,3},{3,4},{4,5},{5,6},{6,7},{7,0},{8,9},{9,10},{10,1... | collective-permute-start | bytes 30728 | tf_op jit(solution)/shard_map/ppermute | solution.py:286
  14.1 10.4 %collective-permute-start.1 = (f32[8,320]{1,0:T(8,128)S(1)}, f32[8,320]{1,0:T(8,128)S(1)}, u32[]{:S(2)}, u32[]{:S(2)}) collective-permute-start(f32[8,320]{1,0:T(8,128)S(1)} %get-tuple-element.13), channel_id=1, source_target_pairs={{1,0},{2,1},{3,2},{4,3},{5,4},{6,5},{7,6},{0,7},{9,8},{10,9},{11,1... | collective-permute-start | bytes 30728 | tf_op jit(solution)/shard_map/ppermute | solution.py:286
  24.5 3.8 %copy-start = (bf16[512,6,5,320]{0,3,2,1:T(8,128)(2,1)S(1)}, bf16[512,6,5,320]{0,3,2,1:T(8,128)(2,1)}, u32[]{:S(2)}) copy-start(bf16[512,6,5,320]{0,3,2,1:T(8,128)(2,1)} %param.11) | copy-start | bytes 29491204
  28.3 1.1 %copy-start.4 = (f32[512,320]{0,1:T(8,128)S(1)}, f32[512,320]{0,1:T(8,128)}, u32[]{:S(2)}) copy-start(f32[512,320]{0,1:T(8,128)} %param.9) | copy-start | bytes 1966084
  29.4 1.1 %copy-start.6 = (f32[512,320]{0,1:T(8,128)S(1)}, f32[512,320]{0,1:T(8,128)}, u32[]{:S(2)}) copy-start(f32[512,320]{0,1:T(8,128)} %param.10) | copy-start | bytes 1966084
  30.5 0.7 copy-start.16
  31.2 7.7 %copy-start.2 = (bf16[512,5,320]{0,2,1:T(8,128)(2,1)S(1)}, bf16[512,5,320]{0,2,1:T(8,128)(2,1)}, u32[]{:S(2)}) copy-start(bf16[512,5,320]{0,2,1:T(8,128)(2,1)} %param.12) | copy-start | bytes 4915204
  38.0 0.8 copy-start.10
  38.9 1.1 %copy-start.11 = (f32[320,512]{1,0:T(8,128)S(1)}, f32[320,512]{1,0:T(8,128)}, u32[]{:S(2)}) copy-start(f32[320,512]{1,0:T(8,128)} %copy-done.10) | copy-start | bytes 1966084
  42.0 0.8 copy-start.8
  42.8 0.7 copy-start.15
  43.5 27.7 %all-to-all-start.1 = ((f32[32,8,320]{2,1,0:T(8,128)}), f32[32,8,320]{2,1,0:T(8,128)S(1)}, u32[]{:S(2)}, u32[]{:S(2)}) async-start(f32[32,8,320]{2,1,0:T(8,128)} %bitcast.23), calls=%async_computation.1 | async-start | bytes 786432 | tf_op jit(solution)/shard_map/all_to_all | solution.py:285
  46.5 12.2 %collective-permute-start.2 = (f32[8,320]{1,0:T(8,128)S(1)}, f32[8,320]{1,0:T(8,128)S(1)}, u32[]{:S(2)}, u32[]{:S(2)}) collective-permute-start(f32[8,320]{1,0:T(8,128)S(1)} %get-tuple-element.16), channel_id=1, source_target_pairs={{0,1},{1,2},{2,3},{3,4},{4,5},{5,6},{6,7},{7,0},{8,9},{9,10},{10,1... | collective-permute-start | bytes 30728 | tf_op jit(solution)/shard_map/ppermute | solution.py:286
  48.4 10.4 %collective-permute-start.3 = (f32[8,320]{1,0:T(8,128)S(1)}, f32[8,320]{1,0:T(8,128)S(1)}, u32[]{:S(2)}, u32[]{:S(2)}) collective-permute-start(f32[8,320]{1,0:T(8,128)S(1)} %get-tuple-element.17), channel_id=1, source_target_pairs={{1,0},{2,1},{3,2},{4,3},{5,4},{6,5},{7,6},{0,7},{9,8},{10,9},{11,1... | collective-permute-start | bytes 30728 | tf_op jit(solution)/shard_map/ppermute | solution.py:286
  58.8 3.8 %copy-start.1 = (bf16[512,6,5,320]{0,3,2,1:T(8,128)(2,1)S(1)}, bf16[512,6,5,320]{0,3,2,1:T(8,128)(2,1)}, u32[]{:S(2)}) copy-start(bf16[512,6,5,320]{0,3,2,1:T(8,128)(2,1)} %param.11) | copy-start | bytes 29491204
  62.6 1.1 %copy-start.9 = (f32[320,512]{1,0:T(8,128)S(1)}, f32[320,512]{1,0:T(8,128)}, u32[]{:S(2)}) copy-start(f32[320,512]{1,0:T(8,128)} %copy-done.8) | copy-start | bytes 1966084
  70.4 0.8 copy-start.12
  71.3 1.1 %copy-start.13 = (f32[320,512]{1,0:T(8,128)S(1)}, f32[320,512]{1,0:T(8,128)}, u32[]{:S(2)}) copy-start(f32[320,512]{1,0:T(8,128)} %copy-done.12) | copy-start | bytes 1966084
  73.6 10.2 %all-to-all-start.2 = ((f32[32,2,128]{2,1,0:T(2,128)}), f32[32,2,128]{2,1,0:T(2,128)S(1)}, u32[]{:S(2)}, u32[]{:S(2)}) async-start(f32[32,2,128]{2,1,0:T(2,128)} %get-tuple-element.20), calls=%async_computation.2 | async-start | bytes 65536 | tf_op jit(solution)/shard_map/all_to_all | solution.py:294
  76.6 1.1 %copy-start.14 = (f32[320,512]{1,0:T(8,128)S(1)}, f32[320,512]{1,0:T(8,128)}, u32[]{:S(2)}) copy-start(f32[320,512]{1,0:T(8,128)} %get-tuple-element.21.resid_ref) | copy-start | bytes 1966084

commit v2 on v1

--- a/solution.py
+++ b/solution.py
@@ -33,30 +33,16 @@
     )
 
 
-def send_blocks(x, src, perm_ref, out_ref, up_ref, down_ref):
-    blocks = x.shape[1]
-    slots = src.shape[1]
+def send_blocks(x, table, sel_up, sel_down, out_ref, up_ref, down_ref):
     rim = up_ref.shape[0]
     index = lax.axis_index("blk")
     at_last = index == lax.axis_size("blk") - 1
     at_first = index == 0
-    rows = lax.broadcasted_iota(jnp.int32, (blocks, slots), 0)
-    out_ref[...] = pick(x, onehot(rows == src)).T
-    sub = lax.broadcasted_iota(jnp.int32, (LANES, LANES), 0)
-    lane = lax.broadcasted_iota(jnp.int32, (LANES, LANES), 1)
-    lane_row = lane[:1]
-    sub_col = sub[:, :1]
-    wanted = lane_row
-    target = sub_col
-    for j in range(rim):
-        partner = perm_ref[0, j]
-        wanted = jnp.where((lane_row == j) & at_last, partner, wanted)
-        target = jnp.where((sub_col == j) & at_first, partner, target)
-    to_up = (sub == wanted + (LANES - rim)) & (lane < rim)
-    to_down = (target + rim == lane) & (sub < rim)
-    rims = pick(x[:, blocks - LANES :], onehot(to_up)) + pick(x[:, :LANES], onehot(to_down))
-    turn_up = (lane_row < rim) & at_last
-    turn_down = (lane_row >= rim) & at_first
+    out_ref[...] = pick(x, table).T
+    rims = pick(x[:, x.shape[1] - LANES :], sel_up) + pick(x[:, :LANES], sel_down)
+    lane = lax.broadcasted_iota(jnp.int32, (1, LANES), 1)
+    turn_up = (lane < rim) & at_last
+    turn_down = (lane >= rim) & at_first
     angle = 2.0 * math.pi / 3.0
     cosine = jnp.where(turn_up | turn_down, math.cos(angle), 1.0)
     sine = jnp.where(turn_up, math.sin(angle), jnp.where(turn_down, -math.sin(angle), 0.0))
@@ -75,25 +61,39 @@
     down_ref[...] = rims[rim : 2 * rim]
 
 
-def donors_kernel(x_ref, src_ref, perm_ref, out_ref, up_ref, down_ref):
-    send_blocks(x_ref[...], src_ref[...], perm_ref, out_ref, up_ref, down_ref)
-
-
-def local_kernel(x_ref, lower_ref, upper_ref, nbr_ref, coup_ref, source_ref, out_ref, high, low, near):
+def donors_kernel(x_ref, src_ref, perm_ref, out_ref, up_ref, down_ref, table_ref, sel_up_ref, sel_down_ref):
+    rim = up_ref.shape[0]
+    index = lax.axis_index("blk")
+    at_last = index == lax.axis_size("blk") - 1
+    at_first = index == 0
+    sub = lax.broadcasted_iota(jnp.int32, (LANES, LANES), 0)
+    lane = lax.broadcasted_iota(jnp.int32, (LANES, LANES), 1)
+    wanted = lane[:1]
+    target = sub[:, :1]
+    for j in range(rim):
+        partner = perm_ref[0, j]
+        wanted = jnp.where((lane[:1] == j) & at_last, partner, wanted)
+        target = jnp.where((sub[:, :1] == j) & at_first, partner, target)
+    sel_up = onehot((sub == wanted + (LANES - rim)) & (lane < rim))
+    sel_down = onehot((target + rim == lane) & (sub < rim))
+    rows = lax.broadcasted_iota(jnp.int32, table_ref.shape, 0)
+    table = onehot(rows == src_ref[...])
+    send_blocks(x_ref[...], table, sel_up, sel_down, out_ref, up_ref, down_ref)
+    table_ref[...] = table
+    sel_up_ref[...] = sel_up
+    sel_down_ref[...] = sel_down
+
+
+def local_kernel(rim, x_ref, nbr_ref, coup_ref, source_ref, out_ref, high, low, near):
     step = pl.program_id(0)
-    blocks = x_ref.shape[1]
-    rim = lower_ref.shape[0]
     slots = nbr_ref.shape[0]
 
     @pl.when(step == 0)
     def _():
-        rims = jnp.concatenate(
-            [lower_ref[...], upper_ref[...], jnp.zeros((LANES - 2 * rim, BW), jnp.float32)], axis=0
-        ).T
         lane = lax.broadcasted_iota(jnp.int32, (BW, LANES), 1)
         moved = pltpu.roll(x_ref[...], rim, 1)
-        head = jnp.where(lane < rim, rims, moved[:, :LANES])
-        tail = jnp.where(lane < rim, moved[:, :LANES], jnp.where(lane < 2 * rim, rims, 0.0))
+        head = jnp.where(lane < rim, 0.0, moved[:, :LANES])
+        tail = jnp.where(lane < rim, moved[:, :LANES], 0.0)
         ext = jnp.concatenate([head, moved[:, LANES:], tail], axis=1)
         high[...], low[...] = split(ext)
 
@@ -125,12 +125,71 @@
     lax.fori_loop(0, CELLS // PACK, cells, 0)
 
 
-def fringe_residual(local_ref, inc_ref, dst_ref, weight_ref):
+def first_local_kernel(
+    rim, x_ref, nbr_ref, coup_ref, source_ref, diag_ref, dst_ref, weight_ref,
+    out_ref, rimcoup_ref, rimrow_ref, x_out, diag_out, dst_out, weight_out, high, low, near,
+):
+    step = pl.program_id(0)
+    last = pl.num_programs(0) - 1
+    slots = nbr_ref.shape[0]
+    blocks = x_ref.shape[1]
+    local_kernel(rim, x_ref, nbr_ref, coup_ref, source_ref, out_ref, high, low, near)
+    x_out[...] = x_ref[:, pl.ds(pl.multiple_of(step * LANES, LANES), LANES)]
+    diag_out[...] = diag_ref[...]
+    dst_out[...] = dst_ref[...]
+    weight_out[...] = weight_ref[...]
+
+    @pl.when((step == 0) | (step == last))
+    def _():
+        sub = lax.broadcasted_iota(jnp.int32, (LANES, LANES), 0)
+        lane = lax.broadcasted_iota(jnp.int32, (LANES, LANES), 1)
+        base = jnp.where(step == 0, 0, rim)
+        at = sub - jnp.where(step == 0, 0, LANES - 2 * rim)
+        inside = (at >= base) & (at < base + rim)
+        place = jnp.concatenate(
+            [onehot((lane == at + m * 2 * rim) & inside) for m in range(slots)], axis=0
+        )
+        reads = []
+        for m in range(slots):
+            row = nbr_ref[m : m + 1, :]
+            lower = jnp.where(row < rim, row + 1, 0)
+            upper = jnp.where(row >= blocks + rim, row - blocks + 1, 0)
+            reads.append(jnp.where(step == 0, lower, upper))
+        reads = jnp.broadcast_to(jnp.concatenate(reads, axis=1), (PACK, slots * LANES))
+        reads = reads.astype(jnp.float32).astype(jnp.bfloat16)
+        kept = jnp.where(step == 0, 0.0, rimrow_ref[...])
+        rimrow_ref[...] = kept + jnp.dot(reads, place, preferred_element_type=jnp.float32)
+        for u in range(VARS):
+            rows = jnp.concatenate([coup_ref[m, u] for m in range(slots)], axis=1)
+            moved = jnp.dot(rows, place, preferred_element_type=jnp.float32)
+            kept = jnp.where(step == 0, 0.0, rimcoup_ref[u].astype(jnp.float32))
+            rimcoup_ref[u] = (kept + moved).astype(jnp.bfloat16)
+
+
+def full_residual(local_ref, inc_ref, lower_ref, upper_ref, dst_ref, weight_ref, rimcoup_ref, rimrow_ref):
     blocks = local_ref.shape[1]
     slots = inc_ref.shape[0]
+    rim = lower_ref.shape[0]
+    rims = jnp.concatenate(
+        [lower_ref[...], upper_ref[...], jnp.zeros((LANES - 2 * rim, BW), jnp.float32)], axis=0
+    ).T
+    sub = lax.broadcasted_iota(jnp.int32, (LANES, LANES), 0)
+    near = pick(rims, onehot(sub + 1 == rimrow_ref[:1].astype(jnp.int32)))
+    edge = []
+    for u in range(VARS):
+        total = None
+        for v in range(VARS):
+            span = slice(v * CELLS, (v + 1) * CELLS)
+            term = rimcoup_ref[u, span, :].astype(jnp.float32) * near[span]
+            total = term if total is None else total + term
+        edge.append(total)
+    edge = jnp.concatenate(edge, axis=0)
     rows = lax.broadcasted_iota(jnp.int32, (blocks, slots), 0)
-    table = onehot(rows == dst_ref[...])
-    high, low = split(inc_ref[...].T * weight_ref[...])
+    edge_rows = lax.broadcasted_iota(jnp.int32, (blocks, LANES), 0)
+    place = lax.rem(lax.broadcasted_iota(jnp.int32, (1, LANES), 1), 2 * rim)
+    place = jnp.where(place < rim, place, place + (blocks - 2 * rim))
+    table = jnp.concatenate([onehot(rows == dst_ref[...]), onehot(edge_rows == place)], axis=1)
+    high, low = split(jnp.concatenate([inc_ref[...].T * weight_ref[...], edge], axis=1))
     contract = (((1,), (1,)), ((), ()))
     return (
         local_ref[...]
@@ -154,11 +213,13 @@
 
 
 def advance_kernel(
-    local_ref, inc_ref, dst_ref, weight_ref, diag_ref, x_ref, src_ref, perm_ref,
+    local_ref, inc_ref, lower_ref, upper_ref, dst_ref, weight_ref, rimcoup_ref, rimrow_ref,
+    diag_ref, x_ref, table_ref, sel_up_ref, sel_down_ref,
     next_ref, norm_ref, out_ref, up_ref, down_ref, resid,
 ):
-    resid[...] = fringe_residual(local_ref, inc_ref, dst_ref, weight_ref)
-    norm_ref[...] = lane_sums(resid[...])
+    resid[...] = full_residual(
+        local_ref, inc_ref, lower_ref, upper_ref, dst_ref, weight_ref, rimcoup_ref, rimrow_ref
+    )
 
     def cells(part, carry):
         at = pl.multiple_of(part * PACK, PACK)
@@ -168,17 +229,27 @@
         return carry
 
     lax.fori_loop(0, CELLS // PACK, cells, 0)
-    send_blocks(next_ref[...], src_ref[...], perm_ref, out_ref, up_ref, down_ref)
-
-
-def residual_kernel(local_ref, inc_ref, dst_ref, weight_ref, norm_ref, resid_ref, sums_ref):
-    resid = fringe_residual(local_ref, inc_ref, dst_ref, weight_ref)
+    send_blocks(
+        next_ref[...], table_ref[...], sel_up_ref[...], sel_down_ref[...], out_ref, up_ref, down_ref
+    )
+    norm_ref[...] = lane_sums(resid[...])
+
+
+def residual_kernel(
+    local_ref, inc_ref, lower_ref, upper_ref, dst_ref, weight_ref, rimcoup_ref, rimrow_ref, norm_ref,
+    resid_ref, sums_ref,
+):
+    resid = full_residual(
+        local_ref, inc_ref, lower_ref, upper_ref, dst_ref, weight_ref, rimcoup_ref, rimrow_ref
+    )
     resid_ref[...] = resid
     both = jnp.concatenate([norm_ref[...], lane_sums(resid)], axis=0)
     sums_ref[...] = jnp.broadcast_to(both[None], sums_ref.shape)
 
 
-def direction_kernel(diag_ref, resid_ref, out_ref):
+def direction_kernel(diag_ref, resid_ref, out_ref, resid_out):
+    resid_out[...] = resid_ref[...]
+
     def cells(part, carry):
         at = pl.multiple_of(part * PACK, PACK)
         for u in range(VARS):
@@ -200,6 +271,10 @@
 
 def f32(*shape):
     return jax.ShapeDtypeStruct(shape, jnp.float32)
+
+
+def bf16(*shape):
+    return jax.ShapeDtypeStruct(shape, jnp.bfloat16)
 
 
 def call(kernel, in_specs, out_shape, flops, moved, **more):
@@ -226,40 +301,70 @@
     devices = lax.axis_size("body") * peers
     up = [(i, (i + 1) % peers) for i in range(peers)]
     down = [(j, i) for i, j in up]
-    x = psi_init.T
-    source_t = source.T
-    coup = coupling.transpose(1, 2, 3, 0)
-    diag = diag_inv.transpose(1, 2, 0)
-    nbr = neighbours.T
+    here = functools.partial(pltpu.with_memory_space_constraint, memory_space=pltpu.HBM)
+    x = here(psi_init.T)
+    source_t = here(source.T)
+    coup = here(coupling.transpose(1, 2, 3, 0))
+    diag = here(diag_inv.transpose(1, 2, 0))
+    nbr = here(neighbours.T)
     state = f32(BW, blocks)
     sent = [f32(fringe, BW), f32(rim, BW), f32(rim, BW)]
     size = 4 * BW * blocks
-
-    donors = call(donors_kernel, [VMEM, VMEM, SMEM], sent, 4 * BW * blocks * fringe, 2 * size)
-    local = call(
-        local_kernel,
-        [
-            pl.BlockSpec((BW, blocks), lambda i: (0, 0)),
-            pl.BlockSpec((rim, BW), lambda i: (0, 0)),
-            pl.BlockSpec((rim, BW), lambda i: (0, 0)),
-            pl.BlockSpec((slots, LANES), lambda i: (0, i)),
-            pl.BlockSpec((slots, VARS, BW, LANES), lambda i: (0, 0, 0, i)),
-            pl.BlockSpec((BW, LANES), lambda i: (0, i)),
-        ],
-        state,
-        4 * BW * 2 * LANES * slots * blocks,
-        coup.size * 2 + 4 * size,
+    square = bf16(LANES, LANES)
+
+    donors = call(
+        donors_kernel,
+        [VMEM, VMEM, SMEM],
+        sent + [bf16(blocks, fringe), square, square],
+        4 * BW * blocks * fringe,
+        2 * size,
+    )
+    column = pl.BlockSpec((BW, LANES), lambda i: (0, i))
+    diag_column = pl.BlockSpec((VARS, BW, LANES), lambda i: (0, 0, i))
+    whole_row = pl.BlockSpec((1, fringe), lambda i: (0, 0))
+    local_in = [
+        pl.BlockSpec((BW, blocks), lambda i: (0, 0)),
+        pl.BlockSpec((slots, LANES), lambda i: (0, i)),
+        pl.BlockSpec((slots, VARS, BW, LANES), lambda i: (0, 0, 0, i)),
+        column,
+    ]
+    local_more = dict(
+        flops=4 * BW * 2 * LANES * slots * blocks,
+        moved=coup.size * 2 + 4 * size,
         grid=(blocks // LANES,),
-        out_specs=pl.BlockSpec((BW, LANES), lambda i: (0, i)),
         scratch_shapes=[
             pltpu.VMEM((BW, blocks + LANES), jnp.bfloat16),
             pltpu.VMEM((BW, blocks + LANES), jnp.bfloat16),
             pltpu.VMEM((BW, slots * LANES), jnp.float32),
         ],
     )
+    first_local = call(
+        functools.partial(first_local_kernel, rim),
+        local_in + [diag_column, whole_row, whole_row],
+        [
+            state,
+            bf16(VARS, BW, LANES),
+            f32(PACK, LANES),
+            state,
+            bf16(VARS, BW, blocks),
+            jax.ShapeDtypeStruct((1, fringe), jnp.int32),
+            f32(1, fringe),
+        ],
+        out_specs=[
+            column,
+            pl.BlockSpec((VARS, BW, LANES), lambda i: (0, 0, 0)),
+            pl.BlockSpec((PACK, LANES), lambda i: (0, 0)),
+            column,
+            diag_column,
+            whole_row,
+            whole_row,
+        ],
+        **local_more,
+    )
+    local = call(functools.partial(local_kernel, rim), local_in, state, out_specs=column, **local_more)
     advance = call(
         advance_kernel,
-        [VMEM] * 7 + [SMEM],
+        [VMEM] * 13,
         [state, f32(1, LANES)] + sent,
         8 * BW * blocks * fringe,
         diag.size * 2 + 4 * size,
@@ -267,12 +372,14 @@
     )
     residual = call(
         residual_kernel,
-        [VMEM] * 5,
+        [VMEM] * 9,
         [state, f32(devices, 2, LANES)],
         4 * BW * blocks * fringe,
         3 * size,
     )
-    direction = call(direction_kernel, [VMEM] * 2, state, diag.size * 2, diag.size * 2 + 2 * size)
+    direction = call(
+        direction_kernel, [VMEM] * 2, [state, state], diag.size * 2, diag.size * 2 + 2 * size
+    )
     finish = call(
         functools.partial(finish_kernel, float(blocks * devices * BW)),
         [VMEM] * 3,
@@ -285,14 +392,19 @@
         rows = lax.all_to_all(rows, ("body", "blk"), split_axis=0, concat_axis=0, tiled=True)
         return rows, lax.ppermute(to_up, "blk", up), lax.ppermute(to_down, "blk", down)
 
-    incoming, lower, upper = exchange(*donors(x, fringe_src, seam_perm))
-    part = local(x, lower, upper, nbr, coup, source_t)
-    x, norm, *out = advance(part, incoming, fringe_dst, fringe_weight, diag, x, fringe_src, seam_perm)
-    incoming, lower, upper = exchange(*out)
-    part = local(x, lower, upper, nbr, coup, source_t)
-    resid, sums = residual(part, incoming, fringe_dst, fringe_weight, norm)
+    *out, table, sel_up, sel_down = donors(x, here(fringe_src), here(seam_perm))
+    arrived = exchange(*out)
+    part, rimcoup, rimrow, x, diag, dst, weight = first_local(
+        x, nbr, coup, source_t, diag, here(fringe_dst), here(fringe_weight)
+    )
+    across = (dst, weight, rimcoup, rimrow)
+    x, norm, *out = advance(part, *arrived, *across, diag, x, table, sel_up, sel_down)
+    arrived = exchange(*out)
+    part = local(x, nbr, coup, source_t)
+    resid, sums = residual(part, *arrived, *across, norm)
     sums = lax.all_to_all(sums, ("body", "blk"), split_axis=0, concat_axis=0, tiled=True)
-    x = finish(sums, x, direction(diag, resid))
+    update, resid = direction(diag, resid)
+    x = finish(sums, x, update)
     return (x.T, resid.T)
 
 

time: 85.6 us -> 63.9 us (0.75)
  local copies, waits for them, and re-layouts: 20.5 us -> 5.75 us
  waiting for transfers between devices: 20.6 us -> 6.63 us
  Pallas kernels: 20.1 us -> 27.5 us
    ppermute x2, waiting for transfers between devices: 14.9 us -> 0.05 us  [exchange(): lax.ppermute(to_up, 'blk', up)]
    unnamed x48 -> x12, local copies, waits for them, and re-layouts: 20.5 us -> 5.75 us
    pallas_call x7, Pallas kernels: 20.1 us -> 27.5 us  [the longest x1 10.7 us: shards(): first_local(x, nbr, coup, source_t, diag, here(fringe_dst), here(fringe_w...]
    all_to_all x2, waiting for transfers between devices: 0.01 us -> 1.69 us  [exchange(): lax.all_to_all(rows, ('body', 'blk'), split_axis=0, concat_axis=0, tiled=...]
    all_to_all x1, waiting for transfers between devices: 5.75 us -> 4.89 us  [shards(): lax.all_to_all(sums, ('body', 'blk'), split_axis=0, concat_axis=0, tiled=...]
  transfers between devices with their start and end apart: 7 -> 7, of which waited for: 3 -> 2; matrix products, arithmetic and copies ran while one was open for 0% -> 0% of each run, Pallas kernels for 16% -> 30%
where the time goes in v2:
time: 63.9 us; the launch traced here: 63.3 us
  Pallas kernels  27.5 us (43%)
  starting transfers between devices  22.7 us (36%)
  waiting for transfers between devices  6.63 us (10%)
  local copies, waits for them, and re-layouts  5.75 us (9%)
  between operations  0.71 us (1%)
    pallas_call x1, Pallas kernels, shards(): first_local(x, nbr, coup, source_t, diag, here(fringe_dst), here(fringe_w...  10.7 us
    all_to_all x2, starting transfers between devices, exchange(): lax.all_to_all(rows, ('body', 'blk'), split_axis=0, concat_axis=0, tiled=...  10.6 us
    pallas_call x1, Pallas kernels, shards(): part = local(x, nbr, coup, source_t)  7.28 us
    ppermute x2, starting transfers between devices, exchange(): lax.ppermute(to_down, 'blk', down)  6.02 us
    unnamed x12, local copies, waits for them, and re-layouts  5.75 us
    all_to_all x1, waiting for transfers between devices, shards(): lax.all_to_all(sums, ('body', 'blk'), split_axis=0, concat_axis=0, tiled=...  4.89 us
    ppermute x2, starting transfers between devices, exchange(): lax.ppermute(to_up, 'blk', up)  3.53 us
    all_to_all x1, starting transfers between devices, shards(): lax.all_to_all(sums, ('body', 'blk'), split_axis=0, concat_axis=0, tiled=...  2.56 us
  transfers between devices with their start and end apart: 7, of which 2 were waited for; matrix products, arithmetic and copies ran while one was open for 0% of the time, Pallas kernels for 30%

profile of v2, /device:TPU:0, one launch (start us, length us, event | category | flops | bytes accessed | tf_op | source)
XLA Modules:
  0.0 63.3 jit_solution(11870553807879763507)
XLA Ops:
  0.6 2.5 %shard_map.105 = (f32[256,320]{1,0:T(8,128)}, f32[8,320]{1,0:T(8,128)S(1)}, f32[8,320]{1,0:T(8,128)S(1)}, bf16[512,256]{1,0:T(8,128)(2,1)S(1)}, bf16[128,128]{1,...) custom-call(f32[320,512]{1,0:T(8,128)} %bitcast.16, s32[1,256]{1,0:T(1,128)} %src_ref.1, s32[1,8]{1,0:T(1,128)} %perm_ref.1), custom_call_target="tpu_custom_call" | custom-call | flops 167772160 | bytes 1310720 | tf_op jit(solution)/shard_map/pallas_call | solution.py:395
  3.1 7.3 %all-to-all-start = ((f32[32,8,320]{2,1,0:T(8,128)}), f32[32,8,320]{2,1,0:T(8,128)S(1)}, u32[]{:S(2)}, u32[]{:S(2)}) async-start(f32[32,8,320]{2,1,0:T(8,128)} %bitcast.5), calls=%async_computation | async-start | bytes 786432 | tf_op jit(solution)/shard_map/all_to_all | solution.py:392
  10.4 1.8 %collective-permute-start = (f32[8,320]{1,0:T(8,128)S(1)}, f32[8,320]{1,0:T(8,128)S(1)}, u32[]{:S(2)}, u32[]{:S(2)}) collective-permute-start(f32[8,320]{1,0:T(8,128)S(1)} %get-tuple-element.26), channel_id=1, source_target_pairs={{0,1},{1,2},{2,3},{3,4},{4,5},{5,6},{6,7},{7,0},{8,9},{9,10},{10,1... | collective-permute-start | bytes 30728 | tf_op jit(solution)/shard_map/ppermute | solution.py:393
  12.2 3.0 %collective-permute-start.1 = (f32[8,320]{1,0:T(8,128)S(1)}, f32[8,320]{1,0:T(8,128)S(1)}, u32[]{:S(2)}, u32[]{:S(2)}) collective-permute-start(f32[8,320]{1,0:T(8,128)S(1)} %get-tuple-element.27), channel_id=1, source_target_pairs={{1,0},{2,1},{3,2},{4,3},{5,4},{6,5},{7,6},{0,7},{9,8},{10,9},{11,1... | collective-permute-start | bytes 30728 | tf_op jit(solution)/shard_map/ppermute | solution.py:393
  15.2 10.7 %shard_map.104 = (f32[320,512]{1,0:T(8,128)S(1)}, bf16[5,320,128]{2,1,0:T(8,128)(2,1)S(1)}, f32[16,128]{1,0:T(8,128)S(1)}, f32[320,512]{1,0:T(8,128)S(1)}, bf16[...) custom-call(f32[320,512]{1,0:T(8,128)} %bitcast.17, s32[6,512]{1,0:T(8,128)} %bitcast.20, ...), custom_call_target="tpu_custom_call" | custom-call | flops 1006632960 | bytes 12451840 | tf_op jit(solution)/shard_map/pallas_call | solution.py:397
  25.9 0.0 copy-start
  25.9 0.8 %copy-done = f32[320,512]{1,0:T(8,128)} copy-done((f32[320,512]{1,0:T(8,128)}, f32[320,512]{1,0:T(8,128)S(1)}, u32[]{:S(2)}) %copy-start) | copy-done | bytes 655384
  26.7 0.0 copy-start.2
  26.7 0.8 %copy-done.2 = f32[320,512]{1,0:T(8,128)} copy-done((f32[320,512]{1,0:T(8,128)}, f32[320,512]{1,0:T(8,128)S(1)}, u32[]{:S(2)}) %copy-start.2) | copy-done | bytes 655384
  27.5 0.0 collective-permute-done.lower_ref
  27.5 0.0 collective-permute-done.1.upper_ref
  27.5 0.0 all-to-all-done
  27.5 0.0 copy-start.1
  27.6 1.1 %copy-done.1 = f32[320,512]{1,0:T(8,128)S(1)} copy-done((f32[320,512]{1,0:T(8,128)S(1)}, f32[320,512]{1,0:T(8,128)}, u32[]{:S(2)}) %copy-start.1) | copy-done | bytes 655384
  28.6 0.0 copy-start.3
  28.6 1.1 %copy-done.3 = f32[320,512]{1,0:T(8,128)S(1)} copy-done((f32[320,512]{1,0:T(8,128)S(1)}, f32[320,512]{1,0:T(8,128)}, u32[]{:S(2)}) %copy-start.3) | copy-done | bytes 655384
  29.7 2.5 %shard_map.106 = (f32[320,512]{1,0:T(8,128)S(1)}, f32[1,128]{1,0:T(1,128)S(1)}, f32[256,320]{1,0:T(8,128)}, f32[8,320]{1,0:T(8,128)S(1)}, f32[8,320]{1,0:T(8,128)S(1)}) custom-call(f32[320,512]{1,0:T(8,128)S(1)} %copy-done.1, f32[256,320]{1,0:T(8,128)S(1)} %bitcast.11, f32[8,320]{1,0:T(8,128)S(1)} %collective-permute-done.lower_ref, ...), custom_call_target="tpu_custom_call" | custom-call | flops 335544320 | bytes 4259840 | tf_op jit(solution)/shard_map/pallas_call | solution.py:401
  32.2 3.3 %all-to-all-start.1 = ((f32[32,8,320]{2,1,0:T(8,128)}), f32[32,8,320]{2,1,0:T(8,128)}, u32[]{:S(2)}, u32[]{:S(2)}) async-start(f32[32,8,320]{2,1,0:T(8,128)} %bitcast.7), calls=%async_computation.1 | async-start | bytes 786432 | tf_op jit(solution)/shard_map/all_to_all | solution.py:392
  35.5 1.7 %collective-permute-start.2 = (f32[8,320]{1,0:T(8,128)S(1)}, f32[8,320]{1,0:T(8,128)S(1)}, u32[]{:S(2)}, u32[]{:S(2)}) collective-permute-start(f32[8,320]{1,0:T(8,128)S(1)} %get-tuple-element.39), channel_id=1, source_target_pairs={{0,1},{1,2},{2,3},{3,4},{4,5},{5,6},{6,7},{7,0},{8,9},{9,10},{10,1... | collective-permute-start | bytes 30728 | tf_op jit(solution)/shard_map/ppermute | solution.py:393
  37.2 3.1 %collective-permute-start.3 = (f32[8,320]{1,0:T(8,128)S(1)}, f32[8,320]{1,0:T(8,128)S(1)}, u32[]{:S(2)}, u32[]{:S(2)}) collective-permute-start(f32[8,320]{1,0:T(8,128)S(1)} %get-tuple-element.40), channel_id=1, source_target_pairs={{1,0},{2,1},{3,2},{4,3},{5,4},{6,5},{7,6},{0,7},{9,8},{10,9},{11,1... | collective-permute-start | bytes 30728 | tf_op jit(solution)/shard_map/ppermute | solution.py:393
  40.3 7.3 %shard_map.107.local_ref = f32[320,512]{1,0:T(8,128)S(1)} custom-call(f32[320,512]{1,0:T(8,128)S(1)} %get-tuple-element.37.x_ref, s32[6,512]{1,0:T(8,128)} %bitcast.21, bf16[6,5,320,512]{3,2,1,0:T(8,128)(2,1)} %bitcast.13, f32[320,512]{1,0:T(8,128)} %bitcast.15), custom_call_target="tpu_custom_call" | custom-call | flops 1006632960 | bytes 12451840 | tf_op jit(solution)/shard_map/pallas_call | solution.py:403
  47.6 0.0 collective-permute-done.2.lower_ref
  47.6 0.0 collective-permute-done.3.upper_ref
  47.6 1.7 %all-to-all-done.1 = f32[32,8,320]{2,1,0:T(8,128)} async-done(((f32[32,8,320]{2,1,0:T(8,128)}), f32[32,8,320]{2,1,0:T(8,128)}, u32[]{:S(2)}, u32[]{:S(2)}) %all-to-all-start.1) | async-done | bytes 327712 | tf_op jit(solution)/shard_map/all_to_all | solution.py:392
  49.3 2.3 %shard_map.108 = (f32[320,512]{1,0:T(8,128)S(1)}, f32[32,2,128]{2,1,0:T(2,128)}) custom-call(f32[320,512]{1,0:T(8,128)S(1)} %shard_map.107.local_ref, f32[256,320]{1,0:T(8,128)} %bitcast.8.inc_ref, f32[8,320]{1,0:T(8,128)S(1)} %collective-permute-done.2.lower_ref, f32[8,320]{1,0:T(8,128)S(1)} %collective-permute-done.3.upper_ref, ...), custom_call_target="tpu_custom_call" | custom-call | flops 167772160 | bytes 1966080 | tf_op jit(solution)/shard_map/pallas_call | solution.py:404
  51.6 0.8 %copy-done.4 = f32[320,512]{1,0:T(8,128)} copy-done((f32[320,512]{1,0:T(8,128)}, f32[320,512]{1,0:T(8,128)S(1)}, u32[]{:S(2)}) %copy-start.4) | copy-done | bytes 655384
  52.5 2.6 %all-to-all-start.2 = ((f32[32,2,128]{2,1,0:T(2,128)}), f32[32,2,128]{2,1,0:T(2,128)S(1)}, u32[]{:S(2)}, u32[]{:S(2)}) async-start(f32[32,2,128]{2,1,0:T(2,128)} %get-tuple-element.42), calls=%async_computation.2 | async-start | bytes 65536 | tf_op jit(solution)/shard_map/all_to_all | solution.py:405
  55.0 0.0 copy-start.5
  55.1 1.1 %copy-done.5 = f32[320,512]{1,0:T(8,128)S(1)} copy-done((f32[320,512]{1,0:T(8,128)S(1)}, f32[320,512]{1,0:T(8,128)}, u32[]{:S(2)}) %copy-start.5) | copy-done | bytes 655384
  56.1 1.2 %shard_map.109 = (f32[320,512]{1,0:T(8,128)S(1)}, f32[320,512]{1,0:T(8,128)}) custom-call(bf16[5,320,512]{2,1,0:T(8,128)(2,1)S(1)} %get-tuple-element.32.diag_ref, f32[320,512]{1,0:T(8,128)S(1)} %copy-done.5), custom_call_target="tpu_custom_call" | custom-call | flops 1638400 | bytes 2949120 | tf_op jit(solution)/shard_map/pallas_call | solution.py:406
  57.3 4.9 %all-to-all-done.2.sums_ref = f32[32,2,128]{2,1,0:T(2,128)S(1)} async-done(((f32[32,2,128]{2,1,0:T(2,128)}), f32[32,2,128]{2,1,0:T(2,128)S(1)}, u32[]{:S(2)}, u32[]{:S(2)}) %all-to-all-start.2) | async-done | bytes 32800 | tf_op jit(solution)/shard_map/all_to_all | solution.py:405
  62.2 1.1 %shard_map.110 = f32[320,512]{1,0:T(8,128)} custom-call(f32[32,2,128]{2,1,0:T(2,128)S(1)} %all-to-all-done.2.sums_ref, f32[320,512]{1,0:T(8,128)S(1)} %get-tuple-element.37.x_ref, f32[320,512]{1,0:T(8,128)S(1)} %get-tuple-element.44.update_ref), custom_call_target="tpu_custom_call" | custom-call | flops 327680 | bytes 1966080 | tf_op jit(solution)/shard_map/pallas_call | solution.py:407
  (1 shorter events, 0.0 us)
Async XLA Ops:
  3.1 24.5 %all-to-all-start = ((f32[32,8,320]{2,1,0:T(8,128)}), f32[32,8,320]{2,1,0:T(8,128)S(1)}, u32[]{:S(2)}, u32[]{:S(2)}) async-start(f32[32,8,320]{2,1,0:T(8,128)} %bitcast.5), calls=%async_computation | async-start | bytes 786432 | tf_op jit(solution)/shard_map/all_to_all | solution.py:392
  10.4 17.1 %collective-permute-start = (f32[8,320]{1,0:T(8,128)S(1)}, f32[8,320]{1,0:T(8,128)S(1)}, u32[]{:S(2)}, u32[]{:S(2)}) collective-permute-start(f32[8,320]{1,0:T(8,128)S(1)} %get-tuple-element.26), channel_id=1, source_target_pairs={{0,1},{1,2},{2,3},{3,4},{4,5},{5,6},{6,7},{7,0},{8,9},{9,10},{10,1... | collective-permute-start | bytes 30728 | tf_op jit(solution)/shard_map/ppermute | solution.py:393
  12.2 15.3 %collective-permute-start.1 = (f32[8,320]{1,0:T(8,128)S(1)}, f32[8,320]{1,0:T(8,128)S(1)}, u32[]{:S(2)}, u32[]{:S(2)}) collective-permute-start(f32[8,320]{1,0:T(8,128)S(1)} %get-tuple-element.27), channel_id=1, source_target_pairs={{1,0},{2,1},{3,2},{4,3},{5,4},{6,5},{7,6},{0,7},{9,8},{10,9},{11,1... | collective-permute-start | bytes 30728 | tf_op jit(solution)/shard_map/ppermute | solution.py:393
  25.9 0.8 %copy-start = (f32[320,512]{1,0:T(8,128)}, f32[320,512]{1,0:T(8,128)S(1)}, u32[]{:S(2)}) copy-start(f32[320,512]{1,0:T(8,128)S(1)} %get-tuple-element.24.local_ref) | copy-start | bytes 1966084
  26.7 0.8 %copy-start.2 = (f32[320,512]{1,0:T(8,128)}, f32[320,512]{1,0:T(8,128)S(1)}, u32[]{:S(2)}) copy-start(f32[320,512]{1,0:T(8,128)S(1)} %get-tuple-element.33.x_ref) | copy-start | bytes 1966084
  27.5 1.1 %copy-start.1 = (f32[320,512]{1,0:T(8,128)S(1)}, f32[320,512]{1,0:T(8,128)}, u32[]{:S(2)}) copy-start(f32[320,512]{1,0:T(8,128)} %copy-done) | copy-start | bytes 1966084
  28.6 1.1 %copy-start.3 = (f32[320,512]{1,0:T(8,128)S(1)}, f32[320,512]{1,0:T(8,128)}, u32[]{:S(2)}) copy-start(f32[320,512]{1,0:T(8,128)} %copy-done.2) | copy-start | bytes 1966084
  32.2 17.1 %all-to-all-start.1 = ((f32[32,8,320]{2,1,0:T(8,128)}), f32[32,8,320]{2,1,0:T(8,128)}, u32[]{:S(2)}, u32[]{:S(2)}) async-start(f32[32,8,320]{2,1,0:T(8,128)} %bitcast.7), calls=%async_computation.1 | async-start | bytes 786432 | tf_op jit(solution)/shard_map/all_to_all | solution.py:392
  35.5 12.1 %collective-permute-start.2 = (f32[8,320]{1,0:T(8,128)S(1)}, f32[8,320]{1,0:T(8,128)S(1)}, u32[]{:S(2)}, u32[]{:S(2)}) collective-permute-start(f32[8,320]{1,0:T(8,128)S(1)} %get-tuple-element.39), channel_id=1, source_target_pairs={{0,1},{1,2},{2,3},{3,4},{4,5},{5,6},{6,7},{7,0},{8,9},{9,10},{10,1... | collective-permute-start | bytes 30728 | tf_op jit(solution)/shard_map/ppermute | solution.py:393
  37.2 10.4 %collective-permute-start.3 = (f32[8,320]{1,0:T(8,128)S(1)}, f32[8,320]{1,0:T(8,128)S(1)}, u32[]{:S(2)}, u32[]{:S(2)}) collective-permute-start(f32[8,320]{1,0:T(8,128)S(1)} %get-tuple-element.40), channel_id=1, source_target_pairs={{1,0},{2,1},{3,2},{4,3},{5,4},{6,5},{7,6},{0,7},{9,8},{10,9},{11,1... | collective-permute-start | bytes 30728 | tf_op jit(solution)/shard_map/ppermute | solution.py:393
  51.6 0.8 %copy-start.4 = (f32[320,512]{1,0:T(8,128)}, f32[320,512]{1,0:T(8,128)S(1)}, u32[]{:S(2)}) copy-start(f32[320,512]{1,0:T(8,128)S(1)} %get-tuple-element.43.resid_ref) | copy-start | bytes 1966084
  52.5 9.7 %all-to-all-start.2 = ((f32[32,2,128]{2,1,0:T(2,128)}), f32[32,2,128]{2,1,0:T(2,128)S(1)}, u32[]{:S(2)}, u32[]{:S(2)}) async-start(f32[32,2,128]{2,1,0:T(2,128)} %get-tuple-element.42), calls=%async_computation.2 | async-start | bytes 65536 | tf_op jit(solution)/shard_map/all_to_all | solution.py:405
  55.0 1.1 %copy-start.5 = (f32[320,512]{1,0:T(8,128)S(1)}, f32[320,512]{1,0:T(8,128)}, u32[]{:S(2)}) copy-start(f32[320,512]{1,0:T(8,128)} %copy-done.4) | copy-start | bytes 1966084

commit v3 on v2

--- a/solution.py
+++ b/solution.py
@@ -14,7 +14,7 @@
 STEP_CFL = 0.5
 LANES = 128
 PACK = 16
-VMEM_LIMIT = 40 * 1024 * 1024
+VMEM_LIMIT = 32 * 1024 * 1024
 
 
 def split(x):
@@ -126,8 +126,8 @@
 
 
 def first_local_kernel(
-    rim, x_ref, nbr_ref, coup_ref, source_ref, diag_ref, dst_ref, weight_ref,
-    out_ref, rimcoup_ref, rimrow_ref, x_out, diag_out, dst_out, weight_out, high, low, near,
+    rim, x_ref, nbr_ref, coup_ref, source_ref, dst_ref, weight_ref,
+    out_ref, rimcoup_ref, rimrow_ref, x_out, dst_out, weight_out, high, low, near,
 ):
     step = pl.program_id(0)
     last = pl.num_programs(0) - 1
@@ -135,7 +135,6 @@
     blocks = x_ref.shape[1]
     local_kernel(rim, x_ref, nbr_ref, coup_ref, source_ref, out_ref, high, low, near)
     x_out[...] = x_ref[:, pl.ds(pl.multiple_of(step * LANES, LANES), LANES)]
-    diag_out[...] = diag_ref[...]
     dst_out[...] = dst_ref[...]
     weight_out[...] = weight_ref[...]
 
@@ -215,17 +214,20 @@
 def advance_kernel(
     local_ref, inc_ref, lower_ref, upper_ref, dst_ref, weight_ref, rimcoup_ref, rimrow_ref,
     diag_ref, x_ref, table_ref, sel_up_ref, sel_down_ref,
-    next_ref, norm_ref, out_ref, up_ref, down_ref, resid,
+    next_ref, norm_ref, out_ref, up_ref, down_ref, resid, diag, diag_sem,
 ):
+    fetch = pltpu.make_async_copy(diag_ref, diag, diag_sem)
+    fetch.start()
     resid[...] = full_residual(
         local_ref, inc_ref, lower_ref, upper_ref, dst_ref, weight_ref, rimcoup_ref, rimrow_ref
     )
+    fetch.wait()
 
     def cells(part, carry):
         at = pl.multiple_of(part * PACK, PACK)
         for u in range(VARS):
             span = pl.ds(u * CELLS + at, PACK)
-            next_ref[span, :] = x_ref[span, :] + STEP_CFL * precondition(diag_ref, resid, u, at)
+            next_ref[span, :] = x_ref[span, :] + STEP_CFL * precondition(diag, resid, u, at)
         return carry
 
     lax.fori_loop(0, CELLS // PACK, cells, 0)
@@ -320,7 +322,6 @@
         2 * size,
     )
     column = pl.BlockSpec((BW, LANES), lambda i: (0, i))
-    diag_column = pl.BlockSpec((VARS, BW, LANES), lambda i: (0, 0, i))
     whole_row = pl.BlockSpec((1, fringe), lambda i: (0, 0))
     local_in = [
         pl.BlockSpec((BW, blocks), lambda i: (0, 0)),
@@ -340,13 +341,12 @@
     )
     first_local = call(
         functools.partial(first_local_kernel, rim),
-        local_in + [diag_column, whole_row, whole_row],
+        local_in + [whole_row, whole_row],
         [
             state,
             bf16(VARS, BW, LANES),
             f32(PACK, LANES),
             state,
-            bf16(VARS, BW, blocks),
             jax.ShapeDtypeStruct((1, fringe), jnp.int32),
             f32(1, fringe),
         ],
@@ -355,7 +355,6 @@
             pl.BlockSpec((VARS, BW, LANES), lambda i: (0, 0, 0)),
             pl.BlockSpec((PACK, LANES), lambda i: (0, 0)),
             column,
-            diag_column,
             whole_row,
             whole_row,
         ],
@@ -364,11 +363,15 @@
     local = call(functools.partial(local_kernel, rim), local_in, state, out_specs=column, **local_more)
     advance = call(
         advance_kernel,
-        [VMEM] * 13,
+        [VMEM] * 8 + [pl.BlockSpec(memory_space=pltpu.HBM)] + [VMEM] * 4,
         [state, f32(1, LANES)] + sent,
         8 * BW * blocks * fringe,
         diag.size * 2 + 4 * size,
-        scratch_shapes=[pltpu.VMEM((BW, blocks), jnp.float32)],
+        scratch_shapes=[
+            pltpu.VMEM((BW, blocks), jnp.float32),
+            pltpu.VMEM((VARS, BW, blocks), jnp.bfloat16),
+            pltpu.SemaphoreType.DMA,
+        ],
     )
     residual = call(
         residual_kernel,
@@ -394,8 +397,8 @@
 
     *out, table, sel_up, sel_down = donors(x, here(fringe_src), here(seam_perm))
     arrived = exchange(*out)
-    part, rimcoup, rimrow, x, diag, dst, weight = first_local(
-        x, nbr, coup, source_t, diag, here(fringe_dst), here(fringe_weight)
+    part, rimcoup, rimrow, x, dst, weight = first_local(
+        x, nbr, coup, source_t, here(fringe_dst), here(fringe_weight)
     )
     across = (dst, weight, rimcoup, rimrow)
     x, norm, *out = advance(part, *arrived, *across, diag, x, table, sel_up, sel_down)

time: 63.9 us -> 58.2 us (0.911)
  local copies, waits for them, and re-layouts: 5.75 us -> 0 us
    unnamed x12 -> x0, local copies, waits for them, and re-layouts: 5.75 us -> none
    pallas_call x1, Pallas kernels: 1.2 us -> 2.64 us  [shards(): update, resid = direction(diag, resid)]
    pallas_call x1, Pallas kernels: 2.34 us -> 1.35 us  [shards(): resid, sums = residual(part, *arrived, *across, norm)]
    pallas_call x1, Pallas kernels: 2.47 us -> 3.22 us  [shards(): advance(part, *arrived, *across, diag, x, table, sel_up, sel_down)]
  transfers between devices with their start and end apart: 7 -> 7, of which waited for: 2 -> 3; matrix products, arithmetic and copies ran while one was open for 0% -> 0% of each run, Pallas kernels for 30% -> 35%
where the time goes in v3:
time: 58.2 us; the launch traced here: 57.7 us
  Pallas kernels  28.1 us (48%)
  starting transfers between devices  22.6 us (39%)
  waiting for transfers between devices  6.3 us (11%)
  between operations  0.71 us (1%)
    all_to_all x2, starting transfers between devices, exchange(): lax.all_to_all(rows, ('body', 'blk'), split_axis=0, concat_axis=0, tiled=...  10.4 us
    pallas_call x1, Pallas kernels, shards(): first_local(x, nbr, coup, source_t, here(fringe_dst), here(fringe_weight))  10.1 us
    pallas_call x1, Pallas kernels, shards(): part = local(x, nbr, coup, source_t)  7.27 us
    ppermute x2, starting transfers between devices, exchange(): lax.ppermute(to_down, 'blk', down)  5.91 us
    all_to_all x1, waiting for transfers between devices, shards(): lax.all_to_all(sums, ('body', 'blk'), split_axis=0, concat_axis=0, tiled=...  4.55 us
    ppermute x2, starting transfers between devices, exchange(): lax.ppermute(to_up, 'blk', up)  3.64 us
    pallas_call x1, Pallas kernels, shards(): advance(part, *arrived, *across, diag, x, table, sel_up, sel_down)  3.22 us
    pallas_call x1, Pallas kernels, shards(): update, resid = direction(diag, resid)  2.64 us
  transfers between devices with their start and end apart: 7, of which 3 were waited for; matrix products, arithmetic and copies ran while one was open for 0% of the time, Pallas kernels for 35%

profile of v3, /device:TPU:0, one launch (start us, length us, event | category | flops | bytes accessed | tf_op | source)
XLA Modules:
  0.0 57.7 jit_solution(5968955605847703508)
XLA Ops:
  0.6 2.4 %shard_map.105 = (f32[256,320]{1,0:T(8,128)}, f32[8,320]{1,0:T(8,128)S(1)}, f32[8,320]{1,0:T(8,128)S(1)}, bf16[512,256]{1,0:T(8,128)(2,1)S(1)}, bf16[128,128]{1,...) custom-call(f32[320,512]{1,0:T(8,128)} %bitcast.19, s32[1,256]{1,0:T(1,128)} %src_ref.1, s32[1,8]{1,0:T(1,128)} %perm_ref.1), custom_call_target="tpu_custom_call" | custom-call | flops 167772160 | bytes 1310720 | tf_op jit(solution)/shard_map/pallas_call | solution.py:398
  3.1 7.3 %all-to-all-start = ((f32[32,8,320]{2,1,0:T(8,128)}), f32[32,8,320]{2,1,0:T(8,128)S(1)}, u32[]{:S(2)}, u32[]{:S(2)}) async-start(f32[32,8,320]{2,1,0:T(8,128)} %bitcast.4), calls=%async_computation | async-start | bytes 786432 | tf_op jit(solution)/shard_map/all_to_all | solution.py:395
  10.4 1.8 %collective-permute-start = (f32[8,320]{1,0:T(8,128)S(1)}, f32[8,320]{1,0:T(8,128)S(1)}, u32[]{:S(2)}, u32[]{:S(2)}) collective-permute-start(f32[8,320]{1,0:T(8,128)S(1)} %get-tuple-element.25), channel_id=1, source_target_pairs={{0,1},{1,2},{2,3},{3,4},{4,5},{5,6},{6,7},{7,0},{8,9},{9,10},{10,1... | collective-permute-start | bytes 30728 | tf_op jit(solution)/shard_map/ppermute | solution.py:396
  12.2 3.0 %collective-permute-start.1 = (f32[8,320]{1,0:T(8,128)S(1)}, f32[8,320]{1,0:T(8,128)S(1)}, u32[]{:S(2)}, u32[]{:S(2)}) collective-permute-start(f32[8,320]{1,0:T(8,128)S(1)} %get-tuple-element.26), channel_id=1, source_target_pairs={{1,0},{2,1},{3,2},{4,3},{5,4},{6,5},{7,6},{0,7},{9,8},{10,9},{11,1... | collective-permute-start | bytes 30728 | tf_op jit(solution)/shard_map/ppermute | solution.py:396
  15.2 10.1 %shard_map.104 = (f32[320,512]{1,0:T(8,128)S(1)}, bf16[5,320,128]{2,1,0:T(8,128)(2,1)S(1)}, f32[16,128]{1,0:T(8,128)S(1)}, f32[320,512]{1,0:T(8,128)S(1)}, s32[1,256]{1,0:T(1,128)S(1)}, /*index=5*/f32[1,256]{1,0:T(1,128)S(1)}) custom-call(f32[320,512]{1,0:T(8,128)} %bitcast.20, s32[6,512]{1,0:T(8,128)} %bitcast.22, bf16[6,5,320,512]{3,2,1,0:T(8,128)(2,1)} %bitcast.13, ...), custom_call_target="tpu_custom_call" | custom-call | flops 1006632960 | bytes 12451840 | tf_op jit(solution)/shard_map/pallas_call | solution.py:400
  25.3 0.0 collective-permute-done.lower_ref
  25.3 0.0 collective-permute-done.1.upper_ref
  25.3 0.0 all-to-all-done
  25.3 3.2 %shard_map.106 = (f32[320,512]{1,0:T(8,128)S(1)}, f32[1,128]{1,0:T(1,128)S(1)}, f32[256,320]{1,0:T(8,128)}, f32[8,320]{1,0:T(8,128)S(1)}, f32[8,320]{1,0:T(8,128)S(1)}) custom-call(f32[320,512]{1,0:T(8,128)S(1)} %get-tuple-element.23.local_ref, f32[256,320]{1,0:T(8,128)S(1)} %bitcast.11, f32[8,320]{1,0:T(8,128)S(1)} %collective-permute-done.lower_ref, ...), custom_call_target="tpu_custom_call" | custom-call | flops 335544320 | bytes 4259840 | tf_op jit(solution)/shard_map/pallas_call | solution.py:404
  28.6 3.1 %all-to-all-start.1 = ((f32[32,8,320]{2,1,0:T(8,128)}), f32[32,8,320]{2,1,0:T(8,128)S(1)}, u32[]{:S(2)}, u32[]{:S(2)}) async-start(f32[32,8,320]{2,1,0:T(8,128)} %bitcast.7), calls=%async_computation.1 | async-start | bytes 786432 | tf_op jit(solution)/shard_map/all_to_all | solution.py:395
  31.7 1.8 %collective-permute-start.2 = (f32[8,320]{1,0:T(8,128)S(1)}, f32[8,320]{1,0:T(8,128)S(1)}, u32[]{:S(2)}, u32[]{:S(2)}) collective-permute-start(f32[8,320]{1,0:T(8,128)S(1)} %get-tuple-element.37), channel_id=1, source_target_pairs={{0,1},{1,2},{2,3},{3,4},{4,5},{5,6},{6,7},{7,0},{8,9},{9,10},{10,1... | collective-permute-start | bytes 30728 | tf_op jit(solution)/shard_map/ppermute | solution.py:396
  33.5 3.0 %collective-permute-start.3 = (f32[8,320]{1,0:T(8,128)S(1)}, f32[8,320]{1,0:T(8,128)S(1)}, u32[]{:S(2)}, u32[]{:S(2)}) collective-permute-start(f32[8,320]{1,0:T(8,128)S(1)} %get-tuple-element.38), channel_id=1, source_target_pairs={{1,0},{2,1},{3,2},{4,3},{5,4},{6,5},{7,6},{0,7},{9,8},{10,9},{11,1... | collective-permute-start | bytes 30728 | tf_op jit(solution)/shard_map/ppermute | solution.py:396
  36.5 7.3 %shard_map.107.local_ref = f32[320,512]{1,0:T(8,128)S(1)} custom-call(f32[320,512]{1,0:T(8,128)S(1)} %get-tuple-element.35.x_ref, s32[6,512]{1,0:T(8,128)} %bitcast.23, bf16[6,5,320,512]{3,2,1,0:T(8,128)(2,1)} %bitcast.14, f32[320,512]{1,0:T(8,128)} %bitcast.18), custom_call_target="tpu_custom_call" | custom-call | flops 1006632960 | bytes 12451840 | tf_op jit(solution)/shard_map/pallas_call | solution.py:406
  43.8 0.2 collective-permute-done.2.lower_ref
  43.9 0.0 collective-permute-done.3.upper_ref
  43.9 1.6 %all-to-all-done.1 = f32[32,8,320]{2,1,0:T(8,128)S(1)} async-done(((f32[32,8,320]{2,1,0:T(8,128)}), f32[32,8,320]{2,1,0:T(8,128)S(1)}, u32[]{:S(2)}, u32[]{:S(2)}) %all-to-all-start.1) | async-done | bytes 327712 | tf_op jit(solution)/shard_map/all_to_all | solution.py:395
  45.5 1.3 %shard_map.108 = (f32[320,512]{1,0:T(8,128)S(1)}, f32[32,2,128]{2,1,0:T(2,128)}) custom-call(f32[320,512]{1,0:T(8,128)S(1)} %shard_map.107.local_ref, f32[256,320]{1,0:T(8,128)S(1)} %bitcast.12, f32[8,320]{1,0:T(8,128)S(1)} %collective-permute-done.2.lower_ref, f32[8,320]{1,0:T(8,128)S(1)} %collective-permute-done.3.upper_ref, ...), custom_call_target="tpu_custom_call" | custom-call | flops 167772160 | bytes 1966080 | tf_op jit(solution)/shard_map/pallas_call | solution.py:407
  46.9 2.6 %all-to-all-start.2 = ((f32[32,2,128]{2,1,0:T(2,128)}), f32[32,2,128]{2,1,0:T(2,128)S(1)}, u32[]{:S(2)}, u32[]{:S(2)}) async-start(f32[32,2,128]{2,1,0:T(2,128)} %get-tuple-element.40), calls=%async_computation.2 | async-start | bytes 65536 | tf_op jit(solution)/shard_map/all_to_all | solution.py:408
  49.4 2.6 %shard_map.109 = (f32[320,512]{1,0:T(8,128)S(1)}, f32[320,512]{1,0:T(8,128)}) custom-call(bf16[5,320,512]{2,1,0:T(8,128)(2,1)} %bitcast.16, f32[320,512]{1,0:T(8,128)S(1)} %get-tuple-element.41.resid_ref), custom_call_target="tpu_custom_call" | custom-call | flops 1638400 | bytes 2949120 | tf_op jit(solution)/shard_map/pallas_call | solution.py:409
  52.1 4.5 %all-to-all-done.2.sums_ref = f32[32,2,128]{2,1,0:T(2,128)S(1)} async-done(((f32[32,2,128]{2,1,0:T(2,128)}), f32[32,2,128]{2,1,0:T(2,128)S(1)}, u32[]{:S(2)}, u32[]{:S(2)}) %all-to-all-start.2) | async-done | bytes 32800 | tf_op jit(solution)/shard_map/all_to_all | solution.py:408
  56.6 1.1 %shard_map.110 = f32[320,512]{1,0:T(8,128)} custom-call(f32[32,2,128]{2,1,0:T(2,128)S(1)} %all-to-all-done.2.sums_ref, f32[320,512]{1,0:T(8,128)S(1)} %get-tuple-element.35.x_ref, f32[320,512]{1,0:T(8,128)S(1)} %get-tuple-element.42.update_ref), custom_call_target="tpu_custom_call" | custom-call | flops 327680 | bytes 1966080 | tf_op jit(solution)/shard_map/pallas_call | solution.py:410
Async XLA Ops:
  3.1 22.2 %all-to-all-start = ((f32[32,8,320]{2,1,0:T(8,128)}), f32[32,8,320]{2,1,0:T(8,128)S(1)}, u32[]{:S(2)}, u32[]{:S(2)}) async-start(f32[32,8,320]{2,1,0:T(8,128)} %bitcast.4), calls=%async_computation | async-start | bytes 786432 | tf_op jit(solution)/shard_map/all_to_all | solution.py:395
  10.4 14.9 %collective-permute-start = (f32[8,320]{1,0:T(8,128)S(1)}, f32[8,320]{1,0:T(8,128)S(1)}, u32[]{:S(2)}, u32[]{:S(2)}) collective-permute-start(f32[8,320]{1,0:T(8,128)S(1)} %get-tuple-element.25), channel_id=1, source_target_pairs={{0,1},{1,2},{2,3},{3,4},{4,5},{5,6},{6,7},{7,0},{8,9},{9,10},{10,1... | collective-permute-start | bytes 30728 | tf_op jit(solution)/shard_map/ppermute | solution.py:396
  12.2 13.1 %collective-permute-start.1 = (f32[8,320]{1,0:T(8,128)S(1)}, f32[8,320]{1,0:T(8,128)S(1)}, u32[]{:S(2)}, u32[]{:S(2)}) collective-permute-start(f32[8,320]{1,0:T(8,128)S(1)} %get-tuple-element.26), channel_id=1, source_target_pairs={{1,0},{2,1},{3,2},{4,3},{5,4},{6,5},{7,6},{0,7},{9,8},{10,9},{11,1... | collective-permute-start | bytes 30728 | tf_op jit(solution)/shard_map/ppermute | solution.py:396
  28.6 17.0 %all-to-all-start.1 = ((f32[32,8,320]{2,1,0:T(8,128)}), f32[32,8,320]{2,1,0:T(8,128)S(1)}, u32[]{:S(2)}, u32[]{:S(2)}) async-start(f32[32,8,320]{2,1,0:T(8,128)} %bitcast.7), calls=%async_computation.1 | async-start | bytes 786432 | tf_op jit(solution)/shard_map/all_to_all | solution.py:395
  31.7 12.2 %collective-permute-start.2 = (f32[8,320]{1,0:T(8,128)S(1)}, f32[8,320]{1,0:T(8,128)S(1)}, u32[]{:S(2)}, u32[]{:S(2)}) collective-permute-start(f32[8,320]{1,0:T(8,128)S(1)} %get-tuple-element.37), channel_id=1, source_target_pairs={{0,1},{1,2},{2,3},{3,4},{4,5},{5,6},{6,7},{7,0},{8,9},{9,10},{10,1... | collective-permute-start | bytes 30728 | tf_op jit(solution)/shard_map/ppermute | solution.py:396
  33.5 10.4 %collective-permute-start.3 = (f32[8,320]{1,0:T(8,128)S(1)}, f32[8,320]{1,0:T(8,128)S(1)}, u32[]{:S(2)}, u32[]{:S(2)}) collective-permute-start(f32[8,320]{1,0:T(8,128)S(1)} %get-tuple-element.38), channel_id=1, source_target_pairs={{1,0},{2,1},{3,2},{4,3},{5,4},{6,5},{7,6},{0,7},{9,8},{10,9},{11,1... | collective-permute-start | bytes 30728 | tf_op jit(solution)/shard_map/ppermute | solution.py:396
  46.9 9.8 %all-to-all-start.2 = ((f32[32,2,128]{2,1,0:T(2,128)}), f32[32,2,128]{2,1,0:T(2,128)S(1)}, u32[]{:S(2)}, u32[]{:S(2)}) async-start(f32[32,2,128]{2,1,0:T(2,128)} %get-tuple-element.40), calls=%async_computation.2 | async-start | bytes 65536 | tf_op jit(solution)/shard_map/all_to_all | solution.py:408

commit v4 on v3

--- a/solution.py
+++ b/solution.py
@@ -84,90 +84,106 @@
     sel_down_ref[...] = sel_down
 
 
-def local_kernel(rim, x_ref, nbr_ref, coup_ref, source_ref, out_ref, high, low, near):
-    step = pl.program_id(0)
-    slots = nbr_ref.shape[0]
-
-    @pl.when(step == 0)
-    def _():
-        lane = lax.broadcasted_iota(jnp.int32, (BW, LANES), 1)
-        moved = pltpu.roll(x_ref[...], rim, 1)
-        head = jnp.where(lane < rim, 0.0, moved[:, :LANES])
-        tail = jnp.where(lane < rim, moved[:, :LANES], 0.0)
-        ext = jnp.concatenate([head, moved[:, LANES:], tail], axis=1)
-        high[...], low[...] = split(ext)
-
-    start = pl.multiple_of(step * LANES, LANES)
-    here = pl.ds(start, LANES)
-    window = pl.ds(start, 2 * LANES)
+def local_kernel(
+    rim, x_ref, nbr_ref, coup_ref, source_ref, out_ref, high, low, near, coup, source, sems, source_sem
+):
+    slots, blocks = nbr_ref.shape
+    chunks = blocks // LANES
+    spans = [slice(c * LANES, (c + 1) * LANES) for c in range(chunks)]
+    copies = [
+        pltpu.make_async_copy(coup_ref.at[:, :, :, spans[c]], coup.at[c], sems.at[c])
+        for c in range(chunks)
+    ]
+    for copy in copies:
+        copy.start()
+    source_copy = pltpu.make_async_copy(source_ref, source, source_sem)
+    source_copy.start()
+    lane = lax.broadcasted_iota(jnp.int32, (BW, LANES), 1)
+    moved = pltpu.roll(x_ref[...], rim, 1)
+    head = jnp.where(lane < rim, 0.0, moved[:, :LANES])
+    tail = jnp.where(lane < rim, moved[:, :LANES], 0.0)
+    high[...], low[...] = split(jnp.concatenate([head, moved[:, LANES:], tail], axis=1))
     rows = lax.broadcasted_iota(jnp.int32, (2 * LANES, LANES), 0)
-    table = jnp.concatenate(
-        [onehot(rows == nbr_ref[m : m + 1, :] - start) for m in range(slots)], axis=1
-    )
-    near[...] = jnp.dot(high[:, window], table, preferred_element_type=jnp.float32) + jnp.dot(
-        low[:, window], table, preferred_element_type=jnp.float32
-    )
-
-    def cells(part, carry):
-        at = pl.multiple_of(part * PACK, PACK)
-        total = [None] * VARS
-        for m in range(slots):
-            for v in range(VARS):
-                value = near[pl.ds(v * CELLS + at, PACK), m * LANES : (m + 1) * LANES]
-                for u in range(VARS):
-                    term = coup_ref[m, u, pl.ds(v * CELLS + at, PACK), :].astype(jnp.float32) * value
-                    total[u] = term if total[u] is None else total[u] + term
-        for u in range(VARS):
-            span = pl.ds(u * CELLS + at, PACK)
-            out_ref[span, :] = source_ref[span, :] - x_ref[span, here] + total[u]
-        return carry
-
-    lax.fori_loop(0, CELLS // PACK, cells, 0)
+
+    def gather(c):
+        window = slice(c * LANES, (c + 2) * LANES)
+        table = jnp.concatenate(
+            [onehot(rows == nbr_ref[m : m + 1, spans[c]] - c * LANES) for m in range(slots)], axis=1
+        )
+        near[c][...] = jnp.dot(high[:, window], table, preferred_element_type=jnp.float32) + jnp.dot(
+            low[:, window], table, preferred_element_type=jnp.float32
+        )
+
+    gather(0)
+    for c in range(chunks):
+        copies[c].wait()
+        if c == 0:
+            source_copy.wait()
+        if c + 1 < chunks:
+            gather(c + 1)
+        for at in range(0, CELLS, PACK):
+            total = [None] * VARS
+            for m in range(slots):
+                for v in range(VARS):
+                    span = slice(v * CELLS + at, v * CELLS + at + PACK)
+                    value = near[c][span, m * LANES : (m + 1) * LANES]
+                    for u in range(VARS):
+                        term = coup[c, m, u, span, :].astype(jnp.float32) * value
+                        total[u] = term if total[u] is None else total[u] + term
+            for u in range(VARS):
+                span = slice(u * CELLS + at, u * CELLS + at + PACK)
+                out_ref[span, spans[c]] = source[span, spans[c]] - x_ref[span, spans[c]] + total[u]
 
 
 def first_local_kernel(
     rim, x_ref, nbr_ref, coup_ref, source_ref, dst_ref, weight_ref,
-    out_ref, rimcoup_ref, rimrow_ref, x_out, dst_out, weight_out, high, low, near,
+    out_ref, rimcoup_ref, rimrow_ref, x_out, table_ref, weight_out,
+    high, low, near, coup, source, sems, source_sem,
 ):
-    step = pl.program_id(0)
-    last = pl.num_programs(0) - 1
-    slots = nbr_ref.shape[0]
-    blocks = x_ref.shape[1]
-    local_kernel(rim, x_ref, nbr_ref, coup_ref, source_ref, out_ref, high, low, near)
-    x_out[...] = x_ref[:, pl.ds(pl.multiple_of(step * LANES, LANES), LANES)]
-    dst_out[...] = dst_ref[...]
+    slots, blocks = nbr_ref.shape
+    fringe = dst_ref.shape[1]
+    local_kernel(
+        rim, x_ref, nbr_ref, coup_ref, source_ref, out_ref, high, low, near, coup, source, sems, source_sem
+    )
+    x_out[...] = x_ref[...]
     weight_out[...] = weight_ref[...]
-
-    @pl.when((step == 0) | (step == last))
-    def _():
-        sub = lax.broadcasted_iota(jnp.int32, (LANES, LANES), 0)
-        lane = lax.broadcasted_iota(jnp.int32, (LANES, LANES), 1)
-        base = jnp.where(step == 0, 0, rim)
-        at = sub - jnp.where(step == 0, 0, LANES - 2 * rim)
-        inside = (at >= base) & (at < base + rim)
-        place = jnp.concatenate(
-            [onehot((lane == at + m * 2 * rim) & inside) for m in range(slots)], axis=0
+    sub = lax.broadcasted_iota(jnp.int32, (LANES, LANES), 0)
+    lane = lax.broadcasted_iota(jnp.int32, (LANES, LANES), 1)
+    at_end = sub >= LANES // 2
+    source_lane = sub - jnp.where(at_end, LANES - 2 * rim, 0)
+    valid = (sub < rim) | (sub >= LANES - rim)
+    place = jnp.concatenate(
+        [onehot((lane == source_lane + m * 2 * rim) & valid) for m in range(slots)], axis=0
+    )
+    first_row = lane[:1] < LANES // 2
+    reads = []
+    for m in range(slots):
+        lower = nbr_ref[m : m + 1, :LANES]
+        upper = nbr_ref[m : m + 1, blocks - LANES :]
+        lower = jnp.where(lower < rim, lower + 1, 0)
+        upper = jnp.where(upper >= blocks + rim, upper - blocks + 1, 0)
+        reads.append(jnp.where(first_row, lower, upper))
+    reads = jnp.broadcast_to(jnp.concatenate(reads, axis=1), (PACK, slots * LANES))
+    reads = reads.astype(jnp.float32).astype(jnp.bfloat16)
+    rimrow_ref[...] = jnp.dot(reads, place, preferred_element_type=jnp.float32)
+    first = lax.broadcasted_iota(jnp.int32, (BW, LANES), 1) < LANES // 2
+    end = blocks // LANES - 1
+    for u in range(VARS):
+        rows = jnp.concatenate(
+            [jnp.where(first, coup[0, m, u], coup[end, m, u]) for m in range(slots)], axis=1
         )
-        reads = []
-        for m in range(slots):
-            row = nbr_ref[m : m + 1, :]
-            lower = jnp.where(row < rim, row + 1, 0)
-            upper = jnp.where(row >= blocks + rim, row - blocks + 1, 0)
-            reads.append(jnp.where(step == 0, lower, upper))
-        reads = jnp.broadcast_to(jnp.concatenate(reads, axis=1), (PACK, slots * LANES))
-        reads = reads.astype(jnp.float32).astype(jnp.bfloat16)
-        kept = jnp.where(step == 0, 0.0, rimrow_ref[...])
-        rimrow_ref[...] = kept + jnp.dot(reads, place, preferred_element_type=jnp.float32)
-        for u in range(VARS):
-            rows = jnp.concatenate([coup_ref[m, u] for m in range(slots)], axis=1)
-            moved = jnp.dot(rows, place, preferred_element_type=jnp.float32)
-            kept = jnp.where(step == 0, 0.0, rimcoup_ref[u].astype(jnp.float32))
-            rimcoup_ref[u] = (kept + moved).astype(jnp.bfloat16)
-
-
-def full_residual(local_ref, inc_ref, lower_ref, upper_ref, dst_ref, weight_ref, rimcoup_ref, rimrow_ref):
-    blocks = local_ref.shape[1]
-    slots = inc_ref.shape[0]
+        rimcoup_ref[u] = jnp.dot(rows, place, preferred_element_type=jnp.float32).astype(jnp.bfloat16)
+    targets = jnp.broadcast_to(dst_ref[...], (LANES, fringe)).T
+    edge = lax.rem(sub, 2 * rim)
+    edge = jnp.where(edge < rim, edge, edge + (blocks - 2 * rim))
+    for c in range(blocks // LANES):
+        span = slice(c * LANES, (c + 1) * LANES)
+        block = lane[:1] + c * LANES
+        table_ref[:fringe, span] = onehot(targets == block)
+        table_ref[fringe:, span] = onehot(edge == block)
+
+
+def full_residual(local_ref, inc_ref, lower_ref, upper_ref, table_ref, weight_ref, rimcoup_ref, rimrow_ref):
     rim = lower_ref.shape[0]
     rims = jnp.concatenate(
         [lower_ref[...], upper_ref[...], jnp.zeros((LANES - 2 * rim, BW), jnp.float32)], axis=0
@@ -183,18 +199,8 @@
             total = term if total is None else total + term
         edge.append(total)
     edge = jnp.concatenate(edge, axis=0)
-    rows = lax.broadcasted_iota(jnp.int32, (blocks, slots), 0)
-    edge_rows = lax.broadcasted_iota(jnp.int32, (blocks, LANES), 0)
-    place = lax.rem(lax.broadcasted_iota(jnp.int32, (1, LANES), 1), 2 * rim)
-    place = jnp.where(place < rim, place, place + (blocks - 2 * rim))
-    table = jnp.concatenate([onehot(rows == dst_ref[...]), onehot(edge_rows == place)], axis=1)
-    high, low = split(jnp.concatenate([inc_ref[...].T * weight_ref[...], edge], axis=1))
-    contract = (((1,), (1,)), ((), ()))
-    return (
-        local_ref[...]
-        + lax.dot_general(high, table, contract, preferred_element_type=jnp.float32)
-        + lax.dot_general(low, table, contract, preferred_element_type=jnp.float32)
-    )
+    arrived = jnp.concatenate([inc_ref[...].T * weight_ref[...], edge], axis=1)
+    return local_ref[...] + pick(arrived, table_ref[...])
 
 
 def precondition(diag_ref, resid_ref, u, at):
@@ -212,14 +218,14 @@
 
 
 def advance_kernel(
-    local_ref, inc_ref, lower_ref, upper_ref, dst_ref, weight_ref, rimcoup_ref, rimrow_ref,
+    local_ref, inc_ref, lower_ref, upper_ref, across_ref, weight_ref, rimcoup_ref, rimrow_ref,
     diag_ref, x_ref, table_ref, sel_up_ref, sel_down_ref,
     next_ref, norm_ref, out_ref, up_ref, down_ref, resid, diag, diag_sem,
 ):
     fetch = pltpu.make_async_copy(diag_ref, diag, diag_sem)
     fetch.start()
     resid[...] = full_residual(
-        local_ref, inc_ref, lower_ref, upper_ref, dst_ref, weight_ref, rimcoup_ref, rimrow_ref
+        local_ref, inc_ref, lower_ref, upper_ref, across_ref, weight_ref, rimcoup_ref, rimrow_ref
     )
     fetch.wait()
 
@@ -238,11 +244,11 @@
 
 
 def residual_kernel(
-    local_ref, inc_ref, lower_ref, upper_ref, dst_ref, weight_ref, rimcoup_ref, rimrow_ref, norm_ref,
+    local_ref, inc_ref, lower_ref, upper_ref, across_ref, weight_ref, rimcoup_ref, rimrow_ref, norm_ref,
     resid_ref, sums_ref,
 ):
     resid = full_residual(
-        local_ref, inc_ref, lower_ref, upper_ref, dst_ref, weight_ref, rimcoup_ref, rimrow_ref
+        local_ref, inc_ref, lower_ref, upper_ref, across_ref, weight_ref, rimcoup_ref, rimrow_ref
     )
     resid_ref[...] = resid
     both = jnp.concatenate([norm_ref[...], lane_sums(resid)], axis=0)
@@ -321,49 +327,38 @@
         4 * BW * blocks * fringe,
         2 * size,
     )
-    column = pl.BlockSpec((BW, LANES), lambda i: (0, i))
-    whole_row = pl.BlockSpec((1, fringe), lambda i: (0, 0))
-    local_in = [
-        pl.BlockSpec((BW, blocks), lambda i: (0, 0)),
-        pl.BlockSpec((slots, LANES), lambda i: (0, i)),
-        pl.BlockSpec((slots, VARS, BW, LANES), lambda i: (0, 0, 0, i)),
-        column,
-    ]
+    hbm = pl.BlockSpec(memory_space=pltpu.HBM)
+    chunks = blocks // LANES
     local_more = dict(
         flops=4 * BW * 2 * LANES * slots * blocks,
         moved=coup.size * 2 + 4 * size,
-        grid=(blocks // LANES,),
         scratch_shapes=[
             pltpu.VMEM((BW, blocks + LANES), jnp.bfloat16),
             pltpu.VMEM((BW, blocks + LANES), jnp.bfloat16),
-            pltpu.VMEM((BW, slots * LANES), jnp.float32),
+            [pltpu.VMEM((BW, slots * LANES), jnp.float32)] * chunks,
+            pltpu.VMEM((chunks, slots, VARS, BW, LANES), jnp.bfloat16),
+            pltpu.VMEM((BW, blocks), jnp.float32),
+            pltpu.SemaphoreType.DMA((chunks,)),
+            pltpu.SemaphoreType.DMA,
         ],
     )
     first_local = call(
         functools.partial(first_local_kernel, rim),
-        local_in + [whole_row, whole_row],
+        [VMEM, VMEM, hbm, hbm, VMEM, VMEM],
         [
             state,
             bf16(VARS, BW, LANES),
             f32(PACK, LANES),
             state,
-            jax.ShapeDtypeStruct((1, fringe), jnp.int32),
+            bf16(fringe + LANES, blocks),
             f32(1, fringe),
         ],
-        out_specs=[
-            column,
-            pl.BlockSpec((VARS, BW, LANES), lambda i: (0, 0, 0)),
-            pl.BlockSpec((PACK, LANES), lambda i: (0, 0)),
-            column,
-            whole_row,
-            whole_row,
-        ],
         **local_more,
     )
-    local = call(functools.partial(local_kernel, rim), local_in, state, out_specs=column, **local_more)
+    local = call(functools.partial(local_kernel, rim), [VMEM, VMEM, hbm, hbm], state, **local_more)
     advance = call(
         advance_kernel,
-        [VMEM] * 8 + [pl.BlockSpec(memory_space=pltpu.HBM)] + [VMEM] * 4,
+        [VMEM] * 8 + [hbm] + [VMEM] * 4,
         [state, f32(1, LANES)] + sent,
         8 * BW * blocks * fringe,
         diag.size * 2 + 4 * size,
@@ -376,7 +371,7 @@
     residual = call(
         residual_kernel,
         [VMEM] * 9,
-        [state, f32(devices, 2, LANES)],
+        [state, f32(peers, 2, LANES)],
         4 * BW * blocks * fringe,
         3 * size,
     )
@@ -397,15 +392,17 @@
 
     *out, table, sel_up, sel_down = donors(x, here(fringe_src), here(seam_perm))
     arrived = exchange(*out)
-    part, rimcoup, rimrow, x, dst, weight = first_local(
+    part, rimcoup, rimrow, x, across, weight = first_local(
         x, nbr, coup, source_t, here(fringe_dst), here(fringe_weight)
     )
-    across = (dst, weight, rimcoup, rimrow)
+    across = (across, weight, rimcoup, rimrow)
     x, norm, *out = advance(part, *arrived, *across, diag, x, table, sel_up, sel_down)
     arrived = exchange(*out)
     part = local(x, nbr, coup, source_t)
     resid, sums = residual(part, *arrived, *across, norm)
-    sums = lax.all_to_all(sums, ("body", "blk"), split_axis=0, concat_axis=0, tiled=True)
+    sums = lax.all_to_all(sums, "blk", split_axis=0, concat_axis=0, tiled=True)
+    sums = jnp.broadcast_to(jnp.sum(sums, axis=0, keepdims=True), (devices // peers, 2, LANES))
+    sums = lax.all_to_all(sums, "body", split_axis=0, concat_axis=0, tiled=True)
     update, resid = direction(diag, resid)
     x = finish(sums, x, update)
     return (x.T, resid.T)

time: 58.2 us -> 64.4 us (1.11)
  blocking collectives: 0 us -> 9.36 us
  waiting for transfers between devices: 6.3 us -> 3.79 us
  Pallas kernels: 28.1 us -> 26.2 us
    all_to_all x0 -> x1, blocking collectives: none -> 9.36 us  [shards(): sums = lax.all_to_all(sums, 'blk', split_axis=0, concat_axis=0, tiled=True)]
    all_to_all x1, waiting for transfers between devices: 4.55 us -> 1.11 us  [shards(): sums = lax.all_to_all(sums, 'body', split_axis=0, concat_axis=0, tiled=True)]
    ppermute x2, waiting for transfers between devices: 0.16 us -> 1.08 us  [exchange(): lax.ppermute(to_up, 'blk', up)]
    pallas_call x1, Pallas kernels: 7.27 us -> 6.35 us  [shards(): part = local(x, nbr, coup, source_t)]
    all_to_all x1, starting transfers between devices: 2.57 us -> 3.25 us  [shards(): sums = lax.all_to_all(sums, 'body', split_axis=0, concat_axis=0, tiled=True)]
    pallas_call x1, Pallas kernels: 1.35 us -> 0.69 us  [shards(): resid, sums = residual(part, *arrived, *across, norm)]
  transfers between devices with their start and end apart: 7 -> 7, of which waited for: 3 -> 3; matrix products, arithmetic and copies ran while one was open for 0% -> 0% of each run, Pallas kernels for 35% -> 29%
where the time goes in v4:
time: 64.4 us; the launch traced here: 63.9 us
  Pallas kernels  26.2 us (41%)
  starting transfers between devices  23.2 us (36%)
  blocking collectives  9.36 us (15%)
  waiting for transfers between devices  3.79 us (6%)
  between operations  0.71 us (1%)
    all_to_all x2, starting transfers between devices, exchange(): lax.all_to_all(rows, ('body', 'blk'), split_axis=0, concat_axis=0, tiled=...  10.4 us
    pallas_call x1, Pallas kernels, shards(): first_local(x, nbr, coup, source_t, here(fringe_dst), here(fringe_weight))  9.79 us
    all_to_all x1, blocking collectives, shards(): sums = lax.all_to_all(sums, 'blk', split_axis=0, concat_axis=0, tiled=True)  9.36 us
    pallas_call x1, Pallas kernels, shards(): part = local(x, nbr, coup, source_t)  6.35 us
    ppermute x2, starting transfers between devices, exchange(): lax.ppermute(to_down, 'blk', down)  5.91 us
    ppermute x2, starting transfers between devices, exchange(): lax.ppermute(to_up, 'blk', up)  3.64 us
    all_to_all x1, starting transfers between devices, shards(): sums = lax.all_to_all(sums, 'body', split_axis=0, concat_axis=0, tiled=True)  3.25 us
    pallas_call x1, Pallas kernels, shards(): advance(part, *arrived, *across, diag, x, table, sel_up, sel_down)  3.17 us
  transfers between devices with their start and end apart: 7, of which 3 were waited for; matrix products, arithmetic and copies ran while one was open for 0% of the time, Pallas kernels for 29%

profile of v4, /device:TPU:0, one launch (start us, length us, event | category | flops | bytes accessed | tf_op | source)
XLA Modules:
  0.0 63.9 jit_solution(7702798838476056283)
XLA Ops:
  0.6 2.4 %shard_map.105 = (f32[256,320]{1,0:T(8,128)}, f32[8,320]{1,0:T(8,128)S(1)}, f32[8,320]{1,0:T(8,128)S(1)}, bf16[512,256]{1,0:T(8,128)(2,1)S(1)}, bf16[128,128]{1,...) custom-call(f32[320,512]{1,0:T(8,128)} %bitcast.19, s32[1,256]{1,0:T(1,128)} %src_ref.1, s32[1,8]{1,0:T(1,128)} %perm_ref.1), custom_call_target="tpu_custom_call" | custom-call | flops 167772160 | bytes 1310720 | tf_op jit(solution)/shard_map/pallas_call | solution.py:393
  3.1 7.3 %all-to-all-start = ((f32[32,8,320]{2,1,0:T(8,128)}), f32[32,8,320]{2,1,0:T(8,128)S(1)}, u32[]{:S(2)}, u32[]{:S(2)}) async-start(f32[32,8,320]{2,1,0:T(8,128)} %bitcast.4), calls=%async_computation | async-start | bytes 786432 | tf_op jit(solution)/shard_map/all_to_all | solution.py:390
  10.4 1.8 %collective-permute-start = (f32[8,320]{1,0:T(8,128)S(1)}, f32[8,320]{1,0:T(8,128)S(1)}, u32[]{:S(2)}, u32[]{:S(2)}) collective-permute-start(f32[8,320]{1,0:T(8,128)S(1)} %get-tuple-element.25), channel_id=1, source_target_pairs={{0,1},{1,2},{2,3},{3,4},{4,5},{5,6},{6,7},{7,0},{8,9},{9,10},{10,1... | collective-permute-start | bytes 30728 | tf_op jit(solution)/shard_map/ppermute | solution.py:391
  12.2 3.0 %collective-permute-start.1 = (f32[8,320]{1,0:T(8,128)S(1)}, f32[8,320]{1,0:T(8,128)S(1)}, u32[]{:S(2)}, u32[]{:S(2)}) collective-permute-start(f32[8,320]{1,0:T(8,128)S(1)} %get-tuple-element.26), channel_id=1, source_target_pairs={{1,0},{2,1},{3,2},{4,3},{5,4},{6,5},{7,6},{0,7},{9,8},{10,9},{11,1... | collective-permute-start | bytes 30728 | tf_op jit(solution)/shard_map/ppermute | solution.py:391
  15.2 9.8 %shard_map.104 = (f32[320,512]{1,0:T(8,128)S(1)}, bf16[5,320,128]{2,1,0:T(8,128)(2,1)S(1)}, f32[16,128]{1,0:T(8,128)S(1)}, f32[320,512]{1,0:T(8,128)S(1)}, bf16[...) custom-call(f32[320,512]{1,0:T(8,128)} %bitcast.20, s32[6,512]{1,0:T(8,128)} %bitcast.22, ...), custom_call_target="tpu_custom_call" | custom-call | flops 1006632960 | bytes 12451840 | tf_op jit(solution)/shard_map/pallas_call | solution.py:395
  25.0 0.0 collective-permute-done.lower_ref
  25.0 0.0 collective-permute-done.1.upper_ref
  25.0 0.0 all-to-all-done
  25.0 3.2 %shard_map.106 = (f32[320,512]{1,0:T(8,128)S(1)}, f32[1,128]{1,0:T(1,128)S(1)}, f32[256,320]{1,0:T(8,128)}, f32[8,320]{1,0:T(8,128)S(1)}, f32[8,320]{1,0:T(8,128)S(1)}) custom-call(f32[320,512]{1,0:T(8,128)S(1)} %get-tuple-element.23.local_ref, f32[256,320]{1,0:T(8,128)S(1)} %bitcast.11, f32[8,320]{1,0:T(8,128)S(1)} %collective-permute-done.lower_ref, ...), custom_call_target="tpu_custom_call" | custom-call | flops 335544320 | bytes 4259840 | tf_op jit(solution)/shard_map/pallas_call | solution.py:399
  28.2 3.1 %all-to-all-start.1 = ((f32[32,8,320]{2,1,0:T(8,128)}), f32[32,8,320]{2,1,0:T(8,128)S(1)}, u32[]{:S(2)}, u32[]{:S(2)}) async-start(f32[32,8,320]{2,1,0:T(8,128)} %bitcast.7), calls=%async_computation.1 | async-start | bytes 786432 | tf_op jit(solution)/shard_map/all_to_all | solution.py:390
  31.3 1.8 %collective-permute-start.2 = (f32[8,320]{1,0:T(8,128)S(1)}, f32[8,320]{1,0:T(8,128)S(1)}, u32[]{:S(2)}, u32[]{:S(2)}) collective-permute-start(f32[8,320]{1,0:T(8,128)S(1)} %get-tuple-element.37), channel_id=1, source_target_pairs={{0,1},{1,2},{2,3},{3,4},{4,5},{5,6},{6,7},{7,0},{8,9},{9,10},{10,1... | collective-permute-start | bytes 30728 | tf_op jit(solution)/shard_map/ppermute | solution.py:391
  33.1 3.0 %collective-permute-start.3 = (f32[8,320]{1,0:T(8,128)S(1)}, f32[8,320]{1,0:T(8,128)S(1)}, u32[]{:S(2)}, u32[]{:S(2)}) collective-permute-start(f32[8,320]{1,0:T(8,128)S(1)} %get-tuple-element.38), channel_id=1, source_target_pairs={{1,0},{2,1},{3,2},{4,3},{5,4},{6,5},{7,6},{0,7},{9,8},{10,9},{11,1... | collective-permute-start | bytes 30728 | tf_op jit(solution)/shard_map/ppermute | solution.py:391
  36.1 6.4 %shard_map.107.local_ref = f32[320,512]{1,0:T(8,128)S(1)} custom-call(f32[320,512]{1,0:T(8,128)S(1)} %get-tuple-element.35.x_ref, s32[6,512]{1,0:T(8,128)} %bitcast.23, bf16[6,5,320,512]{3,2,1,0:T(8,128)(2,1)} %bitcast.14, f32[320,512]{1,0:T(8,128)} %bitcast.18), custom_call_target="tpu_custom_call" | custom-call | flops 1006632960 | bytes 12451840 | tf_op jit(solution)/shard_map/pallas_call | solution.py:401
  42.5 1.1 %collective-permute-done.2.lower_ref = f32[8,320]{1,0:T(8,128)S(1)} collective-permute-done((f32[8,320]{1,0:T(8,128)S(1)}, f32[8,320]{1,0:T(8,128)S(1)}, u32[]{:S(2)}, u32[]{:S(2)}) %collective-permute-start.2) | collective-permute-done | bytes 10272 | tf_op jit(solution)/shard_map/ppermute | solution.py:391
  43.5 0.0 collective-permute-done.3.upper_ref
  43.5 1.6 %all-to-all-done.1 = f32[32,8,320]{2,1,0:T(8,128)S(1)} async-done(((f32[32,8,320]{2,1,0:T(8,128)}), f32[32,8,320]{2,1,0:T(8,128)S(1)}, u32[]{:S(2)}, u32[]{:S(2)}) %all-to-all-start.1) | async-done | bytes 327712 | tf_op jit(solution)/shard_map/all_to_all | solution.py:390
  45.1 0.7 %shard_map.108 = (f32[320,512]{1,0:T(8,128)S(1)}, f32[8,2,128]{2,1,0:T(2,128)S(1)}) custom-call(f32[320,512]{1,0:T(8,128)S(1)} %shard_map.107.local_ref, f32[256,320]{1,0:T(8,128)S(1)} %bitcast.12, f32[8,320]{1,0:T(8,128)S(1)} %collective-permute-done.2.lower_ref, f32[8,320]{1,0:T(8,128)S(1)} %collective-permute-done.3.upper_ref, ...), custom_call_target="tpu_custom_call" | custom-call | flops 167772160 | bytes 1966080 | tf_op jit(solution)/shard_map/pallas_call | solution.py:402
  45.8 9.4 %all_to_all.32 = f32[8,2,128]{2,1,0:T(2,128)S(1)} all-to-all(f32[8,2,128]{2,1,0:T(2,128)S(1)} %get-tuple-element.40), channel_id=1, replica_groups=mesh['body'=4,'blk'=8] {'blk'}, dimensions={0} | all-to-all | bytes 16384 | tf_op jit(solution)/shard_map/all_to_all | solution.py:403
  55.2 0.6 broadcast_in_dim.2
  55.8 3.2 %all-to-all-start.3 = ((f32[4,2,128]{2,1,0:T(2,128)}), f32[4,2,128]{2,1,0:T(2,128)S(1)}, u32[]{:S(2)}, u32[]{:S(2)}) async-start(f32[4,2,128]{2,1,0:T(2,128)} %broadcast_in_dim.2), calls=%async_computation.3 | async-start | bytes 8192 | tf_op jit(solution)/shard_map/all_to_all | solution.py:405
  59.1 2.6 %shard_map.109 = (f32[320,512]{1,0:T(8,128)S(1)}, f32[320,512]{1,0:T(8,128)}) custom-call(bf16[5,320,512]{2,1,0:T(8,128)(2,1)} %bitcast.16, f32[320,512]{1,0:T(8,128)S(1)} %get-tuple-element.41.resid_ref), custom_call_target="tpu_custom_call" | custom-call | flops 1638400 | bytes 2949120 | tf_op jit(solution)/shard_map/pallas_call | solution.py:406
  61.7 1.1 %all-to-all-done.3.sums_ref = f32[4,2,128]{2,1,0:T(2,128)S(1)} async-done(((f32[4,2,128]{2,1,0:T(2,128)}), f32[4,2,128]{2,1,0:T(2,128)S(1)}, u32[]{:S(2)}, u32[]{:S(2)}) %all-to-all-start.3) | async-done | bytes 4128 | tf_op jit(solution)/shard_map/all_to_all | solution.py:405
  62.8 1.1 %shard_map.110 = f32[320,512]{1,0:T(8,128)} custom-call(f32[4,2,128]{2,1,0:T(2,128)S(1)} %all-to-all-done.3.sums_ref, f32[320,512]{1,0:T(8,128)S(1)} %get-tuple-element.35.x_ref, f32[320,512]{1,0:T(8,128)S(1)} %get-tuple-element.42.update_ref), custom_call_target="tpu_custom_call" | custom-call | flops 327680 | bytes 1966080 | tf_op jit(solution)/shard_map/pallas_call | solution.py:407
  (1 shorter events, 0.0 us)
Async XLA Ops:
  3.1 21.9 %all-to-all-start = ((f32[32,8,320]{2,1,0:T(8,128)}), f32[32,8,320]{2,1,0:T(8,128)S(1)}, u32[]{:S(2)}, u32[]{:S(2)}) async-start(f32[32,8,320]{2,1,0:T(8,128)} %bitcast.4), calls=%async_computation | async-start | bytes 786432 | tf_op jit(solution)/shard_map/all_to_all | solution.py:390
  10.4 14.6 %collective-permute-start = (f32[8,320]{1,0:T(8,128)S(1)}, f32[8,320]{1,0:T(8,128)S(1)}, u32[]{:S(2)}, u32[]{:S(2)}) collective-permute-start(f32[8,320]{1,0:T(8,128)S(1)} %get-tuple-element.25), channel_id=1, source_target_pairs={{0,1},{1,2},{2,3},{3,4},{4,5},{5,6},{6,7},{7,0},{8,9},{9,10},{10,1... | collective-permute-start | bytes 30728 | tf_op jit(solution)/shard_map/ppermute | solution.py:391
  12.2 12.8 %collective-permute-start.1 = (f32[8,320]{1,0:T(8,128)S(1)}, f32[8,320]{1,0:T(8,128)S(1)}, u32[]{:S(2)}, u32[]{:S(2)}) collective-permute-start(f32[8,320]{1,0:T(8,128)S(1)} %get-tuple-element.26), channel_id=1, source_target_pairs={{1,0},{2,1},{3,2},{4,3},{5,4},{6,5},{7,6},{0,7},{9,8},{10,9},{11,1... | collective-permute-start | bytes 30728 | tf_op jit(solution)/shard_map/ppermute | solution.py:391
  28.2 17.0 %all-to-all-start.1 = ((f32[32,8,320]{2,1,0:T(8,128)}), f32[32,8,320]{2,1,0:T(8,128)S(1)}, u32[]{:S(2)}, u32[]{:S(2)}) async-start(f32[32,8,320]{2,1,0:T(8,128)} %bitcast.7), calls=%async_computation.1 | async-start | bytes 786432 | tf_op jit(solution)/shard_map/all_to_all | solution.py:390
  31.3 12.2 %collective-permute-start.2 = (f32[8,320]{1,0:T(8,128)S(1)}, f32[8,320]{1,0:T(8,128)S(1)}, u32[]{:S(2)}, u32[]{:S(2)}) collective-permute-start(f32[8,320]{1,0:T(8,128)S(1)} %get-tuple-element.37), channel_id=1, source_target_pairs={{0,1},{1,2},{2,3},{3,4},{4,5},{5,6},{6,7},{7,0},{8,9},{9,10},{10,1... | collective-permute-start | bytes 30728 | tf_op jit(solution)/shard_map/ppermute | solution.py:391
  33.1 10.4 %collective-permute-start.3 = (f32[8,320]{1,0:T(8,128)S(1)}, f32[8,320]{1,0:T(8,128)S(1)}, u32[]{:S(2)}, u32[]{:S(2)}) collective-permute-start(f32[8,320]{1,0:T(8,128)S(1)} %get-tuple-element.38), channel_id=1, source_target_pairs={{1,0},{2,1},{3,2},{4,3},{5,4},{6,5},{7,6},{0,7},{9,8},{10,9},{11,1... | collective-permute-start | bytes 30728 | tf_op jit(solution)/shard_map/ppermute | solution.py:391
  55.8 7.0 %all-to-all-start.3 = ((f32[4,2,128]{2,1,0:T(2,128)}), f32[4,2,128]{2,1,0:T(2,128)S(1)}, u32[]{:S(2)}, u32[]{:S(2)}) async-start(f32[4,2,128]{2,1,0:T(2,128)} %broadcast_in_dim.2), calls=%async_computation.3 | async-start | bytes 8192 | tf_op jit(solution)/shard_map/all_to_all | solution.py:405

commit v5 on v4

--- a/solution.py
+++ b/solution.py
@@ -33,12 +33,20 @@
     )
 
 
-def send_blocks(x, table, sel_up, sel_down, out_ref, up_ref, down_ref):
+def send_blocks(x, table, sel_up, sel_down, out_ref, up_ref, down_ref, rows_ref, sem):
     rim = up_ref.shape[0]
+    half = rows_ref.shape[2]
+    rows = pick(x, table).T.reshape(rows_ref.shape[0], 2 * half, BW)
+    for h in range(2):
+        for tile in range(2):
+            rows_ref[:, 2 * tile + h] = rows[:, h * half : (h + 1) * half, tile * LANES : (tile + 1) * LANES]
+    rest = rows[:, :, 2 * LANES :]
+    rows_ref[:, 4] = jnp.concatenate([rest[:, :half], rest[:, half:]], axis=2)
+    copy = pltpu.make_async_copy(rows_ref, out_ref, sem)
+    copy.start()
     index = lax.axis_index("blk")
     at_last = index == lax.axis_size("blk") - 1
     at_first = index == 0
-    out_ref[...] = pick(x, table).T
     rims = pick(x[:, x.shape[1] - LANES :], sel_up) + pick(x[:, :LANES], sel_down)
     lane = lax.broadcasted_iota(jnp.int32, (1, LANES), 1)
     turn_up = (lane < rim) & at_last
@@ -59,9 +67,13 @@
     ).T
     up_ref[...] = rims[:rim]
     down_ref[...] = rims[rim : 2 * rim]
-
-
-def donors_kernel(x_ref, src_ref, perm_ref, out_ref, up_ref, down_ref, table_ref, sel_up_ref, sel_down_ref):
+    return copy
+
+
+def donors_kernel(
+    x_ref, src_ref, perm_ref,
+    out_ref, up_ref, down_ref, table_ref, sel_up_ref, sel_down_ref, x_out, rows_ref, sem,
+):
     rim = up_ref.shape[0]
     index = lax.axis_index("blk")
     at_last = index == lax.axis_size("blk") - 1
@@ -78,14 +90,19 @@
     sel_down = onehot((target + rim == lane) & (sub < rim))
     rows = lax.broadcasted_iota(jnp.int32, table_ref.shape, 0)
     table = onehot(rows == src_ref[...])
-    send_blocks(x_ref[...], table, sel_up, sel_down, out_ref, up_ref, down_ref)
+    copy = send_blocks(
+        x_ref[...], table, sel_up, sel_down, out_ref, up_ref, down_ref, rows_ref, sem
+    )
     table_ref[...] = table
     sel_up_ref[...] = sel_up
     sel_down_ref[...] = sel_down
+    x_out[...] = x_ref[...]
+    copy.wait()
 
 
 def local_kernel(
-    rim, x_ref, nbr_ref, coup_ref, source_ref, out_ref, high, low, near, coup, source, sems, source_sem
+    rim, x_ref, nbr_ref, coup_ref, source_ref, out_ref, high, low, near, coup, source, sems, source_sem,
+    beside=None,
 ):
     slots, blocks = nbr_ref.shape
     chunks = blocks // LANES
@@ -121,6 +138,8 @@
             source_copy.wait()
         if c + 1 < chunks:
             gather(c + 1)
+        if beside is not None:
+            beside(c)
         for at in range(0, CELLS, PACK):
             total = [None] * VARS
             for m in range(slots):
@@ -137,46 +156,64 @@
 
 def first_local_kernel(
     rim, x_ref, nbr_ref, coup_ref, source_ref, dst_ref, weight_ref,
-    out_ref, rimcoup_ref, rimrow_ref, x_out, table_ref, weight_out,
-    high, low, near, coup, source, sems, source_sem,
+    out_ref, rimcoup_ref, rimrow_ref, table_ref, weight_out,
+    high, low, near, coup, source, sems, source_sem, lower_end,
 ):
     slots, blocks = nbr_ref.shape
+    chunks = blocks // LANES
     fringe = dst_ref.shape[1]
-    local_kernel(
-        rim, x_ref, nbr_ref, coup_ref, source_ref, out_ref, high, low, near, coup, source, sems, source_sem
-    )
-    x_out[...] = x_ref[...]
-    weight_out[...] = weight_ref[...]
     sub = lax.broadcasted_iota(jnp.int32, (LANES, LANES), 0)
     lane = lax.broadcasted_iota(jnp.int32, (LANES, LANES), 1)
-    at_end = sub >= LANES // 2
-    source_lane = sub - jnp.where(at_end, LANES - 2 * rim, 0)
-    valid = (sub < rim) | (sub >= LANES - rim)
-    place = jnp.concatenate(
-        [onehot((lane == source_lane + m * 2 * rim) & valid) for m in range(slots)], axis=0
-    )
-    first_row = lane[:1] < LANES // 2
-    reads = []
-    for m in range(slots):
-        lower = nbr_ref[m : m + 1, :LANES]
-        upper = nbr_ref[m : m + 1, blocks - LANES :]
-        lower = jnp.where(lower < rim, lower + 1, 0)
-        upper = jnp.where(upper >= blocks + rim, upper - blocks + 1, 0)
-        reads.append(jnp.where(first_row, lower, upper))
-    reads = jnp.broadcast_to(jnp.concatenate(reads, axis=1), (PACK, slots * LANES))
-    reads = reads.astype(jnp.float32).astype(jnp.bfloat16)
-    rimrow_ref[...] = jnp.dot(reads, place, preferred_element_type=jnp.float32)
-    first = lax.broadcasted_iota(jnp.int32, (BW, LANES), 1) < LANES // 2
-    end = blocks // LANES - 1
-    for u in range(VARS):
-        rows = jnp.concatenate(
-            [jnp.where(first, coup[0, m, u], coup[end, m, u]) for m in range(slots)], axis=1
+
+    def place(first, to):
+        at = sub - first
+        inside = (at >= 0) & (at < rim)
+        return jnp.concatenate(
+            [onehot((lane == at + to + m * 2 * rim) & inside) for m in range(slots)], axis=0
         )
-        rimcoup_ref[u] = jnp.dot(rows, place, preferred_element_type=jnp.float32).astype(jnp.bfloat16)
-    targets = jnp.broadcast_to(dst_ref[...], (LANES, fringe)).T
+
+    def read(rows, table):
+        rows = jnp.broadcast_to(jnp.concatenate(rows, axis=1), (PACK, slots * LANES))
+        rows = rows.astype(jnp.float32).astype(jnp.bfloat16)
+        return jnp.dot(rows, table, preferred_element_type=jnp.float32)
+
+    def beside(c):
+        if c not in (0, chunks - 1):
+            return
+        table = place(0, 0) if c == 0 else place(LANES - rim, rim)
+        rows = [nbr_ref[m : m + 1, c * LANES : (c + 1) * LANES] for m in range(slots)]
+        if c == 0:
+            rows = [jnp.where(row < rim, row + 1, 0) for row in rows]
+            rimrow_ref[...] = read(rows, table)
+        else:
+            rows = [jnp.where(row >= blocks + rim, row - blocks + 1, 0) for row in rows]
+            rimrow_ref[...] += read(rows, table)
+        for u in range(VARS):
+            rows = jnp.concatenate([coup[c, m, u] for m in range(slots)], axis=1)
+            moved = jnp.dot(rows, table, preferred_element_type=jnp.float32)
+            if c == 0:
+                lower_end[u] = moved
+            else:
+                rimcoup_ref[u] = (lower_end[u] + moved).astype(jnp.bfloat16)
+
+    local_kernel(
+        rim, x_ref, nbr_ref, coup_ref, source_ref, out_ref, high, low, near, coup, source, sems, source_sem,
+        beside,
+    )
+    half = rim // 2
+    column = lax.broadcasted_iota(jnp.int32, (fringe, fringe), 1)
+    within = lax.rem(column, fringe // 2)
+    slot = 2 * within - lax.rem(within, half) + jnp.where(column < fringe // 2, 0, half)
+    order = onehot(lax.broadcasted_iota(jnp.int32, (fringe, fringe), 0) == slot)
+    weights = jnp.broadcast_to(weight_ref[...], (PACK, fringe))
+    top = weights.astype(jnp.bfloat16)
+    rest = pick(weights - top.astype(jnp.float32), order)
+    weight_out[...] = (jnp.dot(top, order, preferred_element_type=jnp.float32) + rest)[:1]
+    targets = pick(jnp.broadcast_to(dst_ref[...], (LANES, fringe)).astype(jnp.float32), order).T
+    targets = targets.astype(jnp.int32)
     edge = lax.rem(sub, 2 * rim)
     edge = jnp.where(edge < rim, edge, edge + (blocks - 2 * rim))
-    for c in range(blocks // LANES):
+    for c in range(chunks):
         span = slice(c * LANES, (c + 1) * LANES)
         block = lane[:1] + c * LANES
         table_ref[:fringe, span] = onehot(targets == block)
@@ -199,7 +236,12 @@
             total = term if total is None else total + term
         edge.append(total)
     edge = jnp.concatenate(edge, axis=0)
-    arrived = jnp.concatenate([inc_ref[...].T * weight_ref[...], edge], axis=1)
+    tiles = [inc_ref[:, tile].reshape(-1, LANES).T for tile in range(inc_ref.shape[1])]
+    fringe = [
+        jnp.concatenate([tiles[h], tiles[2 + h], tiles[4][h * CELLS : (h + 1) * CELLS]], axis=0)
+        for h in range(2)
+    ]
+    arrived = jnp.concatenate([jnp.concatenate(fringe, axis=1) * weight_ref[...], edge], axis=1)
     return local_ref[...] + pick(arrived, table_ref[...])
 
 
@@ -220,27 +262,38 @@
 def advance_kernel(
     local_ref, inc_ref, lower_ref, upper_ref, across_ref, weight_ref, rimcoup_ref, rimrow_ref,
     diag_ref, x_ref, table_ref, sel_up_ref, sel_down_ref,
-    next_ref, norm_ref, out_ref, up_ref, down_ref, resid, diag, diag_sem,
-):
-    fetch = pltpu.make_async_copy(diag_ref, diag, diag_sem)
-    fetch.start()
+    next_ref, norm_ref, out_ref, up_ref, down_ref, resid, diag, diag_sems, rows_ref, sem,
+):
+    parts = CELLS // PACK
+    fetches = []
+    for part in range(parts):
+        span = pl.ds(part * PACK, PACK)
+        fetches.append(
+            pltpu.make_async_copy(
+                diag_ref.at[:, :, span], diag.at[:, :, span], diag_sems.at[part]
+            )
+        )
+        fetches[part].start()
     resid[...] = full_residual(
         local_ref, inc_ref, lower_ref, upper_ref, across_ref, weight_ref, rimcoup_ref, rimrow_ref
     )
-    fetch.wait()
-
-    def cells(part, carry):
-        at = pl.multiple_of(part * PACK, PACK)
+    for part in range(parts):
+        fetches[part].wait()
+        at = part * PACK
         for u in range(VARS):
-            span = pl.ds(u * CELLS + at, PACK)
-            next_ref[span, :] = x_ref[span, :] + STEP_CFL * precondition(diag, resid, u, at)
-        return carry
-
-    lax.fori_loop(0, CELLS // PACK, cells, 0)
-    send_blocks(
-        next_ref[...], table_ref[...], sel_up_ref[...], sel_down_ref[...], out_ref, up_ref, down_ref
+            total = None
+            for v in range(VARS):
+                term = diag[u, v, at : at + PACK].astype(jnp.float32)
+                term = term * resid[v * CELLS + at : v * CELLS + at + PACK]
+                total = term if total is None else total + term
+            span = slice(u * CELLS + at, u * CELLS + at + PACK)
+            next_ref[span, :] = x_ref[span, :] + STEP_CFL * total
+    copy = send_blocks(
+        next_ref[...], table_ref[...], sel_up_ref[...], sel_down_ref[...],
+        out_ref, up_ref, down_ref, rows_ref, sem,
     )
     norm_ref[...] = lane_sums(resid[...])
+    copy.wait()
 
 
 def residual_kernel(
@@ -316,31 +369,36 @@
     diag = here(diag_inv.transpose(1, 2, 0))
     nbr = here(neighbours.T)
     state = f32(BW, blocks)
-    sent = [f32(fringe, BW), f32(rim, BW), f32(rim, BW)]
+    hbm = pl.BlockSpec(memory_space=pltpu.HBM)
+    message = (devices, BW * fringe // devices // (rim // 2 * LANES), rim // 2, LANES)
+    sent = [f32(*message), f32(rim, BW), f32(rim, BW)]
+    rows_scratch = [pltpu.VMEM(message, jnp.float32), pltpu.SemaphoreType.DMA]
     size = 4 * BW * blocks
     square = bf16(LANES, LANES)
 
     donors = call(
         donors_kernel,
         [VMEM, VMEM, SMEM],
-        sent + [bf16(blocks, fringe), square, square],
+        sent + [bf16(blocks, fringe), square, square, state],
         4 * BW * blocks * fringe,
         2 * size,
-    )
-    hbm = pl.BlockSpec(memory_space=pltpu.HBM)
+        out_specs=[hbm] + [VMEM] * 6,
+        scratch_shapes=rows_scratch,
+    )
     chunks = blocks // LANES
+    scratch = [
+        pltpu.VMEM((BW, blocks + LANES), jnp.bfloat16),
+        pltpu.VMEM((BW, blocks + LANES), jnp.bfloat16),
+        [pltpu.VMEM((BW, slots * LANES), jnp.float32)] * chunks,
+        pltpu.VMEM((chunks, slots, VARS, BW, LANES), jnp.bfloat16),
+        pltpu.VMEM((BW, blocks), jnp.float32),
+        pltpu.SemaphoreType.DMA((chunks,)),
+        pltpu.SemaphoreType.DMA,
+    ]
     local_more = dict(
         flops=4 * BW * 2 * LANES * slots * blocks,
         moved=coup.size * 2 + 4 * size,
-        scratch_shapes=[
-            pltpu.VMEM((BW, blocks + LANES), jnp.bfloat16),
-            pltpu.VMEM((BW, blocks + LANES), jnp.bfloat16),
-            [pltpu.VMEM((BW, slots * LANES), jnp.float32)] * chunks,
-            pltpu.VMEM((chunks, slots, VARS, BW, LANES), jnp.bfloat16),
-            pltpu.VMEM((BW, blocks), jnp.float32),
-            pltpu.SemaphoreType.DMA((chunks,)),
-            pltpu.SemaphoreType.DMA,
-        ],
+        scratch_shapes=scratch,
     )
     first_local = call(
         functools.partial(first_local_kernel, rim),
@@ -349,11 +407,10 @@
             state,
             bf16(VARS, BW, LANES),
             f32(PACK, LANES),
-            state,
             bf16(fringe + LANES, blocks),
             f32(1, fringe),
         ],
-        **local_more,
+        **dict(local_more, scratch_shapes=scratch + [pltpu.VMEM((VARS, BW, LANES), jnp.float32)]),
     )
     local = call(functools.partial(local_kernel, rim), [VMEM, VMEM, hbm, hbm], state, **local_more)
     advance = call(
@@ -362,16 +419,18 @@
         [state, f32(1, LANES)] + sent,
         8 * BW * blocks * fringe,
         diag.size * 2 + 4 * size,
+        out_specs=[VMEM, VMEM, hbm, VMEM, VMEM],
         scratch_shapes=[
             pltpu.VMEM((BW, blocks), jnp.float32),
-            pltpu.VMEM((VARS, BW, blocks), jnp.bfloat16),
-            pltpu.SemaphoreType.DMA,
-        ],
+            pltpu.VMEM((VARS, VARS, CELLS, blocks), jnp.bfloat16),
+            pltpu.SemaphoreType.DMA((CELLS // PACK,)),
+        ]
+        + rows_scratch,
     )
     residual = call(
         residual_kernel,
         [VMEM] * 9,
-        [state, f32(peers, 2, LANES)],
+        [state, f32(devices, 2, LANES)],
         4 * BW * blocks * fringe,
         3 * size,
     )
@@ -390,19 +449,18 @@
         rows = lax.all_to_all(rows, ("body", "blk"), split_axis=0, concat_axis=0, tiled=True)
         return rows, lax.ppermute(to_up, "blk", up), lax.ppermute(to_down, "blk", down)
 
-    *out, table, sel_up, sel_down = donors(x, here(fringe_src), here(seam_perm))
+    *out, table, sel_up, sel_down, x_here = donors(x, here(fringe_src), here(seam_perm))
     arrived = exchange(*out)
-    part, rimcoup, rimrow, x, across, weight = first_local(
-        x, nbr, coup, source_t, here(fringe_dst), here(fringe_weight)
+    part, rimcoup, rimrow, across, weight = first_local(
+        x_here, nbr, coup, source_t, here(fringe_dst), here(fringe_weight)
     )
     across = (across, weight, rimcoup, rimrow)
-    x, norm, *out = advance(part, *arrived, *across, diag, x, table, sel_up, sel_down)
+    parts = here(diag_inv.transpose(1, 2, 0).reshape(VARS, VARS, CELLS, blocks))
+    x, norm, *out = advance(part, *arrived, *across, parts, x_here, table, sel_up, sel_down)
     arrived = exchange(*out)
     part = local(x, nbr, coup, source_t)
     resid, sums = residual(part, *arrived, *across, norm)
-    sums = lax.all_to_all(sums, "blk", split_axis=0, concat_axis=0, tiled=True)
-    sums = jnp.broadcast_to(jnp.sum(sums, axis=0, keepdims=True), (devices // peers, 2, LANES))
-    sums = lax.all_to_all(sums, "body", split_axis=0, concat_axis=0, tiled=True)
+    sums = lax.all_to_all(sums, ("body", "blk"), split_axis=0, concat_axis=0, tiled=True)
     update, resid = direction(diag, resid)
     x = finish(sums, x, update)
     return (x.T, resid.T)

time: 64.4 us -> 57.2 us (0.89)
  blocking collectives: 9.36 us -> 0 us
  waiting for transfers between devices: 3.79 us -> 5.74 us
  Pallas kernels: 26.2 us -> 27.6 us
    all_to_all x1 -> x0, blocking collectives: 9.36 us -> none  [shards(): sums = lax.all_to_all(sums, 'blk', split_axis=0, concat_axis=0, tiled=True)]
    all_to_all x1, waiting for transfers between devices: 1.11 us -> 4.55 us  [shards(): lax.all_to_all(sums, ('body', 'blk'), split_axis=0, concat_axis=0, tiled=...]
    ppermute x2, waiting for transfers between devices: 1.08 us -> 0.01 us  [exchange(): lax.ppermute(to_up, 'blk', up)]
    pallas_call x3, Pallas kernels: 15.4 us -> 16.2 us  [the longest x1 10.5 us: shards(): first_local(x_here, nbr, coup, source_t, here(fringe_dst), here(fringe_we...]
    all_to_all x1, starting transfers between devices: 3.25 us -> 2.57 us  [shards(): lax.all_to_all(sums, ('body', 'blk'), split_axis=0, concat_axis=0, tiled=...]
  transfers between devices with their start and end apart: 7 -> 7, of which waited for: 3 -> 2; matrix products, arithmetic and copies ran while one was open for 0% -> 0% of each run, Pallas kernels for 29% -> 34%
where the time goes in v5:
time: 57.2 us; the launch traced here: 56.7 us
  Pallas kernels  27.6 us (48%)
  starting transfers between devices  22.6 us (40%)
  waiting for transfers between devices  5.74 us (10%)
  between operations  0.73 us (1%)
    pallas_call x1, Pallas kernels, shards(): first_local(x_here, nbr, coup, source_t, here(fringe_dst), here(fringe_we...  10.5 us
    all_to_all x2, starting transfers between devices, exchange(): lax.all_to_all(rows, ('body', 'blk'), split_axis=0, concat_axis=0, tiled=...  10.4 us
    pallas_call x1, Pallas kernels, shards(): part = local(x, nbr, coup, source_t)  6.36 us
    ppermute x2, starting transfers between devices, exchange(): lax.ppermute(to_down, 'blk', down)  5.97 us
    all_to_all x1, waiting for transfers between devices, shards(): lax.all_to_all(sums, ('body', 'blk'), split_axis=0, concat_axis=0, tiled=...  4.55 us
    ppermute x2, starting transfers between devices, exchange(): lax.ppermute(to_up, 'blk', up)  3.64 us
    pallas_call x1, Pallas kernels, shards(): advance(part, *arrived, *across, parts, x_here, table, sel_up, sel_down)  3.22 us
    pallas_call x1, Pallas kernels, shards(): update, resid = direction(diag, resid)  2.64 us
  transfers between devices with their start and end apart: 7, of which 2 were waited for; matrix products, arithmetic and copies ran while one was open for 0% of the time, Pallas kernels for 34%

profile of v5, /device:TPU:0, one launch (start us, length us, event | category | flops | bytes accessed | tf_op | source)
XLA Modules:
  0.0 56.7 jit_solution(8798310491563780359)
XLA Ops:
  0.6 2.5 %shard_map.104 = (f32[32,5,4,128]{3,2,1,0:T(4,128)}, f32[8,320]{1,0:T(8,128)S(1)}, f32[8,320]{1,0:T(8,128)S(1)}, bf16[512,256]{1,0:T(8,128)(2,1)S(1)}, bf16[128,...) custom-call(f32[320,512]{1,0:T(8,128)} %bitcast.15, s32[1,256]{1,0:T(1,128)} %src_ref.1, ...), custom_call_target="tpu_custom_call" | custom-call | flops 167772160 | bytes 1310720 | tf_op jit(solution)/shard_map/pallas_call | solution.py:452
  3.1 7.3 %all-to-all-start = ((f32[32,5,4,128]{3,2,1,0:T(4,128)}), f32[32,5,4,128]{3,2,1,0:T(4,128)S(1)}, u32[]{:S(2)}, u32[]{:S(2)}) async-start(f32[32,5,4,128]{3,2,1,0:T(4,128)} %get-tuple-element.25), calls=%async_computation | async-start | bytes 655360 | tf_op jit(solution)/shard_map/all_to_all | solution.py:449
  10.4 1.8 %collective-permute-start = (f32[8,320]{1,0:T(8,128)S(1)}, f32[8,320]{1,0:T(8,128)S(1)}, u32[]{:S(2)}, u32[]{:S(2)}) collective-permute-start(f32[8,320]{1,0:T(8,128)S(1)} %get-tuple-element.26), channel_id=1, source_target_pairs={{0,1},{1,2},{2,3},{3,4},{4,5},{5,6},{6,7},{7,0},{8,9},{9,10},{10,1... | collective-permute-start | bytes 30728 | tf_op jit(solution)/shard_map/ppermute | solution.py:450
  12.3 3.0 %collective-permute-start.1 = (f32[8,320]{1,0:T(8,128)S(1)}, f32[8,320]{1,0:T(8,128)S(1)}, u32[]{:S(2)}, u32[]{:S(2)}) collective-permute-start(f32[8,320]{1,0:T(8,128)S(1)} %get-tuple-element.27), channel_id=1, source_target_pairs={{1,0},{2,1},{3,2},{4,3},{5,4},{6,5},{7,6},{0,7},{9,8},{10,9},{11,1... | collective-permute-start | bytes 30728 | tf_op jit(solution)/shard_map/ppermute | solution.py:450
  15.2 10.5 %shard_map.105 = (f32[320,512]{1,0:T(8,128)S(1)}, bf16[5,320,128]{2,1,0:T(8,128)(2,1)S(1)}, f32[16,128]{1,0:T(8,128)S(1)}, bf16[384,512]{1,0:T(8,128)(2,1)S(1)}, f32[1,256]{1,0:T(1,128)S(1)}) custom-call(f32[320,512]{1,0:T(8,128)S(1)} %get-tuple-element.23.x_ref, s32[6,512]{1,0:T(8,128)} %bitcast.17, bf16[6,5,320,512]{3,2,1,0:T(8,128)(2,1)} %bitcast.9, ...), custom_call_target="tpu_custom_call" | custom-call | flops 1006632960 | bytes 12451840 | tf_op jit(solution)/shard_map/pallas_call | solution.py:454
  25.7 0.0 collective-permute-done.lower_ref
  25.7 0.0 collective-permute-done.1.upper_ref
  25.8 0.0 all-to-all-done.inc_ref
  25.8 3.2 %shard_map.106 = (f32[320,512]{1,0:T(8,128)S(1)}, f32[1,128]{1,0:T(1,128)S(1)}, f32[32,5,4,128]{3,2,1,0:T(4,128)}, f32[8,320]{1,0:T(8,128)S(1)}, f32[8,320]{1,0:T(8,128)S(1)}) custom-call(f32[320,512]{1,0:T(8,128)S(1)} %get-tuple-element.24.local_ref, f32[32,5,4,128]{3,2,1,0:T(4,128)S(1)} %all-to-all-done.inc_ref, ...), custom_call_target="tpu_custom_call" | custom-call | flops 335544320 | bytes 4259840 | tf_op jit(solution)/shard_map/pallas_call | solution.py:459
  29.0 3.1 %all-to-all-start.1 = ((f32[32,5,4,128]{3,2,1,0:T(4,128)}), f32[32,5,4,128]{3,2,1,0:T(4,128)S(1)}, u32[]{:S(2)}, u32[]{:S(2)}) async-start(f32[32,5,4,128]{3,2,1,0:T(4,128)} %get-tuple-element.36), calls=%async_computation.1 | async-start | bytes 655360 | tf_op jit(solution)/shard_map/all_to_all | solution.py:449
  32.1 1.8 %collective-permute-start.2 = (f32[8,320]{1,0:T(8,128)S(1)}, f32[8,320]{1,0:T(8,128)S(1)}, u32[]{:S(2)}, u32[]{:S(2)}) collective-permute-start(f32[8,320]{1,0:T(8,128)S(1)} %get-tuple-element.37), channel_id=1, source_target_pairs={{0,1},{1,2},{2,3},{3,4},{4,5},{5,6},{6,7},{7,0},{8,9},{9,10},{10,1... | collective-permute-start | bytes 30728 | tf_op jit(solution)/shard_map/ppermute | solution.py:450
  34.0 3.0 %collective-permute-start.3 = (f32[8,320]{1,0:T(8,128)S(1)}, f32[8,320]{1,0:T(8,128)S(1)}, u32[]{:S(2)}, u32[]{:S(2)}) collective-permute-start(f32[8,320]{1,0:T(8,128)S(1)} %get-tuple-element.38), channel_id=1, source_target_pairs={{1,0},{2,1},{3,2},{4,3},{5,4},{6,5},{7,6},{0,7},{9,8},{10,9},{11,1... | collective-permute-start | bytes 30728 | tf_op jit(solution)/shard_map/ppermute | solution.py:450
  37.0 6.4 %shard_map.107.local_ref = f32[320,512]{1,0:T(8,128)S(1)} custom-call(f32[320,512]{1,0:T(8,128)S(1)} %get-tuple-element.35.x_ref, s32[6,512]{1,0:T(8,128)} %bitcast.18, bf16[6,5,320,512]{3,2,1,0:T(8,128)(2,1)} %bitcast.10, f32[320,512]{1,0:T(8,128)} %bitcast.14), custom_call_target="tpu_custom_call" | custom-call | flops 1006632960 | bytes 12451840 | tf_op jit(solution)/shard_map/pallas_call | solution.py:461
  43.3 0.0 collective-permute-done.2.lower_ref
  43.4 0.0 collective-permute-done.3.upper_ref
  43.4 1.2 %all-to-all-done.1.inc_ref = f32[32,5,4,128]{3,2,1,0:T(4,128)S(1)} async-done(((f32[32,5,4,128]{3,2,1,0:T(4,128)}), f32[32,5,4,128]{3,2,1,0:T(4,128)S(1)}, u32[]{:S(2)}, u32[]{:S(2)}) %all-to-all-start.1) | async-done | bytes 327712 | tf_op jit(solution)/shard_map/all_to_all | solution.py:449
  44.5 1.3 %shard_map.108 = (f32[320,512]{1,0:T(8,128)S(1)}, f32[32,2,128]{2,1,0:T(2,128)}) custom-call(f32[320,512]{1,0:T(8,128)S(1)} %shard_map.107.local_ref, f32[32,5,4,128]{3,2,1,0:T(4,128)S(1)} %all-to-all-done.1.inc_ref, f32[8,320]{1,0:T(8,128)S(1)} %collective-permute-done.2.lower_ref, f32[8,320]{1,0:T(8,128)S(1)} %collective-permute-done.3.upper_ref, ...), custom_call_target="tpu_custom_call" | custom-call | flops 167772160 | bytes 1966080 | tf_op jit(solution)/shard_map/pallas_call | solution.py:462
  45.9 2.6 %all-to-all-start.2 = ((f32[32,2,128]{2,1,0:T(2,128)}), f32[32,2,128]{2,1,0:T(2,128)S(1)}, u32[]{:S(2)}, u32[]{:S(2)}) async-start(f32[32,2,128]{2,1,0:T(2,128)} %get-tuple-element.40), calls=%async_computation.2 | async-start | bytes 65536 | tf_op jit(solution)/shard_map/all_to_all | solution.py:463
  48.4 2.6 %shard_map.109 = (f32[320,512]{1,0:T(8,128)S(1)}, f32[320,512]{1,0:T(8,128)}) custom-call(bf16[5,320,512]{2,1,0:T(8,128)(2,1)} %bitcast.12, f32[320,512]{1,0:T(8,128)S(1)} %get-tuple-element.41.resid_ref), custom_call_target="tpu_custom_call" | custom-call | flops 1638400 | bytes 2949120 | tf_op jit(solution)/shard_map/pallas_call | solution.py:464
  51.1 4.5 %all-to-all-done.2.sums_ref = f32[32,2,128]{2,1,0:T(2,128)S(1)} async-done(((f32[32,2,128]{2,1,0:T(2,128)}), f32[32,2,128]{2,1,0:T(2,128)S(1)}, u32[]{:S(2)}, u32[]{:S(2)}) %all-to-all-start.2) | async-done | bytes 32800 | tf_op jit(solution)/shard_map/all_to_all | solution.py:463
  55.6 1.1 %shard_map.110 = f32[320,512]{1,0:T(8,128)} custom-call(f32[32,2,128]{2,1,0:T(2,128)S(1)} %all-to-all-done.2.sums_ref, f32[320,512]{1,0:T(8,128)S(1)} %get-tuple-element.35.x_ref, f32[320,512]{1,0:T(8,128)S(1)} %get-tuple-element.42.update_ref), custom_call_target="tpu_custom_call" | custom-call | flops 327680 | bytes 1966080 | tf_op jit(solution)/shard_map/pallas_call | solution.py:465
Async XLA Ops:
  3.1 22.6 %all-to-all-start = ((f32[32,5,4,128]{3,2,1,0:T(4,128)}), f32[32,5,4,128]{3,2,1,0:T(4,128)S(1)}, u32[]{:S(2)}, u32[]{:S(2)}) async-start(f32[32,5,4,128]{3,2,1,0:T(4,128)} %get-tuple-element.25), calls=%async_computation | async-start | bytes 655360 | tf_op jit(solution)/shard_map/all_to_all | solution.py:449
  10.4 15.3 %collective-permute-start = (f32[8,320]{1,0:T(8,128)S(1)}, f32[8,320]{1,0:T(8,128)S(1)}, u32[]{:S(2)}, u32[]{:S(2)}) collective-permute-start(f32[8,320]{1,0:T(8,128)S(1)} %get-tuple-element.26), channel_id=1, source_target_pairs={{0,1},{1,2},{2,3},{3,4},{4,5},{5,6},{6,7},{7,0},{8,9},{9,10},{10,1... | collective-permute-start | bytes 30728 | tf_op jit(solution)/shard_map/ppermute | solution.py:450
  12.3 13.5 %collective-permute-start.1 = (f32[8,320]{1,0:T(8,128)S(1)}, f32[8,320]{1,0:T(8,128)S(1)}, u32[]{:S(2)}, u32[]{:S(2)}) collective-permute-start(f32[8,320]{1,0:T(8,128)S(1)} %get-tuple-element.27), channel_id=1, source_target_pairs={{1,0},{2,1},{3,2},{4,3},{5,4},{6,5},{7,6},{0,7},{9,8},{10,9},{11,1... | collective-permute-start | bytes 30728 | tf_op jit(solution)/shard_map/ppermute | solution.py:450
  29.0 15.6 %all-to-all-start.1 = ((f32[32,5,4,128]{3,2,1,0:T(4,128)}), f32[32,5,4,128]{3,2,1,0:T(4,128)S(1)}, u32[]{:S(2)}, u32[]{:S(2)}) async-start(f32[32,5,4,128]{3,2,1,0:T(4,128)} %get-tuple-element.36), calls=%async_computation.1 | async-start | bytes 655360 | tf_op jit(solution)/shard_map/all_to_all | solution.py:449
  32.1 11.2 %collective-permute-start.2 = (f32[8,320]{1,0:T(8,128)S(1)}, f32[8,320]{1,0:T(8,128)S(1)}, u32[]{:S(2)}, u32[]{:S(2)}) collective-permute-start(f32[8,320]{1,0:T(8,128)S(1)} %get-tuple-element.37), channel_id=1, source_target_pairs={{0,1},{1,2},{2,3},{3,4},{4,5},{5,6},{6,7},{7,0},{8,9},{9,10},{10,1... | collective-permute-start | bytes 30728 | tf_op jit(solution)/shard_map/ppermute | solution.py:450
  34.0 9.4 %collective-permute-start.3 = (f32[8,320]{1,0:T(8,128)S(1)}, f32[8,320]{1,0:T(8,128)S(1)}, u32[]{:S(2)}, u32[]{:S(2)}) collective-permute-start(f32[8,320]{1,0:T(8,128)S(1)} %get-tuple-element.38), channel_id=1, source_target_pairs={{1,0},{2,1},{3,2},{4,3},{5,4},{6,5},{7,6},{0,7},{9,8},{10,9},{11,1... | collective-permute-start | bytes 30728 | tf_op jit(solution)/shard_map/ppermute | solution.py:450
  45.9 9.8 %all-to-all-start.2 = ((f32[32,2,128]{2,1,0:T(2,128)}), f32[32,2,128]{2,1,0:T(2,128)S(1)}, u32[]{:S(2)}, u32[]{:S(2)}) async-start(f32[32,2,128]{2,1,0:T(2,128)} %get-tuple-element.40), calls=%async_computation.2 | async-start | bytes 65536 | tf_op jit(solution)/shard_map/all_to_all | solution.py:463

commit v6 on v5

--- a/solution.py
+++ b/solution.py
@@ -188,29 +188,20 @@
         else:
             rows = [jnp.where(row >= blocks + rim, row - blocks + 1, 0) for row in rows]
             rimrow_ref[...] += read(rows, table)
-        for u in range(VARS):
-            rows = jnp.concatenate([coup[c, m, u] for m in range(slots)], axis=1)
-            moved = jnp.dot(rows, table, preferred_element_type=jnp.float32)
-            if c == 0:
-                lower_end[u] = moved
-            else:
-                rimcoup_ref[u] = (lower_end[u] + moved).astype(jnp.bfloat16)
+        rows = jnp.concatenate([coup[c, m].reshape(VARS * BW, LANES) for m in range(slots)], axis=1)
+        moved = jnp.dot(rows, table, preferred_element_type=jnp.float32)
+        if c == 0:
+            lower_end[...] = moved
+        else:
+            moved = (lower_end[...] + moved).astype(jnp.bfloat16)
+            rimcoup_ref[...] = moved.reshape(VARS, BW, LANES)
 
     local_kernel(
         rim, x_ref, nbr_ref, coup_ref, source_ref, out_ref, high, low, near, coup, source, sems, source_sem,
         beside,
     )
-    half = rim // 2
-    column = lax.broadcasted_iota(jnp.int32, (fringe, fringe), 1)
-    within = lax.rem(column, fringe // 2)
-    slot = 2 * within - lax.rem(within, half) + jnp.where(column < fringe // 2, 0, half)
-    order = onehot(lax.broadcasted_iota(jnp.int32, (fringe, fringe), 0) == slot)
-    weights = jnp.broadcast_to(weight_ref[...], (PACK, fringe))
-    top = weights.astype(jnp.bfloat16)
-    rest = pick(weights - top.astype(jnp.float32), order)
-    weight_out[...] = (jnp.dot(top, order, preferred_element_type=jnp.float32) + rest)[:1]
-    targets = pick(jnp.broadcast_to(dst_ref[...], (LANES, fringe)).astype(jnp.float32), order).T
-    targets = targets.astype(jnp.int32)
+    weight_out[...] = weight_ref[...]
+    targets = jnp.broadcast_to(dst_ref[...], (LANES, fringe)).T
     edge = lax.rem(sub, 2 * rim)
     edge = jnp.where(edge < rim, edge, edge + (blocks - 2 * rim))
     for c in range(chunks):
@@ -236,12 +227,10 @@
             total = term if total is None else total + term
         edge.append(total)
     edge = jnp.concatenate(edge, axis=0)
-    tiles = [inc_ref[:, tile].reshape(-1, LANES).T for tile in range(inc_ref.shape[1])]
-    fringe = [
-        jnp.concatenate([tiles[h], tiles[2 + h], tiles[4][h * CELLS : (h + 1) * CELLS]], axis=0)
-        for h in range(2)
-    ]
-    arrived = jnp.concatenate([jnp.concatenate(fringe, axis=1) * weight_ref[...], edge], axis=1)
+    rest = inc_ref[:, 4]
+    rest = jnp.concatenate([rest[:, :, :CELLS], rest[:, :, CELLS:]], axis=1).reshape(-1, CELLS)
+    fringe = [inc_ref[:, 0:2].reshape(-1, LANES).T, inc_ref[:, 2:4].reshape(-1, LANES).T, rest.T]
+    arrived = jnp.concatenate([jnp.concatenate(fringe, axis=0) * weight_ref[...], edge], axis=1)
     return local_ref[...] + pick(arrived, table_ref[...])
 
 
@@ -410,7 +399,7 @@
             bf16(fringe + LANES, blocks),
             f32(1, fringe),
         ],
-        **dict(local_more, scratch_shapes=scratch + [pltpu.VMEM((VARS, BW, LANES), jnp.float32)]),
+        **dict(local_more, scratch_shapes=scratch + [pltpu.VMEM((VARS * BW, LANES), jnp.float32)]),
     )
     local = call(functools.partial(local_kernel, rim), [VMEM, VMEM, hbm, hbm], state, **local_more)
     advance = call(

time: 57.2 us -> 57.3 us (level)
  no operation moved by 1% of the time
where the time goes in v6:
time: 57.3 us; the launch traced here: 56.8 us
  Pallas kernels  27.7 us (48%)
  starting transfers between devices  22.6 us (39%)
  waiting for transfers between devices  5.74 us (10%)
  between operations  0.73 us (1%)
    pallas_call x1, Pallas kernels, shards(): first_local(x_here, nbr, coup, source_t, here(fringe_dst), here(fringe_we...  10.5 us
    all_to_all x2, starting transfers between devices, exchange(): lax.all_to_all(rows, ('body', 'blk'), split_axis=0, concat_axis=0, tiled=...  10.4 us
    pallas_call x1, Pallas kernels, shards(): part = local(x, nbr, coup, source_t)  6.36 us
    ppermute x2, starting transfers between devices, exchange(): lax.ppermute(to_down, 'blk', down)  5.97 us
    all_to_all x1, waiting for transfers between devices, shards(): lax.all_to_all(sums, ('body', 'blk'), split_axis=0, concat_axis=0, tiled=...  4.55 us
    ppermute x2, starting transfers between devices, exchange(): lax.ppermute(to_up, 'blk', up)  3.64 us
    pallas_call x1, Pallas kernels, shards(): advance(part, *arrived, *across, parts, x_here, table, sel_up, sel_down)  3.31 us
    pallas_call x1, Pallas kernels, shards(): update, resid = direction(diag, resid)  2.64 us
  transfers between devices with their start and end apart: 7, of which 2 were waited for; matrix products, arithmetic and copies ran while one was open for 0% of the time, Pallas kernels for 34%

profile of v6, /device:TPU:0, one launch (start us, length us, event | category | flops | bytes accessed | tf_op | source)
XLA Modules:
  0.0 56.8 jit_solution(12701028202778649984)
XLA Ops:
  0.6 2.5 %shard_map.104 = (f32[32,5,4,128]{3,2,1,0:T(4,128)}, f32[8,320]{1,0:T(8,128)S(1)}, f32[8,320]{1,0:T(8,128)S(1)}, bf16[512,256]{1,0:T(8,128)(2,1)S(1)}, bf16[128,...) custom-call(f32[320,512]{1,0:T(8,128)} %bitcast.15, s32[1,256]{1,0:T(1,128)} %src_ref.1, ...), custom_call_target="tpu_custom_call" | custom-call | flops 167772160 | bytes 1310720 | tf_op jit(solution)/shard_map/pallas_call | solution.py:441
  3.1 7.3 %all-to-all-start = ((f32[32,5,4,128]{3,2,1,0:T(4,128)}), f32[32,5,4,128]{3,2,1,0:T(4,128)S(1)}, u32[]{:S(2)}, u32[]{:S(2)}) async-start(f32[32,5,4,128]{3,2,1,0:T(4,128)} %get-tuple-element.25), calls=%async_computation | async-start | bytes 655360 | tf_op jit(solution)/shard_map/all_to_all | solution.py:438
  10.4 1.8 %collective-permute-start = (f32[8,320]{1,0:T(8,128)S(1)}, f32[8,320]{1,0:T(8,128)S(1)}, u32[]{:S(2)}, u32[]{:S(2)}) collective-permute-start(f32[8,320]{1,0:T(8,128)S(1)} %get-tuple-element.26), channel_id=1, source_target_pairs={{0,1},{1,2},{2,3},{3,4},{4,5},{5,6},{6,7},{7,0},{8,9},{9,10},{10,1... | collective-permute-start | bytes 30728 | tf_op jit(solution)/shard_map/ppermute | solution.py:439
  12.3 3.0 %collective-permute-start.1 = (f32[8,320]{1,0:T(8,128)S(1)}, f32[8,320]{1,0:T(8,128)S(1)}, u32[]{:S(2)}, u32[]{:S(2)}) collective-permute-start(f32[8,320]{1,0:T(8,128)S(1)} %get-tuple-element.27), channel_id=1, source_target_pairs={{1,0},{2,1},{3,2},{4,3},{5,4},{6,5},{7,6},{0,7},{9,8},{10,9},{11,1... | collective-permute-start | bytes 30728 | tf_op jit(solution)/shard_map/ppermute | solution.py:439
  15.2 10.5 %shard_map.105 = (f32[320,512]{1,0:T(8,128)S(1)}, bf16[5,320,128]{2,1,0:T(8,128)(2,1)S(1)}, f32[16,128]{1,0:T(8,128)S(1)}, bf16[384,512]{1,0:T(8,128)(2,1)S(1)}, f32[1,256]{1,0:T(1,128)S(1)}) custom-call(f32[320,512]{1,0:T(8,128)S(1)} %get-tuple-element.23.x_ref, s32[6,512]{1,0:T(8,128)} %bitcast.17, bf16[6,5,320,512]{3,2,1,0:T(8,128)(2,1)} %bitcast.9, ...), custom_call_target="tpu_custom_call" | custom-call | flops 1006632960 | bytes 12451840 | tf_op jit(solution)/shard_map/pallas_call | solution.py:443
  25.7 0.0 collective-permute-done.lower_ref
  25.7 0.0 collective-permute-done.1.upper_ref
  25.7 0.0 all-to-all-done.inc_ref
  25.7 3.3 %shard_map.106 = (f32[320,512]{1,0:T(8,128)S(1)}, f32[1,128]{1,0:T(1,128)S(1)}, f32[32,5,4,128]{3,2,1,0:T(4,128)}, f32[8,320]{1,0:T(8,128)S(1)}, f32[8,320]{1,0:T(8,128)S(1)}) custom-call(f32[320,512]{1,0:T(8,128)S(1)} %get-tuple-element.24.local_ref, f32[32,5,4,128]{3,2,1,0:T(4,128)S(1)} %all-to-all-done.inc_ref, ...), custom_call_target="tpu_custom_call" | custom-call | flops 335544320 | bytes 4259840 | tf_op jit(solution)/shard_map/pallas_call | solution.py:448
  29.0 3.1 %all-to-all-start.1 = ((f32[32,5,4,128]{3,2,1,0:T(4,128)}), f32[32,5,4,128]{3,2,1,0:T(4,128)S(1)}, u32[]{:S(2)}, u32[]{:S(2)}) async-start(f32[32,5,4,128]{3,2,1,0:T(4,128)} %get-tuple-element.36), calls=%async_computation.1 | async-start | bytes 655360 | tf_op jit(solution)/shard_map/all_to_all | solution.py:438
  32.2 1.8 %collective-permute-start.2 = (f32[8,320]{1,0:T(8,128)S(1)}, f32[8,320]{1,0:T(8,128)S(1)}, u32[]{:S(2)}, u32[]{:S(2)}) collective-permute-start(f32[8,320]{1,0:T(8,128)S(1)} %get-tuple-element.37), channel_id=1, source_target_pairs={{0,1},{1,2},{2,3},{3,4},{4,5},{5,6},{6,7},{7,0},{8,9},{9,10},{10,1... | collective-permute-start | bytes 30728 | tf_op jit(solution)/shard_map/ppermute | solution.py:439
  34.0 3.0 %collective-permute-start.3 = (f32[8,320]{1,0:T(8,128)S(1)}, f32[8,320]{1,0:T(8,128)S(1)}, u32[]{:S(2)}, u32[]{:S(2)}) collective-permute-start(f32[8,320]{1,0:T(8,128)S(1)} %get-tuple-element.38), channel_id=1, source_target_pairs={{1,0},{2,1},{3,2},{4,3},{5,4},{6,5},{7,6},{0,7},{9,8},{10,9},{11,1... | collective-permute-start | bytes 30728 | tf_op jit(solution)/shard_map/ppermute | solution.py:439
  37.0 6.4 %shard_map.107.local_ref = f32[320,512]{1,0:T(8,128)S(1)} custom-call(f32[320,512]{1,0:T(8,128)S(1)} %get-tuple-element.35.x_ref, s32[6,512]{1,0:T(8,128)} %bitcast.18, bf16[6,5,320,512]{3,2,1,0:T(8,128)(2,1)} %bitcast.10, f32[320,512]{1,0:T(8,128)} %bitcast.14), custom_call_target="tpu_custom_call" | custom-call | flops 1006632960 | bytes 12451840 | tf_op jit(solution)/shard_map/pallas_call | solution.py:450
  43.4 0.0 collective-permute-done.2.lower_ref
  43.4 0.0 collective-permute-done.3.upper_ref
  43.4 1.2 %all-to-all-done.1.inc_ref = f32[32,5,4,128]{3,2,1,0:T(4,128)S(1)} async-done(((f32[32,5,4,128]{3,2,1,0:T(4,128)}), f32[32,5,4,128]{3,2,1,0:T(4,128)S(1)}, u32[]{:S(2)}, u32[]{:S(2)}) %all-to-all-start.1) | async-done | bytes 327712 | tf_op jit(solution)/shard_map/all_to_all | solution.py:438
  44.6 1.4 %shard_map.108 = (f32[320,512]{1,0:T(8,128)S(1)}, f32[32,2,128]{2,1,0:T(2,128)}) custom-call(f32[320,512]{1,0:T(8,128)S(1)} %shard_map.107.local_ref, f32[32,5,4,128]{3,2,1,0:T(4,128)S(1)} %all-to-all-done.1.inc_ref, f32[8,320]{1,0:T(8,128)S(1)} %collective-permute-done.2.lower_ref, f32[8,320]{1,0:T(8,128)S(1)} %collective-permute-done.3.upper_ref, ...), custom_call_target="tpu_custom_call" | custom-call | flops 167772160 | bytes 1966080 | tf_op jit(solution)/shard_map/pallas_call | solution.py:451
  45.9 2.6 %all-to-all-start.2 = ((f32[32,2,128]{2,1,0:T(2,128)}), f32[32,2,128]{2,1,0:T(2,128)S(1)}, u32[]{:S(2)}, u32[]{:S(2)}) async-start(f32[32,2,128]{2,1,0:T(2,128)} %get-tuple-element.40), calls=%async_computation.2 | async-start | bytes 65536 | tf_op jit(solution)/shard_map/all_to_all | solution.py:452
  48.5 2.6 %shard_map.109 = (f32[320,512]{1,0:T(8,128)S(1)}, f32[320,512]{1,0:T(8,128)}) custom-call(bf16[5,320,512]{2,1,0:T(8,128)(2,1)} %bitcast.12, f32[320,512]{1,0:T(8,128)S(1)} %get-tuple-element.41.resid_ref), custom_call_target="tpu_custom_call" | custom-call | flops 1638400 | bytes 2949120 | tf_op jit(solution)/shard_map/pallas_call | solution.py:453
  51.2 4.5 %all-to-all-done.2.sums_ref = f32[32,2,128]{2,1,0:T(2,128)S(1)} async-done(((f32[32,2,128]{2,1,0:T(2,128)}), f32[32,2,128]{2,1,0:T(2,128)S(1)}, u32[]{:S(2)}, u32[]{:S(2)}) %all-to-all-start.2) | async-done | bytes 32800 | tf_op jit(solution)/shard_map/all_to_all | solution.py:452
  55.7 1.1 %shard_map.110 = f32[320,512]{1,0:T(8,128)} custom-call(f32[32,2,128]{2,1,0:T(2,128)S(1)} %all-to-all-done.2.sums_ref, f32[320,512]{1,0:T(8,128)S(1)} %get-tuple-element.35.x_ref, f32[320,512]{1,0:T(8,128)S(1)} %get-tuple-element.42.update_ref), custom_call_target="tpu_custom_call" | custom-call | flops 327680 | bytes 1966080 | tf_op jit(solution)/shard_map/pallas_call | solution.py:454
Async XLA Ops:
  3.1 22.6 %all-to-all-start = ((f32[32,5,4,128]{3,2,1,0:T(4,128)}), f32[32,5,4,128]{3,2,1,0:T(4,128)S(1)}, u32[]{:S(2)}, u32[]{:S(2)}) async-start(f32[32,5,4,128]{3,2,1,0:T(4,128)} %get-tuple-element.25), calls=%async_computation | async-start | bytes 655360 | tf_op jit(solution)/shard_map/all_to_all | solution.py:438
  10.4 15.2 %collective-permute-start = (f32[8,320]{1,0:T(8,128)S(1)}, f32[8,320]{1,0:T(8,128)S(1)}, u32[]{:S(2)}, u32[]{:S(2)}) collective-permute-start(f32[8,320]{1,0:T(8,128)S(1)} %get-tuple-element.26), channel_id=1, source_target_pairs={{0,1},{1,2},{2,3},{3,4},{4,5},{5,6},{6,7},{7,0},{8,9},{9,10},{10,1... | collective-permute-start | bytes 30728 | tf_op jit(solution)/shard_map/ppermute | solution.py:439
  12.3 13.4 %collective-permute-start.1 = (f32[8,320]{1,0:T(8,128)S(1)}, f32[8,320]{1,0:T(8,128)S(1)}, u32[]{:S(2)}, u32[]{:S(2)}) collective-permute-start(f32[8,320]{1,0:T(8,128)S(1)} %get-tuple-element.27), channel_id=1, source_target_pairs={{1,0},{2,1},{3,2},{4,3},{5,4},{6,5},{7,6},{0,7},{9,8},{10,9},{11,1... | collective-permute-start | bytes 30728 | tf_op jit(solution)/shard_map/ppermute | solution.py:439
  29.0 15.6 %all-to-all-start.1 = ((f32[32,5,4,128]{3,2,1,0:T(4,128)}), f32[32,5,4,128]{3,2,1,0:T(4,128)S(1)}, u32[]{:S(2)}, u32[]{:S(2)}) async-start(f32[32,5,4,128]{3,2,1,0:T(4,128)} %get-tuple-element.36), calls=%async_computation.1 | async-start | bytes 655360 | tf_op jit(solution)/shard_map/all_to_all | solution.py:438
  32.2 11.2 %collective-permute-start.2 = (f32[8,320]{1,0:T(8,128)S(1)}, f32[8,320]{1,0:T(8,128)S(1)}, u32[]{:S(2)}, u32[]{:S(2)}) collective-permute-start(f32[8,320]{1,0:T(8,128)S(1)} %get-tuple-element.37), channel_id=1, source_target_pairs={{0,1},{1,2},{2,3},{3,4},{4,5},{5,6},{6,7},{7,0},{8,9},{9,10},{10,1... | collective-permute-start | bytes 30728 | tf_op jit(solution)/shard_map/ppermute | solution.py:439
  34.0 9.4 %collective-permute-start.3 = (f32[8,320]{1,0:T(8,128)S(1)}, f32[8,320]{1,0:T(8,128)S(1)}, u32[]{:S(2)}, u32[]{:S(2)}) collective-permute-start(f32[8,320]{1,0:T(8,128)S(1)} %get-tuple-element.38), channel_id=1, source_target_pairs={{1,0},{2,1},{3,2},{4,3},{5,4},{6,5},{7,6},{0,7},{9,8},{10,9},{11,1... | collective-permute-start | bytes 30728 | tf_op jit(solution)/shard_map/ppermute | solution.py:439
  45.9 9.8 %all-to-all-start.2 = ((f32[32,2,128]{2,1,0:T(2,128)}), f32[32,2,128]{2,1,0:T(2,128)S(1)}, u32[]{:S(2)}, u32[]{:S(2)}) async-start(f32[32,2,128]{2,1,0:T(2,128)} %get-tuple-element.40), calls=%async_computation.2 | async-start | bytes 65536 | tf_op jit(solution)/shard_map/all_to_all | solution.py:452

commit v7 on v6

--- a/solution.py
+++ b/solution.py
@@ -33,7 +33,7 @@
     )
 
 
-def send_blocks(x, table, sel_up, sel_down, out_ref, up_ref, down_ref, rows_ref, sem):
+def send_blocks(x, table, select, out_ref, up_ref, down_ref, rows_ref, sem):
     rim = up_ref.shape[0]
     half = rows_ref.shape[2]
     rows = pick(x, table).T.reshape(rows_ref.shape[0], 2 * half, BW)
@@ -47,7 +47,9 @@
     index = lax.axis_index("blk")
     at_last = index == lax.axis_size("blk") - 1
     at_first = index == 0
-    rims = pick(x[:, x.shape[1] - LANES :], sel_up) + pick(x[:, :LANES], sel_down)
+    first = lax.broadcasted_iota(jnp.int32, (BW, LANES), 1) < LANES // 2
+    ends = split(jnp.where(first, x[:, :LANES], x[:, x.shape[1] - LANES :]))
+    rims = jnp.dot(jnp.concatenate(ends, axis=1), select, preferred_element_type=jnp.float32)
     lane = lax.broadcasted_iota(jnp.int32, (1, LANES), 1)
     turn_up = (lane < rim) & at_last
     turn_down = (lane >= rim) & at_first
@@ -72,7 +74,7 @@
 
 def donors_kernel(
     x_ref, src_ref, perm_ref,
-    out_ref, up_ref, down_ref, table_ref, sel_up_ref, sel_down_ref, x_out, rows_ref, sem,
+    out_ref, up_ref, down_ref, table_ref, select_ref, x_out, rows_ref, sem,
 ):
     rim = up_ref.shape[0]
     index = lax.axis_index("blk")
@@ -86,24 +88,26 @@
         partner = perm_ref[0, j]
         wanted = jnp.where((lane[:1] == j) & at_last, partner, wanted)
         target = jnp.where((sub[:, :1] == j) & at_first, partner, target)
-    sel_up = onehot((sub == wanted + (LANES - rim)) & (lane < rim))
-    sel_down = onehot((target + rim == lane) & (sub < rim))
+    to_up = (sub == wanted + (LANES - rim)) & (lane < rim)
+    to_down = (target + rim == lane) & (sub < rim)
+    select = onehot(to_up | to_down)
+    select = jnp.concatenate([select, select], axis=0)
     rows = lax.broadcasted_iota(jnp.int32, table_ref.shape, 0)
     table = onehot(rows == src_ref[...])
     copy = send_blocks(
-        x_ref[...], table, sel_up, sel_down, out_ref, up_ref, down_ref, rows_ref, sem
+        x_ref[...], table, select, out_ref, up_ref, down_ref, rows_ref, sem
     )
     table_ref[...] = table
-    sel_up_ref[...] = sel_up
-    sel_down_ref[...] = sel_down
+    select_ref[...] = select
     x_out[...] = x_ref[...]
     copy.wait()
 
 
-def local_kernel(
-    rim, x_ref, nbr_ref, coup_ref, source_ref, out_ref, high, low, near, coup, source, sems, source_sem,
-    beside=None,
-):
+def take(x, lanes):
+    return jnp.take_along_axis(x, lanes, axis=1, mode="promise_in_bounds")
+
+
+def local_kernel(rim, x_ref, nbr_ref, coup_ref, source_ref, out_ref, coup, source, sems, source_sem):
     slots, blocks = nbr_ref.shape
     chunks = blocks // LANES
     spans = [slice(c * LANES, (c + 1) * LANES) for c in range(chunks)]
@@ -115,37 +119,27 @@
         copy.start()
     source_copy = pltpu.make_async_copy(source_ref, source, source_sem)
     source_copy.start()
-    lane = lax.broadcasted_iota(jnp.int32, (BW, LANES), 1)
-    moved = pltpu.roll(x_ref[...], rim, 1)
-    head = jnp.where(lane < rim, 0.0, moved[:, :LANES])
-    tail = jnp.where(lane < rim, moved[:, :LANES], 0.0)
-    high[...], low[...] = split(jnp.concatenate([head, moved[:, LANES:], tail], axis=1))
-    rows = lax.broadcasted_iota(jnp.int32, (2 * LANES, LANES), 0)
-
-    def gather(c):
-        window = slice(c * LANES, (c + 2) * LANES)
-        table = jnp.concatenate(
-            [onehot(rows == nbr_ref[m : m + 1, spans[c]] - c * LANES) for m in range(slots)], axis=1
-        )
-        near[c][...] = jnp.dot(high[:, window], table, preferred_element_type=jnp.float32) + jnp.dot(
-            low[:, window], table, preferred_element_type=jnp.float32
-        )
-
-    gather(0)
+    first = lax.broadcasted_iota(jnp.int32, (PACK, LANES), 1) < LANES // 2
+    nothing = jnp.zeros((PACK, LANES), jnp.float32)
     for c in range(chunks):
+        picks = []
+        for m in range(slots):
+            at = jnp.broadcast_to(nbr_ref[m : m + 1, spans[c]] - (rim + c * LANES), (PACK, LANES))
+            picks.append((lax.bitwise_and(at, LANES - 1), (at >= 0) & (at < LANES)))
         copies[c].wait()
         if c == 0:
             source_copy.wait()
-        if c + 1 < chunks:
-            gather(c + 1)
-        if beside is not None:
-            beside(c)
         for at in range(0, CELLS, PACK):
             total = [None] * VARS
-            for m in range(slots):
-                for v in range(VARS):
-                    span = slice(v * CELLS + at, v * CELLS + at + PACK)
-                    value = near[c][span, m * LANES : (m + 1) * LANES]
+            for v in range(VARS):
+                span = slice(v * CELLS + at, v * CELLS + at + PACK)
+                own = x_ref[span, spans[c]]
+                after = x_ref[span, spans[c + 1]] if c + 1 < chunks else nothing
+                before = x_ref[span, spans[c - 1]] if c > 0 else nothing
+                beside = jnp.where(first, after, before)
+                for m in range(slots):
+                    lanes, inside = picks[m]
+                    value = jnp.where(inside, take(own, lanes), take(beside, lanes))
                     for u in range(VARS):
                         term = coup[c, m, u, span, :].astype(jnp.float32) * value
                         total[u] = term if total[u] is None else total[u] + term
@@ -156,68 +150,57 @@
 
 def first_local_kernel(
     rim, x_ref, nbr_ref, coup_ref, source_ref, dst_ref, weight_ref,
-    out_ref, rimcoup_ref, rimrow_ref, table_ref, weight_out,
-    high, low, near, coup, source, sems, source_sem, lower_end,
+    out_ref, rimcoup_ref, rimrow_ref, table_ref, weight_out, coup, source, sems, source_sem,
 ):
     slots, blocks = nbr_ref.shape
     chunks = blocks // LANES
     fringe = dst_ref.shape[1]
-    sub = lax.broadcasted_iota(jnp.int32, (LANES, LANES), 0)
-    lane = lax.broadcasted_iota(jnp.int32, (LANES, LANES), 1)
-
-    def place(first, to):
-        at = sub - first
-        inside = (at >= 0) & (at < rim)
-        return jnp.concatenate(
-            [onehot((lane == at + to + m * 2 * rim) & inside) for m in range(slots)], axis=0
-        )
-
-    def read(rows, table):
-        rows = jnp.broadcast_to(jnp.concatenate(rows, axis=1), (PACK, slots * LANES))
-        rows = rows.astype(jnp.float32).astype(jnp.bfloat16)
-        return jnp.dot(rows, table, preferred_element_type=jnp.float32)
-
-    def beside(c):
-        if c not in (0, chunks - 1):
-            return
-        table = place(0, 0) if c == 0 else place(LANES - rim, rim)
-        rows = [nbr_ref[m : m + 1, c * LANES : (c + 1) * LANES] for m in range(slots)]
-        if c == 0:
-            rows = [jnp.where(row < rim, row + 1, 0) for row in rows]
-            rimrow_ref[...] = read(rows, table)
-        else:
-            rows = [jnp.where(row >= blocks + rim, row - blocks + 1, 0) for row in rows]
-            rimrow_ref[...] += read(rows, table)
-        rows = jnp.concatenate([coup[c, m].reshape(VARS * BW, LANES) for m in range(slots)], axis=1)
-        moved = jnp.dot(rows, table, preferred_element_type=jnp.float32)
-        if c == 0:
-            lower_end[...] = moved
-        else:
-            moved = (lower_end[...] + moved).astype(jnp.bfloat16)
-            rimcoup_ref[...] = moved.reshape(VARS, BW, LANES)
-
-    local_kernel(
-        rim, x_ref, nbr_ref, coup_ref, source_ref, out_ref, high, low, near, coup, source, sems, source_sem,
-        beside,
-    )
+    local_kernel(rim, x_ref, nbr_ref, coup_ref, source_ref, out_ref, coup, source, sems, source_sem)
+    lane = lax.broadcasted_iota(jnp.int32, (PACK, LANES), 1)
+    first = lane < LANES // 2
+    masks = [lax.rem(lane + rim + LANES - m * 2 * rim, LANES) < 2 * rim for m in range(slots)]
+
+    def merged(ends, nothing):
+        result = nothing
+        for m in range(slots):
+            both = jnp.where(first, *ends(m))
+            if m > 0:
+                both = pltpu.roll(both, m * 2 * rim, 1)
+            result = jnp.where(masks[m], both, result)
+        return result
+
+    def rows(m):
+        lower = jnp.broadcast_to(nbr_ref[m : m + 1, :LANES], (PACK, LANES))
+        upper = jnp.broadcast_to(nbr_ref[m : m + 1, blocks - LANES :], (PACK, LANES))
+        return jnp.where(lower < rim, lower, -LANES), jnp.where(upper >= blocks + rim, upper - blocks, -LANES)
+
+    rimrow_ref[...] = merged(rows, jnp.full((PACK, LANES), -LANES, jnp.int32))
+    for u in range(VARS):
+        for at in range(0, BW, PACK):
+            span = slice(at, at + PACK)
+            rimcoup_ref[u, span, :] = merged(
+                lambda m: (coup[0, m, u, span, :], coup[chunks - 1, m, u, span, :]),
+                jnp.zeros((PACK, LANES), jnp.bfloat16),
+            )
     weight_out[...] = weight_ref[...]
     targets = jnp.broadcast_to(dst_ref[...], (LANES, fringe)).T
-    edge = lax.rem(sub, 2 * rim)
-    edge = jnp.where(edge < rim, edge, edge + (blocks - 2 * rim))
     for c in range(chunks):
-        span = slice(c * LANES, (c + 1) * LANES)
-        block = lane[:1] + c * LANES
-        table_ref[:fringe, span] = onehot(targets == block)
-        table_ref[fringe:, span] = onehot(edge == block)
+        table_ref[:, c * LANES : (c + 1) * LANES] = onehot(targets == lane[:1] + c * LANES)
 
 
 def full_residual(local_ref, inc_ref, lower_ref, upper_ref, table_ref, weight_ref, rimcoup_ref, rimrow_ref):
     rim = lower_ref.shape[0]
+    blocks = local_ref.shape[1]
     rims = jnp.concatenate(
         [lower_ref[...], upper_ref[...], jnp.zeros((LANES - 2 * rim, BW), jnp.float32)], axis=0
     ).T
+    high, low = split(rims)
+    low = pltpu.roll(low.astype(jnp.float32), 2 * rim, 1)
+    rims = (high.astype(jnp.float32) + low).astype(jnp.bfloat16)
     sub = lax.broadcasted_iota(jnp.int32, (LANES, LANES), 0)
-    near = pick(rims, onehot(sub + 1 == rimrow_ref[:1].astype(jnp.int32)))
+    row = rimrow_ref[:1]
+    reads = onehot((sub == row) | (sub == row + 2 * rim))
+    near = jnp.dot(rims, reads, preferred_element_type=jnp.float32)
     edge = []
     for u in range(VARS):
         total = None
@@ -227,11 +210,18 @@
             total = term if total is None else total + term
         edge.append(total)
     edge = jnp.concatenate(edge, axis=0)
+    shift = LANES // 2
+    while shift >= 2 * rim:
+        edge = edge + pltpu.roll(edge, shift, 1)
+        shift //= 2
+    lane = lax.broadcasted_iota(jnp.int32, (BW, LANES), 1)
     rest = inc_ref[:, 4]
     rest = jnp.concatenate([rest[:, :, :CELLS], rest[:, :, CELLS:]], axis=1).reshape(-1, CELLS)
     fringe = [inc_ref[:, 0:2].reshape(-1, LANES).T, inc_ref[:, 2:4].reshape(-1, LANES).T, rest.T]
-    arrived = jnp.concatenate([jnp.concatenate(fringe, axis=0) * weight_ref[...], edge], axis=1)
-    return local_ref[...] + pick(arrived, table_ref[...])
+    total = local_ref[...] + pick(jnp.concatenate(fringe, axis=0) * weight_ref[...], table_ref[...])
+    lower = total[:, :LANES] + jnp.where(lane < rim, edge, 0.0)
+    upper = total[:, blocks - LANES :] + jnp.where(lane >= LANES - rim, edge, 0.0)
+    return jnp.concatenate([lower, total[:, LANES : blocks - LANES], upper], axis=1)
 
 
 def precondition(diag_ref, resid_ref, u, at):
@@ -250,7 +240,7 @@
 
 def advance_kernel(
     local_ref, inc_ref, lower_ref, upper_ref, across_ref, weight_ref, rimcoup_ref, rimrow_ref,
-    diag_ref, x_ref, table_ref, sel_up_ref, sel_down_ref,
+    diag_ref, x_ref, table_ref, select_ref,
     next_ref, norm_ref, out_ref, up_ref, down_ref, resid, diag, diag_sems, rows_ref, sem,
 ):
     parts = CELLS // PACK
@@ -278,8 +268,7 @@
             span = slice(u * CELLS + at, u * CELLS + at + PACK)
             next_ref[span, :] = x_ref[span, :] + STEP_CFL * total
     copy = send_blocks(
-        next_ref[...], table_ref[...], sel_up_ref[...], sel_down_ref[...],
-        out_ref, up_ref, down_ref, rows_ref, sem,
+        next_ref[...], table_ref[...], select_ref[...], out_ref, up_ref, down_ref, rows_ref, sem
     )
     norm_ref[...] = lane_sums(resid[...])
     copy.wait()
@@ -363,22 +352,18 @@
     sent = [f32(*message), f32(rim, BW), f32(rim, BW)]
     rows_scratch = [pltpu.VMEM(message, jnp.float32), pltpu.SemaphoreType.DMA]
     size = 4 * BW * blocks
-    square = bf16(LANES, LANES)
 
     donors = call(
         donors_kernel,
         [VMEM, VMEM, SMEM],
-        sent + [bf16(blocks, fringe), square, square, state],
+        sent + [bf16(blocks, fringe), bf16(2 * LANES, LANES), state],
         4 * BW * blocks * fringe,
         2 * size,
-        out_specs=[hbm] + [VMEM] * 6,
+        out_specs=[hbm] + [VMEM] * 5,
         scratch_shapes=rows_scratch,
     )
     chunks = blocks // LANES
     scratch = [
-        pltpu.VMEM((BW, blocks + LANES), jnp.bfloat16),
-        pltpu.VMEM((BW, blocks + LANES), jnp.bfloat16),
-        [pltpu.VMEM((BW, slots * LANES), jnp.float32)] * chunks,
         pltpu.VMEM((chunks, slots, VARS, BW, LANES), jnp.bfloat16),
         pltpu.VMEM((BW, blocks), jnp.float32),
         pltpu.SemaphoreType.DMA((chunks,)),
@@ -395,16 +380,16 @@
         [
             state,
             bf16(VARS, BW, LANES),
-            f32(PACK, LANES),
-            bf16(fringe + LANES, blocks),
+            jax.ShapeDtypeStruct((PACK, LANES), jnp.int32),
+            bf16(fringe, blocks),
             f32(1, fringe),
         ],
-        **dict(local_more, scratch_shapes=scratch + [pltpu.VMEM((VARS * BW, LANES), jnp.float32)]),
+        **local_more,
     )
     local = call(functools.partial(local_kernel, rim), [VMEM, VMEM, hbm, hbm], state, **local_more)
     advance = call(
         advance_kernel,
-        [VMEM] * 8 + [hbm] + [VMEM] * 4,
+        [VMEM] * 8 + [hbm] + [VMEM] * 3,
         [state, f32(1, LANES)] + sent,
         8 * BW * blocks * fringe,
         diag.size * 2 + 4 * size,
@@ -438,14 +423,14 @@
         rows = lax.all_to_all(rows, ("body", "blk"), split_axis=0, concat_axis=0, tiled=True)
         return rows, lax.ppermute(to_up, "blk", up), lax.ppermute(to_down, "blk", down)
 
-    *out, table, sel_up, sel_down, x_here = donors(x, here(fringe_src), here(seam_perm))
+    *out, table, select, x_here = donors(x, here(fringe_src), here(seam_perm))
     arrived = exchange(*out)
     part, rimcoup, rimrow, across, weight = first_local(
         x_here, nbr, coup, source_t, here(fringe_dst), here(fringe_weight)
     )
     across = (across, weight, rimcoup, rimrow)
     parts = here(diag_inv.transpose(1, 2, 0).reshape(VARS, VARS, CELLS, blocks))
-    x, norm, *out = advance(part, *arrived, *across, parts, x_here, table, sel_up, sel_down)
+    x, norm, *out = advance(part, *arrived, *across, parts, x_here, table, select)
     arrived = exchange(*out)
     part = local(x, nbr, coup, source_t)
     resid, sums = residual(part, *arrived, *across, norm)

time: 57.3 us -> 58.6 us (1.023)
  Pallas kernels: 27.7 us -> 29.8 us
  waiting for transfers between devices: 5.74 us -> 4.56 us
    pallas_call x1, Pallas kernels: 6.36 us -> 9.18 us  [shards(): part = local(x, nbr, coup, source_t)]
    all_to_all x2, waiting for transfers between devices: 1.18 us -> 0.01 us  [exchange(): lax.all_to_all(rows, ('body', 'blk'), split_axis=0, concat_axis=0, tiled=...]
  transfers between devices with their start and end apart: 7 -> 7, of which waited for: 2 -> 1; matrix products, arithmetic and copies ran while one was open for 0% -> 0% of each run, Pallas kernels for 34% -> 37%
where the time goes in v7:
time: 58.6 us; the launch traced here: 58.2 us
  Pallas kernels  29.8 us (51%)
  starting transfers between devices  23.1 us (39%)
  waiting for transfers between devices  4.56 us (8%)
  between operations  0.74 us (1%)
    all_to_all x2, starting transfers between devices, exchange(): lax.all_to_all(rows, ('body', 'blk'), split_axis=0, concat_axis=0, tiled=...  10.4 us
    pallas_call x1, Pallas kernels, shards(): first_local(x_here, nbr, coup, source_t, here(fringe_dst), here(fringe_we...  9.87 us
    pallas_call x1, Pallas kernels, shards(): part = local(x, nbr, coup, source_t)  9.18 us
    ppermute x2, starting transfers between devices, exchange(): lax.ppermute(to_down, 'blk', down)  5.97 us
    all_to_all x1, waiting for transfers between devices, shards(): lax.all_to_all(sums, ('body', 'blk'), split_axis=0, concat_axis=0, tiled=...  4.55 us
    ppermute x2, starting transfers between devices, exchange(): lax.ppermute(to_up, 'blk', up)  3.64 us
    pallas_call x1, Pallas kernels, shards(): advance(part, *arrived, *across, parts, x_here, table, select)  3.23 us
    all_to_all x1, starting transfers between devices, shards(): lax.all_to_all(sums, ('body', 'blk'), split_axis=0, concat_axis=0, tiled=...  3.08 us
  transfers between devices with their start and end apart: 7, of which 1 were waited for; matrix products, arithmetic and copies ran while one was open for 0% of the time, Pallas kernels for 37%

profile of v7, /device:TPU:0, one launch (start us, length us, event | category | flops | bytes accessed | tf_op | source)
XLA Modules:
  0.0 58.2 jit_solution(13907604874409616116)
XLA Ops:
  0.6 2.4 %shard_map.104 = (f32[32,5,4,128]{3,2,1,0:T(4,128)}, f32[8,320]{1,0:T(8,128)S(1)}, f32[8,320]{1,0:T(8,128)S(1)}, bf16[512,256]{1,0:T(8,128)(2,1)S(1)}, bf16[256,...) custom-call(f32[320,512]{1,0:T(8,128)} %bitcast.15, s32[1,256]{1,0:T(1,128)} %src_ref.1, s32[1,8]{1,0:T(1,128)} %perm_ref.1), custom_call_target="tpu_custom_call" | custom-call | flops 167772160 | bytes 1310720 | tf_op jit(solution)/shard_map/pallas_call | solution.py:426
  3.1 7.3 %all-to-all-start = ((f32[32,5,4,128]{3,2,1,0:T(4,128)}), f32[32,5,4,128]{3,2,1,0:T(4,128)S(1)}, u32[]{:S(2)}, u32[]{:S(2)}) async-start(f32[32,5,4,128]{3,2,1,0:T(4,128)} %get-tuple-element.24), calls=%async_computation | async-start | bytes 655360 | tf_op jit(solution)/shard_map/all_to_all | solution.py:423
  10.4 1.8 %collective-permute-start = (f32[8,320]{1,0:T(8,128)S(1)}, f32[8,320]{1,0:T(8,128)S(1)}, u32[]{:S(2)}, u32[]{:S(2)}) collective-permute-start(f32[8,320]{1,0:T(8,128)S(1)} %get-tuple-element.25), channel_id=1, source_target_pairs={{0,1},{1,2},{2,3},{3,4},{4,5},{5,6},{6,7},{7,0},{8,9},{9,10},{10,1... | collective-permute-start | bytes 30728 | tf_op jit(solution)/shard_map/ppermute | solution.py:424
  12.2 3.0 %collective-permute-start.1 = (f32[8,320]{1,0:T(8,128)S(1)}, f32[8,320]{1,0:T(8,128)S(1)}, u32[]{:S(2)}, u32[]{:S(2)}) collective-permute-start(f32[8,320]{1,0:T(8,128)S(1)} %get-tuple-element.26), channel_id=1, source_target_pairs={{1,0},{2,1},{3,2},{4,3},{5,4},{6,5},{7,6},{0,7},{9,8},{10,9},{11,1... | collective-permute-start | bytes 30728 | tf_op jit(solution)/shard_map/ppermute | solution.py:424
  15.2 9.9 %shard_map.105 = (f32[320,512]{1,0:T(8,128)S(1)}, bf16[5,320,128]{2,1,0:T(8,128)(2,1)S(1)}, s32[16,128]{1,0:T(8,128)S(1)}, bf16[256,512]{1,0:T(8,128)(2,1)S(1)}, f32[1,256]{1,0:T(1,128)S(1)}) custom-call(f32[320,512]{1,0:T(8,128)S(1)} %get-tuple-element.22.x_ref, s32[6,512]{1,0:T(8,128)} %bitcast.17, bf16[6,5,320,512]{3,2,1,0:T(8,128)(2,1)} %bitcast.9, ...), custom_call_target="tpu_custom_call" | custom-call | flops 1006632960 | bytes 12451840 | tf_op jit(solution)/shard_map/pallas_call | solution.py:428
  25.0 0.0 collective-permute-done.lower_ref
  25.0 0.0 collective-permute-done.1.upper_ref
  25.1 0.0 all-to-all-done.inc_ref
  25.1 3.2 %shard_map.106 = (f32[320,512]{1,0:T(8,128)S(1)}, f32[1,128]{1,0:T(1,128)S(1)}, f32[32,5,4,128]{3,2,1,0:T(4,128)}, f32[8,320]{1,0:T(8,128)S(1)}, f32[8,320]{1,0:T(8,128)S(1)}) custom-call(f32[320,512]{1,0:T(8,128)S(1)} %get-tuple-element.23.local_ref, f32[32,5,4,128]{3,2,1,0:T(4,128)S(1)} %all-to-all-done.inc_ref, ...), custom_call_target="tpu_custom_call" | custom-call | flops 335544320 | bytes 4259840 | tf_op jit(solution)/shard_map/pallas_call | solution.py:433
  28.3 3.1 %all-to-all-start.1 = ((f32[32,5,4,128]{3,2,1,0:T(4,128)}), f32[32,5,4,128]{3,2,1,0:T(4,128)S(1)}, u32[]{:S(2)}, u32[]{:S(2)}) async-start(f32[32,5,4,128]{3,2,1,0:T(4,128)} %get-tuple-element.34), calls=%async_computation.1 | async-start | bytes 655360 | tf_op jit(solution)/shard_map/all_to_all | solution.py:423
  31.5 1.8 %collective-permute-start.2 = (f32[8,320]{1,0:T(8,128)S(1)}, f32[8,320]{1,0:T(8,128)S(1)}, u32[]{:S(2)}, u32[]{:S(2)}) collective-permute-start(f32[8,320]{1,0:T(8,128)S(1)} %get-tuple-element.35), channel_id=1, source_target_pairs={{0,1},{1,2},{2,3},{3,4},{4,5},{5,6},{6,7},{7,0},{8,9},{9,10},{10,1... | collective-permute-start | bytes 30728 | tf_op jit(solution)/shard_map/ppermute | solution.py:424
  33.3 3.0 %collective-permute-start.3 = (f32[8,320]{1,0:T(8,128)S(1)}, f32[8,320]{1,0:T(8,128)S(1)}, u32[]{:S(2)}, u32[]{:S(2)}) collective-permute-start(f32[8,320]{1,0:T(8,128)S(1)} %get-tuple-element.36), channel_id=1, source_target_pairs={{1,0},{2,1},{3,2},{4,3},{5,4},{6,5},{7,6},{0,7},{9,8},{10,9},{11,1... | collective-permute-start | bytes 30728 | tf_op jit(solution)/shard_map/ppermute | solution.py:424
  36.3 9.2 %shard_map.107.local_ref = f32[320,512]{1,0:T(8,128)S(1)} custom-call(f32[320,512]{1,0:T(8,128)S(1)} %get-tuple-element.33.x_ref, s32[6,512]{1,0:T(8,128)} %bitcast.18, bf16[6,5,320,512]{3,2,1,0:T(8,128)(2,1)} %bitcast.10, f32[320,512]{1,0:T(8,128)} %bitcast.14), custom_call_target="tpu_custom_call" | custom-call | flops 1006632960 | bytes 12451840 | tf_op jit(solution)/shard_map/pallas_call | solution.py:435
  45.5 0.0 collective-permute-done.2.lower_ref
  45.5 0.0 collective-permute-done.3.upper_ref
  45.5 0.0 all-to-all-done.1.inc_ref
  45.5 1.3 %shard_map.108 = (f32[320,512]{1,0:T(8,128)S(1)}, f32[32,2,128]{2,1,0:T(2,128)}) custom-call(f32[320,512]{1,0:T(8,128)S(1)} %shard_map.107.local_ref, f32[32,5,4,128]{3,2,1,0:T(4,128)S(1)} %all-to-all-done.1.inc_ref, f32[8,320]{1,0:T(8,128)S(1)} %collective-permute-done.2.lower_ref, f32[8,320]{1,0:T(8,128)S(1)} %collective-permute-done.3.upper_ref, ...), custom_call_target="tpu_custom_call" | custom-call | flops 167772160 | bytes 1966080 | tf_op jit(solution)/shard_map/pallas_call | solution.py:436
  46.8 3.1 %all-to-all-start.2 = ((f32[32,2,128]{2,1,0:T(2,128)}), f32[32,2,128]{2,1,0:T(2,128)S(1)}, u32[]{:S(2)}, u32[]{:S(2)}) async-start(f32[32,2,128]{2,1,0:T(2,128)} %get-tuple-element.38), calls=%async_computation.2 | async-start | bytes 65536 | tf_op jit(solution)/shard_map/all_to_all | solution.py:437
  49.9 2.6 %shard_map.109 = (f32[320,512]{1,0:T(8,128)S(1)}, f32[320,512]{1,0:T(8,128)}) custom-call(bf16[5,320,512]{2,1,0:T(8,128)(2,1)} %bitcast.12, f32[320,512]{1,0:T(8,128)S(1)} %get-tuple-element.39.resid_ref), custom_call_target="tpu_custom_call" | custom-call | flops 1638400 | bytes 2949120 | tf_op jit(solution)/shard_map/pallas_call | solution.py:438
  52.5 4.5 %all-to-all-done.2.sums_ref = f32[32,2,128]{2,1,0:T(2,128)S(1)} async-done(((f32[32,2,128]{2,1,0:T(2,128)}), f32[32,2,128]{2,1,0:T(2,128)S(1)}, u32[]{:S(2)}, u32[]{:S(2)}) %all-to-all-start.2) | async-done | bytes 32800 | tf_op jit(solution)/shard_map/all_to_all | solution.py:437
  57.1 1.1 %shard_map.110 = f32[320,512]{1,0:T(8,128)} custom-call(f32[32,2,128]{2,1,0:T(2,128)S(1)} %all-to-all-done.2.sums_ref, f32[320,512]{1,0:T(8,128)S(1)} %get-tuple-element.33.x_ref, f32[320,512]{1,0:T(8,128)S(1)} %get-tuple-element.40.update_ref), custom_call_target="tpu_custom_call" | custom-call | flops 327680 | bytes 1966080 | tf_op jit(solution)/shard_map/pallas_call | solution.py:439
Async XLA Ops:
  3.1 22.0 %all-to-all-start = ((f32[32,5,4,128]{3,2,1,0:T(4,128)}), f32[32,5,4,128]{3,2,1,0:T(4,128)S(1)}, u32[]{:S(2)}, u32[]{:S(2)}) async-start(f32[32,5,4,128]{3,2,1,0:T(4,128)} %get-tuple-element.24), calls=%async_computation | async-start | bytes 655360 | tf_op jit(solution)/shard_map/all_to_all | solution.py:423
  10.4 14.7 %collective-permute-start = (f32[8,320]{1,0:T(8,128)S(1)}, f32[8,320]{1,0:T(8,128)S(1)}, u32[]{:S(2)}, u32[]{:S(2)}) collective-permute-start(f32[8,320]{1,0:T(8,128)S(1)} %get-tuple-element.25), channel_id=1, source_target_pairs={{0,1},{1,2},{2,3},{3,4},{4,5},{5,6},{6,7},{7,0},{8,9},{9,10},{10,1... | collective-permute-start | bytes 30728 | tf_op jit(solution)/shard_map/ppermute | solution.py:424
  12.2 12.8 %collective-permute-start.1 = (f32[8,320]{1,0:T(8,128)S(1)}, f32[8,320]{1,0:T(8,128)S(1)}, u32[]{:S(2)}, u32[]{:S(2)}) collective-permute-start(f32[8,320]{1,0:T(8,128)S(1)} %get-tuple-element.26), channel_id=1, source_target_pairs={{1,0},{2,1},{3,2},{4,3},{5,4},{6,5},{7,6},{0,7},{9,8},{10,9},{11,1... | collective-permute-start | bytes 30728 | tf_op jit(solution)/shard_map/ppermute | solution.py:424
  28.3 17.2 %all-to-all-start.1 = ((f32[32,5,4,128]{3,2,1,0:T(4,128)}), f32[32,5,4,128]{3,2,1,0:T(4,128)S(1)}, u32[]{:S(2)}, u32[]{:S(2)}) async-start(f32[32,5,4,128]{3,2,1,0:T(4,128)} %get-tuple-element.34), calls=%async_computation.1 | async-start | bytes 655360 | tf_op jit(solution)/shard_map/all_to_all | solution.py:423
  31.5 14.0 %collective-permute-start.2 = (f32[8,320]{1,0:T(8,128)S(1)}, f32[8,320]{1,0:T(8,128)S(1)}, u32[]{:S(2)}, u32[]{:S(2)}) collective-permute-start(f32[8,320]{1,0:T(8,128)S(1)} %get-tuple-element.35), channel_id=1, source_target_pairs={{0,1},{1,2},{2,3},{3,4},{4,5},{5,6},{6,7},{7,0},{8,9},{9,10},{10,1... | collective-permute-start | bytes 30728 | tf_op jit(solution)/shard_map/ppermute | solution.py:424
  33.3 12.2 %collective-permute-start.3 = (f32[8,320]{1,0:T(8,128)S(1)}, f32[8,320]{1,0:T(8,128)S(1)}, u32[]{:S(2)}, u32[]{:S(2)}) collective-permute-start(f32[8,320]{1,0:T(8,128)S(1)} %get-tuple-element.36), channel_id=1, source_target_pairs={{1,0},{2,1},{3,2},{4,3},{5,4},{6,5},{7,6},{0,7},{9,8},{10,9},{11,1... | collective-permute-start | bytes 30728 | tf_op jit(solution)/shard_map/ppermute | solution.py:424
  46.8 10.3 %all-to-all-start.2 = ((f32[32,2,128]{2,1,0:T(2,128)}), f32[32,2,128]{2,1,0:T(2,128)S(1)}, u32[]{:S(2)}, u32[]{:S(2)}) async-start(f32[32,2,128]{2,1,0:T(2,128)} %get-tuple-element.38), calls=%async_computation.2 | async-start | bytes 65536 | tf_op jit(solution)/shard_map/all_to_all | solution.py:437

commit v8 on v7

--- a/solution.py
+++ b/solution.py
@@ -103,11 +103,9 @@
     copy.wait()
 
 
-def take(x, lanes):
-    return jnp.take_along_axis(x, lanes, axis=1, mode="promise_in_bounds")
-
-
-def local_kernel(rim, x_ref, nbr_ref, coup_ref, source_ref, out_ref, coup, source, sems, source_sem):
+def local_kernel(
+    rim, x_ref, nbr_ref, coup_ref, source_ref, out_ref, high, low, near, coup, source, sems, source_sem
+):
     slots, blocks = nbr_ref.shape
     chunks = blocks // LANES
     spans = [slice(c * LANES, (c + 1) * LANES) for c in range(chunks)]
@@ -119,27 +117,39 @@
         copy.start()
     source_copy = pltpu.make_async_copy(source_ref, source, source_sem)
     source_copy.start()
-    first = lax.broadcasted_iota(jnp.int32, (PACK, LANES), 1) < LANES // 2
-    nothing = jnp.zeros((PACK, LANES), jnp.float32)
+    lane = lax.broadcasted_iota(jnp.int32, (BW, LANES), 1)
+    moved = pltpu.roll(x_ref[...], rim, 1)
+    head = jnp.where(lane < rim, 0.0, moved[:, :LANES])
+    tail = jnp.where(lane < rim, moved[:, :LANES], 0.0)
+    high[...], low[...] = split(jnp.concatenate([head, moved[:, LANES:], tail], axis=1))
+    rows = lax.broadcasted_iota(jnp.int32, (2 * LANES, LANES), 0)
+
+    pairs = range(0, slots, 2)
+
+    def gather(c, m):
+        window = slice(c * LANES, (c + 2) * LANES)
+        table = jnp.concatenate(
+            [onehot(rows == nbr_ref[i : i + 1, spans[c]] - c * LANES) for i in (m, m + 1)], axis=1
+        )
+        near[c][:, m * LANES : (m + 2) * LANES] = jnp.dot(
+            high[:, window], table, preferred_element_type=jnp.float32
+        ) + jnp.dot(low[:, window], table, preferred_element_type=jnp.float32)
+
+    for m in pairs:
+        gather(0, m)
     for c in range(chunks):
-        picks = []
-        for m in range(slots):
-            at = jnp.broadcast_to(nbr_ref[m : m + 1, spans[c]] - (rim + c * LANES), (PACK, LANES))
-            picks.append((lax.bitwise_and(at, LANES - 1), (at >= 0) & (at < LANES)))
         copies[c].wait()
         if c == 0:
             source_copy.wait()
+        ahead = list(pairs) if c + 1 < chunks else []
         for at in range(0, CELLS, PACK):
+            if ahead:
+                gather(c + 1, ahead.pop(0))
             total = [None] * VARS
-            for v in range(VARS):
-                span = slice(v * CELLS + at, v * CELLS + at + PACK)
-                own = x_ref[span, spans[c]]
-                after = x_ref[span, spans[c + 1]] if c + 1 < chunks else nothing
-                before = x_ref[span, spans[c - 1]] if c > 0 else nothing
-                beside = jnp.where(first, after, before)
-                for m in range(slots):
-                    lanes, inside = picks[m]
-                    value = jnp.where(inside, take(own, lanes), take(beside, lanes))
+            for m in range(slots):
+                for v in range(VARS):
+                    span = slice(v * CELLS + at, v * CELLS + at + PACK)
+                    value = near[c][span, m * LANES : (m + 1) * LANES]
                     for u in range(VARS):
                         term = coup[c, m, u, span, :].astype(jnp.float32) * value
                         total[u] = term if total[u] is None else total[u] + term
@@ -150,12 +160,15 @@
 
 def first_local_kernel(
     rim, x_ref, nbr_ref, coup_ref, source_ref, dst_ref, weight_ref,
-    out_ref, rimcoup_ref, rimrow_ref, table_ref, weight_out, coup, source, sems, source_sem,
+    out_ref, rimcoup_ref, rimrow_ref, table_ref, weight_out,
+    high, low, near, coup, source, sems, source_sem,
 ):
     slots, blocks = nbr_ref.shape
     chunks = blocks // LANES
     fringe = dst_ref.shape[1]
-    local_kernel(rim, x_ref, nbr_ref, coup_ref, source_ref, out_ref, coup, source, sems, source_sem)
+    local_kernel(
+        rim, x_ref, nbr_ref, coup_ref, source_ref, out_ref, high, low, near, coup, source, sems, source_sem
+    )
     lane = lax.broadcasted_iota(jnp.int32, (PACK, LANES), 1)
     first = lane < LANES // 2
     masks = [lax.rem(lane + rim + LANES - m * 2 * rim, LANES) < 2 * rim for m in range(slots)]
@@ -364,6 +377,9 @@
     )
     chunks = blocks // LANES
     scratch = [
+        pltpu.VMEM((BW, blocks + LANES), jnp.bfloat16),
+        pltpu.VMEM((BW, blocks + LANES), jnp.bfloat16),
+        [pltpu.VMEM((BW, slots * LANES), jnp.float32)] * chunks,
         pltpu.VMEM((chunks, slots, VARS, BW, LANES), jnp.bfloat16),
         pltpu.VMEM((BW, blocks), jnp.float32),
         pltpu.SemaphoreType.DMA((chunks,)),

time: 58.6 us -> 55.8 us (0.952)
  Pallas kernels: 29.8 us -> 26.1 us
  waiting for transfers between devices: 4.56 us -> 5.93 us
    pallas_call x1, Pallas kernels: 9.18 us -> 6.24 us  [shards(): part = local(x, nbr, coup, source_t)]
    all_to_all x2, waiting for transfers between devices: 0.01 us -> 1.24 us  [exchange(): lax.all_to_all(rows, ('body', 'blk'), split_axis=0, concat_axis=0, tiled=...]
    pallas_call x1, Pallas kernels: 9.87 us -> 9.18 us  [shards(): first_local(x_here, nbr, coup, source_t, here(fringe_dst), here(fringe_we...]
  transfers between devices with their start and end apart: 7 -> 7, of which waited for: 1 -> 3; matrix products, arithmetic and copies ran while one was open for 0% -> 0% of each run, Pallas kernels for 37% -> 33%
where the time goes in v8:
time: 55.8 us; the launch traced here: 55.3 us
  Pallas kernels  26.1 us (47%)
  starting transfers between devices  22.6 us (41%)
  waiting for transfers between devices  5.93 us (11%)
  between operations  0.71 us (1%)
    all_to_all x2, starting transfers between devices, exchange(): lax.all_to_all(rows, ('body', 'blk'), split_axis=0, concat_axis=0, tiled=...  10.4 us
    pallas_call x1, Pallas kernels, shards(): first_local(x_here, nbr, coup, source_t, here(fringe_dst), here(fringe_we...  9.18 us
    pallas_call x1, Pallas kernels, shards(): part = local(x, nbr, coup, source_t)  6.24 us
    ppermute x2, starting transfers between devices, exchange(): lax.ppermute(to_down, 'blk', down)  5.91 us
    all_to_all x1, waiting for transfers between devices, shards(): lax.all_to_all(sums, ('body', 'blk'), split_axis=0, concat_axis=0, tiled=...  4.55 us
    ppermute x2, starting transfers between devices, exchange(): lax.ppermute(to_up, 'blk', up)  3.64 us
    pallas_call x1, Pallas kernels, shards(): advance(part, *arrived, *across, parts, x_here, table, select)  3.23 us
    pallas_call x1, Pallas kernels, shards(): update, resid = direction(diag, resid)  2.64 us
  transfers between devices with their start and end apart: 7, of which 3 were waited for; matrix products, arithmetic and copies ran while one was open for 0% of the time, Pallas kernels for 33%

profile of v8, /device:TPU:0, one launch (start us, length us, event | category | flops | bytes accessed | tf_op | source)
XLA Modules:
  0.0 55.3 jit_solution(8602366473872391992)
XLA Ops:
  0.6 2.4 %shard_map.104 = (f32[32,5,4,128]{3,2,1,0:T(4,128)}, f32[8,320]{1,0:T(8,128)S(1)}, f32[8,320]{1,0:T(8,128)S(1)}, bf16[512,256]{1,0:T(8,128)(2,1)S(1)}, bf16[256,...) custom-call(f32[320,512]{1,0:T(8,128)} %bitcast.15, s32[1,256]{1,0:T(1,128)} %src_ref.1, s32[1,8]{1,0:T(1,128)} %perm_ref.1), custom_call_target="tpu_custom_call" | custom-call | flops 167772160 | bytes 1310720 | tf_op jit(solution)/shard_map/pallas_call | solution.py:442
  3.1 7.3 %all-to-all-start = ((f32[32,5,4,128]{3,2,1,0:T(4,128)}), f32[32,5,4,128]{3,2,1,0:T(4,128)S(1)}, u32[]{:S(2)}, u32[]{:S(2)}) async-start(f32[32,5,4,128]{3,2,1,0:T(4,128)} %get-tuple-element.24), calls=%async_computation | async-start | bytes 655360 | tf_op jit(solution)/shard_map/all_to_all | solution.py:439
  10.4 1.8 %collective-permute-start = (f32[8,320]{1,0:T(8,128)S(1)}, f32[8,320]{1,0:T(8,128)S(1)}, u32[]{:S(2)}, u32[]{:S(2)}) collective-permute-start(f32[8,320]{1,0:T(8,128)S(1)} %get-tuple-element.25), channel_id=1, source_target_pairs={{0,1},{1,2},{2,3},{3,4},{4,5},{5,6},{6,7},{7,0},{8,9},{9,10},{10,1... | collective-permute-start | bytes 30728 | tf_op jit(solution)/shard_map/ppermute | solution.py:440
  12.2 3.0 %collective-permute-start.1 = (f32[8,320]{1,0:T(8,128)S(1)}, f32[8,320]{1,0:T(8,128)S(1)}, u32[]{:S(2)}, u32[]{:S(2)}) collective-permute-start(f32[8,320]{1,0:T(8,128)S(1)} %get-tuple-element.26), channel_id=1, source_target_pairs={{1,0},{2,1},{3,2},{4,3},{5,4},{6,5},{7,6},{0,7},{9,8},{10,9},{11,1... | collective-permute-start | bytes 30728 | tf_op jit(solution)/shard_map/ppermute | solution.py:440
  15.2 9.2 %shard_map.105 = (f32[320,512]{1,0:T(8,128)S(1)}, bf16[5,320,128]{2,1,0:T(8,128)(2,1)S(1)}, s32[16,128]{1,0:T(8,128)S(1)}, bf16[256,512]{1,0:T(8,128)(2,1)S(1)}, f32[1,256]{1,0:T(1,128)S(1)}) custom-call(f32[320,512]{1,0:T(8,128)S(1)} %get-tuple-element.22.x_ref, s32[6,512]{1,0:T(8,128)} %bitcast.17, bf16[6,5,320,512]{3,2,1,0:T(8,128)(2,1)} %bitcast.9, ...), custom_call_target="tpu_custom_call" | custom-call | flops 1006632960 | bytes 12451840 | tf_op jit(solution)/shard_map/pallas_call | solution.py:444
  24.4 0.0 collective-permute-done.lower_ref
  24.4 0.0 collective-permute-done.1.upper_ref
  24.4 0.0 all-to-all-done.inc_ref
  24.4 3.2 %shard_map.106 = (f32[320,512]{1,0:T(8,128)S(1)}, f32[1,128]{1,0:T(1,128)S(1)}, f32[32,5,4,128]{3,2,1,0:T(4,128)}, f32[8,320]{1,0:T(8,128)S(1)}, f32[8,320]{1,0:T(8,128)S(1)}) custom-call(f32[320,512]{1,0:T(8,128)S(1)} %get-tuple-element.23.local_ref, f32[32,5,4,128]{3,2,1,0:T(4,128)S(1)} %all-to-all-done.inc_ref, ...), custom_call_target="tpu_custom_call" | custom-call | flops 335544320 | bytes 4259840 | tf_op jit(solution)/shard_map/pallas_call | solution.py:449
  27.6 3.1 %all-to-all-start.1 = ((f32[32,5,4,128]{3,2,1,0:T(4,128)}), f32[32,5,4,128]{3,2,1,0:T(4,128)S(1)}, u32[]{:S(2)}, u32[]{:S(2)}) async-start(f32[32,5,4,128]{3,2,1,0:T(4,128)} %get-tuple-element.34), calls=%async_computation.1 | async-start | bytes 655360 | tf_op jit(solution)/shard_map/all_to_all | solution.py:439
  30.8 1.8 %collective-permute-start.2 = (f32[8,320]{1,0:T(8,128)S(1)}, f32[8,320]{1,0:T(8,128)S(1)}, u32[]{:S(2)}, u32[]{:S(2)}) collective-permute-start(f32[8,320]{1,0:T(8,128)S(1)} %get-tuple-element.35), channel_id=1, source_target_pairs={{0,1},{1,2},{2,3},{3,4},{4,5},{5,6},{6,7},{7,0},{8,9},{9,10},{10,1... | collective-permute-start | bytes 30728 | tf_op jit(solution)/shard_map/ppermute | solution.py:440
  32.6 3.0 %collective-permute-start.3 = (f32[8,320]{1,0:T(8,128)S(1)}, f32[8,320]{1,0:T(8,128)S(1)}, u32[]{:S(2)}, u32[]{:S(2)}) collective-permute-start(f32[8,320]{1,0:T(8,128)S(1)} %get-tuple-element.36), channel_id=1, source_target_pairs={{1,0},{2,1},{3,2},{4,3},{5,4},{6,5},{7,6},{0,7},{9,8},{10,9},{11,1... | collective-permute-start | bytes 30728 | tf_op jit(solution)/shard_map/ppermute | solution.py:440
  35.5 6.2 %shard_map.107.local_ref = f32[320,512]{1,0:T(8,128)S(1)} custom-call(f32[320,512]{1,0:T(8,128)S(1)} %get-tuple-element.33.x_ref, s32[6,512]{1,0:T(8,128)} %bitcast.18, bf16[6,5,320,512]{3,2,1,0:T(8,128)(2,1)} %bitcast.10, f32[320,512]{1,0:T(8,128)} %bitcast.14), custom_call_target="tpu_custom_call" | custom-call | flops 1006632960 | bytes 12451840 | tf_op jit(solution)/shard_map/pallas_call | solution.py:451
  41.8 0.1 collective-permute-done.2.lower_ref
  41.9 0.0 collective-permute-done.3.upper_ref
  41.9 1.2 %all-to-all-done.1.inc_ref = f32[32,5,4,128]{3,2,1,0:T(4,128)S(1)} async-done(((f32[32,5,4,128]{3,2,1,0:T(4,128)}), f32[32,5,4,128]{3,2,1,0:T(4,128)S(1)}, u32[]{:S(2)}, u32[]{:S(2)}) %all-to-all-start.1) | async-done | bytes 327712 | tf_op jit(solution)/shard_map/all_to_all | solution.py:439
  43.2 1.3 %shard_map.108 = (f32[320,512]{1,0:T(8,128)S(1)}, f32[32,2,128]{2,1,0:T(2,128)}) custom-call(f32[320,512]{1,0:T(8,128)S(1)} %shard_map.107.local_ref, f32[32,5,4,128]{3,2,1,0:T(4,128)S(1)} %all-to-all-done.1.inc_ref, f32[8,320]{1,0:T(8,128)S(1)} %collective-permute-done.2.lower_ref, f32[8,320]{1,0:T(8,128)S(1)} %collective-permute-done.3.upper_ref, ...), custom_call_target="tpu_custom_call" | custom-call | flops 167772160 | bytes 1966080 | tf_op jit(solution)/shard_map/pallas_call | solution.py:452
  44.5 2.6 %all-to-all-start.2 = ((f32[32,2,128]{2,1,0:T(2,128)}), f32[32,2,128]{2,1,0:T(2,128)S(1)}, u32[]{:S(2)}, u32[]{:S(2)}) async-start(f32[32,2,128]{2,1,0:T(2,128)} %get-tuple-element.38), calls=%async_computation.2 | async-start | bytes 65536 | tf_op jit(solution)/shard_map/all_to_all | solution.py:453
  47.1 2.6 %shard_map.109 = (f32[320,512]{1,0:T(8,128)S(1)}, f32[320,512]{1,0:T(8,128)}) custom-call(bf16[5,320,512]{2,1,0:T(8,128)(2,1)} %bitcast.12, f32[320,512]{1,0:T(8,128)S(1)} %get-tuple-element.39.resid_ref), custom_call_target="tpu_custom_call" | custom-call | flops 1638400 | bytes 2949120 | tf_op jit(solution)/shard_map/pallas_call | solution.py:454
  49.7 4.5 %all-to-all-done.2.sums_ref = f32[32,2,128]{2,1,0:T(2,128)S(1)} async-done(((f32[32,2,128]{2,1,0:T(2,128)}), f32[32,2,128]{2,1,0:T(2,128)S(1)}, u32[]{:S(2)}, u32[]{:S(2)}) %all-to-all-start.2) | async-done | bytes 32800 | tf_op jit(solution)/shard_map/all_to_all | solution.py:453
  54.2 1.1 %shard_map.110 = f32[320,512]{1,0:T(8,128)} custom-call(f32[32,2,128]{2,1,0:T(2,128)S(1)} %all-to-all-done.2.sums_ref, f32[320,512]{1,0:T(8,128)S(1)} %get-tuple-element.33.x_ref, f32[320,512]{1,0:T(8,128)S(1)} %get-tuple-element.40.update_ref), custom_call_target="tpu_custom_call" | custom-call | flops 327680 | bytes 1966080 | tf_op jit(solution)/shard_map/pallas_call | solution.py:455
Async XLA Ops:
  3.1 21.3 %all-to-all-start = ((f32[32,5,4,128]{3,2,1,0:T(4,128)}), f32[32,5,4,128]{3,2,1,0:T(4,128)S(1)}, u32[]{:S(2)}, u32[]{:S(2)}) async-start(f32[32,5,4,128]{3,2,1,0:T(4,128)} %get-tuple-element.24), calls=%async_computation | async-start | bytes 655360 | tf_op jit(solution)/shard_map/all_to_all | solution.py:439
  10.4 14.0 %collective-permute-start = (f32[8,320]{1,0:T(8,128)S(1)}, f32[8,320]{1,0:T(8,128)S(1)}, u32[]{:S(2)}, u32[]{:S(2)}) collective-permute-start(f32[8,320]{1,0:T(8,128)S(1)} %get-tuple-element.25), channel_id=1, source_target_pairs={{0,1},{1,2},{2,3},{3,4},{4,5},{5,6},{6,7},{7,0},{8,9},{9,10},{10,1... | collective-permute-start | bytes 30728 | tf_op jit(solution)/shard_map/ppermute | solution.py:440
  12.2 12.2 %collective-permute-start.1 = (f32[8,320]{1,0:T(8,128)S(1)}, f32[8,320]{1,0:T(8,128)S(1)}, u32[]{:S(2)}, u32[]{:S(2)}) collective-permute-start(f32[8,320]{1,0:T(8,128)S(1)} %get-tuple-element.26), channel_id=1, source_target_pairs={{1,0},{2,1},{3,2},{4,3},{5,4},{6,5},{7,6},{0,7},{9,8},{10,9},{11,1... | collective-permute-start | bytes 30728 | tf_op jit(solution)/shard_map/ppermute | solution.py:440
  27.6 15.5 %all-to-all-start.1 = ((f32[32,5,4,128]{3,2,1,0:T(4,128)}), f32[32,5,4,128]{3,2,1,0:T(4,128)S(1)}, u32[]{:S(2)}, u32[]{:S(2)}) async-start(f32[32,5,4,128]{3,2,1,0:T(4,128)} %get-tuple-element.34), calls=%async_computation.1 | async-start | bytes 655360 | tf_op jit(solution)/shard_map/all_to_all | solution.py:439
  30.8 11.2 %collective-permute-start.2 = (f32[8,320]{1,0:T(8,128)S(1)}, f32[8,320]{1,0:T(8,128)S(1)}, u32[]{:S(2)}, u32[]{:S(2)}) collective-permute-start(f32[8,320]{1,0:T(8,128)S(1)} %get-tuple-element.35), channel_id=1, source_target_pairs={{0,1},{1,2},{2,3},{3,4},{4,5},{5,6},{6,7},{7,0},{8,9},{9,10},{10,1... | collective-permute-start | bytes 30728 | tf_op jit(solution)/shard_map/ppermute | solution.py:440
  32.6 9.3 %collective-permute-start.3 = (f32[8,320]{1,0:T(8,128)S(1)}, f32[8,320]{1,0:T(8,128)S(1)}, u32[]{:S(2)}, u32[]{:S(2)}) collective-permute-start(f32[8,320]{1,0:T(8,128)S(1)} %get-tuple-element.36), channel_id=1, source_target_pairs={{1,0},{2,1},{3,2},{4,3},{5,4},{6,5},{7,6},{0,7},{9,8},{10,9},{11,1... | collective-permute-start | bytes 30728 | tf_op jit(solution)/shard_map/ppermute | solution.py:440
  44.5 9.8 %all-to-all-start.2 = ((f32[32,2,128]{2,1,0:T(2,128)}), f32[32,2,128]{2,1,0:T(2,128)S(1)}, u32[]{:S(2)}, u32[]{:S(2)}) async-start(f32[32,2,128]{2,1,0:T(2,128)} %get-tuple-element.38), calls=%async_computation.2 | async-start | bytes 65536 | tf_op jit(solution)/shard_map/all_to_all | solution.py:453

commit v9 on v8

--- a/solution.py
+++ b/solution.py
@@ -27,10 +27,8 @@
 
 
 def pick(x, table):
-    high, low = split(x)
-    return jnp.dot(high, table, preferred_element_type=jnp.float32) + jnp.dot(
-        low, table, preferred_element_type=jnp.float32
-    )
+    both = jnp.dot(jnp.concatenate(split(x), axis=0), table, preferred_element_type=jnp.float32)
+    return both[: x.shape[0]] + both[x.shape[0] :]
 
 
 def send_blocks(x, table, select, out_ref, up_ref, down_ref, rows_ref, sem):
@@ -104,7 +102,8 @@
 
 
 def local_kernel(
-    rim, x_ref, nbr_ref, coup_ref, source_ref, out_ref, high, low, near, coup, source, sems, source_sem
+    rim, x_ref, nbr_ref, coup_ref, source_ref, out_ref, terms, near, coup, source, sems, source_sem,
+    at_start=None, at_end=None,
 ):
     slots, blocks = nbr_ref.shape
     chunks = blocks // LANES
@@ -121,7 +120,7 @@
     moved = pltpu.roll(x_ref[...], rim, 1)
     head = jnp.where(lane < rim, 0.0, moved[:, :LANES])
     tail = jnp.where(lane < rim, moved[:, :LANES], 0.0)
-    high[...], low[...] = split(jnp.concatenate([head, moved[:, LANES:], tail], axis=1))
+    terms[:BW], terms[BW:] = split(jnp.concatenate([head, moved[:, LANES:], tail], axis=1))
     rows = lax.broadcasted_iota(jnp.int32, (2 * LANES, LANES), 0)
 
     pairs = range(0, slots, 2)
@@ -131,12 +130,13 @@
         table = jnp.concatenate(
             [onehot(rows == nbr_ref[i : i + 1, spans[c]] - c * LANES) for i in (m, m + 1)], axis=1
         )
-        near[c][:, m * LANES : (m + 2) * LANES] = jnp.dot(
-            high[:, window], table, preferred_element_type=jnp.float32
-        ) + jnp.dot(low[:, window], table, preferred_element_type=jnp.float32)
+        both = jnp.dot(terms[:, window], table, preferred_element_type=jnp.float32)
+        near[c][:, m * LANES : (m + 2) * LANES] = both[:BW] + both[BW:]
 
     for m in pairs:
         gather(0, m)
+    if at_start is not None:
+        at_start()
     for c in range(chunks):
         copies[c].wait()
         if c == 0:
@@ -145,6 +145,8 @@
         for at in range(0, CELLS, PACK):
             if ahead:
                 gather(c + 1, ahead.pop(0))
+            if at_end is not None and c + 1 == chunks:
+                at_end(at)
             total = [None] * VARS
             for m in range(slots):
                 for v in range(VARS):
@@ -161,14 +163,11 @@
 def first_local_kernel(
     rim, x_ref, nbr_ref, coup_ref, source_ref, dst_ref, weight_ref,
     out_ref, rimcoup_ref, rimrow_ref, table_ref, weight_out,
-    high, low, near, coup, source, sems, source_sem,
+    terms, near, coup, source, sems, source_sem,
 ):
     slots, blocks = nbr_ref.shape
     chunks = blocks // LANES
     fringe = dst_ref.shape[1]
-    local_kernel(
-        rim, x_ref, nbr_ref, coup_ref, source_ref, out_ref, high, low, near, coup, source, sems, source_sem
-    )
     lane = lax.broadcasted_iota(jnp.int32, (PACK, LANES), 1)
     first = lane < LANES // 2
     masks = [lax.rem(lane + rim + LANES - m * 2 * rim, LANES) < 2 * rim for m in range(slots)]
@@ -187,18 +186,26 @@
         upper = jnp.broadcast_to(nbr_ref[m : m + 1, blocks - LANES :], (PACK, LANES))
         return jnp.where(lower < rim, lower, -LANES), jnp.where(upper >= blocks + rim, upper - blocks, -LANES)
 
-    rimrow_ref[...] = merged(rows, jnp.full((PACK, LANES), -LANES, jnp.int32))
-    for u in range(VARS):
-        for at in range(0, BW, PACK):
-            span = slice(at, at + PACK)
-            rimcoup_ref[u, span, :] = merged(
-                lambda m: (coup[0, m, u, span, :], coup[chunks - 1, m, u, span, :]),
-                jnp.zeros((PACK, LANES), jnp.bfloat16),
-            )
-    weight_out[...] = weight_ref[...]
-    targets = jnp.broadcast_to(dst_ref[...], (LANES, fringe)).T
-    for c in range(chunks):
-        table_ref[:, c * LANES : (c + 1) * LANES] = onehot(targets == lane[:1] + c * LANES)
+    def tables():
+        rimrow_ref[...] = merged(rows, jnp.full((PACK, LANES), -LANES, jnp.int32))
+        weight_out[...] = weight_ref[...]
+        targets = jnp.broadcast_to(dst_ref[...], (LANES, fringe)).T
+        for c in range(chunks):
+            table_ref[:, c * LANES : (c + 1) * LANES] = onehot(targets == lane[:1] + c * LANES)
+
+    def rim_coupling(at):
+        for u in range(VARS):
+            for v in range(VARS):
+                span = slice(v * CELLS + at, v * CELLS + at + PACK)
+                rimcoup_ref[u, span, :] = merged(
+                    lambda m: (coup[0, m, u, span, :], coup[chunks - 1, m, u, span, :]),
+                    jnp.zeros((PACK, LANES), jnp.bfloat16),
+                )
+
+    local_kernel(
+        rim, x_ref, nbr_ref, coup_ref, source_ref, out_ref, terms, near, coup, source, sems, source_sem,
+        tables, rim_coupling,
+    )
 
 
 def full_residual(local_ref, inc_ref, lower_ref, upper_ref, table_ref, weight_ref, rimcoup_ref, rimrow_ref):
@@ -256,27 +263,21 @@
     diag_ref, x_ref, table_ref, select_ref,
     next_ref, norm_ref, out_ref, up_ref, down_ref, resid, diag, diag_sems, rows_ref, sem,
 ):
-    parts = CELLS // PACK
-    fetches = []
-    for part in range(parts):
-        span = pl.ds(part * PACK, PACK)
-        fetches.append(
-            pltpu.make_async_copy(
-                diag_ref.at[:, :, span], diag.at[:, :, span], diag_sems.at[part]
-            )
-        )
-        fetches[part].start()
+    fetches = [
+        pltpu.make_async_copy(diag_ref.at[u], diag.at[u], diag_sems.at[u]) for u in range(VARS)
+    ]
+    for fetch in fetches:
+        fetch.start()
     resid[...] = full_residual(
         local_ref, inc_ref, lower_ref, upper_ref, across_ref, weight_ref, rimcoup_ref, rimrow_ref
     )
-    for part in range(parts):
-        fetches[part].wait()
-        at = part * PACK
-        for u in range(VARS):
+    for u in range(VARS):
+        fetches[u].wait()
+        for at in range(0, CELLS, PACK):
             total = None
             for v in range(VARS):
-                term = diag[u, v, at : at + PACK].astype(jnp.float32)
-                term = term * resid[v * CELLS + at : v * CELLS + at + PACK]
+                span = slice(v * CELLS + at, v * CELLS + at + PACK)
+                term = diag[u, span].astype(jnp.float32) * resid[span]
                 total = term if total is None else total + term
             span = slice(u * CELLS + at, u * CELLS + at + PACK)
             next_ref[span, :] = x_ref[span, :] + STEP_CFL * total
@@ -377,8 +378,7 @@
     )
     chunks = blocks // LANES
     scratch = [
-        pltpu.VMEM((BW, blocks + LANES), jnp.bfloat16),
-        pltpu.VMEM((BW, blocks + LANES), jnp.bfloat16),
+        pltpu.VMEM((2 * BW, blocks + LANES), jnp.bfloat16),
         [pltpu.VMEM((BW, slots * LANES), jnp.float32)] * chunks,
         pltpu.VMEM((chunks, slots, VARS, BW, LANES), jnp.bfloat16),
         pltpu.VMEM((BW, blocks), jnp.float32),
@@ -412,8 +412,8 @@
         out_specs=[VMEM, VMEM, hbm, VMEM, VMEM],
         scratch_shapes=[
             pltpu.VMEM((BW, blocks), jnp.float32),
-            pltpu.VMEM((VARS, VARS, CELLS, blocks), jnp.bfloat16),
-            pltpu.SemaphoreType.DMA((CELLS // PACK,)),
+            pltpu.VMEM((VARS, BW, blocks), jnp.bfloat16),
+            pltpu.SemaphoreType.DMA((VARS,)),
         ]
         + rows_scratch,
     )
@@ -445,8 +445,7 @@
         x_here, nbr, coup, source_t, here(fringe_dst), here(fringe_weight)
     )
     across = (across, weight, rimcoup, rimrow)
-    parts = here(diag_inv.transpose(1, 2, 0).reshape(VARS, VARS, CELLS, blocks))
-    x, norm, *out = advance(part, *arrived, *across, parts, x_here, table, select)
+    x, norm, *out = advance(part, *arrived, *across, diag, x_here, table, select)
     arrived = exchange(*out)
     part = local(x, nbr, coup, source_t)
     resid, sums = residual(part, *arrived, *across, norm)

time: 55.8 us -> 54.9 us (0.984)
  Pallas kernels: 26.1 us -> 25.1 us
    pallas_call x1, Pallas kernels: 9.18 us -> 8.16 us  [shards(): first_local(x_here, nbr, coup, source_t, here(fringe_dst), here(fringe_we...]
  transfers between devices with their start and end apart: 7 -> 7, of which waited for: 3 -> 3; matrix products, arithmetic and copies ran while one was open for 0% -> 0% of each run, Pallas kernels for 33% -> 31%
where the time goes in v9:
time: 54.9 us; the launch traced here: 54.4 us
  Pallas kernels  25.1 us (46%)
  starting transfers between devices  22.6 us (41%)
  waiting for transfers between devices  6.02 us (11%)
  between operations  0.71 us (1%)
    all_to_all x2, starting transfers between devices, exchange(): lax.all_to_all(rows, ('body', 'blk'), split_axis=0, concat_axis=0, tiled=...  10.4 us
    pallas_call x1, Pallas kernels, shards(): first_local(x_here, nbr, coup, source_t, here(fringe_dst), here(fringe_we...  8.16 us
    pallas_call x1, Pallas kernels, shards(): part = local(x, nbr, coup, source_t)  6.15 us
    ppermute x2, starting transfers between devices, exchange(): lax.ppermute(to_down, 'blk', down)  5.91 us
    all_to_all x1, waiting for transfers between devices, shards(): lax.all_to_all(sums, ('body', 'blk'), split_axis=0, concat_axis=0, tiled=...  4.55 us
    ppermute x2, starting transfers between devices, exchange(): lax.ppermute(to_up, 'blk', up)  3.64 us
    pallas_call x1, Pallas kernels, shards(): advance(part, *arrived, *across, diag, x_here, table, select)  3.33 us
    pallas_call x1, Pallas kernels, shards(): update, resid = direction(diag, resid)  2.64 us
  transfers between devices with their start and end apart: 7, of which 3 were waited for; matrix products, arithmetic and copies ran while one was open for 0% of the time, Pallas kernels for 31%

profile of v9, /device:TPU:0, one launch (start us, length us, event | category | flops | bytes accessed | tf_op | source)
XLA Modules:
  0.0 54.4 jit_solution(5734314585733358702)
XLA Ops:
  0.6 2.4 %shard_map.104 = (f32[32,5,4,128]{3,2,1,0:T(4,128)}, f32[8,320]{1,0:T(8,128)S(1)}, f32[8,320]{1,0:T(8,128)S(1)}, bf16[512,256]{1,0:T(8,128)(2,1)S(1)}, bf16[256,...) custom-call(f32[320,512]{1,0:T(8,128)} %bitcast.13, s32[1,256]{1,0:T(1,128)} %src_ref.1, s32[1,8]{1,0:T(1,128)} %perm_ref.1), custom_call_target="tpu_custom_call" | custom-call | flops 167772160 | bytes 1310720 | tf_op jit(solution)/shard_map/pallas_call | solution.py:442
  3.0 7.3 %all-to-all-start = ((f32[32,5,4,128]{3,2,1,0:T(4,128)}), f32[32,5,4,128]{3,2,1,0:T(4,128)S(1)}, u32[]{:S(2)}, u32[]{:S(2)}) async-start(f32[32,5,4,128]{3,2,1,0:T(4,128)} %get-tuple-element.24), calls=%async_computation | async-start | bytes 655360 | tf_op jit(solution)/shard_map/all_to_all | solution.py:439
  10.4 1.8 %collective-permute-start = (f32[8,320]{1,0:T(8,128)S(1)}, f32[8,320]{1,0:T(8,128)S(1)}, u32[]{:S(2)}, u32[]{:S(2)}) collective-permute-start(f32[8,320]{1,0:T(8,128)S(1)} %get-tuple-element.25), channel_id=1, source_target_pairs={{0,1},{1,2},{2,3},{3,4},{4,5},{5,6},{6,7},{7,0},{8,9},{9,10},{10,1... | collective-permute-start | bytes 30728 | tf_op jit(solution)/shard_map/ppermute | solution.py:440
  12.2 3.0 %collective-permute-start.1 = (f32[8,320]{1,0:T(8,128)S(1)}, f32[8,320]{1,0:T(8,128)S(1)}, u32[]{:S(2)}, u32[]{:S(2)}) collective-permute-start(f32[8,320]{1,0:T(8,128)S(1)} %get-tuple-element.26), channel_id=1, source_target_pairs={{1,0},{2,1},{3,2},{4,3},{5,4},{6,5},{7,6},{0,7},{9,8},{10,9},{11,1... | collective-permute-start | bytes 30728 | tf_op jit(solution)/shard_map/ppermute | solution.py:440
  15.1 8.2 %shard_map.105 = (f32[320,512]{1,0:T(8,128)S(1)}, bf16[5,320,128]{2,1,0:T(8,128)(2,1)S(1)}, s32[16,128]{1,0:T(8,128)S(1)}, bf16[256,512]{1,0:T(8,128)(2,1)S(1)}, f32[1,256]{1,0:T(1,128)S(1)}) custom-call(f32[320,512]{1,0:T(8,128)S(1)} %get-tuple-element.22.x_ref, s32[6,512]{1,0:T(8,128)} %bitcast.15, bf16[6,5,320,512]{3,2,1,0:T(8,128)(2,1)} %bitcast.7, ...), custom_call_target="tpu_custom_call" | custom-call | flops 1006632960 | bytes 12451840 | tf_op jit(solution)/shard_map/pallas_call | solution.py:444
  23.3 0.0 collective-permute-done.lower_ref
  23.3 0.0 collective-permute-done.1.upper_ref
  23.3 0.0 all-to-all-done.inc_ref
  23.3 3.3 %shard_map.106 = (f32[320,512]{1,0:T(8,128)S(1)}, f32[1,128]{1,0:T(1,128)S(1)}, f32[32,5,4,128]{3,2,1,0:T(4,128)}, f32[8,320]{1,0:T(8,128)S(1)}, f32[8,320]{1,0:T(8,128)S(1)}) custom-call(f32[320,512]{1,0:T(8,128)S(1)} %get-tuple-element.23.local_ref, f32[32,5,4,128]{3,2,1,0:T(4,128)S(1)} %all-to-all-done.inc_ref, ...), custom_call_target="tpu_custom_call" | custom-call | flops 335544320 | bytes 4259840 | tf_op jit(solution)/shard_map/pallas_call | solution.py:448
  26.7 3.1 %all-to-all-start.1 = ((f32[32,5,4,128]{3,2,1,0:T(4,128)}), f32[32,5,4,128]{3,2,1,0:T(4,128)S(1)}, u32[]{:S(2)}, u32[]{:S(2)}) async-start(f32[32,5,4,128]{3,2,1,0:T(4,128)} %get-tuple-element.34), calls=%async_computation.1 | async-start | bytes 655360 | tf_op jit(solution)/shard_map/all_to_all | solution.py:439
  29.8 1.8 %collective-permute-start.2 = (f32[8,320]{1,0:T(8,128)S(1)}, f32[8,320]{1,0:T(8,128)S(1)}, u32[]{:S(2)}, u32[]{:S(2)}) collective-permute-start(f32[8,320]{1,0:T(8,128)S(1)} %get-tuple-element.35), channel_id=1, source_target_pairs={{0,1},{1,2},{2,3},{3,4},{4,5},{5,6},{6,7},{7,0},{8,9},{9,10},{10,1... | collective-permute-start | bytes 30728 | tf_op jit(solution)/shard_map/ppermute | solution.py:440
  31.6 3.0 %collective-permute-start.3 = (f32[8,320]{1,0:T(8,128)S(1)}, f32[8,320]{1,0:T(8,128)S(1)}, u32[]{:S(2)}, u32[]{:S(2)}) collective-permute-start(f32[8,320]{1,0:T(8,128)S(1)} %get-tuple-element.36), channel_id=1, source_target_pairs={{1,0},{2,1},{3,2},{4,3},{5,4},{6,5},{7,6},{0,7},{9,8},{10,9},{11,1... | collective-permute-start | bytes 30728 | tf_op jit(solution)/shard_map/ppermute | solution.py:440
  34.6 6.1 %shard_map.107.local_ref = f32[320,512]{1,0:T(8,128)S(1)} custom-call(f32[320,512]{1,0:T(8,128)S(1)} %get-tuple-element.33.x_ref, s32[6,512]{1,0:T(8,128)} %bitcast.16, bf16[6,5,320,512]{3,2,1,0:T(8,128)(2,1)} %bitcast.8, f32[320,512]{1,0:T(8,128)} %bitcast.12), custom_call_target="tpu_custom_call" | custom-call | flops 1006632960 | bytes 12451840 | tf_op jit(solution)/shard_map/pallas_call | solution.py:450
  40.8 0.2 collective-permute-done.2.lower_ref
  41.0 0.0 collective-permute-done.3.upper_ref
  41.0 1.2 %all-to-all-done.1.inc_ref = f32[32,5,4,128]{3,2,1,0:T(4,128)S(1)} async-done(((f32[32,5,4,128]{3,2,1,0:T(4,128)}), f32[32,5,4,128]{3,2,1,0:T(4,128)S(1)}, u32[]{:S(2)}, u32[]{:S(2)}) %all-to-all-start.1) | async-done | bytes 327712 | tf_op jit(solution)/shard_map/all_to_all | solution.py:439
  42.2 1.3 %shard_map.108 = (f32[320,512]{1,0:T(8,128)S(1)}, f32[32,2,128]{2,1,0:T(2,128)}) custom-call(f32[320,512]{1,0:T(8,128)S(1)} %shard_map.107.local_ref, f32[32,5,4,128]{3,2,1,0:T(4,128)S(1)} %all-to-all-done.1.inc_ref, f32[8,320]{1,0:T(8,128)S(1)} %collective-permute-done.2.lower_ref, f32[8,320]{1,0:T(8,128)S(1)} %collective-permute-done.3.upper_ref, ...), custom_call_target="tpu_custom_call" | custom-call | flops 167772160 | bytes 1966080 | tf_op jit(solution)/shard_map/pallas_call | solution.py:451
  43.5 2.6 %all-to-all-start.2 = ((f32[32,2,128]{2,1,0:T(2,128)}), f32[32,2,128]{2,1,0:T(2,128)S(1)}, u32[]{:S(2)}, u32[]{:S(2)}) async-start(f32[32,2,128]{2,1,0:T(2,128)} %get-tuple-element.38), calls=%async_computation.2 | async-start | bytes 65536 | tf_op jit(solution)/shard_map/all_to_all | solution.py:452
  46.1 2.6 %shard_map.109 = (f32[320,512]{1,0:T(8,128)S(1)}, f32[320,512]{1,0:T(8,128)}) custom-call(bf16[5,320,512]{2,1,0:T(8,128)(2,1)} %bitcast.10, f32[320,512]{1,0:T(8,128)S(1)} %get-tuple-element.39.resid_ref), custom_call_target="tpu_custom_call" | custom-call | flops 1638400 | bytes 2949120 | tf_op jit(solution)/shard_map/pallas_call | solution.py:453
  48.8 4.5 %all-to-all-done.2.sums_ref = f32[32,2,128]{2,1,0:T(2,128)S(1)} async-done(((f32[32,2,128]{2,1,0:T(2,128)}), f32[32,2,128]{2,1,0:T(2,128)S(1)}, u32[]{:S(2)}, u32[]{:S(2)}) %all-to-all-start.2) | async-done | bytes 32800 | tf_op jit(solution)/shard_map/all_to_all | solution.py:452
  53.3 1.1 %shard_map.110 = f32[320,512]{1,0:T(8,128)} custom-call(f32[32,2,128]{2,1,0:T(2,128)S(1)} %all-to-all-done.2.sums_ref, f32[320,512]{1,0:T(8,128)S(1)} %get-tuple-element.33.x_ref, f32[320,512]{1,0:T(8,128)S(1)} %get-tuple-element.40.update_ref), custom_call_target="tpu_custom_call" | custom-call | flops 327680 | bytes 1966080 | tf_op jit(solution)/shard_map/pallas_call | solution.py:454
Async XLA Ops:
  3.0 20.3 %all-to-all-start = ((f32[32,5,4,128]{3,2,1,0:T(4,128)}), f32[32,5,4,128]{3,2,1,0:T(4,128)S(1)}, u32[]{:S(2)}, u32[]{:S(2)}) async-start(f32[32,5,4,128]{3,2,1,0:T(4,128)} %get-tuple-element.24), calls=%async_computation | async-start | bytes 655360 | tf_op jit(solution)/shard_map/all_to_all | solution.py:439
  10.4 12.9 %collective-permute-start = (f32[8,320]{1,0:T(8,128)S(1)}, f32[8,320]{1,0:T(8,128)S(1)}, u32[]{:S(2)}, u32[]{:S(2)}) collective-permute-start(f32[8,320]{1,0:T(8,128)S(1)} %get-tuple-element.25), channel_id=1, source_target_pairs={{0,1},{1,2},{2,3},{3,4},{4,5},{5,6},{6,7},{7,0},{8,9},{9,10},{10,1... | collective-permute-start | bytes 30728 | tf_op jit(solution)/shard_map/ppermute | solution.py:440
  12.2 11.1 %collective-permute-start.1 = (f32[8,320]{1,0:T(8,128)S(1)}, f32[8,320]{1,0:T(8,128)S(1)}, u32[]{:S(2)}, u32[]{:S(2)}) collective-permute-start(f32[8,320]{1,0:T(8,128)S(1)} %get-tuple-element.26), channel_id=1, source_target_pairs={{1,0},{2,1},{3,2},{4,3},{5,4},{6,5},{7,6},{0,7},{9,8},{10,9},{11,1... | collective-permute-start | bytes 30728 | tf_op jit(solution)/shard_map/ppermute | solution.py:440
  26.7 15.6 %all-to-all-start.1 = ((f32[32,5,4,128]{3,2,1,0:T(4,128)}), f32[32,5,4,128]{3,2,1,0:T(4,128)S(1)}, u32[]{:S(2)}, u32[]{:S(2)}) async-start(f32[32,5,4,128]{3,2,1,0:T(4,128)} %get-tuple-element.34), calls=%async_computation.1 | async-start | bytes 655360 | tf_op jit(solution)/shard_map/all_to_all | solution.py:439
  29.8 11.2 %collective-permute-start.2 = (f32[8,320]{1,0:T(8,128)S(1)}, f32[8,320]{1,0:T(8,128)S(1)}, u32[]{:S(2)}, u32[]{:S(2)}) collective-permute-start(f32[8,320]{1,0:T(8,128)S(1)} %get-tuple-element.35), channel_id=1, source_target_pairs={{0,1},{1,2},{2,3},{3,4},{4,5},{5,6},{6,7},{7,0},{8,9},{9,10},{10,1... | collective-permute-start | bytes 30728 | tf_op jit(solution)/shard_map/ppermute | solution.py:440
  31.6 9.3 %collective-permute-start.3 = (f32[8,320]{1,0:T(8,128)S(1)}, f32[8,320]{1,0:T(8,128)S(1)}, u32[]{:S(2)}, u32[]{:S(2)}) collective-permute-start(f32[8,320]{1,0:T(8,128)S(1)} %get-tuple-element.36), channel_id=1, source_target_pairs={{1,0},{2,1},{3,2},{4,3},{5,4},{6,5},{7,6},{0,7},{9,8},{10,9},{11,1... | collective-permute-start | bytes 30728 | tf_op jit(solution)/shard_map/ppermute | solution.py:440
  43.5 9.8 %all-to-all-start.2 = ((f32[32,2,128]{2,1,0:T(2,128)}), f32[32,2,128]{2,1,0:T(2,128)S(1)}, u32[]{:S(2)}, u32[]{:S(2)}) async-start(f32[32,2,128]{2,1,0:T(2,128)} %get-tuple-element.38), calls=%async_computation.2 | async-start | bytes 65536 | tf_op jit(solution)/shard_map/all_to_all | solution.py:452

commit v10 on v9

--- a/solution.py
+++ b/solution.py
@@ -72,8 +72,22 @@
 
 def donors_kernel(
     x_ref, src_ref, perm_ref,
-    out_ref, up_ref, down_ref, table_ref, select_ref, x_out, rows_ref, sem,
+    out_ref, up_ref, down_ref, table_ref, select_ref, x_out, rows_ref, sem, src, perm, sems,
 ):
+    small = [
+        pltpu.make_async_copy(src_ref, src, sems.at[VARS]),
+        pltpu.make_async_copy(perm_ref, perm, sems.at[VARS + 1]),
+    ]
+    large = []
+    for v in range(VARS):
+        span = pl.ds(v * CELLS, CELLS)
+        large.append(pltpu.make_async_copy(x_ref.at[span], x_out.at[span], sems.at[v]))
+    for copy in small:
+        copy.start()
+    for v in range(VARS):
+        large[v].start(priority=v % 2)
+    for copy in small:
+        copy.wait()
     rim = up_ref.shape[0]
     index = lax.axis_index("blk")
     at_last = index == lax.axis_size("blk") - 1
@@ -83,7 +97,7 @@
     wanted = lane[:1]
     target = sub[:, :1]
     for j in range(rim):
-        partner = perm_ref[0, j]
+        partner = perm[0, j]
         wanted = jnp.where((lane[:1] == j) & at_last, partner, wanted)
         target = jnp.where((sub[:, :1] == j) & at_first, partner, target)
     to_up = (sub == wanted + (LANES - rim)) & (lane < rim)
@@ -91,31 +105,36 @@
     select = onehot(to_up | to_down)
     select = jnp.concatenate([select, select], axis=0)
     rows = lax.broadcasted_iota(jnp.int32, table_ref.shape, 0)
-    table = onehot(rows == src_ref[...])
+    table = onehot(rows == src[...])
+    for copy in large:
+        copy.wait()
     copy = send_blocks(
-        x_ref[...], table, select, out_ref, up_ref, down_ref, rows_ref, sem
+        x_out[...], table, select, out_ref, up_ref, down_ref, rows_ref, sem
     )
     table_ref[...] = table
     select_ref[...] = select
-    x_out[...] = x_ref[...]
     copy.wait()
 
 
 def local_kernel(
     rim, x_ref, nbr_ref, coup_ref, source_ref, out_ref, terms, near, coup, source, sems, source_sem,
-    at_start=None, at_end=None,
+    at_start=None, with_ends=None,
 ):
     slots, blocks = nbr_ref.shape
     chunks = blocks // LANES
     spans = [slice(c * LANES, (c + 1) * LANES) for c in range(chunks)]
-    copies = [
-        pltpu.make_async_copy(coup_ref.at[:, :, :, spans[c]], coup.at[c], sems.at[c])
-        for c in range(chunks)
-    ]
-    for copy in copies:
-        copy.start()
+    order = [0, chunks - 1, *range(1, chunks - 1)]
     source_copy = pltpu.make_async_copy(source_ref, source, source_sem)
-    source_copy.start()
+    copies = {}
+    for c in order:
+        copies[c] = [
+            pltpu.make_async_copy(coup_ref.at[m, :, :, spans[c]], coup.at[c, m], sems.at[c, m])
+            for m in range(slots)
+        ]
+        for m in range(slots):
+            copies[c][m].start(priority=m % 2)
+        if c == order[0]:
+            source_copy.start()
     lane = lax.broadcasted_iota(jnp.int32, (BW, LANES), 1)
     moved = pltpu.roll(x_ref[...], rim, 1)
     head = jnp.where(lane < rim, 0.0, moved[:, :LANES])
@@ -134,19 +153,20 @@
         near[c][:, m * LANES : (m + 2) * LANES] = both[:BW] + both[BW:]
 
     for m in pairs:
-        gather(0, m)
+        gather(order[0], m)
     if at_start is not None:
         at_start()
-    for c in range(chunks):
-        copies[c].wait()
-        if c == 0:
+    for step, c in enumerate(order):
+        for copy in copies[c]:
+            copy.wait()
+        if step == 0:
             source_copy.wait()
-        ahead = list(pairs) if c + 1 < chunks else []
+        ahead = list(pairs) if step + 1 < chunks else []
         for at in range(0, CELLS, PACK):
             if ahead:
-                gather(c + 1, ahead.pop(0))
-            if at_end is not None and c + 1 == chunks:
-                at_end(at)
+                gather(order[step + 1], ahead.pop(0))
+            if with_ends is not None and step in (1, 2) and (at < CELLS // 2) == (step == 1):
+                with_ends(at)
             total = [None] * VARS
             for m in range(slots):
                 for v in range(VARS):
@@ -263,16 +283,23 @@
     diag_ref, x_ref, table_ref, select_ref,
     next_ref, norm_ref, out_ref, up_ref, down_ref, resid, diag, diag_sems, rows_ref, sem,
 ):
-    fetches = [
-        pltpu.make_async_copy(diag_ref.at[u], diag.at[u], diag_sems.at[u]) for u in range(VARS)
-    ]
-    for fetch in fetches:
-        fetch.start()
+    fetches = []
+    for u in range(VARS):
+        halves = [slice(0, BW // 2), slice(BW // 2, BW)]
+        fetches.append(
+            [
+                pltpu.make_async_copy(diag_ref.at[u, halves[i]], diag.at[u, halves[i]], diag_sems.at[u, i])
+                for i in range(2)
+            ]
+        )
+        for i in range(2):
+            fetches[u][i].start(priority=i)
     resid[...] = full_residual(
         local_ref, inc_ref, lower_ref, upper_ref, across_ref, weight_ref, rimcoup_ref, rimrow_ref
     )
     for u in range(VARS):
-        fetches[u].wait()
+        for fetch in fetches[u]:
+            fetch.wait()
         for at in range(0, CELLS, PACK):
             total = None
             for v in range(VARS):
@@ -319,7 +346,6 @@
 
 
 VMEM = pl.BlockSpec(memory_space=pltpu.VMEM)
-SMEM = pl.BlockSpec(memory_space=pltpu.SMEM)
 
 
 def f32(*shape):
@@ -369,12 +395,17 @@
 
     donors = call(
         donors_kernel,
-        [VMEM, VMEM, SMEM],
+        [hbm] * 3,
         sent + [bf16(blocks, fringe), bf16(2 * LANES, LANES), state],
         4 * BW * blocks * fringe,
         2 * size,
         out_specs=[hbm] + [VMEM] * 5,
-        scratch_shapes=rows_scratch,
+        scratch_shapes=rows_scratch
+        + [
+            pltpu.VMEM((1, fringe), jnp.int32),
+            pltpu.SMEM((1, rim), jnp.int32),
+            pltpu.SemaphoreType.DMA((VARS + 2,)),
+        ],
     )
     chunks = blocks // LANES
     scratch = [
@@ -382,7 +413,7 @@
         [pltpu.VMEM((BW, slots * LANES), jnp.float32)] * chunks,
         pltpu.VMEM((chunks, slots, VARS, BW, LANES), jnp.bfloat16),
         pltpu.VMEM((BW, blocks), jnp.float32),
-        pltpu.SemaphoreType.DMA((chunks,)),
+        pltpu.SemaphoreType.DMA((chunks, slots)),
         pltpu.SemaphoreType.DMA,
     ]
     local_more = dict(
@@ -413,7 +444,7 @@
         scratch_shapes=[
             pltpu.VMEM((BW, blocks), jnp.float32),
             pltpu.VMEM((VARS, BW, blocks), jnp.bfloat16),
-            pltpu.SemaphoreType.DMA((VARS,)),
+            pltpu.SemaphoreType.DMA((VARS, 2)),
         ]
         + rows_scratch,
     )

time: 54.9 us -> 55.8 us (1.016)
  Pallas kernels: 25.1 us -> 26.9 us
  waiting for transfers between devices: 6.02 us -> 4.56 us
    pallas_call x1, Pallas kernels: 6.15 us -> 7.69 us  [shards(): part = local(x, nbr, coup, source_t)]
    all_to_all x2, waiting for transfers between devices: 1.24 us -> 0.01 us  [exchange(): lax.all_to_all(rows, ('body', 'blk'), split_axis=0, concat_axis=0, tiled=...]
    all_to_all x1, starting transfers between devices: 2.57 us -> 3.14 us  [shards(): lax.all_to_all(sums, ('body', 'blk'), split_axis=0, concat_axis=0, tiled=...]
  transfers between devices with their start and end apart: 7 -> 7, of which waited for: 3 -> 1; matrix products, arithmetic and copies ran while one was open for 0% -> 0% of each run, Pallas kernels for 31% -> 33%
where the time goes in v10:
time: 55.8 us; the launch traced here: 55.3 us
  Pallas kernels  26.9 us (48%)
  starting transfers between devices  23.1 us (41%)
  waiting for transfers between devices  4.56 us (8%)
  between operations  0.74 us (1%)
    all_to_all x2, starting transfers between devices, exchange(): lax.all_to_all(rows, ('body', 'blk'), split_axis=0, concat_axis=0, tiled=...  10.4 us
    pallas_call x1, Pallas kernels, shards(): first_local(x_here, nbr, coup, source_t, here(fringe_dst), here(fringe_we...  7.99 us
    pallas_call x1, Pallas kernels, shards(): part = local(x, nbr, coup, source_t)  7.69 us
    ppermute x2, starting transfers between devices, exchange(): lax.ppermute(to_down, 'blk', down)  5.91 us
    all_to_all x1, waiting for transfers between devices, shards(): lax.all_to_all(sums, ('body', 'blk'), split_axis=0, concat_axis=0, tiled=...  4.55 us
    ppermute x2, starting transfers between devices, exchange(): lax.ppermute(to_up, 'blk', up)  3.64 us
    pallas_call x1, Pallas kernels, shards(): advance(part, *arrived, *across, diag, x_here, table, select)  3.58 us
    all_to_all x1, starting transfers between devices, shards(): lax.all_to_all(sums, ('body', 'blk'), split_axis=0, concat_axis=0, tiled=...  3.14 us
  transfers between devices with their start and end apart: 7, of which 1 were waited for; matrix products, arithmetic and copies ran while one was open for 0% of the time, Pallas kernels for 33%

profile of v10, /device:TPU:0, one launch (start us, length us, event | category | flops | bytes accessed | tf_op | source)
XLA Modules:
  0.0 55.3 jit_solution(3303093214448815000)
XLA Ops:
  0.6 2.6 %shard_map.104 = (f32[32,5,4,128]{3,2,1,0:T(4,128)}, f32[8,320]{1,0:T(8,128)S(1)}, f32[8,320]{1,0:T(8,128)S(1)}, bf16[512,256]{1,0:T(8,128)(2,1)S(1)}, bf16[256,...) custom-call(f32[320,512]{1,0:T(8,128)} %bitcast.13, s32[1,256]{1,0:T(1,128)} %src_ref.1, s32[1,8]{1,0:T(1,128)} %perm_ref.1), custom_call_target="tpu_custom_call" | custom-call | flops 167772160 | bytes 1310720 | tf_op jit(solution)/shard_map/pallas_call | solution.py:473
  3.2 7.3 %all-to-all-start = ((f32[32,5,4,128]{3,2,1,0:T(4,128)}), f32[32,5,4,128]{3,2,1,0:T(4,128)S(1)}, u32[]{:S(2)}, u32[]{:S(2)}) async-start(f32[32,5,4,128]{3,2,1,0:T(4,128)} %get-tuple-element.24), calls=%async_computation | async-start | bytes 655360 | tf_op jit(solution)/shard_map/all_to_all | solution.py:470
  10.5 1.8 %collective-permute-start = (f32[8,320]{1,0:T(8,128)S(1)}, f32[8,320]{1,0:T(8,128)S(1)}, u32[]{:S(2)}, u32[]{:S(2)}) collective-permute-start(f32[8,320]{1,0:T(8,128)S(1)} %get-tuple-element.25), channel_id=1, source_target_pairs={{0,1},{1,2},{2,3},{3,4},{4,5},{5,6},{6,7},{7,0},{8,9},{9,10},{10,1... | collective-permute-start | bytes 30728 | tf_op jit(solution)/shard_map/ppermute | solution.py:471
  12.3 3.0 %collective-permute-start.1 = (f32[8,320]{1,0:T(8,128)S(1)}, f32[8,320]{1,0:T(8,128)S(1)}, u32[]{:S(2)}, u32[]{:S(2)}) collective-permute-start(f32[8,320]{1,0:T(8,128)S(1)} %get-tuple-element.26), channel_id=1, source_target_pairs={{1,0},{2,1},{3,2},{4,3},{5,4},{6,5},{7,6},{0,7},{9,8},{10,9},{11,1... | collective-permute-start | bytes 30728 | tf_op jit(solution)/shard_map/ppermute | solution.py:471
  15.3 8.0 %shard_map.105 = (f32[320,512]{1,0:T(8,128)S(1)}, bf16[5,320,128]{2,1,0:T(8,128)(2,1)S(1)}, s32[16,128]{1,0:T(8,128)S(1)}, bf16[256,512]{1,0:T(8,128)(2,1)S(1)}, f32[1,256]{1,0:T(1,128)S(1)}) custom-call(f32[320,512]{1,0:T(8,128)S(1)} %get-tuple-element.22.x_ref, s32[6,512]{1,0:T(8,128)} %bitcast.15, bf16[6,5,320,512]{3,2,1,0:T(8,128)(2,1)} %bitcast.7, ...), custom_call_target="tpu_custom_call" | custom-call | flops 1006632960 | bytes 12451840 | tf_op jit(solution)/shard_map/pallas_call | solution.py:475
  23.3 0.0 collective-permute-done.lower_ref
  23.3 0.0 collective-permute-done.1.upper_ref
  23.3 0.0 all-to-all-done.inc_ref
  23.3 3.6 %shard_map.106 = (f32[320,512]{1,0:T(8,128)S(1)}, f32[1,128]{1,0:T(1,128)S(1)}, f32[32,5,4,128]{3,2,1,0:T(4,128)}, f32[8,320]{1,0:T(8,128)S(1)}, f32[8,320]{1,0:T(8,128)S(1)}) custom-call(f32[320,512]{1,0:T(8,128)S(1)} %get-tuple-element.23.local_ref, f32[32,5,4,128]{3,2,1,0:T(4,128)S(1)} %all-to-all-done.inc_ref, ...), custom_call_target="tpu_custom_call" | custom-call | flops 335544320 | bytes 4259840 | tf_op jit(solution)/shard_map/pallas_call | solution.py:479
  26.9 3.1 %all-to-all-start.1 = ((f32[32,5,4,128]{3,2,1,0:T(4,128)}), f32[32,5,4,128]{3,2,1,0:T(4,128)S(1)}, u32[]{:S(2)}, u32[]{:S(2)}) async-start(f32[32,5,4,128]{3,2,1,0:T(4,128)} %get-tuple-element.34), calls=%async_computation.1 | async-start | bytes 655360 | tf_op jit(solution)/shard_map/all_to_all | solution.py:470
  30.0 1.8 %collective-permute-start.2 = (f32[8,320]{1,0:T(8,128)S(1)}, f32[8,320]{1,0:T(8,128)S(1)}, u32[]{:S(2)}, u32[]{:S(2)}) collective-permute-start(f32[8,320]{1,0:T(8,128)S(1)} %get-tuple-element.35), channel_id=1, source_target_pairs={{0,1},{1,2},{2,3},{3,4},{4,5},{5,6},{6,7},{7,0},{8,9},{9,10},{10,1... | collective-permute-start | bytes 30728 | tf_op jit(solution)/shard_map/ppermute | solution.py:471
  31.9 3.0 %collective-permute-start.3 = (f32[8,320]{1,0:T(8,128)S(1)}, f32[8,320]{1,0:T(8,128)S(1)}, u32[]{:S(2)}, u32[]{:S(2)}) collective-permute-start(f32[8,320]{1,0:T(8,128)S(1)} %get-tuple-element.36), channel_id=1, source_target_pairs={{1,0},{2,1},{3,2},{4,3},{5,4},{6,5},{7,6},{0,7},{9,8},{10,9},{11,1... | collective-permute-start | bytes 30728 | tf_op jit(solution)/shard_map/ppermute | solution.py:471
  34.8 7.7 %shard_map.107.local_ref = f32[320,512]{1,0:T(8,128)S(1)} custom-call(f32[320,512]{1,0:T(8,128)S(1)} %get-tuple-element.33.x_ref, s32[6,512]{1,0:T(8,128)} %bitcast.16, bf16[6,5,320,512]{3,2,1,0:T(8,128)(2,1)} %bitcast.8, f32[320,512]{1,0:T(8,128)} %bitcast.12), custom_call_target="tpu_custom_call" | custom-call | flops 1006632960 | bytes 12451840 | tf_op jit(solution)/shard_map/pallas_call | solution.py:481
  42.5 0.0 collective-permute-done.2.lower_ref
  42.5 0.0 collective-permute-done.3.upper_ref
  42.5 0.0 all-to-all-done.1.inc_ref
  42.5 1.3 %shard_map.108 = (f32[320,512]{1,0:T(8,128)S(1)}, f32[32,2,128]{2,1,0:T(2,128)}) custom-call(f32[320,512]{1,0:T(8,128)S(1)} %shard_map.107.local_ref, f32[32,5,4,128]{3,2,1,0:T(4,128)S(1)} %all-to-all-done.1.inc_ref, f32[8,320]{1,0:T(8,128)S(1)} %collective-permute-done.2.lower_ref, f32[8,320]{1,0:T(8,128)S(1)} %collective-permute-done.3.upper_ref, ...), custom_call_target="tpu_custom_call" | custom-call | flops 167772160 | bytes 1966080 | tf_op jit(solution)/shard_map/pallas_call | solution.py:482
  43.9 3.1 %all-to-all-start.2 = ((f32[32,2,128]{2,1,0:T(2,128)}), f32[32,2,128]{2,1,0:T(2,128)S(1)}, u32[]{:S(2)}, u32[]{:S(2)}) async-start(f32[32,2,128]{2,1,0:T(2,128)} %get-tuple-element.38), calls=%async_computation.2 | async-start | bytes 65536 | tf_op jit(solution)/shard_map/all_to_all | solution.py:483
  47.0 2.6 %shard_map.109 = (f32[320,512]{1,0:T(8,128)S(1)}, f32[320,512]{1,0:T(8,128)}) custom-call(bf16[5,320,512]{2,1,0:T(8,128)(2,1)} %bitcast.10, f32[320,512]{1,0:T(8,128)S(1)} %get-tuple-element.39.resid_ref), custom_call_target="tpu_custom_call" | custom-call | flops 1638400 | bytes 2949120 | tf_op jit(solution)/shard_map/pallas_call | solution.py:484
  49.6 4.5 %all-to-all-done.2.sums_ref = f32[32,2,128]{2,1,0:T(2,128)S(1)} async-done(((f32[32,2,128]{2,1,0:T(2,128)}), f32[32,2,128]{2,1,0:T(2,128)S(1)}, u32[]{:S(2)}, u32[]{:S(2)}) %all-to-all-start.2) | async-done | bytes 32800 | tf_op jit(solution)/shard_map/all_to_all | solution.py:483
  54.2 1.1 %shard_map.110 = f32[320,512]{1,0:T(8,128)} custom-call(f32[32,2,128]{2,1,0:T(2,128)S(1)} %all-to-all-done.2.sums_ref, f32[320,512]{1,0:T(8,128)S(1)} %get-tuple-element.33.x_ref, f32[320,512]{1,0:T(8,128)S(1)} %get-tuple-element.40.update_ref), custom_call_target="tpu_custom_call" | custom-call | flops 327680 | bytes 1966080 | tf_op jit(solution)/shard_map/pallas_call | solution.py:485
Async XLA Ops:
  3.2 20.1 %all-to-all-start = ((f32[32,5,4,128]{3,2,1,0:T(4,128)}), f32[32,5,4,128]{3,2,1,0:T(4,128)S(1)}, u32[]{:S(2)}, u32[]{:S(2)}) async-start(f32[32,5,4,128]{3,2,1,0:T(4,128)} %get-tuple-element.24), calls=%async_computation | async-start | bytes 655360 | tf_op jit(solution)/shard_map/all_to_all | solution.py:470
  10.5 12.8 %collective-permute-start = (f32[8,320]{1,0:T(8,128)S(1)}, f32[8,320]{1,0:T(8,128)S(1)}, u32[]{:S(2)}, u32[]{:S(2)}) collective-permute-start(f32[8,320]{1,0:T(8,128)S(1)} %get-tuple-element.25), channel_id=1, source_target_pairs={{0,1},{1,2},{2,3},{3,4},{4,5},{5,6},{6,7},{7,0},{8,9},{9,10},{10,1... | collective-permute-start | bytes 30728 | tf_op jit(solution)/shard_map/ppermute | solution.py:471
  12.3 11.0 %collective-permute-start.1 = (f32[8,320]{1,0:T(8,128)S(1)}, f32[8,320]{1,0:T(8,128)S(1)}, u32[]{:S(2)}, u32[]{:S(2)}) collective-permute-start(f32[8,320]{1,0:T(8,128)S(1)} %get-tuple-element.26), channel_id=1, source_target_pairs={{1,0},{2,1},{3,2},{4,3},{5,4},{6,5},{7,6},{0,7},{9,8},{10,9},{11,1... | collective-permute-start | bytes 30728 | tf_op jit(solution)/shard_map/ppermute | solution.py:471
  26.9 15.6 %all-to-all-start.1 = ((f32[32,5,4,128]{3,2,1,0:T(4,128)}), f32[32,5,4,128]{3,2,1,0:T(4,128)S(1)}, u32[]{:S(2)}, u32[]{:S(2)}) async-start(f32[32,5,4,128]{3,2,1,0:T(4,128)} %get-tuple-element.34), calls=%async_computation.1 | async-start | bytes 655360 | tf_op jit(solution)/shard_map/all_to_all | solution.py:470
  30.0 12.5 %collective-permute-start.2 = (f32[8,320]{1,0:T(8,128)S(1)}, f32[8,320]{1,0:T(8,128)S(1)}, u32[]{:S(2)}, u32[]{:S(2)}) collective-permute-start(f32[8,320]{1,0:T(8,128)S(1)} %get-tuple-element.35), channel_id=1, source_target_pairs={{0,1},{1,2},{2,3},{3,4},{4,5},{5,6},{6,7},{7,0},{8,9},{9,10},{10,1... | collective-permute-start | bytes 30728 | tf_op jit(solution)/shard_map/ppermute | solution.py:471
  31.9 10.7 %collective-permute-start.3 = (f32[8,320]{1,0:T(8,128)S(1)}, f32[8,320]{1,0:T(8,128)S(1)}, u32[]{:S(2)}, u32[]{:S(2)}) collective-permute-start(f32[8,320]{1,0:T(8,128)S(1)} %get-tuple-element.36), channel_id=1, source_target_pairs={{1,0},{2,1},{3,2},{4,3},{5,4},{6,5},{7,6},{0,7},{9,8},{10,9},{11,1... | collective-permute-start | bytes 30728 | tf_op jit(solution)/shard_map/ppermute | solution.py:471
  43.9 10.3 %all-to-all-start.2 = ((f32[32,2,128]{2,1,0:T(2,128)}), f32[32,2,128]{2,1,0:T(2,128)S(1)}, u32[]{:S(2)}, u32[]{:S(2)}) async-start(f32[32,2,128]{2,1,0:T(2,128)} %get-tuple-element.38), calls=%async_computation.2 | async-start | bytes 65536 | tf_op jit(solution)/shard_map/all_to_all | solution.py:483

commit v11 on v9

--- a/solution.py
+++ b/solution.py
@@ -103,19 +103,19 @@
 
 def local_kernel(
     rim, x_ref, nbr_ref, coup_ref, source_ref, out_ref, terms, near, coup, source, sems, source_sem,
-    at_start=None, at_end=None,
+    at_start=None, with_ends=None,
 ):
     slots, blocks = nbr_ref.shape
     chunks = blocks // LANES
     spans = [slice(c * LANES, (c + 1) * LANES) for c in range(chunks)]
-    copies = [
-        pltpu.make_async_copy(coup_ref.at[:, :, :, spans[c]], coup.at[c], sems.at[c])
-        for c in range(chunks)
-    ]
-    for copy in copies:
-        copy.start()
+    order = [0, chunks - 1, *range(1, chunks - 1)]
     source_copy = pltpu.make_async_copy(source_ref, source, source_sem)
-    source_copy.start()
+    copies = {}
+    for c in order:
+        copies[c] = pltpu.make_async_copy(coup_ref.at[:, :, :, spans[c]], coup.at[c], sems.at[c])
+        copies[c].start()
+        if c == order[0]:
+            source_copy.start()
     lane = lax.broadcasted_iota(jnp.int32, (BW, LANES), 1)
     moved = pltpu.roll(x_ref[...], rim, 1)
     head = jnp.where(lane < rim, 0.0, moved[:, :LANES])
@@ -134,19 +134,19 @@
         near[c][:, m * LANES : (m + 2) * LANES] = both[:BW] + both[BW:]
 
     for m in pairs:
-        gather(0, m)
+        gather(order[0], m)
     if at_start is not None:
         at_start()
-    for c in range(chunks):
+    for step, c in enumerate(order):
         copies[c].wait()
-        if c == 0:
+        if step == 0:
             source_copy.wait()
-        ahead = list(pairs) if c + 1 < chunks else []
+        ahead = list(pairs) if step + 1 < chunks else []
         for at in range(0, CELLS, PACK):
             if ahead:
-                gather(c + 1, ahead.pop(0))
-            if at_end is not None and c + 1 == chunks:
-                at_end(at)
+                gather(order[step + 1], ahead.pop(0))
+            if with_ends is not None and step in (1, 2) and (at < CELLS // 2) == (step == 1):
+                with_ends(at)
             total = [None] * VARS
             for m in range(slots):
                 for v in range(VARS):
@@ -261,18 +261,15 @@
 def advance_kernel(
     local_ref, inc_ref, lower_ref, upper_ref, across_ref, weight_ref, rimcoup_ref, rimrow_ref,
     diag_ref, x_ref, table_ref, select_ref,
-    next_ref, norm_ref, out_ref, up_ref, down_ref, resid, diag, diag_sems, rows_ref, sem,
-):
-    fetches = [
-        pltpu.make_async_copy(diag_ref.at[u], diag.at[u], diag_sems.at[u]) for u in range(VARS)
-    ]
-    for fetch in fetches:
-        fetch.start()
+    next_ref, norm_ref, out_ref, up_ref, down_ref, resid, diag, diag_sem, rows_ref, sem,
+):
+    fetch = pltpu.make_async_copy(diag_ref, diag, diag_sem)
+    fetch.start()
     resid[...] = full_residual(
         local_ref, inc_ref, lower_ref, upper_ref, across_ref, weight_ref, rimcoup_ref, rimrow_ref
     )
+    fetch.wait()
     for u in range(VARS):
-        fetches[u].wait()
         for at in range(0, CELLS, PACK):
             total = None
             for v in range(VARS):
@@ -413,7 +410,7 @@
         scratch_shapes=[
             pltpu.VMEM((BW, blocks), jnp.float32),
             pltpu.VMEM((VARS, BW, blocks), jnp.bfloat16),
-            pltpu.SemaphoreType.DMA((VARS,)),
+            pltpu.SemaphoreType.DMA,
         ]
         + rows_scratch,
     )

time: 54.9 us -> 53.6 us (0.976)
  Pallas kernels: 25.1 us -> 23.1 us
  waiting for transfers between devices: 6.02 us -> 7.38 us
  starting transfers between devices: 22.6 us -> 22 us
    pallas_call x1, Pallas kernels: 8.16 us -> 6.26 us  [shards(): first_local(x_here, nbr, coup, source_t, here(fringe_dst), here(fringe_we...]
    all_to_all x2, waiting for transfers between devices: 1.24 us -> 2.47 us  [exchange(): lax.all_to_all(rows, ('body', 'blk'), split_axis=0, concat_axis=0, tiled=...]
  transfers between devices with their start and end apart: 7 -> 7, of which waited for: 3 -> 5; matrix products, arithmetic and copies ran while one was open for 0% -> 0% of each run, Pallas kernels for 31% -> 28%
where the time goes in v11:
time: 53.6 us; the launch traced here: 53.2 us
  Pallas kernels  23.1 us (43%)
  starting transfers between devices  22 us (41%)
  waiting for transfers between devices  7.38 us (14%)
  between operations  0.69 us (1%)
    all_to_all x2, starting transfers between devices, exchange(): lax.all_to_all(rows, ('body', 'blk'), split_axis=0, concat_axis=0, tiled=...  9.91 us
    pallas_call x1, Pallas kernels, shards(): first_local(x_here, nbr, coup, source_t, here(fringe_dst), here(fringe_we...  6.26 us
    pallas_call x1, Pallas kernels, shards(): part = local(x, nbr, coup, source_t)  6.15 us
    ppermute x2, starting transfers between devices, exchange(): lax.ppermute(to_down, 'blk', down)  6.04 us
    all_to_all x1, waiting for transfers between devices, shards(): lax.all_to_all(sums, ('body', 'blk'), split_axis=0, concat_axis=0, tiled=...  4.55 us
    ppermute x2, starting transfers between devices, exchange(): lax.ppermute(to_up, 'blk', up)  3.51 us
    pallas_call x1, Pallas kernels, shards(): advance(part, *arrived, *across, diag, x_here, table, select)  3.23 us
    pallas_call x1, Pallas kernels, shards(): update, resid = direction(diag, resid)  2.64 us
  transfers between devices with their start and end apart: 7, of which 5 were waited for; matrix products, arithmetic and copies ran while one was open for 0% of the time, Pallas kernels for 28%

profile of v11, /device:TPU:0, one launch (start us, length us, event | category | flops | bytes accessed | tf_op | source)
XLA Modules:
  0.0 53.2 jit_solution(18277855048920222045)
XLA Ops:
  0.6 2.4 %shard_map.104 = (f32[32,5,4,128]{3,2,1,0:T(4,128)}, f32[8,320]{1,0:T(8,128)S(1)}, f32[8,320]{1,0:T(8,128)S(1)}, bf16[512,256]{1,0:T(8,128)(2,1)S(1)}, bf16[256,...) custom-call(f32[320,512]{1,0:T(8,128)} %bitcast.13, s32[1,256]{1,0:T(1,128)} %src_ref.1, s32[1,8]{1,0:T(1,128)} %perm_ref.1), custom_call_target="tpu_custom_call" | custom-call | flops 167772160 | bytes 1310720 | tf_op jit(solution)/shard_map/pallas_call | solution.py:439
  3.0 7.3 %all-to-all-start = ((f32[32,5,4,128]{3,2,1,0:T(4,128)}), f32[32,5,4,128]{3,2,1,0:T(4,128)S(1)}, u32[]{:S(2)}, u32[]{:S(2)}) async-start(f32[32,5,4,128]{3,2,1,0:T(4,128)} %get-tuple-element.24), calls=%async_computation | async-start | bytes 655360 | tf_op jit(solution)/shard_map/all_to_all | solution.py:436
  10.4 1.8 %collective-permute-start = (f32[8,320]{1,0:T(8,128)S(1)}, f32[8,320]{1,0:T(8,128)S(1)}, u32[]{:S(2)}, u32[]{:S(2)}) collective-permute-start(f32[8,320]{1,0:T(8,128)S(1)} %get-tuple-element.25), channel_id=1, source_target_pairs={{0,1},{1,2},{2,3},{3,4},{4,5},{5,6},{6,7},{7,0},{8,9},{9,10},{10,1... | collective-permute-start | bytes 30728 | tf_op jit(solution)/shard_map/ppermute | solution.py:437
  12.2 3.0 %collective-permute-start.1 = (f32[8,320]{1,0:T(8,128)S(1)}, f32[8,320]{1,0:T(8,128)S(1)}, u32[]{:S(2)}, u32[]{:S(2)}) collective-permute-start(f32[8,320]{1,0:T(8,128)S(1)} %get-tuple-element.26), channel_id=1, source_target_pairs={{1,0},{2,1},{3,2},{4,3},{5,4},{6,5},{7,6},{0,7},{9,8},{10,9},{11,1... | collective-permute-start | bytes 30728 | tf_op jit(solution)/shard_map/ppermute | solution.py:437
  15.1 6.3 %shard_map.105 = (f32[320,512]{1,0:T(8,128)S(1)}, bf16[5,320,128]{2,1,0:T(8,128)(2,1)S(1)}, s32[16,128]{1,0:T(8,128)S(1)}, bf16[256,512]{1,0:T(8,128)(2,1)S(1)}, f32[1,256]{1,0:T(1,128)S(1)}) custom-call(f32[320,512]{1,0:T(8,128)S(1)} %get-tuple-element.22.x_ref, s32[6,512]{1,0:T(8,128)} %bitcast.15, bf16[6,5,320,512]{3,2,1,0:T(8,128)(2,1)} %bitcast.7, ...), custom_call_target="tpu_custom_call" | custom-call | flops 1006632960 | bytes 12451840 | tf_op jit(solution)/shard_map/pallas_call | solution.py:441
  21.4 0.1 collective-permute-done.lower_ref
  21.5 0.0 collective-permute-done.1.upper_ref
  21.5 1.2 %all-to-all-done.inc_ref = f32[32,5,4,128]{3,2,1,0:T(4,128)S(1)} async-done(((f32[32,5,4,128]{3,2,1,0:T(4,128)}), f32[32,5,4,128]{3,2,1,0:T(4,128)S(1)}, u32[]{:S(2)}, u32[]{:S(2)}) %all-to-all-start) | async-done | bytes 327712 | tf_op jit(solution)/shard_map/all_to_all | solution.py:436
  22.8 3.2 %shard_map.106 = (f32[320,512]{1,0:T(8,128)S(1)}, f32[1,128]{1,0:T(1,128)S(1)}, f32[32,5,4,128]{3,2,1,0:T(4,128)}, f32[8,320]{1,0:T(8,128)S(1)}, f32[8,320]{1,0:T(8,128)S(1)}) custom-call(f32[320,512]{1,0:T(8,128)S(1)} %get-tuple-element.23.local_ref, f32[32,5,4,128]{3,2,1,0:T(4,128)S(1)} %all-to-all-done.inc_ref, ...), custom_call_target="tpu_custom_call" | custom-call | flops 335544320 | bytes 4259840 | tf_op jit(solution)/shard_map/pallas_call | solution.py:445
  26.0 2.6 %all-to-all-start.1 = ((f32[32,5,4,128]{3,2,1,0:T(4,128)}), f32[32,5,4,128]{3,2,1,0:T(4,128)S(1)}, u32[]{:S(2)}, u32[]{:S(2)}) async-start(f32[32,5,4,128]{3,2,1,0:T(4,128)} %get-tuple-element.34), calls=%async_computation.1 | async-start | bytes 655360 | tf_op jit(solution)/shard_map/all_to_all | solution.py:436
  28.6 1.7 %collective-permute-start.2 = (f32[8,320]{1,0:T(8,128)S(1)}, f32[8,320]{1,0:T(8,128)S(1)}, u32[]{:S(2)}, u32[]{:S(2)}) collective-permute-start(f32[8,320]{1,0:T(8,128)S(1)} %get-tuple-element.35), channel_id=1, source_target_pairs={{0,1},{1,2},{2,3},{3,4},{4,5},{5,6},{6,7},{7,0},{8,9},{9,10},{10,1... | collective-permute-start | bytes 30728 | tf_op jit(solution)/shard_map/ppermute | solution.py:437
  30.3 3.1 %collective-permute-start.3 = (f32[8,320]{1,0:T(8,128)S(1)}, f32[8,320]{1,0:T(8,128)S(1)}, u32[]{:S(2)}, u32[]{:S(2)}) collective-permute-start(f32[8,320]{1,0:T(8,128)S(1)} %get-tuple-element.36), channel_id=1, source_target_pairs={{1,0},{2,1},{3,2},{4,3},{5,4},{6,5},{7,6},{0,7},{9,8},{10,9},{11,1... | collective-permute-start | bytes 30728 | tf_op jit(solution)/shard_map/ppermute | solution.py:437
  33.4 6.1 %shard_map.107.local_ref = f32[320,512]{1,0:T(8,128)S(1)} custom-call(f32[320,512]{1,0:T(8,128)S(1)} %get-tuple-element.33.x_ref, s32[6,512]{1,0:T(8,128)} %bitcast.16, bf16[6,5,320,512]{3,2,1,0:T(8,128)(2,1)} %bitcast.8, f32[320,512]{1,0:T(8,128)} %bitcast.12), custom_call_target="tpu_custom_call" | custom-call | flops 1006632960 | bytes 12451840 | tf_op jit(solution)/shard_map/pallas_call | solution.py:447
  39.5 0.2 collective-permute-done.2.lower_ref
  39.8 0.0 collective-permute-done.3.upper_ref
  39.8 1.2 %all-to-all-done.1.inc_ref = f32[32,5,4,128]{3,2,1,0:T(4,128)S(1)} async-done(((f32[32,5,4,128]{3,2,1,0:T(4,128)}), f32[32,5,4,128]{3,2,1,0:T(4,128)S(1)}, u32[]{:S(2)}, u32[]{:S(2)}) %all-to-all-start.1) | async-done | bytes 327712 | tf_op jit(solution)/shard_map/all_to_all | solution.py:436
  41.0 1.3 %shard_map.108 = (f32[320,512]{1,0:T(8,128)S(1)}, f32[32,2,128]{2,1,0:T(2,128)}) custom-call(f32[320,512]{1,0:T(8,128)S(1)} %shard_map.107.local_ref, f32[32,5,4,128]{3,2,1,0:T(4,128)S(1)} %all-to-all-done.1.inc_ref, f32[8,320]{1,0:T(8,128)S(1)} %collective-permute-done.2.lower_ref, f32[8,320]{1,0:T(8,128)S(1)} %collective-permute-done.3.upper_ref, ...), custom_call_target="tpu_custom_call" | custom-call | flops 167772160 | bytes 1966080 | tf_op jit(solution)/shard_map/pallas_call | solution.py:448
  42.3 2.6 %all-to-all-start.2 = ((f32[32,2,128]{2,1,0:T(2,128)}), f32[32,2,128]{2,1,0:T(2,128)S(1)}, u32[]{:S(2)}, u32[]{:S(2)}) async-start(f32[32,2,128]{2,1,0:T(2,128)} %get-tuple-element.38), calls=%async_computation.2 | async-start | bytes 65536 | tf_op jit(solution)/shard_map/all_to_all | solution.py:449
  44.9 2.6 %shard_map.109 = (f32[320,512]{1,0:T(8,128)S(1)}, f32[320,512]{1,0:T(8,128)}) custom-call(bf16[5,320,512]{2,1,0:T(8,128)(2,1)} %bitcast.10, f32[320,512]{1,0:T(8,128)S(1)} %get-tuple-element.39.resid_ref), custom_call_target="tpu_custom_call" | custom-call | flops 1638400 | bytes 2949120 | tf_op jit(solution)/shard_map/pallas_call | solution.py:450
  47.5 4.5 %all-to-all-done.2.sums_ref = f32[32,2,128]{2,1,0:T(2,128)S(1)} async-done(((f32[32,2,128]{2,1,0:T(2,128)}), f32[32,2,128]{2,1,0:T(2,128)S(1)}, u32[]{:S(2)}, u32[]{:S(2)}) %all-to-all-start.2) | async-done | bytes 32800 | tf_op jit(solution)/shard_map/all_to_all | solution.py:449
  52.1 1.1 %shard_map.110 = f32[320,512]{1,0:T(8,128)} custom-call(f32[32,2,128]{2,1,0:T(2,128)S(1)} %all-to-all-done.2.sums_ref, f32[320,512]{1,0:T(8,128)S(1)} %get-tuple-element.33.x_ref, f32[320,512]{1,0:T(8,128)S(1)} %get-tuple-element.40.update_ref), custom_call_target="tpu_custom_call" | custom-call | flops 327680 | bytes 1966080 | tf_op jit(solution)/shard_map/pallas_call | solution.py:451
Async XLA Ops:
  3.0 19.7 %all-to-all-start = ((f32[32,5,4,128]{3,2,1,0:T(4,128)}), f32[32,5,4,128]{3,2,1,0:T(4,128)S(1)}, u32[]{:S(2)}, u32[]{:S(2)}) async-start(f32[32,5,4,128]{3,2,1,0:T(4,128)} %get-tuple-element.24), calls=%async_computation | async-start | bytes 655360 | tf_op jit(solution)/shard_map/all_to_all | solution.py:436
  10.4 11.2 %collective-permute-start = (f32[8,320]{1,0:T(8,128)S(1)}, f32[8,320]{1,0:T(8,128)S(1)}, u32[]{:S(2)}, u32[]{:S(2)}) collective-permute-start(f32[8,320]{1,0:T(8,128)S(1)} %get-tuple-element.25), channel_id=1, source_target_pairs={{0,1},{1,2},{2,3},{3,4},{4,5},{5,6},{6,7},{7,0},{8,9},{9,10},{10,1... | collective-permute-start | bytes 30728 | tf_op jit(solution)/shard_map/ppermute | solution.py:437
  12.2 9.3 %collective-permute-start.1 = (f32[8,320]{1,0:T(8,128)S(1)}, f32[8,320]{1,0:T(8,128)S(1)}, u32[]{:S(2)}, u32[]{:S(2)}) collective-permute-start(f32[8,320]{1,0:T(8,128)S(1)} %get-tuple-element.26), channel_id=1, source_target_pairs={{1,0},{2,1},{3,2},{4,3},{5,4},{6,5},{7,6},{0,7},{9,8},{10,9},{11,1... | collective-permute-start | bytes 30728 | tf_op jit(solution)/shard_map/ppermute | solution.py:437
  26.0 15.0 %all-to-all-start.1 = ((f32[32,5,4,128]{3,2,1,0:T(4,128)}), f32[32,5,4,128]{3,2,1,0:T(4,128)S(1)}, u32[]{:S(2)}, u32[]{:S(2)}) async-start(f32[32,5,4,128]{3,2,1,0:T(4,128)} %get-tuple-element.34), calls=%async_computation.1 | async-start | bytes 655360 | tf_op jit(solution)/shard_map/all_to_all | solution.py:436
  28.6 11.2 %collective-permute-start.2 = (f32[8,320]{1,0:T(8,128)S(1)}, f32[8,320]{1,0:T(8,128)S(1)}, u32[]{:S(2)}, u32[]{:S(2)}) collective-permute-start(f32[8,320]{1,0:T(8,128)S(1)} %get-tuple-element.35), channel_id=1, source_target_pairs={{0,1},{1,2},{2,3},{3,4},{4,5},{5,6},{6,7},{7,0},{8,9},{9,10},{10,1... | collective-permute-start | bytes 30728 | tf_op jit(solution)/shard_map/ppermute | solution.py:437
  30.3 9.5 %collective-permute-start.3 = (f32[8,320]{1,0:T(8,128)S(1)}, f32[8,320]{1,0:T(8,128)S(1)}, u32[]{:S(2)}, u32[]{:S(2)}) collective-permute-start(f32[8,320]{1,0:T(8,128)S(1)} %get-tuple-element.36), channel_id=1, source_target_pairs={{1,0},{2,1},{3,2},{4,3},{5,4},{6,5},{7,6},{0,7},{9,8},{10,9},{11,1... | collective-permute-start | bytes 30728 | tf_op jit(solution)/shard_map/ppermute | solution.py:437
  42.3 9.8 %all-to-all-start.2 = ((f32[32,2,128]{2,1,0:T(2,128)}), f32[32,2,128]{2,1,0:T(2,128)S(1)}, u32[]{:S(2)}, u32[]{:S(2)}) async-start(f32[32,2,128]{2,1,0:T(2,128)} %get-tuple-element.38), calls=%async_computation.2 | async-start | bytes 65536 | tf_op jit(solution)/shard_map/all_to_all | solution.py:449

commit v12 on v11

--- a/solution.py
+++ b/solution.py
@@ -31,9 +31,10 @@
     return both[: x.shape[0]] + both[x.shape[0] :]
 
 
-def send_blocks(x, table, select, out_ref, up_ref, down_ref, rows_ref, sem):
+def send_blocks(x, src, select, out_ref, up_ref, down_ref, rows_ref, sem):
     rim = up_ref.shape[0]
     half = rows_ref.shape[2]
+    table = onehot(lax.broadcasted_iota(jnp.int32, (x.shape[1], src.shape[1]), 0) == src)
     rows = pick(x, table).T.reshape(rows_ref.shape[0], 2 * half, BW)
     for h in range(2):
         for tile in range(2):
@@ -72,7 +73,7 @@
 
 def donors_kernel(
     x_ref, src_ref, perm_ref,
-    out_ref, up_ref, down_ref, table_ref, select_ref, x_out, rows_ref, sem,
+    out_ref, up_ref, down_ref, src_out, select_ref, x_out, rows_ref, sem,
 ):
     rim = up_ref.shape[0]
     index = lax.axis_index("blk")
@@ -90,12 +91,10 @@
     to_down = (target + rim == lane) & (sub < rim)
     select = onehot(to_up | to_down)
     select = jnp.concatenate([select, select], axis=0)
-    rows = lax.broadcasted_iota(jnp.int32, table_ref.shape, 0)
-    table = onehot(rows == src_ref[...])
     copy = send_blocks(
-        x_ref[...], table, select, out_ref, up_ref, down_ref, rows_ref, sem
-    )
-    table_ref[...] = table
+        x_ref[...], src_ref[...], select, out_ref, up_ref, down_ref, rows_ref, sem
+    )
+    src_out[...] = src_ref[...]
     select_ref[...] = select
     x_out[...] = x_ref[...]
     copy.wait()
@@ -103,7 +102,7 @@
 
 def local_kernel(
     rim, x_ref, nbr_ref, coup_ref, source_ref, out_ref, terms, near, coup, source, sems, source_sem,
-    at_start=None, with_ends=None,
+    at_start=None, tables=None, with_ends=None, after_part=None, after_chunk=None,
 ):
     slots, blocks = nbr_ref.shape
     chunks = blocks // LANES
@@ -116,6 +115,8 @@
         copies[c].start()
         if c == order[0]:
             source_copy.start()
+            if at_start is not None:
+                at_start()
     lane = lax.broadcasted_iota(jnp.int32, (BW, LANES), 1)
     moved = pltpu.roll(x_ref[...], rim, 1)
     head = jnp.where(lane < rim, 0.0, moved[:, :LANES])
@@ -135,8 +136,8 @@
 
     for m in pairs:
         gather(order[0], m)
-    if at_start is not None:
-        at_start()
+    if tables is not None:
+        tables()
     for step, c in enumerate(order):
         copies[c].wait()
         if step == 0:
@@ -157,13 +158,18 @@
                         total[u] = term if total[u] is None else total[u] + term
             for u in range(VARS):
                 span = slice(u * CELLS + at, u * CELLS + at + PACK)
-                out_ref[span, spans[c]] = source[span, spans[c]] - x_ref[span, spans[c]] + total[u]
+                total[u] = source[span, spans[c]] - x_ref[span, spans[c]] + total[u]
+                out_ref[span, spans[c]] = total[u]
+            if after_part is not None:
+                after_part(at, spans[c], total)
+        if after_chunk is not None:
+            after_chunk(c, spans[c])
 
 
 def first_local_kernel(
-    rim, x_ref, nbr_ref, coup_ref, source_ref, dst_ref, weight_ref,
-    out_ref, rimcoup_ref, rimrow_ref, table_ref, weight_out,
-    terms, near, coup, source, sems, source_sem,
+    rim, x_ref, nbr_ref, coup_ref, source_ref, diag_ref, dst_ref, weight_ref,
+    base_ref, local_ref, rimcoup_ref, rimrow_ref, table_ref, weight_out, diag_out,
+    terms, near, coup, source, sems, source_sem, local, local_sems, diag_sem,
 ):
     slots, blocks = nbr_ref.shape
     chunks = blocks // LANES
@@ -202,15 +208,40 @@
                     jnp.zeros((PACK, LANES), jnp.bfloat16),
                 )
 
+    diag_copy = pltpu.make_async_copy(diag_ref, diag_out, diag_sem)
+    waited = []
+
+    def step(at, lanes, resid):
+        if not waited:
+            diag_copy.wait()
+            waited.append(True)
+        for u in range(VARS):
+            total = None
+            for v in range(VARS):
+                span = slice(v * CELLS + at, v * CELLS + at + PACK)
+                term = diag_out[u, span, lanes].astype(jnp.float32) * resid[v]
+                total = term if total is None else total + term
+            span = slice(u * CELLS + at, u * CELLS + at + PACK)
+            base_ref[span, lanes] = x_ref[span, lanes] + STEP_CFL * total
+
+    stores = []
+
+    def store(c, lanes):
+        copy = pltpu.make_async_copy(local.at[:, lanes], local_ref.at[:, lanes], local_sems.at[c])
+        copy.start()
+        stores.append(copy)
+
     local_kernel(
-        rim, x_ref, nbr_ref, coup_ref, source_ref, out_ref, terms, near, coup, source, sems, source_sem,
-        tables, rim_coupling,
-    )
-
-
-def full_residual(local_ref, inc_ref, lower_ref, upper_ref, table_ref, weight_ref, rimcoup_ref, rimrow_ref):
+        rim, x_ref, nbr_ref, coup_ref, source_ref, local, terms, near, coup, source, sems, source_sem,
+        diag_copy.start, tables, rim_coupling, step, store,
+    )
+    for copy in stores:
+        copy.wait()
+
+
+def arrived(inc_ref, lower_ref, upper_ref, table_ref, weight_ref, rimcoup_ref, rimrow_ref):
     rim = lower_ref.shape[0]
-    blocks = local_ref.shape[1]
+    blocks = table_ref.shape[1]
     rims = jnp.concatenate(
         [lower_ref[...], upper_ref[...], jnp.zeros((LANES - 2 * rim, BW), jnp.float32)], axis=0
     ).T
@@ -238,7 +269,7 @@
     rest = inc_ref[:, 4]
     rest = jnp.concatenate([rest[:, :, :CELLS], rest[:, :, CELLS:]], axis=1).reshape(-1, CELLS)
     fringe = [inc_ref[:, 0:2].reshape(-1, LANES).T, inc_ref[:, 2:4].reshape(-1, LANES).T, rest.T]
-    total = local_ref[...] + pick(jnp.concatenate(fringe, axis=0) * weight_ref[...], table_ref[...])
+    total = pick(jnp.concatenate(fringe, axis=0) * weight_ref[...], table_ref[...])
     lower = total[:, :LANES] + jnp.where(lane < rim, edge, 0.0)
     upper = total[:, blocks - LANES :] + jnp.where(lane >= LANES - rim, edge, 0.0)
     return jnp.concatenate([lower, total[:, LANES : blocks - LANES], upper], axis=1)
@@ -259,29 +290,29 @@
 
 
 def advance_kernel(
-    local_ref, inc_ref, lower_ref, upper_ref, across_ref, weight_ref, rimcoup_ref, rimrow_ref,
-    diag_ref, x_ref, table_ref, select_ref,
-    next_ref, norm_ref, out_ref, up_ref, down_ref, resid, diag, diag_sem, rows_ref, sem,
+    base_ref, inc_ref, lower_ref, upper_ref, across_ref, weight_ref, rimcoup_ref, rimrow_ref,
+    diag_ref, local_ref, src_ref, select_ref,
+    next_ref, norm_ref, out_ref, up_ref, down_ref, came, local, local_sem, rows_ref, sem,
 ):
-    fetch = pltpu.make_async_copy(diag_ref, diag, diag_sem)
+    fetch = pltpu.make_async_copy(local_ref, local, local_sem)
     fetch.start()
-    resid[...] = full_residual(
-        local_ref, inc_ref, lower_ref, upper_ref, across_ref, weight_ref, rimcoup_ref, rimrow_ref
-    )
-    fetch.wait()
-    for u in range(VARS):
-        for at in range(0, CELLS, PACK):
+    came[...] = arrived(
+        inc_ref, lower_ref, upper_ref, across_ref, weight_ref, rimcoup_ref, rimrow_ref
+    )
+    for at in range(0, CELLS, PACK):
+        for u in range(VARS):
             total = None
             for v in range(VARS):
                 span = slice(v * CELLS + at, v * CELLS + at + PACK)
-                term = diag[u, span].astype(jnp.float32) * resid[span]
+                term = diag_ref[u, span].astype(jnp.float32) * came[span]
                 total = term if total is None else total + term
             span = slice(u * CELLS + at, u * CELLS + at + PACK)
-            next_ref[span, :] = x_ref[span, :] + STEP_CFL * total
+            next_ref[span, :] = base_ref[span, :] + STEP_CFL * total
     copy = send_blocks(
-        next_ref[...], table_ref[...], select_ref[...], out_ref, up_ref, down_ref, rows_ref, sem
-    )
-    norm_ref[...] = lane_sums(resid[...])
+        next_ref[...], src_ref[...], select_ref[...], out_ref, up_ref, down_ref, rows_ref, sem
+    )
+    fetch.wait()
+    norm_ref[...] = lane_sums(local[...] + came[...])
     copy.wait()
 
 
@@ -289,8 +320,8 @@
     local_ref, inc_ref, lower_ref, upper_ref, across_ref, weight_ref, rimcoup_ref, rimrow_ref, norm_ref,
     resid_ref, sums_ref,
 ):
-    resid = full_residual(
-        local_ref, inc_ref, lower_ref, upper_ref, across_ref, weight_ref, rimcoup_ref, rimrow_ref
+    resid = local_ref[...] + arrived(
+        inc_ref, lower_ref, upper_ref, across_ref, weight_ref, rimcoup_ref, rimrow_ref
     )
     resid_ref[...] = resid
     both = jnp.concatenate([norm_ref[...], lane_sums(resid)], axis=0)
@@ -321,6 +352,10 @@
 
 def f32(*shape):
     return jax.ShapeDtypeStruct(shape, jnp.float32)
+
+
+def i32(*shape):
+    return jax.ShapeDtypeStruct(shape, jnp.int32)
 
 
 def bf16(*shape):
@@ -360,14 +395,14 @@
     state = f32(BW, blocks)
     hbm = pl.BlockSpec(memory_space=pltpu.HBM)
     message = (devices, BW * fringe // devices // (rim // 2 * LANES), rim // 2, LANES)
-    sent = [f32(*message), f32(rim, BW), f32(rim, BW)]
+    sent = [pltpu.HBM(message, jnp.float32), f32(rim, BW), f32(rim, BW)]
     rows_scratch = [pltpu.VMEM(message, jnp.float32), pltpu.SemaphoreType.DMA]
     size = 4 * BW * blocks
 
     donors = call(
         donors_kernel,
         [VMEM, VMEM, SMEM],
-        sent + [bf16(blocks, fringe), bf16(2 * LANES, LANES), state],
+        sent + [i32(1, fringe), bf16(2 * LANES, LANES), state],
         4 * BW * blocks * fringe,
         2 * size,
         out_specs=[hbm] + [VMEM] * 5,
@@ -389,27 +424,40 @@
     )
     first_local = call(
         functools.partial(first_local_kernel, rim),
-        [VMEM, VMEM, hbm, hbm, VMEM, VMEM],
+        [VMEM, VMEM, hbm, hbm, hbm, VMEM, VMEM],
         [
             state,
+            pltpu.HBM((BW, blocks), jnp.float32),
             bf16(VARS, BW, LANES),
-            jax.ShapeDtypeStruct((PACK, LANES), jnp.int32),
+            i32(PACK, LANES),
             bf16(fringe, blocks),
             f32(1, fringe),
+            bf16(VARS, BW, blocks),
         ],
-        **local_more,
+        out_specs=[VMEM, hbm] + [VMEM] * 5,
+        input_output_aliases={0: 0},
+        **dict(
+            local_more,
+            scratch_shapes=scratch
+            + [
+                pltpu.VMEM((BW, blocks), jnp.float32),
+                pltpu.SemaphoreType.DMA((chunks,)),
+                pltpu.SemaphoreType.DMA,
+            ],
+        ),
     )
     local = call(functools.partial(local_kernel, rim), [VMEM, VMEM, hbm, hbm], state, **local_more)
     advance = call(
         advance_kernel,
-        [VMEM] * 8 + [hbm] + [VMEM] * 3,
+        [VMEM] * 9 + [hbm] + [VMEM] * 2,
         [state, f32(1, LANES)] + sent,
         8 * BW * blocks * fringe,
         diag.size * 2 + 4 * size,
         out_specs=[VMEM, VMEM, hbm, VMEM, VMEM],
+        input_output_aliases={0: 0},
         scratch_shapes=[
             pltpu.VMEM((BW, blocks), jnp.float32),
-            pltpu.VMEM((VARS, BW, blocks), jnp.bfloat16),
+            pltpu.VMEM((BW, blocks), jnp.float32),
             pltpu.SemaphoreType.DMA,
         ]
         + rows_scratch,
@@ -436,16 +484,16 @@
         rows = lax.all_to_all(rows, ("body", "blk"), split_axis=0, concat_axis=0, tiled=True)
         return rows, lax.ppermute(to_up, "blk", up), lax.ppermute(to_down, "blk", down)
 
-    *out, table, select, x_here = donors(x, here(fringe_src), here(seam_perm))
-    arrived = exchange(*out)
-    part, rimcoup, rimrow, across, weight = first_local(
-        x_here, nbr, coup, source_t, here(fringe_dst), here(fringe_weight)
+    *out, src, select, x_here = donors(x, here(fringe_src), here(seam_perm))
+    arrivals = exchange(*out)
+    base, part, rimcoup, rimrow, across, weight, diag_here = first_local(
+        x_here, nbr, coup, source_t, diag, here(fringe_dst), here(fringe_weight)
     )
     across = (across, weight, rimcoup, rimrow)
-    x, norm, *out = advance(part, *arrived, *across, diag, x_here, table, select)
-    arrived = exchange(*out)
+    x, norm, *out = advance(base, *arrivals, *across, diag_here, here(part), src, select)
+    arrivals = exchange(*out)
     part = local(x, nbr, coup, source_t)
-    resid, sums = residual(part, *arrived, *across, norm)
+    resid, sums = residual(part, *arrivals, *across, norm)
     sums = lax.all_to_all(sums, ("body", "blk"), split_axis=0, concat_axis=0, tiled=True)
     update, resid = direction(diag, resid)
     x = finish(sums, x, update)

time: 53.6 us -> 55.6 us (1.037)
  Pallas kernels: 23.1 us -> 25.8 us
  waiting for transfers between devices: 7.38 us -> 6 us
  starting transfers between devices: 22 us -> 22.6 us
    pallas_call x4, Pallas kernels: 13.2 us -> 15.9 us  [the longest x1 9.35 us: shards(): first_local(x_here, nbr, coup, source_t, diag, here(fringe_dst), here(fri...]
    all_to_all x2, waiting for transfers between devices: 2.47 us -> 1.24 us  [exchange(): lax.all_to_all(rows, ('body', 'blk'), split_axis=0, concat_axis=0, tiled=...]
  transfers between devices with their start and end apart: 7 -> 7, of which waited for: 5 -> 3; matrix products, arithmetic and copies ran while one was open for 0% -> 0% of each run, Pallas kernels for 28% -> 33%
where the time goes in v12:
time: 55.6 us; the launch traced here: 55.1 us
  Pallas kernels  25.8 us (46%)
  starting transfers between devices  22.6 us (41%)
  waiting for transfers between devices  6 us (11%)
  between operations  0.71 us (1%)
    all_to_all x2, starting transfers between devices, exchange(): lax.all_to_all(rows, ('body', 'blk'), split_axis=0, concat_axis=0, tiled=...  10.4 us
    pallas_call x1, Pallas kernels, shards(): first_local(x_here, nbr, coup, source_t, diag, here(fringe_dst), here(fri...  9.35 us
    pallas_call x1, Pallas kernels, shards(): part = local(x, nbr, coup, source_t)  6.15 us
    ppermute x2, starting transfers between devices, exchange(): lax.ppermute(to_down, 'blk', down)  5.91 us
    all_to_all x1, waiting for transfers between devices, shards(): lax.all_to_all(sums, ('body', 'blk'), split_axis=0, concat_axis=0, tiled=...  4.53 us
    ppermute x2, starting transfers between devices, exchange(): lax.ppermute(to_up, 'blk', up)  3.64 us
    pallas_call x1, Pallas kernels, shards(): advance(base, *arrivals, *across, diag_here, here(part), src, select)  2.88 us
    pallas_call x1, Pallas kernels, shards(): update, resid = direction(diag, resid)  2.66 us
  transfers between devices with their start and end apart: 7, of which 3 were waited for; matrix products, arithmetic and copies ran while one was open for 0% of the time, Pallas kernels for 33%

profile of v12, /device:TPU:0, one launch (start us, length us, event | category | flops | bytes accessed | tf_op | source)
XLA Modules:
  0.0 55.1 jit_solution(15586782075337792276)
XLA Ops:
  0.6 2.4 %shard_map.104 = (f32[32,5,4,128]{3,2,1,0:T(4,128)}, f32[8,320]{1,0:T(8,128)S(1)}, f32[8,320]{1,0:T(8,128)S(1)}, s32[1,256]{1,0:T(1,128)S(1)}, bf16[256,128]{1,0:T(8,128)(2,1)S(1)}, /*index=5*/f32[320,512]{1,0:T(8,128)S(1)}) custom-call(f32[320,512]{1,0:T(8,128)} %bitcast.13, s32[1,256]{1,0:T(1,128)} %src_ref.1, s32[1,8]{1,0:T(1,128)} %perm_ref.1), custom_call_target="tpu_custom_call" | custom-call | flops 167772160 | bytes 1310720 | tf_op jit(solution)/shard_map/pallas_call | solution.py:487
  3.0 7.3 %all-to-all-start = ((f32[32,5,4,128]{3,2,1,0:T(4,128)}), f32[32,5,4,128]{3,2,1,0:T(4,128)S(1)}, u32[]{:S(2)}, u32[]{:S(2)}) async-start(f32[32,5,4,128]{3,2,1,0:T(4,128)} %get-tuple-element.26), calls=%async_computation | async-start | bytes 655360 | tf_op jit(solution)/shard_map/all_to_all | solution.py:484
  10.3 1.8 %collective-permute-start = (f32[8,320]{1,0:T(8,128)S(1)}, f32[8,320]{1,0:T(8,128)S(1)}, u32[]{:S(2)}, u32[]{:S(2)}) collective-permute-start(f32[8,320]{1,0:T(8,128)S(1)} %get-tuple-element.27), channel_id=1, source_target_pairs={{0,1},{1,2},{2,3},{3,4},{4,5},{5,6},{6,7},{7,0},{8,9},{9,10},{10,1... | collective-permute-start | bytes 30728 | tf_op jit(solution)/shard_map/ppermute | solution.py:485
  12.2 3.0 %collective-permute-start.1 = (f32[8,320]{1,0:T(8,128)S(1)}, f32[8,320]{1,0:T(8,128)S(1)}, u32[]{:S(2)}, u32[]{:S(2)}) collective-permute-start(f32[8,320]{1,0:T(8,128)S(1)} %get-tuple-element.28), channel_id=1, source_target_pairs={{1,0},{2,1},{3,2},{4,3},{5,4},{6,5},{7,6},{0,7},{9,8},{10,9},{11,1... | collective-permute-start | bytes 30728 | tf_op jit(solution)/shard_map/ppermute | solution.py:485
  15.1 9.3 %shard_map.105 = (f32[320,512]{1,0:T(8,128)S(1)}, f32[320,512]{1,0:T(8,128)}, bf16[5,320,128]{2,1,0:T(8,128)(2,1)S(1)}, s32[16,128]{1,0:T(8,128)S(1)}, bf16[256,...) custom-call(f32[320,512]{1,0:T(8,128)S(1)} %get-tuple-element.24.x_r, ...), custom_call_target="tpu_custom_call", output_to_operand_aliasing={{0}: (0, {})} | custom-call | flops 1006632960 | bytes 12451840 | tf_op jit(solution)/shard_map/pallas_call | solution.py:489
  24.5 0.0 collective-permute-done.lower_ref
  24.5 0.0 collective-permute-done.1.upper_ref
  24.5 0.0 all-to-all-done.inc_ref
  24.5 2.9 %shard_map.106 = (f32[320,512]{1,0:T(8,128)S(1)}, f32[1,128]{1,0:T(1,128)S(1)}, f32[32,5,4,128]{3,2,1,0:T(4,128)}, f32[8,320]{1,0:T(8,128)S(1)}, f32[8,320]{1,0:T(8,128)S(1)}) custom-call(f32[320,512]{1,0:T(8,128)S(1)} %get-tuple-element.25.base_ref, f32[32,5,4,128]{3,2,1,0:T(4,128)S(1)} %all-to-all-done.inc_ref, ...), custom_call_target="tpu_custom_call", output_to_operand_aliasing={{0}: (0, {})} | custom-call | flops 335544320 | bytes 4259840 | tf_op jit(solution)/shard_map/pallas_call | solution.py:493
  27.4 3.1 %all-to-all-start.1 = ((f32[32,5,4,128]{3,2,1,0:T(4,128)}), f32[32,5,4,128]{3,2,1,0:T(4,128)S(1)}, u32[]{:S(2)}, u32[]{:S(2)}) async-start(f32[32,5,4,128]{3,2,1,0:T(4,128)} %get-tuple-element.38), calls=%async_computation.1 | async-start | bytes 655360 | tf_op jit(solution)/shard_map/all_to_all | solution.py:484
  30.5 1.8 %collective-permute-start.2 = (f32[8,320]{1,0:T(8,128)S(1)}, f32[8,320]{1,0:T(8,128)S(1)}, u32[]{:S(2)}, u32[]{:S(2)}) collective-permute-start(f32[8,320]{1,0:T(8,128)S(1)} %get-tuple-element.39), channel_id=1, source_target_pairs={{0,1},{1,2},{2,3},{3,4},{4,5},{5,6},{6,7},{7,0},{8,9},{9,10},{10,1... | collective-permute-start | bytes 30728 | tf_op jit(solution)/shard_map/ppermute | solution.py:485
  32.4 3.0 %collective-permute-start.3 = (f32[8,320]{1,0:T(8,128)S(1)}, f32[8,320]{1,0:T(8,128)S(1)}, u32[]{:S(2)}, u32[]{:S(2)}) collective-permute-start(f32[8,320]{1,0:T(8,128)S(1)} %get-tuple-element.40), channel_id=1, source_target_pairs={{1,0},{2,1},{3,2},{4,3},{5,4},{6,5},{7,6},{0,7},{9,8},{10,9},{11,1... | collective-permute-start | bytes 30728 | tf_op jit(solution)/shard_map/ppermute | solution.py:485
  35.3 6.1 %shard_map.107.local_ref = f32[320,512]{1,0:T(8,128)S(1)} custom-call(f32[320,512]{1,0:T(8,128)S(1)} %get-tuple-element.37.x_ref, s32[6,512]{1,0:T(8,128)} %bitcast.16, bf16[6,5,320,512]{3,2,1,0:T(8,128)(2,1)} %bitcast.8, f32[320,512]{1,0:T(8,128)} %bitcast.12), custom_call_target="tpu_custom_call" | custom-call | flops 1006632960 | bytes 12451840 | tf_op jit(solution)/shard_map/pallas_call | solution.py:495
  41.5 0.2 collective-permute-done.2.lower_ref
  41.7 0.0 collective-permute-done.3.upper_ref
  41.7 1.2 %all-to-all-done.1.inc_ref = f32[32,5,4,128]{3,2,1,0:T(4,128)S(1)} async-done(((f32[32,5,4,128]{3,2,1,0:T(4,128)}), f32[32,5,4,128]{3,2,1,0:T(4,128)S(1)}, u32[]{:S(2)}, u32[]{:S(2)}) %all-to-all-start.1) | async-done | bytes 327712 | tf_op jit(solution)/shard_map/all_to_all | solution.py:484
  42.9 1.3 %shard_map.108 = (f32[320,512]{1,0:T(8,128)S(1)}, f32[32,2,128]{2,1,0:T(2,128)}) custom-call(f32[320,512]{1,0:T(8,128)S(1)} %shard_map.107.local_ref, f32[32,5,4,128]{3,2,1,0:T(4,128)S(1)} %all-to-all-done.1.inc_ref, f32[8,320]{1,0:T(8,128)S(1)} %collective-permute-done.2.lower_ref, f32[8,320]{1,0:T(8,128)S(1)} %collective-permute-done.3.upper_ref, ...), custom_call_target="tpu_custom_call" | custom-call | flops 167772160 | bytes 1966080 | tf_op jit(solution)/shard_map/pallas_call | solution.py:496
  44.3 2.6 %all-to-all-start.2 = ((f32[32,2,128]{2,1,0:T(2,128)}), f32[32,2,128]{2,1,0:T(2,128)S(1)}, u32[]{:S(2)}, u32[]{:S(2)}) async-start(f32[32,2,128]{2,1,0:T(2,128)} %get-tuple-element.42), calls=%async_computation.2 | async-start | bytes 65536 | tf_op jit(solution)/shard_map/all_to_all | solution.py:497
  46.8 2.7 %shard_map.109 = (f32[320,512]{1,0:T(8,128)S(1)}, f32[320,512]{1,0:T(8,128)}) custom-call(bf16[5,320,512]{2,1,0:T(8,128)(2,1)} %bitcast.10, f32[320,512]{1,0:T(8,128)S(1)} %get-tuple-element.43.resid_ref), custom_call_target="tpu_custom_call" | custom-call | flops 1638400 | bytes 2949120 | tf_op jit(solution)/shard_map/pallas_call | solution.py:498
  49.5 4.5 %all-to-all-done.2.sums_ref = f32[32,2,128]{2,1,0:T(2,128)S(1)} async-done(((f32[32,2,128]{2,1,0:T(2,128)}), f32[32,2,128]{2,1,0:T(2,128)S(1)}, u32[]{:S(2)}, u32[]{:S(2)}) %all-to-all-start.2) | async-done | bytes 32800 | tf_op jit(solution)/shard_map/all_to_all | solution.py:497
  54.0 1.1 %shard_map.110 = f32[320,512]{1,0:T(8,128)} custom-call(f32[32,2,128]{2,1,0:T(2,128)S(1)} %all-to-all-done.2.sums_ref, f32[320,512]{1,0:T(8,128)S(1)} %get-tuple-element.37.x_ref, f32[320,512]{1,0:T(8,128)S(1)} %get-tuple-element.44.update_ref), custom_call_target="tpu_custom_call" | custom-call | flops 327680 | bytes 1966080 | tf_op jit(solution)/shard_map/pallas_call | solution.py:499
Async XLA Ops:
  3.0 21.5 %all-to-all-start = ((f32[32,5,4,128]{3,2,1,0:T(4,128)}), f32[32,5,4,128]{3,2,1,0:T(4,128)S(1)}, u32[]{:S(2)}, u32[]{:S(2)}) async-start(f32[32,5,4,128]{3,2,1,0:T(4,128)} %get-tuple-element.26), calls=%async_computation | async-start | bytes 655360 | tf_op jit(solution)/shard_map/all_to_all | solution.py:484
  10.3 14.1 %collective-permute-start = (f32[8,320]{1,0:T(8,128)S(1)}, f32[8,320]{1,0:T(8,128)S(1)}, u32[]{:S(2)}, u32[]{:S(2)}) collective-permute-start(f32[8,320]{1,0:T(8,128)S(1)} %get-tuple-element.27), channel_id=1, source_target_pairs={{0,1},{1,2},{2,3},{3,4},{4,5},{5,6},{6,7},{7,0},{8,9},{9,10},{10,1... | collective-permute-start | bytes 30728 | tf_op jit(solution)/shard_map/ppermute | solution.py:485
  12.2 12.3 %collective-permute-start.1 = (f32[8,320]{1,0:T(8,128)S(1)}, f32[8,320]{1,0:T(8,128)S(1)}, u32[]{:S(2)}, u32[]{:S(2)}) collective-permute-start(f32[8,320]{1,0:T(8,128)S(1)} %get-tuple-element.28), channel_id=1, source_target_pairs={{1,0},{2,1},{3,2},{4,3},{5,4},{6,5},{7,6},{0,7},{9,8},{10,9},{11,1... | collective-permute-start | bytes 30728 | tf_op jit(solution)/shard_map/ppermute | solution.py:485
  27.4 15.6 %all-to-all-start.1 = ((f32[32,5,4,128]{3,2,1,0:T(4,128)}), f32[32,5,4,128]{3,2,1,0:T(4,128)S(1)}, u32[]{:S(2)}, u32[]{:S(2)}) async-start(f32[32,5,4,128]{3,2,1,0:T(4,128)} %get-tuple-element.38), calls=%async_computation.1 | async-start | bytes 655360 | tf_op jit(solution)/shard_map/all_to_all | solution.py:484
  30.5 11.2 %collective-permute-start.2 = (f32[8,320]{1,0:T(8,128)S(1)}, f32[8,320]{1,0:T(8,128)S(1)}, u32[]{:S(2)}, u32[]{:S(2)}) collective-permute-start(f32[8,320]{1,0:T(8,128)S(1)} %get-tuple-element.39), channel_id=1, source_target_pairs={{0,1},{1,2},{2,3},{3,4},{4,5},{5,6},{6,7},{7,0},{8,9},{9,10},{10,1... | collective-permute-start | bytes 30728 | tf_op jit(solution)/shard_map/ppermute | solution.py:485
  32.4 9.3 %collective-permute-start.3 = (f32[8,320]{1,0:T(8,128)S(1)}, f32[8,320]{1,0:T(8,128)S(1)}, u32[]{:S(2)}, u32[]{:S(2)}) collective-permute-start(f32[8,320]{1,0:T(8,128)S(1)} %get-tuple-element.40), channel_id=1, source_target_pairs={{1,0},{2,1},{3,2},{4,3},{5,4},{6,5},{7,6},{0,7},{9,8},{10,9},{11,1... | collective-permute-start | bytes 30728 | tf_op jit(solution)/shard_map/ppermute | solution.py:485
  44.3 9.8 %all-to-all-start.2 = ((f32[32,2,128]{2,1,0:T(2,128)}), f32[32,2,128]{2,1,0:T(2,128)S(1)}, u32[]{:S(2)}, u32[]{:S(2)}) async-start(f32[32,2,128]{2,1,0:T(2,128)} %get-tuple-element.42), calls=%async_computation.2 | async-start | bytes 65536 | tf_op jit(solution)/shard_map/all_to_all | solution.py:497

commit v13 on v11

--- a/solution.py
+++ b/solution.py
@@ -31,22 +31,23 @@
     return both[: x.shape[0]] + both[x.shape[0] :]
 
 
-def send_blocks(x, table, select, out_ref, up_ref, down_ref, rows_ref, sem):
+def send_blocks(x_ref, groups, table, select, out_ref, up_ref, down_ref, rows_ref, sem):
     rim = up_ref.shape[0]
     half = rows_ref.shape[2]
-    rows = pick(x, table).T.reshape(rows_ref.shape[0], 2 * half, BW)
-    for h in range(2):
-        for tile in range(2):
-            rows_ref[:, 2 * tile + h] = rows[:, h * half : (h + 1) * half, tile * LANES : (tile + 1) * LANES]
-    rest = rows[:, :, 2 * LANES :]
-    rows_ref[:, 4] = jnp.concatenate([rest[:, :half], rest[:, half:]], axis=2)
+    devices = rows_ref.shape[0]
+    for tile in range(2):
+        rows = pick(groups(2 * tile, 2 * tile + 2), table).T.reshape(devices, 2 * half, LANES)
+        rows_ref[:, 2 * tile] = rows[:, :half]
+        rows_ref[:, 2 * tile + 1] = rows[:, half:]
+    rows = pick(groups(4, 5), table).T.reshape(devices, 2 * half, CELLS)
+    rows_ref[:, 4] = jnp.concatenate([rows[:, :half], rows[:, half:]], axis=2)
     copy = pltpu.make_async_copy(rows_ref, out_ref, sem)
     copy.start()
     index = lax.axis_index("blk")
     at_last = index == lax.axis_size("blk") - 1
     at_first = index == 0
     first = lax.broadcasted_iota(jnp.int32, (BW, LANES), 1) < LANES // 2
-    ends = split(jnp.where(first, x[:, :LANES], x[:, x.shape[1] - LANES :]))
+    ends = split(jnp.where(first, x_ref[:, :LANES], x_ref[:, x_ref.shape[1] - LANES :]))
     rims = jnp.dot(jnp.concatenate(ends, axis=1), select, preferred_element_type=jnp.float32)
     lane = lax.broadcasted_iota(jnp.int32, (1, LANES), 1)
     turn_up = (lane < rim) & at_last
@@ -93,7 +94,8 @@
     rows = lax.broadcasted_iota(jnp.int32, table_ref.shape, 0)
     table = onehot(rows == src_ref[...])
     copy = send_blocks(
-        x_ref[...], table, select, out_ref, up_ref, down_ref, rows_ref, sem
+        x_ref, lambda a, b: x_ref[a * CELLS : b * CELLS], table, select,
+        out_ref, up_ref, down_ref, rows_ref, sem,
     )
     table_ref[...] = table
     select_ref[...] = select
@@ -269,17 +271,21 @@
         local_ref, inc_ref, lower_ref, upper_ref, across_ref, weight_ref, rimcoup_ref, rimrow_ref
     )
     fetch.wait()
-    for u in range(VARS):
-        for at in range(0, CELLS, PACK):
-            total = None
-            for v in range(VARS):
-                span = slice(v * CELLS + at, v * CELLS + at + PACK)
-                term = diag[u, span].astype(jnp.float32) * resid[span]
-                total = term if total is None else total + term
-            span = slice(u * CELLS + at, u * CELLS + at + PACK)
-            next_ref[span, :] = x_ref[span, :] + STEP_CFL * total
+
+    def groups(a, b):
+        for u in range(a, b):
+            for at in range(0, CELLS, PACK):
+                total = None
+                for v in range(VARS):
+                    span = slice(v * CELLS + at, v * CELLS + at + PACK)
+                    term = diag[u, span].astype(jnp.float32) * resid[span]
+                    total = term if total is None else total + term
+                span = slice(u * CELLS + at, u * CELLS + at + PACK)
+                next_ref[span, :] = x_ref[span, :] + STEP_CFL * total
+        return next_ref[a * CELLS : b * CELLS]
+
     copy = send_blocks(
-        next_ref[...], table_ref[...], select_ref[...], out_ref, up_ref, down_ref, rows_ref, sem
+        next_ref, groups, table_ref[...], select_ref[...], out_ref, up_ref, down_ref, rows_ref, sem
     )
     norm_ref[...] = lane_sums(resid[...])
     copy.wait()

time: 53.6 us -> 54 us (level)
  no operation moved by 1% of the time
where the time goes in v13:
time: 54 us; the launch traced here: 53.5 us
  Pallas kernels  23.4 us (43%)
  starting transfers between devices  22 us (41%)
  waiting for transfers between devices  7.37 us (14%)
  between operations  0.69 us (1%)
    all_to_all x2, starting transfers between devices, exchange(): lax.all_to_all(rows, ('body', 'blk'), split_axis=0, concat_axis=0, tiled=...  9.91 us
    pallas_call x1, Pallas kernels, shards(): first_local(x_here, nbr, coup, source_t, here(fringe_dst), here(fringe_we...  6.26 us
    pallas_call x1, Pallas kernels, shards(): part = local(x, nbr, coup, source_t)  6.15 us
    ppermute x2, starting transfers between devices, exchange(): lax.ppermute(to_down, 'blk', down)  6.04 us
    all_to_all x1, waiting for transfers between devices, shards(): lax.all_to_all(sums, ('body', 'blk'), split_axis=0, concat_axis=0, tiled=...  4.55 us
    pallas_call x1, Pallas kernels, shards(): advance(part, *arrived, *across, diag, x_here, table, select)  3.61 us
    ppermute x2, starting transfers between devices, exchange(): lax.ppermute(to_up, 'blk', up)  3.51 us
    pallas_call x1, Pallas kernels, shards(): update, resid = direction(diag, resid)  2.64 us
  transfers between devices with their start and end apart: 7, of which 5 were waited for; matrix products, arithmetic and copies ran while one was open for 0% of the time, Pallas kernels for 28%

profile of v13, /device:TPU:0, one launch (start us, length us, event | category | flops | bytes accessed | tf_op | source)
XLA Modules:
  0.0 53.5 jit_solution(1809046241276600689)
XLA Ops:
  0.6 2.4 %shard_map.104 = (f32[32,5,4,128]{3,2,1,0:T(4,128)}, f32[8,320]{1,0:T(8,128)S(1)}, f32[8,320]{1,0:T(8,128)S(1)}, bf16[512,256]{1,0:T(8,128)(2,1)S(1)}, bf16[256,...) custom-call(f32[320,512]{1,0:T(8,128)} %bitcast.13, s32[1,256]{1,0:T(1,128)} %src_ref.1, s32[1,8]{1,0:T(1,128)} %perm_ref.1), custom_call_target="tpu_custom_call" | custom-call | flops 167772160 | bytes 1310720 | tf_op jit(solution)/shard_map/pallas_call | solution.py:445
  3.0 7.3 %all-to-all-start = ((f32[32,5,4,128]{3,2,1,0:T(4,128)}), f32[32,5,4,128]{3,2,1,0:T(4,128)S(1)}, u32[]{:S(2)}, u32[]{:S(2)}) async-start(f32[32,5,4,128]{3,2,1,0:T(4,128)} %get-tuple-element.24), calls=%async_computation | async-start | bytes 655360 | tf_op jit(solution)/shard_map/all_to_all | solution.py:442
  10.3 1.8 %collective-permute-start = (f32[8,320]{1,0:T(8,128)S(1)}, f32[8,320]{1,0:T(8,128)S(1)}, u32[]{:S(2)}, u32[]{:S(2)}) collective-permute-start(f32[8,320]{1,0:T(8,128)S(1)} %get-tuple-element.25), channel_id=1, source_target_pairs={{0,1},{1,2},{2,3},{3,4},{4,5},{5,6},{6,7},{7,0},{8,9},{9,10},{10,1... | collective-permute-start | bytes 30728 | tf_op jit(solution)/shard_map/ppermute | solution.py:443
  12.2 3.0 %collective-permute-start.1 = (f32[8,320]{1,0:T(8,128)S(1)}, f32[8,320]{1,0:T(8,128)S(1)}, u32[]{:S(2)}, u32[]{:S(2)}) collective-permute-start(f32[8,320]{1,0:T(8,128)S(1)} %get-tuple-element.26), channel_id=1, source_target_pairs={{1,0},{2,1},{3,2},{4,3},{5,4},{6,5},{7,6},{0,7},{9,8},{10,9},{11,1... | collective-permute-start | bytes 30728 | tf_op jit(solution)/shard_map/ppermute | solution.py:443
  15.1 6.3 %shard_map.105 = (f32[320,512]{1,0:T(8,128)S(1)}, bf16[5,320,128]{2,1,0:T(8,128)(2,1)S(1)}, s32[16,128]{1,0:T(8,128)S(1)}, bf16[256,512]{1,0:T(8,128)(2,1)S(1)}, f32[1,256]{1,0:T(1,128)S(1)}) custom-call(f32[320,512]{1,0:T(8,128)S(1)} %get-tuple-element.22.x_ref, s32[6,512]{1,0:T(8,128)} %bitcast.15, bf16[6,5,320,512]{3,2,1,0:T(8,128)(2,1)} %bitcast.7, ...), custom_call_target="tpu_custom_call" | custom-call | flops 1006632960 | bytes 12451840 | tf_op jit(solution)/shard_map/pallas_call | solution.py:447
  21.4 0.1 collective-permute-done.lower_ref
  21.5 0.0 collective-permute-done.1.upper_ref
  21.5 1.2 %all-to-all-done.inc_ref = f32[32,5,4,128]{3,2,1,0:T(4,128)S(1)} async-done(((f32[32,5,4,128]{3,2,1,0:T(4,128)}), f32[32,5,4,128]{3,2,1,0:T(4,128)S(1)}, u32[]{:S(2)}, u32[]{:S(2)}) %all-to-all-start) | async-done | bytes 327712 | tf_op jit(solution)/shard_map/all_to_all | solution.py:442
  22.7 3.6 %shard_map.106 = (f32[320,512]{1,0:T(8,128)S(1)}, f32[1,128]{1,0:T(1,128)S(1)}, f32[32,5,4,128]{3,2,1,0:T(4,128)}, f32[8,320]{1,0:T(8,128)S(1)}, f32[8,320]{1,0:T(8,128)S(1)}) custom-call(f32[320,512]{1,0:T(8,128)S(1)} %get-tuple-element.23.local_ref, f32[32,5,4,128]{3,2,1,0:T(4,128)S(1)} %all-to-all-done.inc_ref, ...), custom_call_target="tpu_custom_call" | custom-call | flops 335544320 | bytes 4259840 | tf_op jit(solution)/shard_map/pallas_call | solution.py:451
  26.4 2.6 %all-to-all-start.1 = ((f32[32,5,4,128]{3,2,1,0:T(4,128)}), f32[32,5,4,128]{3,2,1,0:T(4,128)S(1)}, u32[]{:S(2)}, u32[]{:S(2)}) async-start(f32[32,5,4,128]{3,2,1,0:T(4,128)} %get-tuple-element.34), calls=%async_computation.1 | async-start | bytes 655360 | tf_op jit(solution)/shard_map/all_to_all | solution.py:442
  29.0 1.7 %collective-permute-start.2 = (f32[8,320]{1,0:T(8,128)S(1)}, f32[8,320]{1,0:T(8,128)S(1)}, u32[]{:S(2)}, u32[]{:S(2)}) collective-permute-start(f32[8,320]{1,0:T(8,128)S(1)} %get-tuple-element.35), channel_id=1, source_target_pairs={{0,1},{1,2},{2,3},{3,4},{4,5},{5,6},{6,7},{7,0},{8,9},{9,10},{10,1... | collective-permute-start | bytes 30728 | tf_op jit(solution)/shard_map/ppermute | solution.py:443
  30.7 3.1 %collective-permute-start.3 = (f32[8,320]{1,0:T(8,128)S(1)}, f32[8,320]{1,0:T(8,128)S(1)}, u32[]{:S(2)}, u32[]{:S(2)}) collective-permute-start(f32[8,320]{1,0:T(8,128)S(1)} %get-tuple-element.36), channel_id=1, source_target_pairs={{1,0},{2,1},{3,2},{4,3},{5,4},{6,5},{7,6},{0,7},{9,8},{10,9},{11,1... | collective-permute-start | bytes 30728 | tf_op jit(solution)/shard_map/ppermute | solution.py:443
  33.8 6.2 %shard_map.107.local_ref = f32[320,512]{1,0:T(8,128)S(1)} custom-call(f32[320,512]{1,0:T(8,128)S(1)} %get-tuple-element.33.x_ref, s32[6,512]{1,0:T(8,128)} %bitcast.16, bf16[6,5,320,512]{3,2,1,0:T(8,128)(2,1)} %bitcast.8, f32[320,512]{1,0:T(8,128)} %bitcast.12), custom_call_target="tpu_custom_call" | custom-call | flops 1006632960 | bytes 12451840 | tf_op jit(solution)/shard_map/pallas_call | solution.py:453
  39.9 0.2 collective-permute-done.2.lower_ref
  40.1 0.0 collective-permute-done.3.upper_ref
  40.1 1.2 %all-to-all-done.1.inc_ref = f32[32,5,4,128]{3,2,1,0:T(4,128)S(1)} async-done(((f32[32,5,4,128]{3,2,1,0:T(4,128)}), f32[32,5,4,128]{3,2,1,0:T(4,128)S(1)}, u32[]{:S(2)}, u32[]{:S(2)}) %all-to-all-start.1) | async-done | bytes 327712 | tf_op jit(solution)/shard_map/all_to_all | solution.py:442
  41.4 1.3 %shard_map.108 = (f32[320,512]{1,0:T(8,128)S(1)}, f32[32,2,128]{2,1,0:T(2,128)}) custom-call(f32[320,512]{1,0:T(8,128)S(1)} %shard_map.107.local_ref, f32[32,5,4,128]{3,2,1,0:T(4,128)S(1)} %all-to-all-done.1.inc_ref, f32[8,320]{1,0:T(8,128)S(1)} %collective-permute-done.2.lower_ref, f32[8,320]{1,0:T(8,128)S(1)} %collective-permute-done.3.upper_ref, ...), custom_call_target="tpu_custom_call" | custom-call | flops 167772160 | bytes 1966080 | tf_op jit(solution)/shard_map/pallas_call | solution.py:454
  42.7 2.6 %all-to-all-start.2 = ((f32[32,2,128]{2,1,0:T(2,128)}), f32[32,2,128]{2,1,0:T(2,128)S(1)}, u32[]{:S(2)}, u32[]{:S(2)}) async-start(f32[32,2,128]{2,1,0:T(2,128)} %get-tuple-element.38), calls=%async_computation.2 | async-start | bytes 65536 | tf_op jit(solution)/shard_map/all_to_all | solution.py:455
  45.3 2.6 %shard_map.109 = (f32[320,512]{1,0:T(8,128)S(1)}, f32[320,512]{1,0:T(8,128)}) custom-call(bf16[5,320,512]{2,1,0:T(8,128)(2,1)} %bitcast.10, f32[320,512]{1,0:T(8,128)S(1)} %get-tuple-element.39.resid_ref), custom_call_target="tpu_custom_call" | custom-call | flops 1638400 | bytes 2949120 | tf_op jit(solution)/shard_map/pallas_call | solution.py:456
  47.9 4.5 %all-to-all-done.2.sums_ref = f32[32,2,128]{2,1,0:T(2,128)S(1)} async-done(((f32[32,2,128]{2,1,0:T(2,128)}), f32[32,2,128]{2,1,0:T(2,128)S(1)}, u32[]{:S(2)}, u32[]{:S(2)}) %all-to-all-start.2) | async-done | bytes 32800 | tf_op jit(solution)/shard_map/all_to_all | solution.py:455
  52.4 1.1 %shard_map.110 = f32[320,512]{1,0:T(8,128)} custom-call(f32[32,2,128]{2,1,0:T(2,128)S(1)} %all-to-all-done.2.sums_ref, f32[320,512]{1,0:T(8,128)S(1)} %get-tuple-element.33.x_ref, f32[320,512]{1,0:T(8,128)S(1)} %get-tuple-element.40.update_ref), custom_call_target="tpu_custom_call" | custom-call | flops 327680 | bytes 1966080 | tf_op jit(solution)/shard_map/pallas_call | solution.py:457
Async XLA Ops:
  3.0 19.7 %all-to-all-start = ((f32[32,5,4,128]{3,2,1,0:T(4,128)}), f32[32,5,4,128]{3,2,1,0:T(4,128)S(1)}, u32[]{:S(2)}, u32[]{:S(2)}) async-start(f32[32,5,4,128]{3,2,1,0:T(4,128)} %get-tuple-element.24), calls=%async_computation | async-start | bytes 655360 | tf_op jit(solution)/shard_map/all_to_all | solution.py:442
  10.3 11.2 %collective-permute-start = (f32[8,320]{1,0:T(8,128)S(1)}, f32[8,320]{1,0:T(8,128)S(1)}, u32[]{:S(2)}, u32[]{:S(2)}) collective-permute-start(f32[8,320]{1,0:T(8,128)S(1)} %get-tuple-element.25), channel_id=1, source_target_pairs={{0,1},{1,2},{2,3},{3,4},{4,5},{5,6},{6,7},{7,0},{8,9},{9,10},{10,1... | collective-permute-start | bytes 30728 | tf_op jit(solution)/shard_map/ppermute | solution.py:443
  12.2 9.3 %collective-permute-start.1 = (f32[8,320]{1,0:T(8,128)S(1)}, f32[8,320]{1,0:T(8,128)S(1)}, u32[]{:S(2)}, u32[]{:S(2)}) collective-permute-start(f32[8,320]{1,0:T(8,128)S(1)} %get-tuple-element.26), channel_id=1, source_target_pairs={{1,0},{2,1},{3,2},{4,3},{5,4},{6,5},{7,6},{0,7},{9,8},{10,9},{11,1... | collective-permute-start | bytes 30728 | tf_op jit(solution)/shard_map/ppermute | solution.py:443
  26.4 15.0 %all-to-all-start.1 = ((f32[32,5,4,128]{3,2,1,0:T(4,128)}), f32[32,5,4,128]{3,2,1,0:T(4,128)S(1)}, u32[]{:S(2)}, u32[]{:S(2)}) async-start(f32[32,5,4,128]{3,2,1,0:T(4,128)} %get-tuple-element.34), calls=%async_computation.1 | async-start | bytes 655360 | tf_op jit(solution)/shard_map/all_to_all | solution.py:442
  29.0 11.2 %collective-permute-start.2 = (f32[8,320]{1,0:T(8,128)S(1)}, f32[8,320]{1,0:T(8,128)S(1)}, u32[]{:S(2)}, u32[]{:S(2)}) collective-permute-start(f32[8,320]{1,0:T(8,128)S(1)} %get-tuple-element.35), channel_id=1, source_target_pairs={{0,1},{1,2},{2,3},{3,4},{4,5},{5,6},{6,7},{7,0},{8,9},{9,10},{10,1... | collective-permute-start | bytes 30728 | tf_op jit(solution)/shard_map/ppermute | solution.py:443
  30.7 9.5 %collective-permute-start.3 = (f32[8,320]{1,0:T(8,128)S(1)}, f32[8,320]{1,0:T(8,128)S(1)}, u32[]{:S(2)}, u32[]{:S(2)}) collective-permute-start(f32[8,320]{1,0:T(8,128)S(1)} %get-tuple-element.36), channel_id=1, source_target_pairs={{1,0},{2,1},{3,2},{4,3},{5,4},{6,5},{7,6},{0,7},{9,8},{10,9},{11,1... | collective-permute-start | bytes 30728 | tf_op jit(solution)/shard_map/ppermute | solution.py:443
  42.7 9.8 %all-to-all-start.2 = ((f32[32,2,128]{2,1,0:T(2,128)}), f32[32,2,128]{2,1,0:T(2,128)S(1)}, u32[]{:S(2)}, u32[]{:S(2)}) async-start(f32[32,2,128]{2,1,0:T(2,128)} %get-tuple-element.38), calls=%async_computation.2 | async-start | bytes 65536 | tf_op jit(solution)/shard_map/all_to_all | solution.py:455

commit v14 on v11

--- a/solution.py
+++ b/solution.py
@@ -3,6 +3,7 @@
 
 import jax
 import jax.numpy as jnp
+import numpy as np
 from jax import lax
 from jax.experimental import pallas as pl
 from jax.experimental.pallas import tpu as pltpu
@@ -31,10 +32,11 @@
     return both[: x.shape[0]] + both[x.shape[0] :]
 
 
-def send_blocks(x, table, select, out_ref, up_ref, down_ref, rows_ref, sem):
+def send_blocks(order, x, table, select, out_ref, up_ref, down_ref, rows_ref, sem):
     rim = up_ref.shape[0]
     half = rows_ref.shape[2]
     rows = pick(x, table).T.reshape(rows_ref.shape[0], 2 * half, BW)
+    rows = jnp.concatenate([rows[r : r + 1] for r in order], axis=0)
     for h in range(2):
         for tile in range(2):
             rows_ref[:, 2 * tile + h] = rows[:, h * half : (h + 1) * half, tile * LANES : (tile + 1) * LANES]
@@ -71,7 +73,7 @@
 
 
 def donors_kernel(
-    x_ref, src_ref, perm_ref,
+    order, x_ref, src_ref, perm_ref,
     out_ref, up_ref, down_ref, table_ref, select_ref, x_out, rows_ref, sem,
 ):
     rim = up_ref.shape[0]
@@ -93,7 +95,7 @@
     rows = lax.broadcasted_iota(jnp.int32, table_ref.shape, 0)
     table = onehot(rows == src_ref[...])
     copy = send_blocks(
-        x_ref[...], table, select, out_ref, up_ref, down_ref, rows_ref, sem
+        order, x_ref[...], table, select, out_ref, up_ref, down_ref, rows_ref, sem
     )
     table_ref[...] = table
     select_ref[...] = select
@@ -208,7 +210,7 @@
     )
 
 
-def full_residual(local_ref, inc_ref, lower_ref, upper_ref, table_ref, weight_ref, rimcoup_ref, rimrow_ref):
+def full_residual(order, local_ref, inc_ref, lower_ref, upper_ref, table_ref, weight_ref, rimcoup_ref, rimrow_ref):
     rim = lower_ref.shape[0]
     blocks = local_ref.shape[1]
     rims = jnp.concatenate(
@@ -235,9 +237,10 @@
         edge = edge + pltpu.roll(edge, shift, 1)
         shift //= 2
     lane = lax.broadcasted_iota(jnp.int32, (BW, LANES), 1)
-    rest = inc_ref[:, 4]
+    inc = jnp.concatenate([inc_ref[i : i + 1] for i in np.argsort(order).tolist()], axis=0)
+    rest = inc[:, 4]
     rest = jnp.concatenate([rest[:, :, :CELLS], rest[:, :, CELLS:]], axis=1).reshape(-1, CELLS)
-    fringe = [inc_ref[:, 0:2].reshape(-1, LANES).T, inc_ref[:, 2:4].reshape(-1, LANES).T, rest.T]
+    fringe = [inc[:, 0:2].reshape(-1, LANES).T, inc[:, 2:4].reshape(-1, LANES).T, rest.T]
     total = local_ref[...] + pick(jnp.concatenate(fringe, axis=0) * weight_ref[...], table_ref[...])
     lower = total[:, :LANES] + jnp.where(lane < rim, edge, 0.0)
     upper = total[:, blocks - LANES :] + jnp.where(lane >= LANES - rim, edge, 0.0)
@@ -259,14 +262,14 @@
 
 
 def advance_kernel(
-    local_ref, inc_ref, lower_ref, upper_ref, across_ref, weight_ref, rimcoup_ref, rimrow_ref,
+    order, local_ref, inc_ref, lower_ref, upper_ref, across_ref, weight_ref, rimcoup_ref, rimrow_ref,
     diag_ref, x_ref, table_ref, select_ref,
     next_ref, norm_ref, out_ref, up_ref, down_ref, resid, diag, diag_sem, rows_ref, sem,
 ):
     fetch = pltpu.make_async_copy(diag_ref, diag, diag_sem)
     fetch.start()
     resid[...] = full_residual(
-        local_ref, inc_ref, lower_ref, upper_ref, across_ref, weight_ref, rimcoup_ref, rimrow_ref
+        order, local_ref, inc_ref, lower_ref, upper_ref, across_ref, weight_ref, rimcoup_ref, rimrow_ref
     )
     fetch.wait()
     for u in range(VARS):
@@ -279,18 +282,18 @@
             span = slice(u * CELLS + at, u * CELLS + at + PACK)
             next_ref[span, :] = x_ref[span, :] + STEP_CFL * total
     copy = send_blocks(
-        next_ref[...], table_ref[...], select_ref[...], out_ref, up_ref, down_ref, rows_ref, sem
+        order, next_ref[...], table_ref[...], select_ref[...], out_ref, up_ref, down_ref, rows_ref, sem
     )
     norm_ref[...] = lane_sums(resid[...])
     copy.wait()
 
 
 def residual_kernel(
-    local_ref, inc_ref, lower_ref, upper_ref, across_ref, weight_ref, rimcoup_ref, rimrow_ref, norm_ref,
+    order, local_ref, inc_ref, lower_ref, upper_ref, across_ref, weight_ref, rimcoup_ref, rimrow_ref, norm_ref,
     resid_ref, sums_ref,
 ):
     resid = full_residual(
-        local_ref, inc_ref, lower_ref, upper_ref, across_ref, weight_ref, rimcoup_ref, rimrow_ref
+        order, local_ref, inc_ref, lower_ref, upper_ref, across_ref, weight_ref, rimcoup_ref, rimrow_ref
     )
     resid_ref[...] = resid
     both = jnp.concatenate([norm_ref[...], lane_sums(resid)], axis=0)
@@ -340,6 +343,14 @@
     )
 
 
+def message_order(bodies, peers):
+    middle = peers // 2
+    far_first = sorted(range(peers), key=lambda k: -abs(2 * k + 1 - peers))
+    order = [b * peers + k for b in reversed(range(bodies)) for k in far_first]
+    order.remove(middle)
+    return [middle, *order]
+
+
 def shards(
     psi_init, source, coupling, diag_inv, neighbours, seam_perm, fringe_src, fringe_dst, fringe_weight
 ):
@@ -349,6 +360,7 @@
     fringe = fringe_src.shape[1]
     peers = lax.axis_size("blk")
     devices = lax.axis_size("body") * peers
+    order = message_order(devices // peers, peers)
     up = [(i, (i + 1) % peers) for i in range(peers)]
     down = [(j, i) for i, j in up]
     here = functools.partial(pltpu.with_memory_space_constraint, memory_space=pltpu.HBM)
@@ -365,7 +377,7 @@
     size = 4 * BW * blocks
 
     donors = call(
-        donors_kernel,
+        functools.partial(donors_kernel, order),
         [VMEM, VMEM, SMEM],
         sent + [bf16(blocks, fringe), bf16(2 * LANES, LANES), state],
         4 * BW * blocks * fringe,
@@ -401,7 +413,7 @@
     )
     local = call(functools.partial(local_kernel, rim), [VMEM, VMEM, hbm, hbm], state, **local_more)
     advance = call(
-        advance_kernel,
+        functools.partial(advance_kernel, order),
         [VMEM] * 8 + [hbm] + [VMEM] * 3,
         [state, f32(1, LANES)] + sent,
         8 * BW * blocks * fringe,
@@ -415,7 +427,7 @@
         + rows_scratch,
     )
     residual = call(
-        residual_kernel,
+        functools.partial(residual_kernel, order),
         [VMEM] * 9,
         [state, f32(devices, 2, LANES)],
         4 * BW * blocks * fringe,
@@ -432,8 +444,17 @@
         3 * size,
     )
 
+    everyone = functools.partial(
+        lax.all_to_all,
+        axis_name=("body", "blk"),
+        split_axis=0,
+        concat_axis=0,
+        tiled=True,
+        axis_index_groups=[order],
+    )
+
     def exchange(rows, to_up, to_down):
-        rows = lax.all_to_all(rows, ("body", "blk"), split_axis=0, concat_axis=0, tiled=True)
+        rows = everyone(rows)
         return rows, lax.ppermute(to_up, "blk", up), lax.ppermute(to_down, "blk", down)
 
     *out, table, select, x_here = donors(x, here(fringe_src), here(seam_perm))
@@ -446,7 +467,7 @@
     arrived = exchange(*out)
     part = local(x, nbr, coup, source_t)
     resid, sums = residual(part, *arrived, *across, norm)
-    sums = lax.all_to_all(sums, ("body", "blk"), split_axis=0, concat_axis=0, tiled=True)
+    sums = everyone(sums)
     update, resid = direction(diag, resid)
     x = finish(sums, x, update)
     return (x.T, resid.T)

time: 53.6 us -> 52.6 us (0.981)
  waiting for transfers between devices: 7.38 us -> 5.6 us
  starting transfers between devices: 22 us -> 22.7 us
    all_to_all x3, waiting for transfers between devices: 7.02 us -> 5.26 us  [the longest x1 4.65 us: shards(): sums = everyone(sums)]
    all_to_all x3, starting transfers between devices: 12.5 us -> 13.2 us  [the longest x2 10.2 us: exchange(): rows = everyone(rows)]
  transfers between devices with their start and end apart: 7 -> 7, of which waited for: 5 -> 5; matrix products, arithmetic and copies ran while one was open for 0% -> 0% of each run, Pallas kernels for 28% -> 29%
where the time goes in v14:
time: 52.6 us; the launch traced here: 52.1 us
  Pallas kernels  23.1 us (44%)
  starting transfers between devices  22.7 us (43%)
  waiting for transfers between devices  5.6 us (11%)
  between operations  0.69 us (1%)
    all_to_all x2, starting transfers between devices, exchange(): rows = everyone(rows)  10.2 us
    pallas_call x1, Pallas kernels, shards(): first_local(x_here, nbr, coup, source_t, here(fringe_dst), here(fringe_we...  6.26 us
    pallas_call x1, Pallas kernels, shards(): part = local(x, nbr, coup, source_t)  6.15 us
    ppermute x2, starting transfers between devices, exchange(): lax.ppermute(to_down, 'blk', down)  5.92 us
    all_to_all x1, waiting for transfers between devices, shards(): sums = everyone(sums)  4.65 us
    ppermute x2, starting transfers between devices, exchange(): lax.ppermute(to_up, 'blk', up)  3.64 us
    pallas_call x1, Pallas kernels, shards(): advance(part, *arrived, *across, diag, x_here, table, select)  3.23 us
    all_to_all x1, starting transfers between devices, shards(): sums = everyone(sums)  2.94 us
  transfers between devices with their start and end apart: 7, of which 5 were waited for; matrix products, arithmetic and copies ran while one was open for 0% of the time, Pallas kernels for 29%

profile of v14, /device:TPU:0, one launch (start us, length us, event | category | flops | bytes accessed | tf_op | source)
XLA Modules:
  0.0 52.1 jit_solution(3304215827849044174)
XLA Ops:
  0.6 2.4 %shard_map.104 = (f32[32,5,4,128]{3,2,1,0:T(4,128)}, f32[8,320]{1,0:T(8,128)S(1)}, f32[8,320]{1,0:T(8,128)S(1)}, bf16[512,256]{1,0:T(8,128)(2,1)S(1)}, bf16[256,...) custom-call(f32[320,512]{1,0:T(8,128)} %bitcast.13, s32[1,256]{1,0:T(1,128)} %src_ref.1, s32[1,8]{1,0:T(1,128)} %perm_ref.1), custom_call_target="tpu_custom_call" | custom-call | flops 167772160 | bytes 1310720 | tf_op jit(solution)/shard_map/pallas_call | solution.py:460
  3.0 7.3 %all-to-all-start = ((f32[32,5,4,128]{3,2,1,0:T(4,128)}), f32[32,5,4,128]{3,2,1,0:T(4,128)S(1)}, u32[]{:S(2)}, u32[]{:S(2)}) async-start(f32[32,5,4,128]{3,2,1,0:T(4,128)} %get-tuple-element.24), calls=%async_computation | async-start | bytes 655360 | tf_op jit(solution)/shard_map/all_to_all | solution.py:457
  10.4 1.8 %collective-permute-start = (f32[8,320]{1,0:T(8,128)S(1)}, f32[8,320]{1,0:T(8,128)S(1)}, u32[]{:S(2)}, u32[]{:S(2)}) collective-permute-start(f32[8,320]{1,0:T(8,128)S(1)} %get-tuple-element.25), channel_id=1, source_target_pairs={{0,1},{1,2},{2,3},{3,4},{4,5},{5,6},{6,7},{7,0},{8,9},{9,10},{10,1... | collective-permute-start | bytes 30728 | tf_op jit(solution)/shard_map/ppermute | solution.py:458
  12.2 3.0 %collective-permute-start.1 = (f32[8,320]{1,0:T(8,128)S(1)}, f32[8,320]{1,0:T(8,128)S(1)}, u32[]{:S(2)}, u32[]{:S(2)}) collective-permute-start(f32[8,320]{1,0:T(8,128)S(1)} %get-tuple-element.26), channel_id=1, source_target_pairs={{1,0},{2,1},{3,2},{4,3},{5,4},{6,5},{7,6},{0,7},{9,8},{10,9},{11,1... | collective-permute-start | bytes 30728 | tf_op jit(solution)/shard_map/ppermute | solution.py:458
  15.1 6.3 %shard_map.105 = (f32[320,512]{1,0:T(8,128)S(1)}, bf16[5,320,128]{2,1,0:T(8,128)(2,1)S(1)}, s32[16,128]{1,0:T(8,128)S(1)}, bf16[256,512]{1,0:T(8,128)(2,1)S(1)}, f32[1,256]{1,0:T(1,128)S(1)}) custom-call(f32[320,512]{1,0:T(8,128)S(1)} %get-tuple-element.22.x_ref, s32[6,512]{1,0:T(8,128)} %bitcast.15, bf16[6,5,320,512]{3,2,1,0:T(8,128)(2,1)} %bitcast.7, ...), custom_call_target="tpu_custom_call" | custom-call | flops 1006632960 | bytes 12451840 | tf_op jit(solution)/shard_map/pallas_call | solution.py:462
  21.4 0.1 collective-permute-done.lower_ref
  21.5 0.0 collective-permute-done.1.upper_ref
  21.5 0.3 all-to-all-done.inc_ref
  21.8 3.2 %shard_map.106 = (f32[320,512]{1,0:T(8,128)S(1)}, f32[1,128]{1,0:T(1,128)S(1)}, f32[32,5,4,128]{3,2,1,0:T(4,128)}, f32[8,320]{1,0:T(8,128)S(1)}, f32[8,320]{1,0:T(8,128)S(1)}) custom-call(f32[320,512]{1,0:T(8,128)S(1)} %get-tuple-element.23.local_ref, f32[32,5,4,128]{3,2,1,0:T(4,128)S(1)} %all-to-all-done.inc_ref, ...), custom_call_target="tpu_custom_call" | custom-call | flops 335544320 | bytes 4259840 | tf_op jit(solution)/shard_map/pallas_call | solution.py:466
  25.1 2.9 %all-to-all-start.1 = ((f32[32,5,4,128]{3,2,1,0:T(4,128)}), f32[32,5,4,128]{3,2,1,0:T(4,128)S(1)}, u32[]{:S(2)}, u32[]{:S(2)}) async-start(f32[32,5,4,128]{3,2,1,0:T(4,128)} %get-tuple-element.34), calls=%async_computation.1 | async-start | bytes 655360 | tf_op jit(solution)/shard_map/all_to_all | solution.py:457
  28.0 1.8 %collective-permute-start.2 = (f32[8,320]{1,0:T(8,128)S(1)}, f32[8,320]{1,0:T(8,128)S(1)}, u32[]{:S(2)}, u32[]{:S(2)}) collective-permute-start(f32[8,320]{1,0:T(8,128)S(1)} %get-tuple-element.35), channel_id=1, source_target_pairs={{0,1},{1,2},{2,3},{3,4},{4,5},{5,6},{6,7},{7,0},{8,9},{9,10},{10,1... | collective-permute-start | bytes 30728 | tf_op jit(solution)/shard_map/ppermute | solution.py:458
  29.8 3.0 %collective-permute-start.3 = (f32[8,320]{1,0:T(8,128)S(1)}, f32[8,320]{1,0:T(8,128)S(1)}, u32[]{:S(2)}, u32[]{:S(2)}) collective-permute-start(f32[8,320]{1,0:T(8,128)S(1)} %get-tuple-element.36), channel_id=1, source_target_pairs={{1,0},{2,1},{3,2},{4,3},{5,4},{6,5},{7,6},{0,7},{9,8},{10,9},{11,1... | collective-permute-start | bytes 30728 | tf_op jit(solution)/shard_map/ppermute | solution.py:458
  32.8 6.1 %shard_map.107.local_ref = f32[320,512]{1,0:T(8,128)S(1)} custom-call(f32[320,512]{1,0:T(8,128)S(1)} %get-tuple-element.33.x_ref, s32[6,512]{1,0:T(8,128)} %bitcast.16, bf16[6,5,320,512]{3,2,1,0:T(8,128)(2,1)} %bitcast.8, f32[320,512]{1,0:T(8,128)} %bitcast.12), custom_call_target="tpu_custom_call" | custom-call | flops 1006632960 | bytes 12451840 | tf_op jit(solution)/shard_map/pallas_call | solution.py:468
  39.0 0.2 collective-permute-done.2.lower_ref
  39.2 0.0 collective-permute-done.3.upper_ref
  39.2 0.3 all-to-all-done.1.inc_ref
  39.5 1.3 %shard_map.108 = (f32[320,512]{1,0:T(8,128)S(1)}, f32[32,2,128]{2,1,0:T(2,128)}) custom-call(f32[320,512]{1,0:T(8,128)S(1)} %shard_map.107.local_ref, f32[32,5,4,128]{3,2,1,0:T(4,128)S(1)} %all-to-all-done.1.inc_ref, f32[8,320]{1,0:T(8,128)S(1)} %collective-permute-done.2.lower_ref, f32[8,320]{1,0:T(8,128)S(1)} %collective-permute-done.3.upper_ref, ...), custom_call_target="tpu_custom_call" | custom-call | flops 167772160 | bytes 1966080 | tf_op jit(solution)/shard_map/pallas_call | solution.py:469
  40.8 2.9 %all-to-all-start.2 = ((f32[32,2,128]{2,1,0:T(2,128)}), f32[32,2,128]{2,1,0:T(2,128)S(1)}, u32[]{:S(2)}, u32[]{:S(2)}) async-start(f32[32,2,128]{2,1,0:T(2,128)} %get-tuple-element.38), calls=%async_computation.2 | async-start | bytes 65536 | tf_op jit(solution)/shard_map/all_to_all | solution.py:470
  43.7 2.6 %shard_map.109 = (f32[320,512]{1,0:T(8,128)S(1)}, f32[320,512]{1,0:T(8,128)}) custom-call(bf16[5,320,512]{2,1,0:T(8,128)(2,1)} %bitcast.10, f32[320,512]{1,0:T(8,128)S(1)} %get-tuple-element.39.resid_ref), custom_call_target="tpu_custom_call" | custom-call | flops 1638400 | bytes 2949120 | tf_op jit(solution)/shard_map/pallas_call | solution.py:471
  46.4 4.6 %all-to-all-done.2.sums_ref = f32[32,2,128]{2,1,0:T(2,128)S(1)} async-done(((f32[32,2,128]{2,1,0:T(2,128)}), f32[32,2,128]{2,1,0:T(2,128)S(1)}, u32[]{:S(2)}, u32[]{:S(2)}) %all-to-all-start.2) | async-done | bytes 32800 | tf_op jit(solution)/shard_map/all_to_all | solution.py:470
  51.0 1.1 %shard_map.110 = f32[320,512]{1,0:T(8,128)} custom-call(f32[32,2,128]{2,1,0:T(2,128)S(1)} %all-to-all-done.2.sums_ref, f32[320,512]{1,0:T(8,128)S(1)} %get-tuple-element.33.x_ref, f32[320,512]{1,0:T(8,128)S(1)} %get-tuple-element.40.update_ref), custom_call_target="tpu_custom_call" | custom-call | flops 327680 | bytes 1966080 | tf_op jit(solution)/shard_map/pallas_call | solution.py:472
Async XLA Ops:
  3.0 18.8 %all-to-all-start = ((f32[32,5,4,128]{3,2,1,0:T(4,128)}), f32[32,5,4,128]{3,2,1,0:T(4,128)S(1)}, u32[]{:S(2)}, u32[]{:S(2)}) async-start(f32[32,5,4,128]{3,2,1,0:T(4,128)} %get-tuple-element.24), calls=%async_computation | async-start | bytes 655360 | tf_op jit(solution)/shard_map/all_to_all | solution.py:457
  10.4 11.2 %collective-permute-start = (f32[8,320]{1,0:T(8,128)S(1)}, f32[8,320]{1,0:T(8,128)S(1)}, u32[]{:S(2)}, u32[]{:S(2)}) collective-permute-start(f32[8,320]{1,0:T(8,128)S(1)} %get-tuple-element.25), channel_id=1, source_target_pairs={{0,1},{1,2},{2,3},{3,4},{4,5},{5,6},{6,7},{7,0},{8,9},{9,10},{10,1... | collective-permute-start | bytes 30728 | tf_op jit(solution)/shard_map/ppermute | solution.py:458
  12.2 9.3 %collective-permute-start.1 = (f32[8,320]{1,0:T(8,128)S(1)}, f32[8,320]{1,0:T(8,128)S(1)}, u32[]{:S(2)}, u32[]{:S(2)}) collective-permute-start(f32[8,320]{1,0:T(8,128)S(1)} %get-tuple-element.26), channel_id=1, source_target_pairs={{1,0},{2,1},{3,2},{4,3},{5,4},{6,5},{7,6},{0,7},{9,8},{10,9},{11,1... | collective-permute-start | bytes 30728 | tf_op jit(solution)/shard_map/ppermute | solution.py:458
  25.1 14.4 %all-to-all-start.1 = ((f32[32,5,4,128]{3,2,1,0:T(4,128)}), f32[32,5,4,128]{3,2,1,0:T(4,128)S(1)}, u32[]{:S(2)}, u32[]{:S(2)}) async-start(f32[32,5,4,128]{3,2,1,0:T(4,128)} %get-tuple-element.34), calls=%async_computation.1 | async-start | bytes 655360 | tf_op jit(solution)/shard_map/all_to_all | solution.py:457
  28.0 11.2 %collective-permute-start.2 = (f32[8,320]{1,0:T(8,128)S(1)}, f32[8,320]{1,0:T(8,128)S(1)}, u32[]{:S(2)}, u32[]{:S(2)}) collective-permute-start(f32[8,320]{1,0:T(8,128)S(1)} %get-tuple-element.35), channel_id=1, source_target_pairs={{0,1},{1,2},{2,3},{3,4},{4,5},{5,6},{6,7},{7,0},{8,9},{9,10},{10,1... | collective-permute-start | bytes 30728 | tf_op jit(solution)/shard_map/ppermute | solution.py:458
  29.8 9.3 %collective-permute-start.3 = (f32[8,320]{1,0:T(8,128)S(1)}, f32[8,320]{1,0:T(8,128)S(1)}, u32[]{:S(2)}, u32[]{:S(2)}) collective-permute-start(f32[8,320]{1,0:T(8,128)S(1)} %get-tuple-element.36), channel_id=1, source_target_pairs={{1,0},{2,1},{3,2},{4,3},{5,4},{6,5},{7,6},{0,7},{9,8},{10,9},{11,1... | collective-permute-start | bytes 30728 | tf_op jit(solution)/shard_map/ppermute | solution.py:458
  40.8 10.2 %all-to-all-start.2 = ((f32[32,2,128]{2,1,0:T(2,128)}), f32[32,2,128]{2,1,0:T(2,128)S(1)}, u32[]{:S(2)}, u32[]{:S(2)}) async-start(f32[32,2,128]{2,1,0:T(2,128)} %get-tuple-element.38), calls=%async_computation.2 | async-start | bytes 65536 | tf_op jit(solution)/shard_map/all_to_all | solution.py:470

commit v15 on v14

--- a/solution.py
+++ b/solution.py
@@ -344,11 +344,7 @@
 
 
 def message_order(bodies, peers):
-    middle = peers // 2
-    far_first = sorted(range(peers), key=lambda k: -abs(2 * k + 1 - peers))
-    order = [b * peers + k for b in reversed(range(bodies)) for k in far_first]
-    order.remove(middle)
-    return [middle, *order]
+    return sorted(range(bodies * peers), key=lambda i: i * 0.6180339887 % 1.0)
 
 
 def shards(

time: 52.6 us -> 53.7 us (1.021)
  waiting for transfers between devices: 5.6 us -> 7.41 us
  starting transfers between devices: 22.7 us -> 22 us
    all_to_all x2, waiting for transfers between devices: 0.62 us -> 2.47 us  [exchange(): rows = everyone(rows)]
  transfers between devices with their start and end apart: 7 -> 7, of which waited for: 5 -> 5; matrix products, arithmetic and copies ran while one was open for 0% -> 0% of each run, Pallas kernels for 29% -> 28%
where the time goes in v15:
time: 53.7 us; the launch traced here: 53.2 us
  Pallas kernels  23.1 us (43%)
  starting transfers between devices  22 us (41%)
  waiting for transfers between devices  7.41 us (14%)
  between operations  0.69 us (1%)
    all_to_all x2, starting transfers between devices, exchange(): rows = everyone(rows)  9.91 us
    pallas_call x1, Pallas kernels, shards(): first_local(x_here, nbr, coup, source_t, here(fringe_dst), here(fringe_we...  6.25 us
    pallas_call x1, Pallas kernels, shards(): part = local(x, nbr, coup, source_t)  6.15 us
    ppermute x2, starting transfers between devices, exchange(): lax.ppermute(to_down, 'blk', down)  6.04 us
    all_to_all x1, waiting for transfers between devices, shards(): sums = everyone(sums)  4.58 us
    ppermute x2, starting transfers between devices, exchange(): lax.ppermute(to_up, 'blk', up)  3.51 us
    pallas_call x1, Pallas kernels, shards(): advance(part, *arrived, *across, diag, x_here, table, select)  3.24 us
    pallas_call x1, Pallas kernels, shards(): update, resid = direction(diag, resid)  2.64 us
  transfers between devices with their start and end apart: 7, of which 5 were waited for; matrix products, arithmetic and copies ran while one was open for 0% of the time, Pallas kernels for 28%

profile of v15, /device:TPU:0, one launch (start us, length us, event | category | flops | bytes accessed | tf_op | source)
XLA Modules:
  0.0 53.2 jit_solution(4806868203655347974)
XLA Ops:
  0.6 2.4 %shard_map.104 = (f32[32,5,4,128]{3,2,1,0:T(4,128)}, f32[8,320]{1,0:T(8,128)S(1)}, f32[8,320]{1,0:T(8,128)S(1)}, bf16[512,256]{1,0:T(8,128)(2,1)S(1)}, bf16[256,...) custom-call(f32[320,512]{1,0:T(8,128)} %bitcast.13, s32[1,256]{1,0:T(1,128)} %src_ref.1, s32[1,8]{1,0:T(1,128)} %perm_ref.1), custom_call_target="tpu_custom_call" | custom-call | flops 167772160 | bytes 1310720 | tf_op jit(solution)/shard_map/pallas_call | solution.py:456
  3.0 7.3 %all-to-all-start = ((f32[32,5,4,128]{3,2,1,0:T(4,128)}), f32[32,5,4,128]{3,2,1,0:T(4,128)S(1)}, u32[]{:S(2)}, u32[]{:S(2)}) async-start(f32[32,5,4,128]{3,2,1,0:T(4,128)} %get-tuple-element.24), calls=%async_computation | async-start | bytes 655360 | tf_op jit(solution)/shard_map/all_to_all | solution.py:453
  10.4 1.8 %collective-permute-start = (f32[8,320]{1,0:T(8,128)S(1)}, f32[8,320]{1,0:T(8,128)S(1)}, u32[]{:S(2)}, u32[]{:S(2)}) collective-permute-start(f32[8,320]{1,0:T(8,128)S(1)} %get-tuple-element.25), channel_id=1, source_target_pairs={{0,1},{1,2},{2,3},{3,4},{4,5},{5,6},{6,7},{7,0},{8,9},{9,10},{10,1... | collective-permute-start | bytes 30728 | tf_op jit(solution)/shard_map/ppermute | solution.py:454
  12.2 3.0 %collective-permute-start.1 = (f32[8,320]{1,0:T(8,128)S(1)}, f32[8,320]{1,0:T(8,128)S(1)}, u32[]{:S(2)}, u32[]{:S(2)}) collective-permute-start(f32[8,320]{1,0:T(8,128)S(1)} %get-tuple-element.26), channel_id=1, source_target_pairs={{1,0},{2,1},{3,2},{4,3},{5,4},{6,5},{7,6},{0,7},{9,8},{10,9},{11,1... | collective-permute-start | bytes 30728 | tf_op jit(solution)/shard_map/ppermute | solution.py:454
  15.1 6.3 %shard_map.105 = (f32[320,512]{1,0:T(8,128)S(1)}, bf16[5,320,128]{2,1,0:T(8,128)(2,1)S(1)}, s32[16,128]{1,0:T(8,128)S(1)}, bf16[256,512]{1,0:T(8,128)(2,1)S(1)}, f32[1,256]{1,0:T(1,128)S(1)}) custom-call(f32[320,512]{1,0:T(8,128)S(1)} %get-tuple-element.22.x_ref, s32[6,512]{1,0:T(8,128)} %bitcast.15, bf16[6,5,320,512]{3,2,1,0:T(8,128)(2,1)} %bitcast.7, ...), custom_call_target="tpu_custom_call" | custom-call | flops 1006632960 | bytes 12451840 | tf_op jit(solution)/shard_map/pallas_call | solution.py:458
  21.4 0.1 collective-permute-done.lower_ref
  21.5 0.0 collective-permute-done.1.upper_ref
  21.5 1.2 %all-to-all-done.inc_ref = f32[32,5,4,128]{3,2,1,0:T(4,128)S(1)} async-done(((f32[32,5,4,128]{3,2,1,0:T(4,128)}), f32[32,5,4,128]{3,2,1,0:T(4,128)S(1)}, u32[]{:S(2)}, u32[]{:S(2)}) %all-to-all-start) | async-done | bytes 327712 | tf_op jit(solution)/shard_map/all_to_all | solution.py:453
  22.8 3.2 %shard_map.106 = (f32[320,512]{1,0:T(8,128)S(1)}, f32[1,128]{1,0:T(1,128)S(1)}, f32[32,5,4,128]{3,2,1,0:T(4,128)}, f32[8,320]{1,0:T(8,128)S(1)}, f32[8,320]{1,0:T(8,128)S(1)}) custom-call(f32[320,512]{1,0:T(8,128)S(1)} %get-tuple-element.23.local_ref, f32[32,5,4,128]{3,2,1,0:T(4,128)S(1)} %all-to-all-done.inc_ref, ...), custom_call_target="tpu_custom_call" | custom-call | flops 335544320 | bytes 4259840 | tf_op jit(solution)/shard_map/pallas_call | solution.py:462
  26.0 2.6 %all-to-all-start.1 = ((f32[32,5,4,128]{3,2,1,0:T(4,128)}), f32[32,5,4,128]{3,2,1,0:T(4,128)S(1)}, u32[]{:S(2)}, u32[]{:S(2)}) async-start(f32[32,5,4,128]{3,2,1,0:T(4,128)} %get-tuple-element.34), calls=%async_computation.1 | async-start | bytes 655360 | tf_op jit(solution)/shard_map/all_to_all | solution.py:453
  28.6 1.7 %collective-permute-start.2 = (f32[8,320]{1,0:T(8,128)S(1)}, f32[8,320]{1,0:T(8,128)S(1)}, u32[]{:S(2)}, u32[]{:S(2)}) collective-permute-start(f32[8,320]{1,0:T(8,128)S(1)} %get-tuple-element.35), channel_id=1, source_target_pairs={{0,1},{1,2},{2,3},{3,4},{4,5},{5,6},{6,7},{7,0},{8,9},{9,10},{10,1... | collective-permute-start | bytes 30728 | tf_op jit(solution)/shard_map/ppermute | solution.py:454
  30.3 3.1 %collective-permute-start.3 = (f32[8,320]{1,0:T(8,128)S(1)}, f32[8,320]{1,0:T(8,128)S(1)}, u32[]{:S(2)}, u32[]{:S(2)}) collective-permute-start(f32[8,320]{1,0:T(8,128)S(1)} %get-tuple-element.36), channel_id=1, source_target_pairs={{1,0},{2,1},{3,2},{4,3},{5,4},{6,5},{7,6},{0,7},{9,8},{10,9},{11,1... | collective-permute-start | bytes 30728 | tf_op jit(solution)/shard_map/ppermute | solution.py:454
  33.4 6.1 %shard_map.107.local_ref = f32[320,512]{1,0:T(8,128)S(1)} custom-call(f32[320,512]{1,0:T(8,128)S(1)} %get-tuple-element.33.x_ref, s32[6,512]{1,0:T(8,128)} %bitcast.16, bf16[6,5,320,512]{3,2,1,0:T(8,128)(2,1)} %bitcast.8, f32[320,512]{1,0:T(8,128)} %bitcast.12), custom_call_target="tpu_custom_call" | custom-call | flops 1006632960 | bytes 12451840 | tf_op jit(solution)/shard_map/pallas_call | solution.py:464
  39.6 0.2 collective-permute-done.2.lower_ref
  39.8 0.0 collective-permute-done.3.upper_ref
  39.8 1.2 %all-to-all-done.1.inc_ref = f32[32,5,4,128]{3,2,1,0:T(4,128)S(1)} async-done(((f32[32,5,4,128]{3,2,1,0:T(4,128)}), f32[32,5,4,128]{3,2,1,0:T(4,128)S(1)}, u32[]{:S(2)}, u32[]{:S(2)}) %all-to-all-start.1) | async-done | bytes 327712 | tf_op jit(solution)/shard_map/all_to_all | solution.py:453
  41.0 1.3 %shard_map.108 = (f32[320,512]{1,0:T(8,128)S(1)}, f32[32,2,128]{2,1,0:T(2,128)}) custom-call(f32[320,512]{1,0:T(8,128)S(1)} %shard_map.107.local_ref, f32[32,5,4,128]{3,2,1,0:T(4,128)S(1)} %all-to-all-done.1.inc_ref, f32[8,320]{1,0:T(8,128)S(1)} %collective-permute-done.2.lower_ref, f32[8,320]{1,0:T(8,128)S(1)} %collective-permute-done.3.upper_ref, ...), custom_call_target="tpu_custom_call" | custom-call | flops 167772160 | bytes 1966080 | tf_op jit(solution)/shard_map/pallas_call | solution.py:465
  42.3 2.6 %all-to-all-start.2 = ((f32[32,2,128]{2,1,0:T(2,128)}), f32[32,2,128]{2,1,0:T(2,128)S(1)}, u32[]{:S(2)}, u32[]{:S(2)}) async-start(f32[32,2,128]{2,1,0:T(2,128)} %get-tuple-element.38), calls=%async_computation.2 | async-start | bytes 65536 | tf_op jit(solution)/shard_map/all_to_all | solution.py:466
  44.9 2.6 %shard_map.109 = (f32[320,512]{1,0:T(8,128)S(1)}, f32[320,512]{1,0:T(8,128)}) custom-call(bf16[5,320,512]{2,1,0:T(8,128)(2,1)} %bitcast.10, f32[320,512]{1,0:T(8,128)S(1)} %get-tuple-element.39.resid_ref), custom_call_target="tpu_custom_call" | custom-call | flops 1638400 | bytes 2949120 | tf_op jit(solution)/shard_map/pallas_call | solution.py:467
  47.5 4.6 %all-to-all-done.2.sums_ref = f32[32,2,128]{2,1,0:T(2,128)S(1)} async-done(((f32[32,2,128]{2,1,0:T(2,128)}), f32[32,2,128]{2,1,0:T(2,128)S(1)}, u32[]{:S(2)}, u32[]{:S(2)}) %all-to-all-start.2) | async-done | bytes 32800 | tf_op jit(solution)/shard_map/all_to_all | solution.py:466
  52.1 1.1 %shard_map.110 = f32[320,512]{1,0:T(8,128)} custom-call(f32[32,2,128]{2,1,0:T(2,128)S(1)} %all-to-all-done.2.sums_ref, f32[320,512]{1,0:T(8,128)S(1)} %get-tuple-element.33.x_ref, f32[320,512]{1,0:T(8,128)S(1)} %get-tuple-element.40.update_ref), custom_call_target="tpu_custom_call" | custom-call | flops 327680 | bytes 1966080 | tf_op jit(solution)/shard_map/pallas_call | solution.py:468
Async XLA Ops:
  3.0 19.7 %all-to-all-start = ((f32[32,5,4,128]{3,2,1,0:T(4,128)}), f32[32,5,4,128]{3,2,1,0:T(4,128)S(1)}, u32[]{:S(2)}, u32[]{:S(2)}) async-start(f32[32,5,4,128]{3,2,1,0:T(4,128)} %get-tuple-element.24), calls=%async_computation | async-start | bytes 655360 | tf_op jit(solution)/shard_map/all_to_all | solution.py:453
  10.4 11.2 %collective-permute-start = (f32[8,320]{1,0:T(8,128)S(1)}, f32[8,320]{1,0:T(8,128)S(1)}, u32[]{:S(2)}, u32[]{:S(2)}) collective-permute-start(f32[8,320]{1,0:T(8,128)S(1)} %get-tuple-element.25), channel_id=1, source_target_pairs={{0,1},{1,2},{2,3},{3,4},{4,5},{5,6},{6,7},{7,0},{8,9},{9,10},{10,1... | collective-permute-start | bytes 30728 | tf_op jit(solution)/shard_map/ppermute | solution.py:454
  12.2 9.3 %collective-permute-start.1 = (f32[8,320]{1,0:T(8,128)S(1)}, f32[8,320]{1,0:T(8,128)S(1)}, u32[]{:S(2)}, u32[]{:S(2)}) collective-permute-start(f32[8,320]{1,0:T(8,128)S(1)} %get-tuple-element.26), channel_id=1, source_target_pairs={{1,0},{2,1},{3,2},{4,3},{5,4},{6,5},{7,6},{0,7},{9,8},{10,9},{11,1... | collective-permute-start | bytes 30728 | tf_op jit(solution)/shard_map/ppermute | solution.py:454
  26.0 15.0 %all-to-all-start.1 = ((f32[32,5,4,128]{3,2,1,0:T(4,128)}), f32[32,5,4,128]{3,2,1,0:T(4,128)S(1)}, u32[]{:S(2)}, u32[]{:S(2)}) async-start(f32[32,5,4,128]{3,2,1,0:T(4,128)} %get-tuple-element.34), calls=%async_computation.1 | async-start | bytes 655360 | tf_op jit(solution)/shard_map/all_to_all | solution.py:453
  28.6 11.2 %collective-permute-start.2 = (f32[8,320]{1,0:T(8,128)S(1)}, f32[8,320]{1,0:T(8,128)S(1)}, u32[]{:S(2)}, u32[]{:S(2)}) collective-permute-start(f32[8,320]{1,0:T(8,128)S(1)} %get-tuple-element.35), channel_id=1, source_target_pairs={{0,1},{1,2},{2,3},{3,4},{4,5},{5,6},{6,7},{7,0},{8,9},{9,10},{10,1... | collective-permute-start | bytes 30728 | tf_op jit(solution)/shard_map/ppermute | solution.py:454
  30.3 9.5 %collective-permute-start.3 = (f32[8,320]{1,0:T(8,128)S(1)}, f32[8,320]{1,0:T(8,128)S(1)}, u32[]{:S(2)}, u32[]{:S(2)}) collective-permute-start(f32[8,320]{1,0:T(8,128)S(1)} %get-tuple-element.36), channel_id=1, source_target_pairs={{1,0},{2,1},{3,2},{4,3},{5,4},{6,5},{7,6},{0,7},{9,8},{10,9},{11,1... | collective-permute-start | bytes 30728 | tf_op jit(solution)/shard_map/ppermute | solution.py:454
  42.3 9.8 %all-to-all-start.2 = ((f32[32,2,128]{2,1,0:T(2,128)}), f32[32,2,128]{2,1,0:T(2,128)S(1)}, u32[]{:S(2)}, u32[]{:S(2)}) async-start(f32[32,2,128]{2,1,0:T(2,128)} %get-tuple-element.38), calls=%async_computation.2 | async-start | bytes 65536 | tf_op jit(solution)/shard_map/all_to_all | solution.py:466

commit v16 on v14

--- a/solution.py
+++ b/solution.py
@@ -346,7 +346,7 @@
 def message_order(bodies, peers):
     middle = peers // 2
     far_first = sorted(range(peers), key=lambda k: -abs(2 * k + 1 - peers))
-    order = [b * peers + k for b in reversed(range(bodies)) for k in far_first]
+    order = [b * peers + k for b in range(bodies) for k in far_first]
     order.remove(middle)
     return [middle, *order]
 

time: 52.6 us -> 52.9 us (level)
  waiting for transfers between devices: 5.6 us -> 6.67 us
  starting transfers between devices: 22.7 us -> 22 us
    all_to_all x2, waiting for transfers between devices: 0.62 us -> 1.6 us  [exchange(): rows = everyone(rows)]
where the time goes in v16:
time: 52.9 us; the launch traced here: 52.5 us
  Pallas kernels  23.1 us (44%)
  starting transfers between devices  22 us (42%)
  waiting for transfers between devices  6.67 us (13%)
  between operations  0.69 us (1%)
    all_to_all x2, starting transfers between devices, exchange(): rows = everyone(rows)  9.91 us
    pallas_call x1, Pallas kernels, shards(): first_local(x_here, nbr, coup, source_t, here(fringe_dst), here(fringe_we...  6.26 us
    pallas_call x1, Pallas kernels, shards(): part = local(x, nbr, coup, source_t)  6.15 us
    ppermute x2, starting transfers between devices, exchange(): lax.ppermute(to_down, 'blk', down)  6.04 us
    all_to_all x1, waiting for transfers between devices, shards(): sums = everyone(sums)  4.72 us
    ppermute x2, starting transfers between devices, exchange(): lax.ppermute(to_up, 'blk', up)  3.51 us
    pallas_call x1, Pallas kernels, shards(): advance(part, *arrived, *across, diag, x_here, table, select)  3.24 us
    pallas_call x1, Pallas kernels, shards(): update, resid = direction(diag, resid)  2.64 us
  transfers between devices with their start and end apart: 7, of which 5 were waited for; matrix products, arithmetic and copies ran while one was open for 0% of the time, Pallas kernels for 29%

profile of v16, /device:TPU:0, one launch (start us, length us, event | category | flops | bytes accessed | tf_op | source)
XLA Modules:
  0.0 52.5 jit_solution(10322464814923737894)
XLA Ops:
  0.6 2.4 %shard_map.104 = (f32[32,5,4,128]{3,2,1,0:T(4,128)}, f32[8,320]{1,0:T(8,128)S(1)}, f32[8,320]{1,0:T(8,128)S(1)}, bf16[512,256]{1,0:T(8,128)(2,1)S(1)}, bf16[256,...) custom-call(f32[320,512]{1,0:T(8,128)} %bitcast.13, s32[1,256]{1,0:T(1,128)} %src_ref.1, s32[1,8]{1,0:T(1,128)} %perm_ref.1), custom_call_target="tpu_custom_call" | custom-call | flops 167772160 | bytes 1310720 | tf_op jit(solution)/shard_map/pallas_call | solution.py:460
  3.0 7.3 %all-to-all-start = ((f32[32,5,4,128]{3,2,1,0:T(4,128)}), f32[32,5,4,128]{3,2,1,0:T(4,128)S(1)}, u32[]{:S(2)}, u32[]{:S(2)}) async-start(f32[32,5,4,128]{3,2,1,0:T(4,128)} %get-tuple-element.24), calls=%async_computation | async-start | bytes 655360 | tf_op jit(solution)/shard_map/all_to_all | solution.py:457
  10.4 1.8 %collective-permute-start = (f32[8,320]{1,0:T(8,128)S(1)}, f32[8,320]{1,0:T(8,128)S(1)}, u32[]{:S(2)}, u32[]{:S(2)}) collective-permute-start(f32[8,320]{1,0:T(8,128)S(1)} %get-tuple-element.25), channel_id=1, source_target_pairs={{0,1},{1,2},{2,3},{3,4},{4,5},{5,6},{6,7},{7,0},{8,9},{9,10},{10,1... | collective-permute-start | bytes 30728 | tf_op jit(solution)/shard_map/ppermute | solution.py:458
  12.2 3.0 %collective-permute-start.1 = (f32[8,320]{1,0:T(8,128)S(1)}, f32[8,320]{1,0:T(8,128)S(1)}, u32[]{:S(2)}, u32[]{:S(2)}) collective-permute-start(f32[8,320]{1,0:T(8,128)S(1)} %get-tuple-element.26), channel_id=1, source_target_pairs={{1,0},{2,1},{3,2},{4,3},{5,4},{6,5},{7,6},{0,7},{9,8},{10,9},{11,1... | collective-permute-start | bytes 30728 | tf_op jit(solution)/shard_map/ppermute | solution.py:458
  15.1 6.3 %shard_map.105 = (f32[320,512]{1,0:T(8,128)S(1)}, bf16[5,320,128]{2,1,0:T(8,128)(2,1)S(1)}, s32[16,128]{1,0:T(8,128)S(1)}, bf16[256,512]{1,0:T(8,128)(2,1)S(1)}, f32[1,256]{1,0:T(1,128)S(1)}) custom-call(f32[320,512]{1,0:T(8,128)S(1)} %get-tuple-element.22.x_ref, s32[6,512]{1,0:T(8,128)} %bitcast.15, bf16[6,5,320,512]{3,2,1,0:T(8,128)(2,1)} %bitcast.7, ...), custom_call_target="tpu_custom_call" | custom-call | flops 1006632960 | bytes 12451840 | tf_op jit(solution)/shard_map/pallas_call | solution.py:462
  21.4 0.1 collective-permute-done.lower_ref
  21.5 0.0 collective-permute-done.1.upper_ref
  21.5 0.8 %all-to-all-done.inc_ref = f32[32,5,4,128]{3,2,1,0:T(4,128)S(1)} async-done(((f32[32,5,4,128]{3,2,1,0:T(4,128)}), f32[32,5,4,128]{3,2,1,0:T(4,128)S(1)}, u32[]{:S(2)}, u32[]{:S(2)}) %all-to-all-start) | async-done | bytes 327712 | tf_op jit(solution)/shard_map/all_to_all | solution.py:457
  22.3 3.2 %shard_map.106 = (f32[320,512]{1,0:T(8,128)S(1)}, f32[1,128]{1,0:T(1,128)S(1)}, f32[32,5,4,128]{3,2,1,0:T(4,128)}, f32[8,320]{1,0:T(8,128)S(1)}, f32[8,320]{1,0:T(8,128)S(1)}) custom-call(f32[320,512]{1,0:T(8,128)S(1)} %get-tuple-element.23.local_ref, f32[32,5,4,128]{3,2,1,0:T(4,128)S(1)} %all-to-all-done.inc_ref, ...), custom_call_target="tpu_custom_call" | custom-call | flops 335544320 | bytes 4259840 | tf_op jit(solution)/shard_map/pallas_call | solution.py:466
  25.6 2.6 %all-to-all-start.1 = ((f32[32,5,4,128]{3,2,1,0:T(4,128)}), f32[32,5,4,128]{3,2,1,0:T(4,128)S(1)}, u32[]{:S(2)}, u32[]{:S(2)}) async-start(f32[32,5,4,128]{3,2,1,0:T(4,128)} %get-tuple-element.34), calls=%async_computation.1 | async-start | bytes 655360 | tf_op jit(solution)/shard_map/all_to_all | solution.py:457
  28.2 1.7 %collective-permute-start.2 = (f32[8,320]{1,0:T(8,128)S(1)}, f32[8,320]{1,0:T(8,128)S(1)}, u32[]{:S(2)}, u32[]{:S(2)}) collective-permute-start(f32[8,320]{1,0:T(8,128)S(1)} %get-tuple-element.35), channel_id=1, source_target_pairs={{0,1},{1,2},{2,3},{3,4},{4,5},{5,6},{6,7},{7,0},{8,9},{9,10},{10,1... | collective-permute-start | bytes 30728 | tf_op jit(solution)/shard_map/ppermute | solution.py:458
  29.9 3.1 %collective-permute-start.3 = (f32[8,320]{1,0:T(8,128)S(1)}, f32[8,320]{1,0:T(8,128)S(1)}, u32[]{:S(2)}, u32[]{:S(2)}) collective-permute-start(f32[8,320]{1,0:T(8,128)S(1)} %get-tuple-element.36), channel_id=1, source_target_pairs={{1,0},{2,1},{3,2},{4,3},{5,4},{6,5},{7,6},{0,7},{9,8},{10,9},{11,1... | collective-permute-start | bytes 30728 | tf_op jit(solution)/shard_map/ppermute | solution.py:458
  33.0 6.2 %shard_map.107.local_ref = f32[320,512]{1,0:T(8,128)S(1)} custom-call(f32[320,512]{1,0:T(8,128)S(1)} %get-tuple-element.33.x_ref, s32[6,512]{1,0:T(8,128)} %bitcast.16, bf16[6,5,320,512]{3,2,1,0:T(8,128)(2,1)} %bitcast.8, f32[320,512]{1,0:T(8,128)} %bitcast.12), custom_call_target="tpu_custom_call" | custom-call | flops 1006632960 | bytes 12451840 | tf_op jit(solution)/shard_map/pallas_call | solution.py:468
  39.1 0.2 collective-permute-done.2.lower_ref
  39.3 0.0 collective-permute-done.3.upper_ref
  39.3 0.8 %all-to-all-done.1.inc_ref = f32[32,5,4,128]{3,2,1,0:T(4,128)S(1)} async-done(((f32[32,5,4,128]{3,2,1,0:T(4,128)}), f32[32,5,4,128]{3,2,1,0:T(4,128)S(1)}, u32[]{:S(2)}, u32[]{:S(2)}) %all-to-all-start.1) | async-done | bytes 327712 | tf_op jit(solution)/shard_map/all_to_all | solution.py:457
  40.1 1.3 %shard_map.108 = (f32[320,512]{1,0:T(8,128)S(1)}, f32[32,2,128]{2,1,0:T(2,128)}) custom-call(f32[320,512]{1,0:T(8,128)S(1)} %shard_map.107.local_ref, f32[32,5,4,128]{3,2,1,0:T(4,128)S(1)} %all-to-all-done.1.inc_ref, f32[8,320]{1,0:T(8,128)S(1)} %collective-permute-done.2.lower_ref, f32[8,320]{1,0:T(8,128)S(1)} %collective-permute-done.3.upper_ref, ...), custom_call_target="tpu_custom_call" | custom-call | flops 167772160 | bytes 1966080 | tf_op jit(solution)/shard_map/pallas_call | solution.py:469
  41.4 2.6 %all-to-all-start.2 = ((f32[32,2,128]{2,1,0:T(2,128)}), f32[32,2,128]{2,1,0:T(2,128)S(1)}, u32[]{:S(2)}, u32[]{:S(2)}) async-start(f32[32,2,128]{2,1,0:T(2,128)} %get-tuple-element.38), calls=%async_computation.2 | async-start | bytes 65536 | tf_op jit(solution)/shard_map/all_to_all | solution.py:470
  44.0 2.6 %shard_map.109 = (f32[320,512]{1,0:T(8,128)S(1)}, f32[320,512]{1,0:T(8,128)}) custom-call(bf16[5,320,512]{2,1,0:T(8,128)(2,1)} %bitcast.10, f32[320,512]{1,0:T(8,128)S(1)} %get-tuple-element.39.resid_ref), custom_call_target="tpu_custom_call" | custom-call | flops 1638400 | bytes 2949120 | tf_op jit(solution)/shard_map/pallas_call | solution.py:471
  46.7 4.7 %all-to-all-done.2.sums_ref = f32[32,2,128]{2,1,0:T(2,128)S(1)} async-done(((f32[32,2,128]{2,1,0:T(2,128)}), f32[32,2,128]{2,1,0:T(2,128)S(1)}, u32[]{:S(2)}, u32[]{:S(2)}) %all-to-all-start.2) | async-done | bytes 32800 | tf_op jit(solution)/shard_map/all_to_all | solution.py:470
  51.4 1.1 %shard_map.110 = f32[320,512]{1,0:T(8,128)} custom-call(f32[32,2,128]{2,1,0:T(2,128)S(1)} %all-to-all-done.2.sums_ref, f32[320,512]{1,0:T(8,128)S(1)} %get-tuple-element.33.x_ref, f32[320,512]{1,0:T(8,128)S(1)} %get-tuple-element.40.update_ref), custom_call_target="tpu_custom_call" | custom-call | flops 327680 | bytes 1966080 | tf_op jit(solution)/shard_map/pallas_call | solution.py:472
Async XLA Ops:
  3.0 19.3 %all-to-all-start = ((f32[32,5,4,128]{3,2,1,0:T(4,128)}), f32[32,5,4,128]{3,2,1,0:T(4,128)S(1)}, u32[]{:S(2)}, u32[]{:S(2)}) async-start(f32[32,5,4,128]{3,2,1,0:T(4,128)} %get-tuple-element.24), calls=%async_computation | async-start | bytes 655360 | tf_op jit(solution)/shard_map/all_to_all | solution.py:457
  10.4 11.2 %collective-permute-start = (f32[8,320]{1,0:T(8,128)S(1)}, f32[8,320]{1,0:T(8,128)S(1)}, u32[]{:S(2)}, u32[]{:S(2)}) collective-permute-start(f32[8,320]{1,0:T(8,128)S(1)} %get-tuple-element.25), channel_id=1, source_target_pairs={{0,1},{1,2},{2,3},{3,4},{4,5},{5,6},{6,7},{7,0},{8,9},{9,10},{10,1... | collective-permute-start | bytes 30728 | tf_op jit(solution)/shard_map/ppermute | solution.py:458
  12.2 9.3 %collective-permute-start.1 = (f32[8,320]{1,0:T(8,128)S(1)}, f32[8,320]{1,0:T(8,128)S(1)}, u32[]{:S(2)}, u32[]{:S(2)}) collective-permute-start(f32[8,320]{1,0:T(8,128)S(1)} %get-tuple-element.26), channel_id=1, source_target_pairs={{1,0},{2,1},{3,2},{4,3},{5,4},{6,5},{7,6},{0,7},{9,8},{10,9},{11,1... | collective-permute-start | bytes 30728 | tf_op jit(solution)/shard_map/ppermute | solution.py:458
  25.6 14.6 %all-to-all-start.1 = ((f32[32,5,4,128]{3,2,1,0:T(4,128)}), f32[32,5,4,128]{3,2,1,0:T(4,128)S(1)}, u32[]{:S(2)}, u32[]{:S(2)}) async-start(f32[32,5,4,128]{3,2,1,0:T(4,128)} %get-tuple-element.34), calls=%async_computation.1 | async-start | bytes 655360 | tf_op jit(solution)/shard_map/all_to_all | solution.py:457
  28.2 11.2 %collective-permute-start.2 = (f32[8,320]{1,0:T(8,128)S(1)}, f32[8,320]{1,0:T(8,128)S(1)}, u32[]{:S(2)}, u32[]{:S(2)}) collective-permute-start(f32[8,320]{1,0:T(8,128)S(1)} %get-tuple-element.35), channel_id=1, source_target_pairs={{0,1},{1,2},{2,3},{3,4},{4,5},{5,6},{6,7},{7,0},{8,9},{9,10},{10,1... | collective-permute-start | bytes 30728 | tf_op jit(solution)/shard_map/ppermute | solution.py:458
  29.9 9.5 %collective-permute-start.3 = (f32[8,320]{1,0:T(8,128)S(1)}, f32[8,320]{1,0:T(8,128)S(1)}, u32[]{:S(2)}, u32[]{:S(2)}) collective-permute-start(f32[8,320]{1,0:T(8,128)S(1)} %get-tuple-element.36), channel_id=1, source_target_pairs={{1,0},{2,1},{3,2},{4,3},{5,4},{6,5},{7,6},{0,7},{9,8},{10,9},{11,1... | collective-permute-start | bytes 30728 | tf_op jit(solution)/shard_map/ppermute | solution.py:458
  41.4 9.9 %all-to-all-start.2 = ((f32[32,2,128]{2,1,0:T(2,128)}), f32[32,2,128]{2,1,0:T(2,128)S(1)}, u32[]{:S(2)}, u32[]{:S(2)}) async-start(f32[32,2,128]{2,1,0:T(2,128)} %get-tuple-element.38), calls=%async_computation.2 | async-start | bytes 65536 | tf_op jit(solution)/shard_map/all_to_all | solution.py:470

commit v17 on v15

--- a/solution.py
+++ b/solution.py
@@ -344,7 +344,7 @@
 
 
 def message_order(bodies, peers):
-    return sorted(range(bodies * peers), key=lambda i: i * 0.6180339887 % 1.0)
+    return list(reversed(range(bodies * peers)))
 
 
 def shards(

time: 53.7 us -> 54.5 us (1.015)
  waiting for transfers between devices: 7.41 us -> 8.21 us
    all_to_all x2, waiting for transfers between devices: 2.47 us -> 3.21 us  [exchange(): rows = everyone(rows)]
where the time goes in v17:
time: 54.5 us; the launch traced here: 54 us
  Pallas kernels  23.1 us (42%)
  starting transfers between devices  22 us (40%)
  waiting for transfers between devices  8.21 us (15%)
  between operations  0.69 us (1%)
    all_to_all x2, starting transfers between devices, exchange(): rows = everyone(rows)  9.92 us
    pallas_call x1, Pallas kernels, shards(): first_local(x_here, nbr, coup, source_t, here(fringe_dst), here(fringe_we...  6.25 us
    pallas_call x1, Pallas kernels, shards(): part = local(x, nbr, coup, source_t)  6.15 us
    ppermute x2, starting transfers between devices, exchange(): lax.ppermute(to_down, 'blk', down)  6.04 us
    all_to_all x1, waiting for transfers between devices, shards(): sums = everyone(sums)  4.65 us
    ppermute x2, starting transfers between devices, exchange(): lax.ppermute(to_up, 'blk', up)  3.51 us
    pallas_call x1, Pallas kernels, shards(): advance(part, *arrived, *across, diag, x_here, table, select)  3.24 us
    all_to_all x2, waiting for transfers between devices, exchange(): rows = everyone(rows)  3.21 us
  transfers between devices with their start and end apart: 7, of which 5 were waited for; matrix products, arithmetic and copies ran while one was open for 0% of the time, Pallas kernels for 28%

profile of v17, /device:TPU:0, one launch (start us, length us, event | category | flops | bytes accessed | tf_op | source)
XLA Modules:
  0.0 54.0 jit_solution(9304996169401479191)
XLA Ops:
  0.6 2.4 %shard_map.104 = (f32[32,5,4,128]{3,2,1,0:T(4,128)}, f32[8,320]{1,0:T(8,128)S(1)}, f32[8,320]{1,0:T(8,128)S(1)}, bf16[512,256]{1,0:T(8,128)(2,1)S(1)}, bf16[256,...) custom-call(f32[320,512]{1,0:T(8,128)} %bitcast.13, s32[1,256]{1,0:T(1,128)} %src_ref.1, s32[1,8]{1,0:T(1,128)} %perm_ref.1), custom_call_target="tpu_custom_call" | custom-call | flops 167772160 | bytes 1310720 | tf_op jit(solution)/shard_map/pallas_call | solution.py:456
  3.0 7.3 %all-to-all-start = ((f32[32,5,4,128]{3,2,1,0:T(4,128)}), f32[32,5,4,128]{3,2,1,0:T(4,128)S(1)}, u32[]{:S(2)}, u32[]{:S(2)}) async-start(f32[32,5,4,128]{3,2,1,0:T(4,128)} %get-tuple-element.24), calls=%async_computation | async-start | bytes 655360 | tf_op jit(solution)/shard_map/all_to_all | solution.py:453
  10.4 1.8 %collective-permute-start = (f32[8,320]{1,0:T(8,128)S(1)}, f32[8,320]{1,0:T(8,128)S(1)}, u32[]{:S(2)}, u32[]{:S(2)}) collective-permute-start(f32[8,320]{1,0:T(8,128)S(1)} %get-tuple-element.25), channel_id=1, source_target_pairs={{0,1},{1,2},{2,3},{3,4},{4,5},{5,6},{6,7},{7,0},{8,9},{9,10},{10,1... | collective-permute-start | bytes 30728 | tf_op jit(solution)/shard_map/ppermute | solution.py:454
  12.2 3.0 %collective-permute-start.1 = (f32[8,320]{1,0:T(8,128)S(1)}, f32[8,320]{1,0:T(8,128)S(1)}, u32[]{:S(2)}, u32[]{:S(2)}) collective-permute-start(f32[8,320]{1,0:T(8,128)S(1)} %get-tuple-element.26), channel_id=1, source_target_pairs={{1,0},{2,1},{3,2},{4,3},{5,4},{6,5},{7,6},{0,7},{9,8},{10,9},{11,1... | collective-permute-start | bytes 30728 | tf_op jit(solution)/shard_map/ppermute | solution.py:454
  15.1 6.2 %shard_map.105 = (f32[320,512]{1,0:T(8,128)S(1)}, bf16[5,320,128]{2,1,0:T(8,128)(2,1)S(1)}, s32[16,128]{1,0:T(8,128)S(1)}, bf16[256,512]{1,0:T(8,128)(2,1)S(1)}, f32[1,256]{1,0:T(1,128)S(1)}) custom-call(f32[320,512]{1,0:T(8,128)S(1)} %get-tuple-element.22.x_ref, s32[6,512]{1,0:T(8,128)} %bitcast.15, bf16[6,5,320,512]{3,2,1,0:T(8,128)(2,1)} %bitcast.7, ...), custom_call_target="tpu_custom_call" | custom-call | flops 1006632960 | bytes 12451840 | tf_op jit(solution)/shard_map/pallas_call | solution.py:458
  21.4 0.1 collective-permute-done.lower_ref
  21.5 0.0 collective-permute-done.1.upper_ref
  21.5 1.6 %all-to-all-done.inc_ref = f32[32,5,4,128]{3,2,1,0:T(4,128)S(1)} async-done(((f32[32,5,4,128]{3,2,1,0:T(4,128)}), f32[32,5,4,128]{3,2,1,0:T(4,128)S(1)}, u32[]{:S(2)}, u32[]{:S(2)}) %all-to-all-start) | async-done | bytes 327712 | tf_op jit(solution)/shard_map/all_to_all | solution.py:453
  23.1 3.2 %shard_map.106 = (f32[320,512]{1,0:T(8,128)S(1)}, f32[1,128]{1,0:T(1,128)S(1)}, f32[32,5,4,128]{3,2,1,0:T(4,128)}, f32[8,320]{1,0:T(8,128)S(1)}, f32[8,320]{1,0:T(8,128)S(1)}) custom-call(f32[320,512]{1,0:T(8,128)S(1)} %get-tuple-element.23.local_ref, f32[32,5,4,128]{3,2,1,0:T(4,128)S(1)} %all-to-all-done.inc_ref, ...), custom_call_target="tpu_custom_call" | custom-call | flops 335544320 | bytes 4259840 | tf_op jit(solution)/shard_map/pallas_call | solution.py:462
  26.4 2.6 %all-to-all-start.1 = ((f32[32,5,4,128]{3,2,1,0:T(4,128)}), f32[32,5,4,128]{3,2,1,0:T(4,128)S(1)}, u32[]{:S(2)}, u32[]{:S(2)}) async-start(f32[32,5,4,128]{3,2,1,0:T(4,128)} %get-tuple-element.34), calls=%async_computation.1 | async-start | bytes 655360 | tf_op jit(solution)/shard_map/all_to_all | solution.py:453
  29.0 1.7 %collective-permute-start.2 = (f32[8,320]{1,0:T(8,128)S(1)}, f32[8,320]{1,0:T(8,128)S(1)}, u32[]{:S(2)}, u32[]{:S(2)}) collective-permute-start(f32[8,320]{1,0:T(8,128)S(1)} %get-tuple-element.35), channel_id=1, source_target_pairs={{0,1},{1,2},{2,3},{3,4},{4,5},{5,6},{6,7},{7,0},{8,9},{9,10},{10,1... | collective-permute-start | bytes 30728 | tf_op jit(solution)/shard_map/ppermute | solution.py:454
  30.7 3.1 %collective-permute-start.3 = (f32[8,320]{1,0:T(8,128)S(1)}, f32[8,320]{1,0:T(8,128)S(1)}, u32[]{:S(2)}, u32[]{:S(2)}) collective-permute-start(f32[8,320]{1,0:T(8,128)S(1)} %get-tuple-element.36), channel_id=1, source_target_pairs={{1,0},{2,1},{3,2},{4,3},{5,4},{6,5},{7,6},{0,7},{9,8},{10,9},{11,1... | collective-permute-start | bytes 30728 | tf_op jit(solution)/shard_map/ppermute | solution.py:454
  33.8 6.2 %shard_map.107.local_ref = f32[320,512]{1,0:T(8,128)S(1)} custom-call(f32[320,512]{1,0:T(8,128)S(1)} %get-tuple-element.33.x_ref, s32[6,512]{1,0:T(8,128)} %bitcast.16, bf16[6,5,320,512]{3,2,1,0:T(8,128)(2,1)} %bitcast.8, f32[320,512]{1,0:T(8,128)} %bitcast.12), custom_call_target="tpu_custom_call" | custom-call | flops 1006632960 | bytes 12451840 | tf_op jit(solution)/shard_map/pallas_call | solution.py:464
  39.9 0.2 collective-permute-done.2.lower_ref
  40.2 0.0 collective-permute-done.3.upper_ref
  40.2 1.6 %all-to-all-done.1.inc_ref = f32[32,5,4,128]{3,2,1,0:T(4,128)S(1)} async-done(((f32[32,5,4,128]{3,2,1,0:T(4,128)}), f32[32,5,4,128]{3,2,1,0:T(4,128)S(1)}, u32[]{:S(2)}, u32[]{:S(2)}) %all-to-all-start.1) | async-done | bytes 327712 | tf_op jit(solution)/shard_map/all_to_all | solution.py:453
  41.8 1.3 %shard_map.108 = (f32[320,512]{1,0:T(8,128)S(1)}, f32[32,2,128]{2,1,0:T(2,128)}) custom-call(f32[320,512]{1,0:T(8,128)S(1)} %shard_map.107.local_ref, f32[32,5,4,128]{3,2,1,0:T(4,128)S(1)} %all-to-all-done.1.inc_ref, f32[8,320]{1,0:T(8,128)S(1)} %collective-permute-done.2.lower_ref, f32[8,320]{1,0:T(8,128)S(1)} %collective-permute-done.3.upper_ref, ...), custom_call_target="tpu_custom_call" | custom-call | flops 167772160 | bytes 1966080 | tf_op jit(solution)/shard_map/pallas_call | solution.py:465
  43.1 2.6 %all-to-all-start.2 = ((f32[32,2,128]{2,1,0:T(2,128)}), f32[32,2,128]{2,1,0:T(2,128)S(1)}, u32[]{:S(2)}, u32[]{:S(2)}) async-start(f32[32,2,128]{2,1,0:T(2,128)} %get-tuple-element.38), calls=%async_computation.2 | async-start | bytes 65536 | tf_op jit(solution)/shard_map/all_to_all | solution.py:466
  45.6 2.6 %shard_map.109 = (f32[320,512]{1,0:T(8,128)S(1)}, f32[320,512]{1,0:T(8,128)}) custom-call(bf16[5,320,512]{2,1,0:T(8,128)(2,1)} %bitcast.10, f32[320,512]{1,0:T(8,128)S(1)} %get-tuple-element.39.resid_ref), custom_call_target="tpu_custom_call" | custom-call | flops 1638400 | bytes 2949120 | tf_op jit(solution)/shard_map/pallas_call | solution.py:467
  48.3 4.6 %all-to-all-done.2.sums_ref = f32[32,2,128]{2,1,0:T(2,128)S(1)} async-done(((f32[32,2,128]{2,1,0:T(2,128)}), f32[32,2,128]{2,1,0:T(2,128)S(1)}, u32[]{:S(2)}, u32[]{:S(2)}) %all-to-all-start.2) | async-done | bytes 32800 | tf_op jit(solution)/shard_map/all_to_all | solution.py:466
  52.9 1.1 %shard_map.110 = f32[320,512]{1,0:T(8,128)} custom-call(f32[32,2,128]{2,1,0:T(2,128)S(1)} %all-to-all-done.2.sums_ref, f32[320,512]{1,0:T(8,128)S(1)} %get-tuple-element.33.x_ref, f32[320,512]{1,0:T(8,128)S(1)} %get-tuple-element.40.update_ref), custom_call_target="tpu_custom_call" | custom-call | flops 327680 | bytes 1966080 | tf_op jit(solution)/shard_map/pallas_call | solution.py:468
Async XLA Ops:
  3.0 20.1 %all-to-all-start = ((f32[32,5,4,128]{3,2,1,0:T(4,128)}), f32[32,5,4,128]{3,2,1,0:T(4,128)S(1)}, u32[]{:S(2)}, u32[]{:S(2)}) async-start(f32[32,5,4,128]{3,2,1,0:T(4,128)} %get-tuple-element.24), calls=%async_computation | async-start | bytes 655360 | tf_op jit(solution)/shard_map/all_to_all | solution.py:453
  10.4 11.2 %collective-permute-start = (f32[8,320]{1,0:T(8,128)S(1)}, f32[8,320]{1,0:T(8,128)S(1)}, u32[]{:S(2)}, u32[]{:S(2)}) collective-permute-start(f32[8,320]{1,0:T(8,128)S(1)} %get-tuple-element.25), channel_id=1, source_target_pairs={{0,1},{1,2},{2,3},{3,4},{4,5},{5,6},{6,7},{7,0},{8,9},{9,10},{10,1... | collective-permute-start | bytes 30728 | tf_op jit(solution)/shard_map/ppermute | solution.py:454
  12.2 9.3 %collective-permute-start.1 = (f32[8,320]{1,0:T(8,128)S(1)}, f32[8,320]{1,0:T(8,128)S(1)}, u32[]{:S(2)}, u32[]{:S(2)}) collective-permute-start(f32[8,320]{1,0:T(8,128)S(1)} %get-tuple-element.26), channel_id=1, source_target_pairs={{1,0},{2,1},{3,2},{4,3},{5,4},{6,5},{7,6},{0,7},{9,8},{10,9},{11,1... | collective-permute-start | bytes 30728 | tf_op jit(solution)/shard_map/ppermute | solution.py:454
  26.4 15.4 %all-to-all-start.1 = ((f32[32,5,4,128]{3,2,1,0:T(4,128)}), f32[32,5,4,128]{3,2,1,0:T(4,128)S(1)}, u32[]{:S(2)}, u32[]{:S(2)}) async-start(f32[32,5,4,128]{3,2,1,0:T(4,128)} %get-tuple-element.34), calls=%async_computation.1 | async-start | bytes 655360 | tf_op jit(solution)/shard_map/all_to_all | solution.py:453
  29.0 11.2 %collective-permute-start.2 = (f32[8,320]{1,0:T(8,128)S(1)}, f32[8,320]{1,0:T(8,128)S(1)}, u32[]{:S(2)}, u32[]{:S(2)}) collective-permute-start(f32[8,320]{1,0:T(8,128)S(1)} %get-tuple-element.35), channel_id=1, source_target_pairs={{0,1},{1,2},{2,3},{3,4},{4,5},{5,6},{6,7},{7,0},{8,9},{9,10},{10,1... | collective-permute-start | bytes 30728 | tf_op jit(solution)/shard_map/ppermute | solution.py:454
  30.7 9.5 %collective-permute-start.3 = (f32[8,320]{1,0:T(8,128)S(1)}, f32[8,320]{1,0:T(8,128)S(1)}, u32[]{:S(2)}, u32[]{:S(2)}) collective-permute-start(f32[8,320]{1,0:T(8,128)S(1)} %get-tuple-element.36), channel_id=1, source_target_pairs={{1,0},{2,1},{3,2},{4,3},{5,4},{6,5},{7,6},{0,7},{9,8},{10,9},{11,1... | collective-permute-start | bytes 30728 | tf_op jit(solution)/shard_map/ppermute | solution.py:454
  43.1 9.9 %all-to-all-start.2 = ((f32[32,2,128]{2,1,0:T(2,128)}), f32[32,2,128]{2,1,0:T(2,128)S(1)}, u32[]{:S(2)}, u32[]{:S(2)}) async-start(f32[32,2,128]{2,1,0:T(2,128)} %get-tuple-element.38), calls=%async_computation.2 | async-start | bytes 65536 | tf_op jit(solution)/shard_map/all_to_all | solution.py:466

commit v18 on v16

--- a/solution.py
+++ b/solution.py
@@ -346,7 +346,7 @@
 def message_order(bodies, peers):
     middle = peers // 2
     far_first = sorted(range(peers), key=lambda k: -abs(2 * k + 1 - peers))
-    order = [b * peers + k for b in range(bodies) for k in far_first]
+    order = [(j + i) % bodies * peers + k for j in reversed(range(bodies)) for i, k in enumerate(far_first)]
     order.remove(middle)
     return [middle, *order]
 

time: 52.9 us -> 52.5 us (level)
  no operation moved by 1% of the time
where the time goes in v18:
time: 52.5 us; the launch traced here: 52 us
  Pallas kernels  23.1 us (44%)
  starting transfers between devices  22.1 us (42%)
  waiting for transfers between devices  6.18 us (12%)
  between operations  0.69 us (1%)
    all_to_all x2, starting transfers between devices, exchange(): rows = everyone(rows)  9.93 us
    pallas_call x1, Pallas kernels, shards(): first_local(x_here, nbr, coup, source_t, here(fringe_dst), here(fringe_we...  6.25 us
    pallas_call x1, Pallas kernels, shards(): part = local(x, nbr, coup, source_t)  6.15 us
    ppermute x2, starting transfers between devices, exchange(): lax.ppermute(to_down, 'blk', down)  5.91 us
    all_to_all x1, waiting for transfers between devices, shards(): sums = everyone(sums)  4.49 us
    ppermute x2, starting transfers between devices, exchange(): lax.ppermute(to_up, 'blk', up)  3.64 us
    pallas_call x1, Pallas kernels, shards(): advance(part, *arrived, *across, diag, x_here, table, select)  3.23 us
    pallas_call x1, Pallas kernels, shards(): update, resid = direction(diag, resid)  2.64 us
  transfers between devices with their start and end apart: 7, of which 5 were waited for; matrix products, arithmetic and copies ran while one was open for 0% of the time, Pallas kernels for 29%

profile of v18, /device:TPU:0, one launch (start us, length us, event | category | flops | bytes accessed | tf_op | source)
XLA Modules:
  0.0 52.0 jit_solution(9690889675894664700)
XLA Ops:
  0.6 2.4 %shard_map.104 = (f32[32,5,4,128]{3,2,1,0:T(4,128)}, f32[8,320]{1,0:T(8,128)S(1)}, f32[8,320]{1,0:T(8,128)S(1)}, bf16[512,256]{1,0:T(8,128)(2,1)S(1)}, bf16[256,...) custom-call(f32[320,512]{1,0:T(8,128)} %bitcast.13, s32[1,256]{1,0:T(1,128)} %src_ref.1, s32[1,8]{1,0:T(1,128)} %perm_ref.1), custom_call_target="tpu_custom_call" | custom-call | flops 167772160 | bytes 1310720 | tf_op jit(solution)/shard_map/pallas_call | solution.py:460
  3.0 7.3 %all-to-all-start = ((f32[32,5,4,128]{3,2,1,0:T(4,128)}), f32[32,5,4,128]{3,2,1,0:T(4,128)S(1)}, u32[]{:S(2)}, u32[]{:S(2)}) async-start(f32[32,5,4,128]{3,2,1,0:T(4,128)} %get-tuple-element.24), calls=%async_computation | async-start | bytes 655360 | tf_op jit(solution)/shard_map/all_to_all | solution.py:457
  10.3 1.8 %collective-permute-start = (f32[8,320]{1,0:T(8,128)S(1)}, f32[8,320]{1,0:T(8,128)S(1)}, u32[]{:S(2)}, u32[]{:S(2)}) collective-permute-start(f32[8,320]{1,0:T(8,128)S(1)} %get-tuple-element.25), channel_id=1, source_target_pairs={{0,1},{1,2},{2,3},{3,4},{4,5},{5,6},{6,7},{7,0},{8,9},{9,10},{10,1... | collective-permute-start | bytes 30728 | tf_op jit(solution)/shard_map/ppermute | solution.py:458
  12.2 3.0 %collective-permute-start.1 = (f32[8,320]{1,0:T(8,128)S(1)}, f32[8,320]{1,0:T(8,128)S(1)}, u32[]{:S(2)}, u32[]{:S(2)}) collective-permute-start(f32[8,320]{1,0:T(8,128)S(1)} %get-tuple-element.26), channel_id=1, source_target_pairs={{1,0},{2,1},{3,2},{4,3},{5,4},{6,5},{7,6},{0,7},{9,8},{10,9},{11,1... | collective-permute-start | bytes 30728 | tf_op jit(solution)/shard_map/ppermute | solution.py:458
  15.1 6.3 %shard_map.105 = (f32[320,512]{1,0:T(8,128)S(1)}, bf16[5,320,128]{2,1,0:T(8,128)(2,1)S(1)}, s32[16,128]{1,0:T(8,128)S(1)}, bf16[256,512]{1,0:T(8,128)(2,1)S(1)}, f32[1,256]{1,0:T(1,128)S(1)}) custom-call(f32[320,512]{1,0:T(8,128)S(1)} %get-tuple-element.22.x_ref, s32[6,512]{1,0:T(8,128)} %bitcast.15, bf16[6,5,320,512]{3,2,1,0:T(8,128)(2,1)} %bitcast.7, ...), custom_call_target="tpu_custom_call" | custom-call | flops 1006632960 | bytes 12451840 | tf_op jit(solution)/shard_map/pallas_call | solution.py:462
  21.4 0.1 collective-permute-done.lower_ref
  21.5 0.0 collective-permute-done.1.upper_ref
  21.5 0.7 %all-to-all-done.inc_ref = f32[32,5,4,128]{3,2,1,0:T(4,128)S(1)} async-done(((f32[32,5,4,128]{3,2,1,0:T(4,128)}), f32[32,5,4,128]{3,2,1,0:T(4,128)S(1)}, u32[]{:S(2)}, u32[]{:S(2)}) %all-to-all-start) | async-done | bytes 327712 | tf_op jit(solution)/shard_map/all_to_all | solution.py:457
  22.2 3.2 %shard_map.106 = (f32[320,512]{1,0:T(8,128)S(1)}, f32[1,128]{1,0:T(1,128)S(1)}, f32[32,5,4,128]{3,2,1,0:T(4,128)}, f32[8,320]{1,0:T(8,128)S(1)}, f32[8,320]{1,0:T(8,128)S(1)}) custom-call(f32[320,512]{1,0:T(8,128)S(1)} %get-tuple-element.23.local_ref, f32[32,5,4,128]{3,2,1,0:T(4,128)S(1)} %all-to-all-done.inc_ref, ...), custom_call_target="tpu_custom_call" | custom-call | flops 335544320 | bytes 4259840 | tf_op jit(solution)/shard_map/pallas_call | solution.py:466
  25.4 2.6 %all-to-all-start.1 = ((f32[32,5,4,128]{3,2,1,0:T(4,128)}), f32[32,5,4,128]{3,2,1,0:T(4,128)S(1)}, u32[]{:S(2)}, u32[]{:S(2)}) async-start(f32[32,5,4,128]{3,2,1,0:T(4,128)} %get-tuple-element.34), calls=%async_computation.1 | async-start | bytes 655360 | tf_op jit(solution)/shard_map/all_to_all | solution.py:457
  28.1 1.8 %collective-permute-start.2 = (f32[8,320]{1,0:T(8,128)S(1)}, f32[8,320]{1,0:T(8,128)S(1)}, u32[]{:S(2)}, u32[]{:S(2)}) collective-permute-start(f32[8,320]{1,0:T(8,128)S(1)} %get-tuple-element.35), channel_id=1, source_target_pairs={{0,1},{1,2},{2,3},{3,4},{4,5},{5,6},{6,7},{7,0},{8,9},{9,10},{10,1... | collective-permute-start | bytes 30728 | tf_op jit(solution)/shard_map/ppermute | solution.py:458
  29.9 3.0 %collective-permute-start.3 = (f32[8,320]{1,0:T(8,128)S(1)}, f32[8,320]{1,0:T(8,128)S(1)}, u32[]{:S(2)}, u32[]{:S(2)}) collective-permute-start(f32[8,320]{1,0:T(8,128)S(1)} %get-tuple-element.36), channel_id=1, source_target_pairs={{1,0},{2,1},{3,2},{4,3},{5,4},{6,5},{7,6},{0,7},{9,8},{10,9},{11,1... | collective-permute-start | bytes 30728 | tf_op jit(solution)/shard_map/ppermute | solution.py:458
  32.8 6.2 %shard_map.107.local_ref = f32[320,512]{1,0:T(8,128)S(1)} custom-call(f32[320,512]{1,0:T(8,128)S(1)} %get-tuple-element.33.x_ref, s32[6,512]{1,0:T(8,128)} %bitcast.16, bf16[6,5,320,512]{3,2,1,0:T(8,128)(2,1)} %bitcast.8, f32[320,512]{1,0:T(8,128)} %bitcast.12), custom_call_target="tpu_custom_call" | custom-call | flops 1006632960 | bytes 12451840 | tf_op jit(solution)/shard_map/pallas_call | solution.py:468
  39.0 0.2 collective-permute-done.2.lower_ref
  39.2 0.0 collective-permute-done.3.upper_ref
  39.2 0.7 %all-to-all-done.1.inc_ref = f32[32,5,4,128]{3,2,1,0:T(4,128)S(1)} async-done(((f32[32,5,4,128]{3,2,1,0:T(4,128)}), f32[32,5,4,128]{3,2,1,0:T(4,128)S(1)}, u32[]{:S(2)}, u32[]{:S(2)}) %all-to-all-start.1) | async-done | bytes 327712 | tf_op jit(solution)/shard_map/all_to_all | solution.py:457
  39.9 1.3 %shard_map.108 = (f32[320,512]{1,0:T(8,128)S(1)}, f32[32,2,128]{2,1,0:T(2,128)}) custom-call(f32[320,512]{1,0:T(8,128)S(1)} %shard_map.107.local_ref, f32[32,5,4,128]{3,2,1,0:T(4,128)S(1)} %all-to-all-done.1.inc_ref, f32[8,320]{1,0:T(8,128)S(1)} %collective-permute-done.2.lower_ref, f32[8,320]{1,0:T(8,128)S(1)} %collective-permute-done.3.upper_ref, ...), custom_call_target="tpu_custom_call" | custom-call | flops 167772160 | bytes 1966080 | tf_op jit(solution)/shard_map/pallas_call | solution.py:469
  41.2 2.6 %all-to-all-start.2 = ((f32[32,2,128]{2,1,0:T(2,128)}), f32[32,2,128]{2,1,0:T(2,128)S(1)}, u32[]{:S(2)}, u32[]{:S(2)}) async-start(f32[32,2,128]{2,1,0:T(2,128)} %get-tuple-element.38), calls=%async_computation.2 | async-start | bytes 65536 | tf_op jit(solution)/shard_map/all_to_all | solution.py:470
  43.8 2.6 %shard_map.109 = (f32[320,512]{1,0:T(8,128)S(1)}, f32[320,512]{1,0:T(8,128)}) custom-call(bf16[5,320,512]{2,1,0:T(8,128)(2,1)} %bitcast.10, f32[320,512]{1,0:T(8,128)S(1)} %get-tuple-element.39.resid_ref), custom_call_target="tpu_custom_call" | custom-call | flops 1638400 | bytes 2949120 | tf_op jit(solution)/shard_map/pallas_call | solution.py:471
  46.5 4.5 %all-to-all-done.2.sums_ref = f32[32,2,128]{2,1,0:T(2,128)S(1)} async-done(((f32[32,2,128]{2,1,0:T(2,128)}), f32[32,2,128]{2,1,0:T(2,128)S(1)}, u32[]{:S(2)}, u32[]{:S(2)}) %all-to-all-start.2) | async-done | bytes 32800 | tf_op jit(solution)/shard_map/all_to_all | solution.py:470
  50.9 1.1 %shard_map.110 = f32[320,512]{1,0:T(8,128)} custom-call(f32[32,2,128]{2,1,0:T(2,128)S(1)} %all-to-all-done.2.sums_ref, f32[320,512]{1,0:T(8,128)S(1)} %get-tuple-element.33.x_ref, f32[320,512]{1,0:T(8,128)S(1)} %get-tuple-element.40.update_ref), custom_call_target="tpu_custom_call" | custom-call | flops 327680 | bytes 1966080 | tf_op jit(solution)/shard_map/pallas_call | solution.py:472
Async XLA Ops:
  3.0 19.1 %all-to-all-start = ((f32[32,5,4,128]{3,2,1,0:T(4,128)}), f32[32,5,4,128]{3,2,1,0:T(4,128)S(1)}, u32[]{:S(2)}, u32[]{:S(2)}) async-start(f32[32,5,4,128]{3,2,1,0:T(4,128)} %get-tuple-element.24), calls=%async_computation | async-start | bytes 655360 | tf_op jit(solution)/shard_map/all_to_all | solution.py:457
  10.3 11.2 %collective-permute-start = (f32[8,320]{1,0:T(8,128)S(1)}, f32[8,320]{1,0:T(8,128)S(1)}, u32[]{:S(2)}, u32[]{:S(2)}) collective-permute-start(f32[8,320]{1,0:T(8,128)S(1)} %get-tuple-element.25), channel_id=1, source_target_pairs={{0,1},{1,2},{2,3},{3,4},{4,5},{5,6},{6,7},{7,0},{8,9},{9,10},{10,1... | collective-permute-start | bytes 30728 | tf_op jit(solution)/shard_map/ppermute | solution.py:458
  12.2 9.3 %collective-permute-start.1 = (f32[8,320]{1,0:T(8,128)S(1)}, f32[8,320]{1,0:T(8,128)S(1)}, u32[]{:S(2)}, u32[]{:S(2)}) collective-permute-start(f32[8,320]{1,0:T(8,128)S(1)} %get-tuple-element.26), channel_id=1, source_target_pairs={{1,0},{2,1},{3,2},{4,3},{5,4},{6,5},{7,6},{0,7},{9,8},{10,9},{11,1... | collective-permute-start | bytes 30728 | tf_op jit(solution)/shard_map/ppermute | solution.py:458
  25.4 14.5 %all-to-all-start.1 = ((f32[32,5,4,128]{3,2,1,0:T(4,128)}), f32[32,5,4,128]{3,2,1,0:T(4,128)S(1)}, u32[]{:S(2)}, u32[]{:S(2)}) async-start(f32[32,5,4,128]{3,2,1,0:T(4,128)} %get-tuple-element.34), calls=%async_computation.1 | async-start | bytes 655360 | tf_op jit(solution)/shard_map/all_to_all | solution.py:457
  28.1 11.2 %collective-permute-start.2 = (f32[8,320]{1,0:T(8,128)S(1)}, f32[8,320]{1,0:T(8,128)S(1)}, u32[]{:S(2)}, u32[]{:S(2)}) collective-permute-start(f32[8,320]{1,0:T(8,128)S(1)} %get-tuple-element.35), channel_id=1, source_target_pairs={{0,1},{1,2},{2,3},{3,4},{4,5},{5,6},{6,7},{7,0},{8,9},{9,10},{10,1... | collective-permute-start | bytes 30728 | tf_op jit(solution)/shard_map/ppermute | solution.py:458
  29.9 9.3 %collective-permute-start.3 = (f32[8,320]{1,0:T(8,128)S(1)}, f32[8,320]{1,0:T(8,128)S(1)}, u32[]{:S(2)}, u32[]{:S(2)}) collective-permute-start(f32[8,320]{1,0:T(8,128)S(1)} %get-tuple-element.36), channel_id=1, source_target_pairs={{1,0},{2,1},{3,2},{4,3},{5,4},{6,5},{7,6},{0,7},{9,8},{10,9},{11,1... | collective-permute-start | bytes 30728 | tf_op jit(solution)/shard_map/ppermute | solution.py:458
  41.2 9.7 %all-to-all-start.2 = ((f32[32,2,128]{2,1,0:T(2,128)}), f32[32,2,128]{2,1,0:T(2,128)S(1)}, u32[]{:S(2)}, u32[]{:S(2)}) async-start(f32[32,2,128]{2,1,0:T(2,128)} %get-tuple-element.38), calls=%async_computation.2 | async-start | bytes 65536 | tf_op jit(solution)/shard_map/all_to_all | solution.py:470
